TPU v7x, 512 devices: a whole 4x4x16 slice. The times are simulated.
512 devices in a mesh: section: 8 (over z_hi, x), dp: 8 (over y, core), tensor: 8 (over z_lo).
Axes of the slice: x: 4, y: 4, z: 16 (z_hi: 2, z_lo: 8; z = z_hi * 8 + z_lo), core: 2. Of those that a mesh axis runs over, the one named last changes fastest.
Arguments:
- hidden: bfloat16 [8, 1280, 8192], P('section', 'dp', 'tensor'), may hold values from -6 to 6
- w_query: bfloat16 [8, 8192, 4096], P('section', 'dp', 'tensor'), may hold values from -0.0625 to 0.0625
- key_weight_stack: bfloat16 [8, 8192, 1024], P('section', 'tensor', 'dp'), may hold values from -0.0625 to 0.0625
- value_weight_stack: bfloat16 [8, 8192, 1024], P('section', 'tensor', 'dp'), may hold values from -0.0625 to 0.0625
- image_tokens: bfloat16 [8, 128, 8192], P('dp', 'section', 'tensor'), may hold values from -6 to 6
- score_bias: float32 [1280, 128], P('dp'), may hold values from -4 to 404, as said below
- gate_logit: float32 [8], P('section'), may hold values from 0.3 to 1.5
- cotangent: bfloat16 [8, 1280, 4096], P('section', 'dp', 'tensor'), may hold values from -48 to 48
Outputs:
- gated_output: bfloat16 [8, 1280, 4096], P('section', 'dp', 'tensor')
- image_grad: float32 [8, 128, 8192], P('dp', 'section', 'tensor')
Inputs may be any that keep to these rules, and one draw needn't show every extreme that they name: `score_bias`: additive bias on the attention scores of each text token and image token.
All inputs are finite; a program needn't handle non-finite values.
Results may differ from a plain program's by a relative error of at most 0.0079.
Values may be sent and summed in bfloat16 or wider, within the bound.
No kernel may reach another device: no remote copies, remote signals or barrier semaphores. Data moves between devices by JAX's collectives and lax.ppermute only.
A program may use at most 64 MiB of HBM per device.

v0:
```python
import jax
import jax.numpy as jnp
from jax import lax
from jax.sharding import PartitionSpec as P

QUERY_HEADS = 32
KEY_VALUE_HEADS = 8
HEAD_SIZE = 128


def local(
    hidden,
    w_query,
    key_weight_stack,
    value_weight_stack,
    image_tokens,
    score_bias,
    gate_logit,
    cotangent,
):
    tok_rows = hidden.shape[1]
    columns = w_query.shape[2]
    query_group_size = QUERY_HEADS // KEY_VALUE_HEADS
    local_heads = columns // HEAD_SIZE // query_group_size
    scaling = HEAD_SIZE ** (-0.5)
    features = lax.all_gather(hidden[0], "tensor", axis=1, tiled=True)
    query_input = jnp.dot(
        features,
        lax.all_gather(w_query[0], "dp", axis=0, tiled=True),
        preferred_element_type=jnp.float32,
    )
    query_input = query_input.astype(jnp.bfloat16).reshape(
        tok_rows, local_heads, query_group_size, HEAD_SIZE
    )
    image_rows = lax.all_gather(image_tokens[0], "section", axis=0, tiled=True)
    image_count = image_rows.shape[0]
    key_cols, value_cols = (
        lax.all_gather(key_weight_stack[0], "dp", axis=1, tiled=True),
        lax.all_gather(value_weight_stack[0], "dp", axis=1, tiled=True),
    )
    key_portion = jnp.dot(image_rows, key_cols, preferred_element_type=jnp.float32).reshape(
        image_count, KEY_VALUE_HEADS, 1, HEAD_SIZE
    )
    value_portion = jnp.dot(image_rows, value_cols, preferred_element_type=jnp.float32).reshape(
        image_count, KEY_VALUE_HEADS, 1, HEAD_SIZE
    )
    joined_rows = jnp.concatenate([key_portion, value_portion], axis=2).reshape(
        image_count, KEY_VALUE_HEADS * 2 * HEAD_SIZE
    )
    own_pairs = lax.psum_scatter(joined_rows, "tensor", scatter_dimension=1, tiled=True)
    own_pairs = own_pairs.astype(jnp.bfloat16).reshape(image_count, local_heads, 2, HEAD_SIZE)
    keys = own_pairs[:, :, 0]
    values = own_pairs[:, :, 1]
    scores = (
        jnp.einsum("tkgh,ikh->kgti", query_input, keys, preferred_element_type=jnp.float32)
        * scaling
    )
    scores = scores + score_bias[None, None]
    row_max = jnp.max(scores, axis=-1, keepdims=True)
    exponent = jnp.exp(scores - row_max)
    attn_weights = exponent / jnp.sum(exponent, axis=-1, keepdims=True)
    weights_low = attn_weights.astype(jnp.bfloat16)
    attended = jnp.einsum("kgti,ikh->tkgh", weights_low, values, preferred_element_type=jnp.float32)
    scale_factor = jnp.tanh(gate_logit[0])
    gated_out = (scale_factor * attended).astype(jnp.bfloat16).reshape(1, tok_rows, columns)
    attended_gradient = (scale_factor * cotangent[0].astype(jnp.float32)).astype(jnp.bfloat16)
    attended_gradient = attended_gradient.reshape(
        tok_rows, local_heads, query_group_size, HEAD_SIZE
    )
    value_gradient = jnp.einsum(
        "kgti,tkgh->ikh", weights_low, attended_gradient, preferred_element_type=jnp.float32
    ).astype(jnp.bfloat16)
    grad_weights = jnp.einsum(
        "tkgh,ikh->kgti", attended_gradient, values, preferred_element_type=jnp.float32
    )
    grad_scores = attn_weights * (
        grad_weights - jnp.sum(attn_weights * grad_weights, axis=-1, keepdims=True)
    )
    grad_low = grad_scores.astype(jnp.bfloat16)
    key_gradient = (
        jnp.einsum("kgti,tkgh->ikh", grad_low, query_input, preferred_element_type=jnp.float32)
        * scaling
    )
    key_gradient = key_gradient.astype(jnp.bfloat16)
    packed_rows = jnp.stack([key_gradient, value_gradient], axis=2).reshape(
        image_count, local_heads * 2 * HEAD_SIZE
    )
    every_gradient = lax.all_gather(packed_rows, "tensor", axis=1, tiled=True).reshape(
        image_count, KEY_VALUE_HEADS, 2, HEAD_SIZE
    )
    key_gradients = every_gradient[:, :, 0].reshape(image_count, KEY_VALUE_HEADS * HEAD_SIZE)
    value_gradients = every_gradient[:, :, 1].reshape(image_count, KEY_VALUE_HEADS * HEAD_SIZE)
    contract = (((1,), (1,)), ((), ()))
    partial_grad = lax.dot_general(
        key_gradients, key_cols, contract, preferred_element_type=jnp.float32
    )
    partial_grad = partial_grad + lax.dot_general(
        value_gradients, value_cols, contract, preferred_element_type=jnp.float32
    )
    image_grad = lax.psum_scatter(partial_grad, "section", scatter_dimension=0, tiled=True)
    return (gated_out, image_grad[None])


def solution(mesh):
    in_specs = (
        P("section", "dp", "tensor"),
        P("section", "dp", "tensor"),
        P("section", "tensor", "dp"),
        P("section", "tensor", "dp"),
        P("dp", "section", "tensor"),
        P("dp", None),
        P("section"),
        P("section", "dp", "tensor"),
    )
    out_specs = (P("section", "dp", "tensor"), P("dp", "section", "tensor"))
    return jax.shard_map(local, mesh=mesh, in_specs=in_specs, out_specs=out_specs, check_vma=False)
```

profile of v0, /device:TPU:24, one launch (start us, length us, event | category | flops | bytes accessed | tf_op | source)
XLA Modules:
  0.0 464.6 jit_solution(17802530231776293217)
XLA Ops:
  7.2 0.0 all-gather.12.cloned.1.call-start
  7.2 0.7 all-gather.12.cloned.1.call-update
  7.9 0.0 all-gather.10.cloned.1.call-start
  7.9 0.7 all-gather.10.cloned.1.call-update
  8.6 0.0 reduce-scatter.3.cloned.1.call-start
  8.7 67.6 %all-gather = bf16[1,128,1024]{2,1,0:T(8,128)(2,1)S(1)} all-gather(bf16[1,16,1024]{2,1,0:T(8,128)(2,1)} %param.12), channel_id=2, replica_groups=mesh['section'=8,'dp'=8,'tensor'=8] {'section'}, dimensions={1}, use_global_device_ids=true | all-gather | bytes 294912 | tf_op jit(solution)/shard_map/all_gather | solution.py:35
  76.3 0.0 all-gather.12.cloned.1.call-done
  76.3 2.5 fusion.5
  78.8 7.9 %all-gather.10.cloned.1.call-done = bf16[1,1024,1024]{2,1,0:T(8,128)(2,1)} async-done(((bf16[1,1024,128]{2,1,0:T(8,128)(2,1)}), bf16[1,1024,1024]{2,1,0:T(8,128)(2,1)}) %all-gather.10.cloned.1.call-update) | async-done | bytes 2097168 | tf_op jit(solution)/shard_map/all_gather | solution.py:38
  86.7 2.5 fusion.9
  89.3 0.0 copy-start.2
  89.3 1.1 pad_maximum_fusion
  90.4 0.0 reduce-scatter.3.cloned.1.call-update
  90.4 0.0 all-gather.14.cloned.1.call-start
  90.4 0.5 all-gather.14.cloned.1.call-update
  91.0 0.0 all-gather.16.cloned.1.call-start
  91.0 0.5 all-gather.16.cloned.1.call-update
  91.6 0.0 reduce-scatter.5.cloned.1.call-start
  92.3 0.0 copy-done.2
  92.4 67.6 %reduce-scatter.3.cloned.1.call-done = f32[128,256]{0,1:T(8,128)} async-done(((f32[128,2048]{0,1:T(8,128)}), f32[128,256]{0,1:T(8,128)}) %reduce-scatter.3.cloned.1.call-update) | async-done | bytes 131088 | tf_op jit(solution)/shard_map/reduce_scatter | solution.py:50
  160.0 0.9 convert_element_type.57
  160.9 0.0 copy-start.3
  160.9 69.1 %all-gather.14.cloned.1.call-done = bf16[1,160,8192]{2,1,0:T(8,128)(2,1)} async-done(((bf16[1,160,1024]{2,1,0:T(8,128)(2,1)}), bf16[1,160,8192]{2,1,0:T(8,128)(2,1)}) %all-gather.14.cloned.1.call-update) | async-done | bytes 2621456 | tf_op jit(solution)/shard_map/all_gather | solution.py:26
  230.1 53.9 %all-gather.16.cloned.1.call-done = bf16[1,8192,512]{2,1,0:T(8,128)(2,1)} async-done(((bf16[1,1024,512]{2,1,0:T(8,128)(2,1)}), bf16[1,8192,512]{2,1,0:T(8,128)(2,1)}) %all-gather.16.cloned.1.call-update) | async-done | bytes 8388624 | tf_op jit(solution)/shard_map/all_gather | solution.py:29
  284.0 5.7 %fusion.22 = bf16[20,4,8,128]{3,2,1,0:T(8,128)(2,1)S(1)} fusion(bf16[1,8192,512]{2,1,0:T(8,128)(2,1)} %all-gather.16.cloned.1.call-done, bf16[1,160,8192]{2,1,0:T(8,128)(2,1)} %all-gather.14.cloned.1.call-done), kind=kOutput, calls=%fused_computation.19 | convolution fusion | flops 1342259200 | bytes 11173888 | tf_op jit(solution)/shard_map/dot_general | solution.py:27
  289.7 0.0 copy-done.3
  289.7 0.4 fusion.54
  290.1 0.4 fusion.34
  290.5 0.4 fusion.31
  290.9 0.5 multiply_reduce_fusion
  291.4 0.0 copy-start
  291.4 0.5 fusion.32
  291.9 48.4 %all_gather.23 = bf16[128,2048]{0,1:T(8,128)(2,1)S(1)} all-gather(bf16[128,256]{0,1:T(8,128)(2,1)S(1)} %bitcast.126), channel_id=1, replica_groups=mesh['section'=8,'dp'=8,'tensor'=8] {'tensor'}, dimensions={1}, use_global_device_ids=true | all-gather | bytes 589824 | tf_op jit(solution)/shard_map/all_gather | solution.py:88
  340.4 0.0 copy-start.1
  340.4 0.0 copy-done
  340.4 0.8 fusion.3
  341.2 0.7 copy-done.1
  341.9 1.6 fusion.11
  343.6 0.0 reduce-scatter.5.cloned.1.call-update
  343.6 0.4 fusion.27
  344.0 0.1 copy.19
  344.0 0.7 reshape.101
  344.8 112.9 %reduce-scatter.5.cloned.1.call-done = f32[16,1024]{1,0:T(8,128)} async-done(((f32[128,1024]{1,0:T(8,128)}), f32[16,1024]{1,0:T(8,128)}) %reduce-scatter.5.cloned.1.call-update) | async-done | bytes 65552 | tf_op jit(solution)/shard_map/reduce_scatter | solution.py:100
  (4 shorter events, 0.1 us)
Async XLA Ops:
  7.2 69.1 %all-gather.12.cloned.1.call-start = ((), (), s32[]{:S(2)}) async-start(), calls=%async_computation.5 | async-start | bytes 2359296 | tf_op jit(solution)/shard_map/all_gather | solution.py:39
  7.9 78.8 %all-gather.10.cloned.1.call-start = ((), (), s32[]{:S(2)}) async-start(), calls=%async_computation.4 | async-start | bytes 2359296 | tf_op jit(solution)/shard_map/all_gather | solution.py:38
  8.6 151.4 %reduce-scatter.3.cloned.1.call-start = ((), (), s32[]{:S(2)}) async-start(), calls=%async_computation.2 | async-start | bytes 1179648 | tf_op jit(solution)/shard_map/reduce_scatter | solution.py:50
  89.3 3.0 copy-start.2
  90.4 139.7 %all-gather.14.cloned.1.call-start = ((), (), s32[]{:S(2)}) async-start(), calls=%async_computation.6 | async-start | bytes 2949120 | tf_op jit(solution)/shard_map/all_gather | solution.py:26
  91.0 193.0 %all-gather.16.cloned.1.call-start = ((), (), s32[]{:S(2)}) async-start(), calls=%async_computation.7 | async-start | bytes 9437184 | tf_op jit(solution)/shard_map/all_gather | solution.py:29
  91.6 366.2 %reduce-scatter.5.cloned.1.call-start = ((), (), s32[]{:S(2)}) async-start(), calls=%async_computation.3 | async-start | bytes 589824 | tf_op jit(solution)/shard_map/reduce_scatter | solution.py:100
  160.9 128.8 %copy-start.3 = (f32[160,128]{1,0:T(8,128)S(1)}, f32[160,128]{1,0:T(8,128)}, u32[]{:S(2)}) copy-start(f32[160,128]{1,0:T(8,128)} %param.13) | copy-start | bytes 245764
  291.4 49.0 %copy-start = (bf16[1,1024,1024]{2,1,0:T(8,128)(2,1)S(1)}, bf16[1,1024,1024]{2,1,0:T(8,128)(2,1)}, u32[]{:S(2)}) copy-start(bf16[1,1024,1024]{2,1,0:T(8,128)(2,1)} %all-gather.12.cloned.1.call-done) | copy-start | bytes 6291460
  340.4 1.6 copy-start.1
Sparse Core Ops, SparseCore 0:
  10.1 38.4 all-gather.11
  50.7 35.9 all-gather.9
  90.5 69.4 reduce-scatter.2
  162.0 68.0 all-gather.13
  232.1 51.8 all-gather.15
  343.7 113.9 reduce-scatter.4
where the time goes:
time: 465 us
  waiting for transfers between devices  314 us (68%)
  blocking collectives  116 us (25%)
  matrix products  15.3 us (3%)
  between operations  14.9 us (3%)
    reduce_scatter x1, waiting for transfers between devices, local(): lax.psum_scatter(partial_grad, 'section', scatter_dimension=0, tiled=True)  113 us
    all_gather x1, waiting for transfers between devices, local(): features = lax.all_gather(hidden[0], 'tensor', axis=1, tiled=True)  69.1 us
    reduce_scatter x1, waiting for transfers between devices, local(): lax.psum_scatter(joined_rows, 'tensor', scatter_dimension=1, tiled=True)  67.6 us
    all_gather x1, blocking collectives, local(): image_rows = lax.all_gather(image_tokens[0], 'section', axis=0, tiled=True)  67.6 us
    all_gather x1, waiting for transfers between devices, local(): lax.all_gather(w_query[0], 'dp', axis=0, tiled=True)  53.9 us
    all_gather x1, blocking collectives, local(): lax.all_gather(packed_rows, 'tensor', axis=1, tiled=True)  48.4 us
  transfers between devices with their start and end apart: 6, of which 5 were waited for; matrix products, arithmetic and copies ran while one was open for 1% of the time, Pallas kernels for 0%

commit v1 on v0

v1 whole, which is shorter than its diff:
```python
import jax
import jax.numpy as jnp
from jax import lax
from jax.sharding import PartitionSpec as P

HEAD_SIZE = 128
X_SIZE = 4
Y_SIZE = 4
BF16 = jnp.bfloat16
F32 = jnp.float32


def x_shift(a, k):
    pairs = [
        (z * X_SIZE + x, z * X_SIZE + (x + k) % X_SIZE) for z in range(2) for x in range(X_SIZE)
    ]
    return lax.ppermute(a, "section", pairs)


def z_swap(a):
    return lax.ppermute(a, "section", [(s, (s + X_SIZE) % (2 * X_SIZE)) for s in range(2 * X_SIZE)])


def y_shift(a, k):
    pairs = [(y * 2 + c, ((y + k) % Y_SIZE) * 2 + c) for y in range(Y_SIZE) for c in range(2)]
    return lax.ppermute(a, "dp", pairs)


def core_swap(a):
    return lax.ppermute(a, "dp", [(d, d ^ 1) for d in range(2 * Y_SIZE)])


def gather_dp(a):
    half = a.shape[0] // 2
    before = y_shift(a, 1)
    after = y_shift(a, -1)
    opposite = jnp.concatenate([y_shift(before[:half], 1), y_shift(after[half:], -1)], axis=0)
    mine = [a, before, opposite, after]
    return [b for block in mine for b in (block, core_swap(block))]


def local(
    hidden,
    w_query,
    key_weight_stack,
    value_weight_stack,
    image_tokens,
    score_bias,
    gate_logit,
    cotangent,
):
    tok_rows = hidden.shape[1]
    columns = w_query.shape[2]
    groups = columns // HEAD_SIZE
    scaling = HEAD_SIZE ** (-0.5)
    section = lax.axis_index("section")
    dp = lax.axis_index("dp")
    z_hi, x = section // X_SIZE, section % X_SIZE
    y, core = dp // 2, dp % 2
    dp_of = [((y - k) % Y_SIZE) * 2 + (core ^ m) for k in range(Y_SIZE) for m in range(2)]
    section_of = [
        (z_hi ^ m) * X_SIZE + (x - k) % X_SIZE for k in range(X_SIZE) for m in range(2)
    ]

    features = lax.all_gather(hidden[0], "tensor", axis=0)

    own = image_tokens[0]
    both = jnp.stack([own, z_swap(own)])
    image_rows = jnp.stack([both, x_shift(both, 1), x_shift(both, 2), x_shift(both, -1)])
    image_rows = image_rows.reshape(-1, own.shape[1])
    image_count = image_rows.shape[0]

    pair_weights = gather_dp(jnp.concatenate([key_weight_stack[0], value_weight_stack[0]], axis=1))
    pair_weights = jnp.stack(pair_weights)
    portions = jnp.einsum("if,wfh->wih", image_rows, pair_weights, preferred_element_type=F32)
    portions = portions.astype(BF16)
    ordered = jnp.zeros_like(portions)
    for slot, d in enumerate(dp_of):
        ordered = lax.dynamic_update_index_in_dim(ordered, portions[slot], d, 0)
    arrived = lax.all_to_all(ordered, "tensor", 0, 0)
    own_pairs = jnp.sum(arrived.astype(F32), axis=0).astype(BF16)
    keys, values = own_pairs[:, :HEAD_SIZE], own_pairs[:, HEAD_SIZE:]

    query_weights = gather_dp(w_query[0])
    query = jnp.zeros((tok_rows, columns), F32)
    for slot, d in enumerate(dp_of):
        block = lax.dynamic_index_in_dim(features, d, 0, keepdims=False)
        query = query + jnp.dot(block, query_weights[slot], preferred_element_type=F32)
    query = query.astype(BF16).reshape(tok_rows, groups, HEAD_SIZE)

    bias = jnp.concatenate(
        [lax.dynamic_slice_in_dim(score_bias, s * own.shape[0], own.shape[0], 1) for s in section_of],
        axis=1,
    )
    scores = jnp.einsum("tgh,ih->gti", query, keys, preferred_element_type=F32) * scaling
    scores = scores + bias[None]
    row_max = jnp.max(scores, axis=-1, keepdims=True)
    exponent = jnp.exp(scores - row_max)
    attn_weights = exponent / jnp.sum(exponent, axis=-1, keepdims=True)
    weights_low = attn_weights.astype(BF16)
    attended = jnp.einsum("gti,ih->tgh", weights_low, values, preferred_element_type=F32)
    scale_factor = jnp.tanh(gate_logit[0])
    gated_out = (scale_factor * attended).astype(BF16).reshape(1, tok_rows, columns)
    attended_gradient = (scale_factor * cotangent[0].astype(F32)).astype(BF16)
    attended_gradient = attended_gradient.reshape(tok_rows, groups, HEAD_SIZE)
    value_gradient = jnp.einsum(
        "gti,tgh->ih", weights_low, attended_gradient, preferred_element_type=F32
    ).astype(BF16)
    grad_weights = jnp.einsum("tgh,ih->gti", attended_gradient, values, preferred_element_type=F32)
    grad_scores = attn_weights * (
        grad_weights - jnp.sum(attn_weights * grad_weights, axis=-1, keepdims=True)
    )
    grad_low = grad_scores.astype(BF16)
    key_gradient = jnp.einsum("gti,tgh->ih", grad_low, query, preferred_element_type=F32) * scaling
    packed = jnp.concatenate([key_gradient.astype(BF16), value_gradient], axis=1)

    copies = jnp.broadcast_to(packed[None], (2 * Y_SIZE, *packed.shape))
    every_gradient = lax.all_to_all(copies, "tensor", 0, 0)
    ordered_gradient = jnp.stack(
        [lax.dynamic_index_in_dim(every_gradient, d, 0, keepdims=False) for d in dp_of]
    )
    partial_grad = jnp.einsum(
        "wih,wfh->if", ordered_gradient, pair_weights, preferred_element_type=F32
    )
    blocks = partial_grad.reshape(X_SIZE, 2, own.shape[0], own.shape[1])
    summed = blocks[0]
    for k, shift in ((1, -1), (2, 2), (3, 1)):
        summed = summed + x_shift(blocks[k].astype(BF16), shift).astype(F32)
    image_grad = summed[0] + z_swap(summed[1])
    return (gated_out, image_grad[None])


def solution(mesh):
    in_specs = (
        P("section", "dp", "tensor"),
        P("section", "dp", "tensor"),
        P("section", "tensor", "dp"),
        P("section", "tensor", "dp"),
        P("dp", "section", "tensor"),
        P("dp", None),
        P("section"),
        P("section", "dp", "tensor"),
    )
    out_specs = (P("section", "dp", "tensor"), P("dp", "section", "tensor"))
    return jax.shard_map(local, mesh=mesh, in_specs=in_specs, out_specs=out_specs, check_vma=False)
```

time: 465 us -> 235 us (0.51)
  waiting for transfers between devices: 314 us -> 44.5 us
  starting transfers between devices: 0.23 us -> 92.1 us
  blocking collectives: 116 us -> 38.8 us
  local copies, waits for them, and re-layouts: 1.62 us -> 18.6 us
  matrix products: 15.3 us -> 20.1 us
    reduce_scatter x2 -> x0, waiting for transfers between devices: 181 us -> none  [the longest x1 113 us: local(): lax.psum_scatter(partial_grad, 'section', scatter_dimension=0, tiled=True)]
    all_gather x4 -> x1, waiting for transfers between devices: 131 us -> 0.02 us  [local(): features = lax.all_gather(hidden[0], 'tensor', axis=0)]
    all_gather x2 -> x0, blocking collectives: 116 us -> none  [the longest x1 67.6 us: local(): image_rows = lax.all_gather(image_tokens[0], 'section', axis=0, tiled=True)]
    ppermute x0 -> x24, starting transfers between devices: none -> 82.8 us  [the longest x8 27.6 us: y_shift(): return lax.ppermute(a, 'dp', pairs)]
    ppermute x0 -> x24, waiting for transfers between devices: none -> 44.5 us  [the longest x8 28.4 us: y_shift(): return lax.ppermute(a, 'dp', pairs)]
    all_to_all x0 -> x1, blocking collectives: none -> 38.8 us  [local(): every_gradient = lax.all_to_all(copies, 'tensor', 0, 0)]
    dot_general x8 -> x14, matrix products: 10.3 us -> 19.6 us  [the longest x8 11.1 us: local(): jnp.dot(block, query_weights[slot], preferred_element_type=F32)]
    all_to_all x0 -> x1, starting transfers between devices: none -> 9.28 us  [local(): arrived = lax.all_to_all(ordered, 'tensor', 0, 0)]
  transfers between devices with their start and end apart: 6 -> 26, of which waited for: 5 -> 9; matrix products, arithmetic and copies ran while one was open for 1% -> 12% of each run, Pallas kernels for 0% -> 0%
where the time goes in v1:
time: 235 us; the launch traced here: 233 us
  starting transfers between devices  92.1 us (39%)
  waiting for transfers between devices  44.5 us (19%)
  blocking collectives  38.8 us (17%)
  matrix products  20.1 us (9%)
  local copies, waits for them, and re-layouts  18.6 us (8%)
  between operations  15.7 us (7%)
  other arithmetic  3.51 us (1%)
    all_to_all x1, blocking collectives, local(): every_gradient = lax.all_to_all(copies, 'tensor', 0, 0)  38.8 us
    ppermute x8, waiting for transfers between devices, y_shift(): return lax.ppermute(a, 'dp', pairs)  28.4 us
    ppermute x8, starting transfers between devices, y_shift(): return lax.ppermute(a, 'dp', pairs)  27.6 us
    ppermute x2, starting transfers between devices, z_swap(): lax.ppermute(a, 'section', [(s, (s + X_SIZE) % (2 * X_SIZE)) for s in ran...  19.8 us
    ppermute x6, starting transfers between devices, x_shift(): return lax.ppermute(a, 'section', pairs)  19.6 us
    ppermute x8, starting transfers between devices, core_swap(): return lax.ppermute(a, 'dp', [(d, d ^ 1) for d in range(2 * Y_SIZE)])  15.8 us
    dot_general x8, matrix products, local(): jnp.dot(block, query_weights[slot], preferred_element_type=F32)  11.1 us
    all_to_all x1, starting transfers between devices, local(): arrived = lax.all_to_all(ordered, 'tensor', 0, 0)  9.28 us
  transfers between devices with their start and end apart: 26, of which 9 were waited for; matrix products, arithmetic and copies ran while one was open for 12% of the time, Pallas kernels for 0%

profile of v1, /device:TPU:24, one launch (start us, length us, event | category | flops | bytes accessed | tf_op | source)
XLA Modules:
  0.0 233.3 jit_solution(7484519044956407104)
XLA Ops:
  10.2 7.5 %collective-permute-start.1 = (bf16[1024,256]{0,1:T(8,128)(2,1)}, bf16[1024,256]{0,1:T(8,128)(2,1)S(1)}, u32[]{:S(2)}, u32[]{:S(2)}) collective-permute-start(bf16[1024,256]{0,1:T(8,128)(2,1)} %pad_maximum_fusion), channel_id=1, source_target_pairs={{0,16},{8,24},{16,32},{24,40},{32,48},{40,56},{48,0},{56,8},{1,17}... | collective-permute-start | bytes 1572872 | tf_op jit(solution)/shard_map/ppermute | solution.py:26
  17.7 1.9 collective-permute-start.4
  19.7 1.9 collective-permute-start
  21.6 12.1 %collective-permute-start.8 = (bf16[16,1024]{1,0:T(8,128)(2,1)}, bf16[16,1024]{1,0:T(8,128)(2,1)S(1)}, u32[]{:S(2)}, u32[]{:S(2)}) collective-permute-start(bf16[16,1024]{1,0:T(8,128)(2,1)} %bitcast.188), channel_id=1, source_target_pairs={{0,256},{64,320},{128,384},{192,448},{256,0},{320,64},{384,128},{4... | collective-permute-start | bytes 98312 | tf_op jit(solution)/shard_map/ppermute | solution.py:21
  33.9 2.4 %collective-permute-done.8 = bf16[16,1024]{1,0:T(8,128)(2,1)S(1)} collective-permute-done((bf16[16,1024]{1,0:T(8,128)(2,1)}, bf16[16,1024]{1,0:T(8,128)(2,1)S(1)}, u32[]{:S(2)}, u32[]{:S(2)}) %collective-permute-start.8) | collective-permute-done | bytes 32800 | tf_op jit(solution)/shard_map/ppermute | solution.py:21
  37.1 3.2 %collective-permute-start.9 = (bf16[2,16,1024]{2,1,0:T(8,128)(2,1)S(1)}, bf16[2,16,1024]{2,1,0:T(8,128)(2,1)S(1)}, u32[]{:S(2)}, u32[]{:S(2)}) collective-permute-start(bf16[2,16,1024]{2,1,0:T(8,128)(2,1)S(1)} %get-tuple-element.14), channel_id=1, source_target_pairs={{0,64},{64,128},{128,192},{192,0},{256,320},{320,384},{384,448},{4... | collective-permute-start | bytes 196616 | tf_op jit(solution)/shard_map/ppermute | solution.py:17
  40.3 4.6 %collective-permute-start.10 = (bf16[2,16,1024]{2,1,0:T(8,128)(2,1)S(1)}, bf16[2,16,1024]{2,1,0:T(8,128)(2,1)S(1)}, u32[]{:S(2)}, u32[]{:S(2)}) collective-permute-start(bf16[2,16,1024]{2,1,0:T(8,128)(2,1)S(1)} %get-tuple-element.14), channel_id=1, source_target_pairs={{0,128},{64,192},{128,0},{192,64},{256,384},{320,448},{384,256},{4... | collective-permute-start | bytes 196616 | tf_op jit(solution)/shard_map/ppermute | solution.py:17
  44.9 3.3 %collective-permute-start.11 = (bf16[2,16,1024]{2,1,0:T(8,128)(2,1)S(1)}, bf16[2,16,1024]{2,1,0:T(8,128)(2,1)S(1)}, u32[]{:S(2)}, u32[]{:S(2)}) collective-permute-start(bf16[2,16,1024]{2,1,0:T(8,128)(2,1)S(1)} %get-tuple-element.14), channel_id=1, source_target_pairs={{0,192},{64,0},{128,64},{192,128},{256,448},{320,256},{384,320},{4... | collective-permute-start | bytes 196616 | tf_op jit(solution)/shard_map/ppermute | solution.py:17
  48.4 3.3 %collective-permute-start.13 = (bf16[1024,512]{1,0:T(8,128)(2,1)}, bf16[1024,512]{1,0:T(8,128)(2,1)S(1)}, u32[]{:S(2)}, u32[]{:S(2)}) collective-permute-start(bf16[1024,512]{1,0:T(8,128)(2,1)} %bitcast.23), channel_id=1, source_target_pairs={{0,16},{8,24},{16,32},{24,40},{32,48},{40,56},{48,0},{56,8},{1,17}... | collective-permute-start | bytes 3145736 | tf_op jit(solution)/shard_map/ppermute | solution.py:26
  51.7 2.5 %collective-permute-start.16 = (bf16[1024,512]{1,0:T(8,128)(2,1)}, bf16[1024,512]{1,0:T(8,128)(2,1)S(1)}, u32[]{:S(2)}, u32[]{:S(2)}) collective-permute-start(bf16[1024,512]{1,0:T(8,128)(2,1)} %bitcast.23), channel_id=1, source_target_pairs={{0,48},{8,56},{16,0},{24,8},{32,16},{40,24},{48,32},{56,40},{1,49}... | collective-permute-start | bytes 3145736 | tf_op jit(solution)/shard_map/ppermute | solution.py:26
  54.3 4.6 %collective-permute-start.3 = (bf16[512,256]{0,1:T(8,128)(2,1)S(1)}, bf16[512,256]{0,1:T(8,128)(2,1)S(1)}, u32[]{:S(2)}, u32[]{:S(2)}) collective-permute-start(bf16[512,256]{0,1:T(8,128)(2,1)S(1)} %slice.87), channel_id=1, source_target_pairs={{0,16},{8,24},{16,32},{24,40},{32,48},{40,56},{48,0},{56,8},{1,17}... | collective-permute-start | bytes 786440 | tf_op jit(solution)/shard_map/ppermute | solution.py:26
  58.9 1.9 collective-permute-start.5
  60.8 1.9 collective-permute-start.2
  63.8 16.3 %collective-permute-done.3 = bf16[512,256]{0,1:T(8,128)(2,1)S(1)} collective-permute-done((bf16[512,256]{0,1:T(8,128)(2,1)S(1)}, bf16[512,256]{0,1:T(8,128)(2,1)S(1)}, u32[]{:S(2)}, u32[]{:S(2)}) %collective-permute-start.3) | collective-permute-done | bytes 262176 | tf_op jit(solution)/shard_map/ppermute | solution.py:26
  80.1 1.9 collective-permute-start.7
  82.1 2.3 %collective-permute-done.5 = bf16[512,256]{0,1:T(8,128)(2,1)S(1)} collective-permute-done((bf16[512,256]{0,1:T(8,128)(2,1)S(1)}, bf16[512,256]{0,1:T(8,128)(2,1)S(1)}, u32[]{:S(2)}, u32[]{:S(2)}) %collective-permute-start.5) | collective-permute-done | bytes 262176 | tf_op jit(solution)/shard_map/ppermute | solution.py:26
  84.4 1.9 collective-permute-start.6
  86.5 1.7 collective-permute-done.6
  88.4 1.9 copy-done
  90.3 1.3 fusion.1
  97.5 9.3 %all-to-all-start = ((bf16[8,128,256]{1,2,0:T(8,128)(2,1)}), bf16[8,128,256]{1,2,0:T(8,128)(2,1)}, u32[]{:S(2)}, u32[]{:S(2)}) async-start(bf16[8,128,256]{1,2,0:T(8,128)(2,1)} %slice_dynamic-update-slice_fusion), calls=%async_computation | async-start | bytes 1048576 | tf_op jit(solution)/shard_map/all_to_all | solution.py:80
  106.8 2.4 %collective-permute-start.15 = (bf16[512,512]{1,0:T(8,128)(2,1)S(1)}, bf16[512,512]{1,0:T(8,128)(2,1)}, u32[]{:S(2)}, u32[]{:S(2)}) collective-permute-start(bf16[512,512]{1,0:T(8,128)(2,1)S(1)} %slice.99), channel_id=1, source_target_pairs={{0,16},{8,24},{16,32},{24,40},{32,48},{40,56},{48,0},{56,8},{1,17}... | collective-permute-start | bytes 1572872 | tf_op jit(solution)/shard_map/ppermute | solution.py:26
  110.0 3.5 %collective-permute-start.17 = (bf16[512,512]{1,0:T(8,128)(2,1)}, bf16[512,512]{1,0:T(8,128)(2,1)}, u32[]{:S(2)}, u32[]{:S(2)}) collective-permute-start(bf16[512,512]{1,0:T(8,128)(2,1)} %slice.100), channel_id=1, source_target_pairs={{0,48},{8,56},{16,0},{24,8},{32,16},{40,24},{48,32},{56,40},{1,49}... | collective-permute-start | bytes 1572872 | tf_op jit(solution)/shard_map/ppermute | solution.py:26
  113.5 1.9 collective-permute-start.12
  116.3 6.2 %collective-permute-done.15 = bf16[512,512]{1,0:T(8,128)(2,1)} collective-permute-done((bf16[512,512]{1,0:T(8,128)(2,1)S(1)}, bf16[512,512]{1,0:T(8,128)(2,1)}, u32[]{:S(2)}, u32[]{:S(2)}) %collective-permute-start.15) | collective-permute-done | bytes 524320 | tf_op jit(solution)/shard_map/ppermute | solution.py:26
  123.5 3.5 %collective-permute-done.17 = bf16[512,512]{1,0:T(8,128)(2,1)} collective-permute-done((bf16[512,512]{1,0:T(8,128)(2,1)}, bf16[512,512]{1,0:T(8,128)(2,1)}, u32[]{:S(2)}, u32[]{:S(2)}) %collective-permute-start.17) | collective-permute-done | bytes 524320 | tf_op jit(solution)/shard_map/ppermute | solution.py:26
  128.2 1.9 collective-permute-start.18
  131.9 1.3 concatenate.18
  133.2 2.4 %collective-permute-start.14 = (bf16[1024,512]{1,0:T(8,128)(2,1)S(1)}, bf16[1024,512]{1,0:T(8,128)(2,1)}, u32[]{:S(2)}, u32[]{:S(2)}) collective-permute-start(bf16[1024,512]{1,0:T(8,128)(2,1)S(1)} %collective-permute-done.13), channel_id=1, source_target_pairs={{0,8},{8,0},{16,24},{24,16},{32,40},{40,32},{48,56},{56,48},{1,9},... | collective-permute-start | bytes 3145736 | tf_op jit(solution)/shard_map/ppermute | solution.py:30
  135.6 1.9 collective-permute-start.19
  138.7 1.5 fusion.21
  140.2 1.7 fusion.26
  141.9 1.3 fusion.17
  143.2 1.6 fusion.19
  144.8 1.6 convolution_add_fusion.3
  146.8 1.6 fusion.8
  148.4 1.6 fusion.12
  150.4 1.4 fusion.14
  152.2 1.4 fusion.15
  153.8 38.8 %all_to_all.10 = bf16[8,128,256]{2,1,0:T(8,128)(2,1)S(1)} all-to-all(bf16[8,128,256]{2,1,0:T(8,128)(2,1)S(1)} %broadcast_in_dim.26), channel_id=1, replica_groups=mesh['section'=8,'dp'=8,'tensor'=8] {'tensor'}, dimensions={0} | all-to-all | bytes 1048576 | tf_op jit(solution)/shard_map/all_to_all | solution.py:118
  192.8 2.9 %fusion.79 = (bf16[128,1024]{1,0:T(8,128)(2,1)S(1)}, f32[128,1024]{1,0:T(8,128)S(1)}) fusion(bf16[8,128,256]{2,1,0:T(8,128)(2,1)S(1)} %dynamic-slice_dynamic-update-slice_fusion, bf16[8,1024,256]{1,2,0:T(8,128)(2,1)} %copy-done), kind=kOutput, calls=%fused_computation.121 | convolution fusion | flops 537001984 | bytes 5505024 | tf_op jit(solution)/shard_map/wih,wfh->if/dot_general | solution.py:122
  195.7 2.2 collective-permute-start.20
  197.9 4.3 %collective-permute-start.21 = (bf16[2,16,1024]{2,1,0:T(8,128)(2,1)S(1)}, bf16[2,16,1024]{2,1,0:T(8,128)(2,1)S(1)}, u32[]{:S(2)}, u32[]{:S(2)}) collective-permute-start(bf16[2,16,1024]{2,1,0:T(8,128)(2,1)S(1)} %bitcast.183), channel_id=1, source_target_pairs={{0,128},{64,192},{128,0},{192,64},{256,384},{320,448},{384,256},{4... | collective-permute-start | bytes 196616 | tf_op jit(solution)/shard_map/ppermute | solution.py:17
  202.2 1.9 collective-permute-start.22
  204.2 1.6 collective-permute-done.21
  205.8 3.8 %collective-permute-done.22 = bf16[2,16,1024]{2,1,0:T(8,128)(2,1)S(1)} collective-permute-done((bf16[2,16,1024]{2,1,0:T(8,128)(2,1)S(1)}, bf16[2,16,1024]{2,1,0:T(8,128)(2,1)S(1)}, u32[]{:S(2)}, u32[]{:S(2)}) %collective-permute-start.22) | collective-permute-done | bytes 65568 | tf_op jit(solution)/shard_map/ppermute | solution.py:17
  209.6 7.6 %collective-permute-start.23 = (f32[16,1024]{1,0:T(8,128)S(1)}, f32[16,1024]{1,0:T(8,128)S(1)}, u32[]{:S(2)}, u32[]{:S(2)}) collective-permute-start(f32[16,1024]{1,0:T(8,128)S(1)} %slice_bitcast_fusion), channel_id=1, source_target_pairs={{0,256},{64,320},{128,384},{192,448},{256,0},{320,64},{384,128},{4... | collective-permute-start | bytes 196616 | tf_op jit(solution)/shard_map/ppermute | solution.py:21
  219.3 6.5 %collective-permute-done.23 = f32[16,1024]{1,0:T(8,128)S(1)} collective-permute-done((f32[16,1024]{1,0:T(8,128)S(1)}, f32[16,1024]{1,0:T(8,128)S(1)}, u32[]{:S(2)}, u32[]{:S(2)}) %collective-permute-start.23) | collective-permute-done | bytes 65568 | tf_op jit(solution)/shard_map/ppermute | solution.py:21
  (84 shorter events, 21.3 us)
Async XLA Ops:
  7.2 131.5 %all-gather.2.cloned.1.call-start = ((), (), s32[]{:S(2)}) async-start(), calls=%async_computation.2 | async-start | bytes 2949120 | tf_op jit(solution)/shard_map/all_gather | solution.py:65
  10.2 34.7 %collective-permute-start.1 = (bf16[1024,256]{0,1:T(8,128)(2,1)}, bf16[1024,256]{0,1:T(8,128)(2,1)S(1)}, u32[]{:S(2)}, u32[]{:S(2)}) collective-permute-start(bf16[1024,256]{0,1:T(8,128)(2,1)} %pad_maximum_fusion), channel_id=1, source_target_pairs={{0,16},{8,24},{16,32},{24,40},{32,48},{40,56},{48,0},{56,8},{1,17}... | collective-permute-start | bytes 1572872 | tf_op jit(solution)/shard_map/ppermute | solution.py:26
  17.7 41.1 %collective-permute-start.4 = (bf16[1024,256]{0,1:T(8,128)(2,1)}, bf16[1024,256]{0,1:T(8,128)(2,1)S(1)}, u32[]{:S(2)}, u32[]{:S(2)}) collective-permute-start(bf16[1024,256]{0,1:T(8,128)(2,1)} %pad_maximum_fusion), channel_id=1, source_target_pairs={{0,48},{8,56},{16,0},{24,8},{32,16},{40,24},{48,32},{56,40},{1,49}... | collective-permute-start | bytes 1572872 | tf_op jit(solution)/shard_map/ppermute | solution.py:26
  19.7 41.2 %collective-permute-start = (bf16[1024,256]{0,1:T(8,128)(2,1)}, bf16[1024,256]{0,1:T(8,128)(2,1)}, u32[]{:S(2)}, u32[]{:S(2)}) collective-permute-start(bf16[1024,256]{0,1:T(8,128)(2,1)} %pad_maximum_fusion), channel_id=1, source_target_pairs={{0,8},{8,0},{16,24},{24,16},{32,40},{40,32},{48,56},{56,48},{1,9},... | collective-permute-start | bytes 1572872 | tf_op jit(solution)/shard_map/ppermute | solution.py:30
  21.6 14.7 %collective-permute-start.8 = (bf16[16,1024]{1,0:T(8,128)(2,1)}, bf16[16,1024]{1,0:T(8,128)(2,1)S(1)}, u32[]{:S(2)}, u32[]{:S(2)}) collective-permute-start(bf16[16,1024]{1,0:T(8,128)(2,1)} %bitcast.188), channel_id=1, source_target_pairs={{0,256},{64,320},{128,384},{192,448},{256,0},{320,64},{384,128},{4... | collective-permute-start | bytes 98312 | tf_op jit(solution)/shard_map/ppermute | solution.py:21
  37.1 11.3 %collective-permute-start.9 = (bf16[2,16,1024]{2,1,0:T(8,128)(2,1)S(1)}, bf16[2,16,1024]{2,1,0:T(8,128)(2,1)S(1)}, u32[]{:S(2)}, u32[]{:S(2)}) collective-permute-start(bf16[2,16,1024]{2,1,0:T(8,128)(2,1)S(1)} %get-tuple-element.14), channel_id=1, source_target_pairs={{0,64},{64,128},{128,192},{192,0},{256,320},{320,384},{384,448},{4... | collective-permute-start | bytes 196616 | tf_op jit(solution)/shard_map/ppermute | solution.py:17
  40.3 11.4 %collective-permute-start.10 = (bf16[2,16,1024]{2,1,0:T(8,128)(2,1)S(1)}, bf16[2,16,1024]{2,1,0:T(8,128)(2,1)S(1)}, u32[]{:S(2)}, u32[]{:S(2)}) collective-permute-start(bf16[2,16,1024]{2,1,0:T(8,128)(2,1)S(1)} %get-tuple-element.14), channel_id=1, source_target_pairs={{0,128},{64,192},{128,0},{192,64},{256,384},{320,448},{384,256},{4... | collective-permute-start | bytes 196616 | tf_op jit(solution)/shard_map/ppermute | solution.py:17
  44.9 9.3 %collective-permute-start.11 = (bf16[2,16,1024]{2,1,0:T(8,128)(2,1)S(1)}, bf16[2,16,1024]{2,1,0:T(8,128)(2,1)S(1)}, u32[]{:S(2)}, u32[]{:S(2)}) collective-permute-start(bf16[2,16,1024]{2,1,0:T(8,128)(2,1)S(1)} %get-tuple-element.14), channel_id=1, source_target_pairs={{0,192},{64,0},{128,64},{192,128},{256,448},{320,256},{384,320},{4... | collective-permute-start | bytes 196616 | tf_op jit(solution)/shard_map/ppermute | solution.py:17
  48.4 58.4 %collective-permute-start.13 = (bf16[1024,512]{1,0:T(8,128)(2,1)}, bf16[1024,512]{1,0:T(8,128)(2,1)S(1)}, u32[]{:S(2)}, u32[]{:S(2)}) collective-permute-start(bf16[1024,512]{1,0:T(8,128)(2,1)} %bitcast.23), channel_id=1, source_target_pairs={{0,16},{8,24},{16,32},{24,40},{32,48},{40,56},{48,0},{56,8},{1,17}... | collective-permute-start | bytes 3145736 | tf_op jit(solution)/shard_map/ppermute | solution.py:26
  51.7 57.4 %collective-permute-start.16 = (bf16[1024,512]{1,0:T(8,128)(2,1)}, bf16[1024,512]{1,0:T(8,128)(2,1)S(1)}, u32[]{:S(2)}, u32[]{:S(2)}) collective-permute-start(bf16[1024,512]{1,0:T(8,128)(2,1)} %bitcast.23), channel_id=1, source_target_pairs={{0,48},{8,56},{16,0},{24,8},{32,16},{40,24},{48,32},{56,40},{1,49}... | collective-permute-start | bytes 3145736 | tf_op jit(solution)/shard_map/ppermute | solution.py:26
  54.3 25.9 %collective-permute-start.3 = (bf16[512,256]{0,1:T(8,128)(2,1)S(1)}, bf16[512,256]{0,1:T(8,128)(2,1)S(1)}, u32[]{:S(2)}, u32[]{:S(2)}) collective-permute-start(bf16[512,256]{0,1:T(8,128)(2,1)S(1)} %slice.87), channel_id=1, source_target_pairs={{0,16},{8,24},{16,32},{24,40},{32,48},{40,56},{48,0},{56,8},{1,17}... | collective-permute-start | bytes 786440 | tf_op jit(solution)/shard_map/ppermute | solution.py:26
  58.9 25.5 %collective-permute-start.5 = (bf16[512,256]{0,1:T(8,128)(2,1)S(1)}, bf16[512,256]{0,1:T(8,128)(2,1)S(1)}, u32[]{:S(2)}, u32[]{:S(2)}) collective-permute-start(bf16[512,256]{0,1:T(8,128)(2,1)S(1)} %slice.88), channel_id=1, source_target_pairs={{0,48},{8,56},{16,0},{24,8},{32,16},{40,24},{48,32},{56,40},{1,49}... | collective-permute-start | bytes 786440 | tf_op jit(solution)/shard_map/ppermute | solution.py:26
  60.8 25.6 %collective-permute-start.2 = (bf16[1024,256]{0,1:T(8,128)(2,1)S(1)}, bf16[1024,256]{0,1:T(8,128)(2,1)S(1)}, u32[]{:S(2)}, u32[]{:S(2)}) collective-permute-start(bf16[1024,256]{0,1:T(8,128)(2,1)S(1)} %collective-permute-done.1), channel_id=1, source_target_pairs={{0,8},{8,0},{16,24},{24,16},{32,40},{40,32},{48,56},{56,48},{1,9},... | collective-permute-start | bytes 1572872 | tf_op jit(solution)/shard_map/ppermute | solution.py:30
  80.1 8.2 %collective-permute-start.7 = (bf16[1024,256]{0,1:T(8,128)(2,1)S(1)}, bf16[1024,256]{0,1:T(8,128)(2,1)S(1)}, u32[]{:S(2)}, u32[]{:S(2)}) collective-permute-start(bf16[1024,256]{0,1:T(8,128)(2,1)S(1)} %collective-permute-done.4), channel_id=1, source_target_pairs={{0,8},{8,0},{16,24},{24,16},{32,40},{40,32},{48,56},{56,48},{1,9},... | collective-permute-start | bytes 1572872 | tf_op jit(solution)/shard_map/ppermute | solution.py:30
  84.4 3.8 %collective-permute-start.6 = (bf16[1024,256]{0,1:T(8,128)(2,1)S(1)}, bf16[1024,256]{0,1:T(8,128)(2,1)S(1)}, u32[]{:S(2)}, u32[]{:S(2)}) collective-permute-start(bf16[1024,256]{0,1:T(8,128)(2,1)S(1)} %constant_dynamic-update-slice_fusion), channel_id=1, source_target_pairs={{0,8},{8,0},{16,24},{24,16},{32,40},{40,32},{48,56},{56,48},{1,9},... | collective-permute-start | bytes 1572872 | tf_op jit(solution)/shard_map/ppermute | solution.py:30
  88.4 2.0 copy-start
  91.6 38.5 %copy-start.3 = (bf16[1,160,512]{2,1,0:T(8,128)(2,1)S(1)}, bf16[1,160,512]{2,1,0:T(8,128)(2,1)}, u32[]{:S(2)}) copy-start(bf16[1,160,512]{2,1,0:T(8,128)(2,1)} %param.15) | copy-start | bytes 491524
  91.6 38.5 %copy-start.1 = (f32[160,128]{1,0:T(8,128)S(1)}, f32[160,128]{1,0:T(8,128)}, u32[]{:S(2)}) copy-start(f32[160,128]{1,0:T(8,128)} %param.13) | copy-start | bytes 245764
  97.5 40.1 %all-to-all-start = ((bf16[8,128,256]{1,2,0:T(8,128)(2,1)}), bf16[8,128,256]{1,2,0:T(8,128)(2,1)}, u32[]{:S(2)}, u32[]{:S(2)}) async-start(bf16[8,128,256]{1,2,0:T(8,128)(2,1)} %slice_dynamic-update-slice_fusion), calls=%async_computation | async-start | bytes 1048576 | tf_op jit(solution)/shard_map/all_to_all | solution.py:80
  106.8 15.7 %collective-permute-start.15 = (bf16[512,512]{1,0:T(8,128)(2,1)S(1)}, bf16[512,512]{1,0:T(8,128)(2,1)}, u32[]{:S(2)}, u32[]{:S(2)}) collective-permute-start(bf16[512,512]{1,0:T(8,128)(2,1)S(1)} %slice.99), channel_id=1, source_target_pairs={{0,16},{8,24},{16,32},{24,40},{32,48},{40,56},{48,0},{56,8},{1,17}... | collective-permute-start | bytes 1572872 | tf_op jit(solution)/shard_map/ppermute | solution.py:26
  110.0 17.0 %collective-permute-start.17 = (bf16[512,512]{1,0:T(8,128)(2,1)}, bf16[512,512]{1,0:T(8,128)(2,1)}, u32[]{:S(2)}, u32[]{:S(2)}) collective-permute-start(bf16[512,512]{1,0:T(8,128)(2,1)} %slice.100), channel_id=1, source_target_pairs={{0,48},{8,56},{16,0},{24,8},{32,16},{40,24},{48,32},{56,40},{1,49}... | collective-permute-start | bytes 1572872 | tf_op jit(solution)/shard_map/ppermute | solution.py:26
  113.5 31.3 %collective-permute-start.12 = (bf16[1024,512]{1,0:T(8,128)(2,1)}, bf16[1024,512]{1,0:T(8,128)(2,1)}, u32[]{:S(2)}, u32[]{:S(2)}) collective-permute-start(bf16[1024,512]{1,0:T(8,128)(2,1)} %bitcast.23), channel_id=1, source_target_pairs={{0,8},{8,0},{16,24},{24,16},{32,40},{40,32},{48,56},{56,48},{1,9},... | collective-permute-start | bytes 3145736 | tf_op jit(solution)/shard_map/ppermute | solution.py:30
  128.2 15.0 %collective-permute-start.18 = (bf16[1024,512]{1,0:T(8,128)(2,1)S(1)}, bf16[1024,512]{1,0:T(8,128)(2,1)}, u32[]{:S(2)}, u32[]{:S(2)}) collective-permute-start(bf16[1024,512]{1,0:T(8,128)(2,1)S(1)} %constant_dynamic-update-slice_fusion.2), channel_id=1, source_target_pairs={{0,8},{8,0},{16,24},{24,16},{32,40},{40,32},{48,56},{56,48},{1,9},... | collective-permute-start | bytes 3145736 | tf_op jit(solution)/shard_map/ppermute | solution.py:30
  133.2 13.5 %collective-permute-start.14 = (bf16[1024,512]{1,0:T(8,128)(2,1)S(1)}, bf16[1024,512]{1,0:T(8,128)(2,1)}, u32[]{:S(2)}, u32[]{:S(2)}) collective-permute-start(bf16[1024,512]{1,0:T(8,128)(2,1)S(1)} %collective-permute-done.13), channel_id=1, source_target_pairs={{0,8},{8,0},{16,24},{24,16},{32,40},{40,32},{48,56},{56,48},{1,9},... | collective-permute-start | bytes 3145736 | tf_op jit(solution)/shard_map/ppermute | solution.py:30
  135.6 12.7 %collective-permute-start.19 = (bf16[1024,512]{1,0:T(8,128)(2,1)S(1)}, bf16[1024,512]{1,0:T(8,128)(2,1)}, u32[]{:S(2)}, u32[]{:S(2)}) collective-permute-start(bf16[1024,512]{1,0:T(8,128)(2,1)S(1)} %collective-permute-done.16), channel_id=1, source_target_pairs={{0,8},{8,0},{16,24},{24,16},{32,40},{40,32},{48,56},{56,48},{1,9},... | collective-permute-start | bytes 3145736 | tf_op jit(solution)/shard_map/ppermute | solution.py:30
  138.7 4.5 %copy-start.2 = (bf16[8,160,1024]{2,1,0:T(8,128)(2,1)S(1)}, bf16[8,160,1024]{2,1,0:T(8,128)(2,1)}, u32[]{:S(2)}) copy-start(bf16[8,160,1024]{2,1,0:T(8,128)(2,1)} %all-gather.2.cloned.1.call-done) | copy-start | bytes 7864324
  146.4 4.1 %copy-start.4 = (bf16[160,4,128]{2,1,0:T(4,128)(2,1)S(1)}, bf16[160,4,128]{2,1,0:T(4,128)(2,1)}, u32[]{:S(2)}) copy-start(bf16[160,4,128]{2,1,0:T(4,128)(2,1)} %convert_element_type.70) | copy-start | bytes 491524
  195.7 8.4 %collective-permute-start.20 = (bf16[2,16,1024]{2,1,0:T(8,128)(2,1)S(1)}, bf16[2,16,1024]{2,1,0:T(8,128)(2,1)S(1)}, u32[]{:S(2)}, u32[]{:S(2)}) collective-permute-start(bf16[2,16,1024]{2,1,0:T(8,128)(2,1)S(1)} %bitcast.184), channel_id=1, source_target_pairs={{0,192},{64,0},{128,64},{192,128},{256,448},{320,256},{384,320},{4... | collective-permute-start | bytes 196616 | tf_op jit(solution)/shard_map/ppermute | solution.py:17
  197.9 7.9 %collective-permute-start.21 = (bf16[2,16,1024]{2,1,0:T(8,128)(2,1)S(1)}, bf16[2,16,1024]{2,1,0:T(8,128)(2,1)S(1)}, u32[]{:S(2)}, u32[]{:S(2)}) collective-permute-start(bf16[2,16,1024]{2,1,0:T(8,128)(2,1)S(1)} %bitcast.183), channel_id=1, source_target_pairs={{0,128},{64,192},{128,0},{192,64},{256,384},{320,448},{384,256},{4... | collective-permute-start | bytes 196616 | tf_op jit(solution)/shard_map/ppermute | solution.py:17
  202.2 7.4 %collective-permute-start.22 = (bf16[2,16,1024]{2,1,0:T(8,128)(2,1)S(1)}, bf16[2,16,1024]{2,1,0:T(8,128)(2,1)S(1)}, u32[]{:S(2)}, u32[]{:S(2)}) collective-permute-start(bf16[2,16,1024]{2,1,0:T(8,128)(2,1)S(1)} %bitcast.182), channel_id=1, source_target_pairs={{0,64},{64,128},{128,192},{192,0},{256,320},{320,384},{384,448},{4... | collective-permute-start | bytes 196616 | tf_op jit(solution)/shard_map/ppermute | solution.py:17
  209.6 16.2 %collective-permute-start.23 = (f32[16,1024]{1,0:T(8,128)S(1)}, f32[16,1024]{1,0:T(8,128)S(1)}, u32[]{:S(2)}, u32[]{:S(2)}) collective-permute-start(f32[16,1024]{1,0:T(8,128)S(1)} %slice_bitcast_fusion), channel_id=1, source_target_pairs={{0,256},{64,320},{128,384},{192,448},{256,0},{320,64},{384,128},{4... | collective-permute-start | bytes 196616 | tf_op jit(solution)/shard_map/ppermute | solution.py:21
Sparse Core Ops, SparseCore 0:
  33.9 68.6 all-gather.1

commit v2 on v1

v2 whole, which is shorter than its diff:
```python
import functools

import jax
import jax.numpy as jnp
from jax import lax
from jax.experimental import pallas as pl
from jax.experimental.pallas import tpu as pltpu
from jax.sharding import PartitionSpec as P

HEAD_SIZE = 128
X_SIZE = 4
Y_SIZE = 4
N_BLOCKS = 8
BF16 = jnp.bfloat16
F32 = jnp.float32
VMEM = pl.BlockSpec(memory_space=pltpu.VMEM)
SMEM = pl.BlockSpec(memory_space=pltpu.SMEM)
BY_ROWS = (((0,), (0,)), ((), ()))
BY_COLUMNS = (((1,), (1,)), ((), ()))


def x_shift(a, k):
    pairs = [
        (z * X_SIZE + x, z * X_SIZE + (x + k) % X_SIZE) for z in range(2) for x in range(X_SIZE)
    ]
    return lax.ppermute(a, "section", pairs)


def z_swap(a):
    return lax.ppermute(a, "section", [(s, (s + X_SIZE) % (2 * X_SIZE)) for s in range(2 * X_SIZE)])


def y_shift(a, k):
    pairs = [(y * 2 + c, ((y + k) % Y_SIZE) * 2 + c) for y in range(Y_SIZE) for c in range(2)]
    return lax.ppermute(a, "dp", pairs)


def core_swap(a):
    return lax.ppermute(a, "dp", [(d, d ^ 1) for d in range(2 * Y_SIZE)])


def dot(a, b, dims=None):
    if dims is None:
        return jnp.dot(a, b, preferred_element_type=F32)
    return lax.dot_general(a, b, dims, preferred_element_type=F32)


def call(kernel, outs, in_specs, args, limit=32 << 20):
    return pl.pallas_call(
        kernel,
        out_shape=outs,
        in_specs=in_specs,
        out_specs=jax.tree.map(lambda _: VMEM, outs),
        compiler_params=pltpu.CompilerParams(vmem_limit_bytes=limit),
    )(*args)


def pair_kernel(dp_ref, i0, i1, i2, i3, *refs):
    weights, out = refs[:-1], refs[-1]
    rows = jnp.concatenate([r[...].reshape(-1, r.shape[-1]) for r in (i0, i1, i2, i3)], axis=0)
    for slot, w in enumerate(weights):
        out[dp_ref[slot]] = dot(rows, w[...]).astype(BF16)


def query_kernel(dp_ref, features, *refs):
    weights, out = refs[:-1], refs[-1]
    total = dot(features[dp_ref[0]], weights[0][...])
    for slot in range(1, N_BLOCKS):
        total = total + dot(features[dp_ref[slot]], weights[slot][...])
    out[...] = total.astype(BF16)


def attention_kernel(query, arrived, bias_ref, cotangent, gate, gated, packed):
    pairs = jnp.sum(arrived[...].astype(F32), axis=0).astype(BF16)
    keys, values = pairs[:, :HEAD_SIZE], pairs[:, HEAD_SIZE:]
    scaling = HEAD_SIZE ** (-0.5)
    scale_factor = jnp.tanh(gate[...])
    bias = bias_ref[...]
    key_gradient = jnp.zeros((keys.shape[0], HEAD_SIZE), F32)
    value_gradient = key_gradient
    for g in range(query.shape[1] // HEAD_SIZE):
        cols = slice(g * HEAD_SIZE, (g + 1) * HEAD_SIZE)
        q = query[:, cols]
        scores = dot(q, keys, BY_COLUMNS) * scaling + bias
        exponent = jnp.exp(scores - jnp.max(scores, axis=-1, keepdims=True))
        attn_weights = exponent / jnp.sum(exponent, axis=-1, keepdims=True)
        weights_low = attn_weights.astype(BF16)
        gated[:, cols] = (scale_factor * dot(weights_low, values)).astype(BF16)
        attended_gradient = (scale_factor * cotangent[:, cols].astype(F32)).astype(BF16)
        value_gradient += dot(weights_low, attended_gradient, BY_ROWS)
        grad_weights = dot(attended_gradient, values, BY_COLUMNS)
        inner = jnp.sum(attn_weights * grad_weights, axis=-1, keepdims=True)
        grad_low = (attn_weights * (grad_weights - inner)).astype(BF16)
        key_gradient += dot(grad_low, q, BY_ROWS)
    pair = jnp.concatenate(
        [(key_gradient * scaling).astype(BF16), value_gradient.astype(BF16)], axis=1
    )
    for t in range(N_BLOCKS):
        packed[t] = pair


def image_kernel(dp_ref, gradients, *refs):
    weights, outs = refs[:N_BLOCKS], refs[N_BLOCKS:]
    total = dot(gradients[dp_ref[0]], weights[0][...], BY_COLUMNS)
    for slot in range(1, N_BLOCKS):
        total = total + dot(gradients[dp_ref[slot]], weights[slot][...], BY_COLUMNS)
    size = total.shape[0] // X_SIZE
    for k, out in enumerate(outs):
        out[...] = total[k * size : (k + 1) * size].astype(out.dtype)


def local(
    hidden,
    w_query,
    key_weight_stack,
    value_weight_stack,
    image_tokens,
    score_bias,
    gate_logit,
    cotangent,
):
    tok_rows = hidden.shape[1]
    columns = w_query.shape[2]
    section = lax.axis_index("section")
    dp = lax.axis_index("dp")
    z_hi, x = section // X_SIZE, section % X_SIZE
    y, core = dp // 2, dp % 2
    dp_of = [((y - k) % Y_SIZE) * 2 + (core ^ m) for k in range(Y_SIZE) for m in range(2)]
    dp_order = jnp.stack(dp_of).astype(jnp.int32)
    section_of = [
        (z_hi ^ m) * X_SIZE + (x - k) % X_SIZE for k in range(X_SIZE) for m in range(2)
    ]

    features = lax.all_gather(hidden[0], "tensor", axis=0)

    own = image_tokens[0]
    both = jnp.stack([own, z_swap(own)])
    images = [both, x_shift(both, 1), x_shift(both, 2), x_shift(both, -1)]
    image_count = 8 * own.shape[0]
    width = own.shape[1]

    pair = jnp.concatenate([key_weight_stack[0], value_weight_stack[0]], axis=1)
    pair_blocks = [pair, y_shift(pair, 1), y_shift(pair, 2), y_shift(pair, -1)]
    pair_weights = [w for b in pair_blocks for w in (b, core_swap(b))]
    portions = call(
        pair_kernel,
        jax.ShapeDtypeStruct((N_BLOCKS, image_count, 2 * HEAD_SIZE), BF16),
        [SMEM] + [VMEM] * 12,
        (dp_order, *images, *pair_weights),
    )
    arrived = lax.all_to_all(portions, "tensor", 0, 0)

    w = w_query[0]
    half = w.shape[0] // 2
    before, after = y_shift(w, 1), y_shift(w, -1)
    opposite = jnp.concatenate([y_shift(before[:half], 1), y_shift(after[half:], -1)], axis=0)
    query_weights = [v for b in (w, before, opposite, after) for v in (b, core_swap(b))]
    query = call(
        query_kernel,
        jax.ShapeDtypeStruct((tok_rows, columns), BF16),
        [SMEM] + [VMEM] * 9,
        (dp_order, features, *query_weights),
    )

    bias = jnp.concatenate(
        [lax.dynamic_slice_in_dim(score_bias, s * own.shape[0], own.shape[0], 1) for s in section_of],
        axis=1,
    )
    gated_out, copies = call(
        attention_kernel,
        (
            jax.ShapeDtypeStruct((tok_rows, columns), BF16),
            jax.ShapeDtypeStruct((N_BLOCKS, image_count, 2 * HEAD_SIZE), BF16),
        ),
        [VMEM] * 5,
        (query, arrived, bias, cotangent[0], gate_logit.reshape(1, 1)),
    )

    every_gradient = lax.all_to_all(copies, "tensor", 0, 0)
    rows = image_count // X_SIZE
    mine, *away = call(
        image_kernel,
        [jax.ShapeDtypeStruct((rows, width), F32)]
        + [jax.ShapeDtypeStruct((rows, width), BF16)] * 3,
        [SMEM] + [VMEM] * 9,
        (dp_order, every_gradient, *pair_weights),
    )
    for block, shift in zip(away, (-1, 2, 1)):
        mine = mine + x_shift(block, shift).astype(F32)
    size = own.shape[0]
    image_grad = mine[:size] + z_swap(mine[size:])
    return (gated_out[None], image_grad[None])


def solution(mesh):
    in_specs = (
        P("section", "dp", "tensor"),
        P("section", "dp", "tensor"),
        P("section", "tensor", "dp"),
        P("section", "tensor", "dp"),
        P("dp", "section", "tensor"),
        P("dp", None),
        P("section"),
        P("section", "dp", "tensor"),
    )
    out_specs = (P("section", "dp", "tensor"), P("dp", "section", "tensor"))
    return jax.shard_map(local, mesh=mesh, in_specs=in_specs, out_specs=out_specs, check_vma=False)
```

time: 235 us -> 207 us (0.88)
  matrix products: 20.1 us -> 0 us
  Pallas kernels: 0 us -> 13 us
  waiting for transfers between devices: 44.5 us -> 34.2 us
  local copies, waits for them, and re-layouts: 18.6 us -> 9.27 us
    dot_general x14 -> x0, matrix products: 19.6 us -> none  [the longest x8 11.1 us: local(): jnp.dot(block, query_weights[slot], preferred_element_type=F32)]
    pallas_call x0 -> x4, Pallas kernels: none -> 13 us  [call(): pl.pallas_call(kernel, out_shape=outs, in_specs=in_specs, out_specs=jax.t...]
    ppermute x8 -> x7, waiting for transfers between devices: 28.4 us -> 19 us  [y_shift(): return lax.ppermute(a, 'dp', pairs)]
    ppermute x8 -> x7, starting transfers between devices: 27.6 us -> 21.9 us  [y_shift(): return lax.ppermute(a, 'dp', pairs)]
    dynamic_update_slice x8 -> x0, local copies, waits for them, and re-layouts: 4.97 us -> none  [local(): ordered = lax.dynamic_update_index_in_dim(ordered, portions[slot], d, 0)]
    ppermute x2, starting transfers between devices: 19.8 us -> 23.8 us  [z_swap(): lax.ppermute(a, 'section', [(s, (s + X_SIZE) % (2 * X_SIZE)) for s in ran...]
    ppermute x6, waiting for transfers between devices: 5.42 us -> 3.05 us  [x_shift(): return lax.ppermute(a, 'section', pairs)]
    unnamed x27 -> x17, local copies, waits for them, and re-layouts: 6.58 us -> 5.9 us
  transfers between devices with their start and end apart: 26 -> 25, of which waited for: 9 -> 11; matrix products, arithmetic and copies ran while one was open for 12% -> 3% of each run, Pallas kernels for 0% -> 3%
where the time goes in v2:
time: 207 us; the launch traced here: 204 us
  starting transfers between devices  91.2 us (44%)
  blocking collectives  38.6 us (19%)
  waiting for transfers between devices  34.2 us (17%)
  between operations  15.3 us (7%)
  Pallas kernels  13 us (6%)
  local copies, waits for them, and re-layouts  9.27 us (4%)
  other arithmetic  2.52 us (1%)
    all_to_all x1, blocking collectives, local(): every_gradient = lax.all_to_all(copies, 'tensor', 0, 0)  38.6 us
    ppermute x2, starting transfers between devices, z_swap(): lax.ppermute(a, 'section', [(s, (s + X_SIZE) % (2 * X_SIZE)) for s in ran...  23.8 us
    ppermute x7, starting transfers between devices, y_shift(): return lax.ppermute(a, 'dp', pairs)  21.9 us
    ppermute x6, starting transfers between devices, x_shift(): return lax.ppermute(a, 'section', pairs)  20.4 us
    ppermute x7, waiting for transfers between devices, y_shift(): return lax.ppermute(a, 'dp', pairs)  19 us
    ppermute x8, starting transfers between devices, core_swap(): return lax.ppermute(a, 'dp', [(d, d ^ 1) for d in range(2 * Y_SIZE)])  15.8 us
    pallas_call x4, Pallas kernels, call(): pl.pallas_call(kernel, out_shape=outs, in_specs=in_specs, out_specs=jax.t...  13 us
    ppermute x2, waiting for transfers between devices, z_swap(): lax.ppermute(a, 'section', [(s, (s + X_SIZE) % (2 * X_SIZE)) for s in ran...  9.4 us
  transfers between devices with their start and end apart: 25, of which 11 were waited for; matrix products, arithmetic and copies ran while one was open for 3% of the time, Pallas kernels for 3%

profile of v2, /device:TPU:24, one launch (start us, length us, event | category | flops | bytes accessed | tf_op | source)
XLA Modules:
  0.0 204.1 jit_solution(1405132875217738450)
XLA Ops:
  7.9 1.1 pad_maximum_fusion.refs_0_
  9.0 1.9 collective-permute-start.12
  10.9 15.7 %collective-permute-start.8 = (bf16[16,1024]{1,0:T(8,128)(2,1)}, bf16[16,1024]{1,0:T(8,128)(2,1)S(1)}, u32[]{:S(2)}, u32[]{:S(2)}) collective-permute-start(bf16[16,1024]{1,0:T(8,128)(2,1)} %bitcast.26), channel_id=1, source_target_pairs={{0,256},{64,320},{128,384},{192,448},{256,0},{320,64},{384,128},{4... | collective-permute-start | bytes 98312 | tf_op jit(solution)/shard_map/ppermute | solution.py:30
  26.6 2.4 %collective-permute-done.8 = bf16[16,1024]{1,0:T(8,128)(2,1)S(1)} collective-permute-done((bf16[16,1024]{1,0:T(8,128)(2,1)}, bf16[16,1024]{1,0:T(8,128)(2,1)S(1)}, u32[]{:S(2)}, u32[]{:S(2)}) %collective-permute-start.8) | collective-permute-done | bytes 32800 | tf_op jit(solution)/shard_map/ppermute | solution.py:30
  29.8 3.4 %collective-permute-start.9 = (bf16[2,16,1024]{2,1,0:T(8,128)(2,1)S(1)}, bf16[2,16,1024]{2,1,0:T(8,128)(2,1)S(1)}, u32[]{:S(2)}, u32[]{:S(2)}) collective-permute-start(bf16[2,16,1024]{2,1,0:T(8,128)(2,1)S(1)} %pad_maximum_fusion.1.i0), channel_id=1, source_target_pairs={{0,64},{64,128},{128,192},{192,0},{256,320},{320,384},{384,448},{4... | collective-permute-start | bytes 196616 | tf_op jit(solution)/shard_map/ppermute | solution.py:26
  33.2 4.6 %collective-permute-start.10 = (bf16[2,16,1024]{2,1,0:T(8,128)(2,1)S(1)}, bf16[2,16,1024]{2,1,0:T(8,128)(2,1)S(1)}, u32[]{:S(2)}, u32[]{:S(2)}) collective-permute-start(bf16[2,16,1024]{2,1,0:T(8,128)(2,1)S(1)} %pad_maximum_fusion.1.i0), channel_id=1, source_target_pairs={{0,128},{64,192},{128,0},{192,64},{256,384},{320,448},{384,256},{4... | collective-permute-start | bytes 196616 | tf_op jit(solution)/shard_map/ppermute | solution.py:26
  37.8 3.3 %collective-permute-start.11 = (bf16[2,16,1024]{2,1,0:T(8,128)(2,1)S(1)}, bf16[2,16,1024]{2,1,0:T(8,128)(2,1)S(1)}, u32[]{:S(2)}, u32[]{:S(2)}) collective-permute-start(bf16[2,16,1024]{2,1,0:T(8,128)(2,1)S(1)} %pad_maximum_fusion.1.i0), channel_id=1, source_target_pairs={{0,192},{64,0},{128,64},{192,128},{256,448},{320,256},{384,320},{4... | collective-permute-start | bytes 196616 | tf_op jit(solution)/shard_map/ppermute | solution.py:26
  41.2 2.1 %collective-permute-start.13 = (bf16[1024,256]{1,0:T(8,128)(2,1)S(1)}, bf16[1024,256]{1,0:T(8,128)(2,1)}, u32[]{:S(2)}, u32[]{:S(2)}) collective-permute-start(bf16[1024,256]{1,0:T(8,128)(2,1)S(1)} %pad_maximum_fusion.refs_0_), channel_id=1, source_target_pairs={{0,16},{8,24},{16,32},{24,40},{32,48},{40,56},{48,0},{56,8},{1,17}... | collective-permute-start | bytes 1572872 | tf_op jit(solution)/shard_map/ppermute | solution.py:35
  43.3 4.5 %collective-permute-start.15 = (bf16[1024,256]{1,0:T(8,128)(2,1)S(1)}, bf16[1024,256]{1,0:T(8,128)(2,1)}, u32[]{:S(2)}, u32[]{:S(2)}) collective-permute-start(bf16[1024,256]{1,0:T(8,128)(2,1)S(1)} %pad_maximum_fusion.refs_0_), channel_id=1, source_target_pairs={{0,32},{8,40},{16,48},{24,56},{32,0},{40,8},{48,16},{56,24},{1,33}... | collective-permute-start | bytes 1572872 | tf_op jit(solution)/shard_map/ppermute | solution.py:35
  47.8 1.9 collective-permute-start.17
  49.8 5.1 %collective-permute-start.1 = (bf16[1024,512]{1,0:T(8,128)(2,1)}, bf16[1024,512]{1,0:T(8,128)(2,1)S(1)}, u32[]{:S(2)}, u32[]{:S(2)}) collective-permute-start(bf16[1024,512]{1,0:T(8,128)(2,1)} %bitcast.19), channel_id=1, source_target_pairs={{0,16},{8,24},{16,32},{24,40},{32,48},{40,56},{48,0},{56,8},{1,17}... | collective-permute-start | bytes 3145736 | tf_op jit(solution)/shard_map/ppermute | solution.py:35
  54.9 1.9 collective-permute-start.4
  56.9 1.2 collective-permute-done.13.refs_2_
  58.0 1.9 collective-permute-start.14
  59.9 1.8 collective-permute-done.15.refs_4_
  61.7 1.9 collective-permute-start.16
  63.6 7.8 %collective-permute-done.17.refs_6_ = bf16[1024,256]{1,0:T(8,128)(2,1)} collective-permute-done((bf16[1024,256]{1,0:T(8,128)(2,1)S(1)}, bf16[1024,256]{1,0:T(8,128)(2,1)}, u32[]{:S(2)}, u32[]{:S(2)}) %collective-permute-start.17) | collective-permute-done | bytes 524320 | tf_op jit(solution)/shard_map/ppermute | solution.py:35
  71.5 1.9 collective-permute-start.18
  73.6 2.0 collective-permute-done.18.refs_7_
  75.6 2.6 %shard_map.96 = bf16[8,128,256]{2,1,0:T(8,128)(2,1)S(1)} custom-call(s32[8]{0:T(128)S(1)} %stack.41.dp_ref, bf16[2,16,1024]{2,1,0:T(8,128)(2,1)S(1)} %pad_maximum_fusion.1.i0, bf16[2,16,1024]{2,1,0:T(8,128)(2,1)S(1)} %collective-permute-done.9.i1, bf16[2,16,1024]{2,1,0:T(8,128)(2,1)S(1)} %collective-permute-done.10.i2, ...), custom_call_target="tpu_custom_call" | custom-call | tf_op jit(solution)/shard_map/pallas_call | solution.py:49
  78.2 0.8 copy-done.1
  79.0 9.3 %all-to-all-start = ((bf16[8,128,256]{2,1,0:T(8,128)(2,1)}), bf16[8,128,256]{2,1,0:T(8,128)(2,1)}, u32[]{:S(2)}, u32[]{:S(2)}) async-start(bf16[8,128,256]{2,1,0:T(8,128)(2,1)} %copy-done.1), calls=%async_computation | async-start | bytes 1048576 | tf_op jit(solution)/shard_map/all_to_all | solution.py:151
  88.3 1.3 collective-permute-done.1.refs_2_
  89.6 3.4 %collective-permute-start.3 = (bf16[512,512]{1,0:T(8,128)(2,1)S(1)}, bf16[512,512]{1,0:T(8,128)(2,1)S(1)}, u32[]{:S(2)}, u32[]{:S(2)}) collective-permute-start(bf16[512,512]{1,0:T(8,128)(2,1)S(1)} %slice.16), channel_id=1, source_target_pairs={{0,16},{8,24},{16,32},{24,40},{32,48},{40,56},{48,0},{56,8},{1,17}... | collective-permute-start | bytes 1572872 | tf_op jit(solution)/shard_map/ppermute | solution.py:35
  93.1 2.9 %collective-permute-start.5 = (bf16[512,512]{1,0:T(8,128)(2,1)S(1)}, bf16[512,512]{1,0:T(8,128)(2,1)S(1)}, u32[]{:S(2)}, u32[]{:S(2)}) collective-permute-start(bf16[512,512]{1,0:T(8,128)(2,1)S(1)} %slice.17), channel_id=1, source_target_pairs={{0,48},{8,56},{16,0},{24,8},{32,16},{40,24},{48,32},{56,40},{1,49}... | collective-permute-start | bytes 1572872 | tf_op jit(solution)/shard_map/ppermute | solution.py:35
  96.0 1.9 collective-permute-start
  98.0 2.4 %collective-permute-start.2 = (bf16[1024,512]{1,0:T(8,128)(2,1)S(1)}, bf16[1024,512]{1,0:T(8,128)(2,1)}, u32[]{:S(2)}, u32[]{:S(2)}) collective-permute-start(bf16[1024,512]{1,0:T(8,128)(2,1)S(1)} %collective-permute-done.1.refs_2_), channel_id=1, source_target_pairs={{0,8},{8,0},{16,24},{24,16},{32,40},{40,32},{48,56},{56,48},{1,9},... | collective-permute-start | bytes 3145736 | tf_op jit(solution)/shard_map/ppermute | solution.py:39
  100.4 1.9 collective-permute-start.7
  102.3 2.8 %collective-permute-done.3 = bf16[512,512]{1,0:T(8,128)(2,1)S(1)} collective-permute-done((bf16[512,512]{1,0:T(8,128)(2,1)S(1)}, bf16[512,512]{1,0:T(8,128)(2,1)S(1)}, u32[]{:S(2)}, u32[]{:S(2)}) %collective-permute-start.3) | collective-permute-done | bytes 524320 | tf_op jit(solution)/shard_map/ppermute | solution.py:35
  105.1 0.8 constant_dynamic-update-slice_fusion.1
  105.9 4.1 %collective-permute-done.5 = bf16[512,512]{1,0:T(8,128)(2,1)S(1)} collective-permute-done((bf16[512,512]{1,0:T(8,128)(2,1)S(1)}, bf16[512,512]{1,0:T(8,128)(2,1)S(1)}, u32[]{:S(2)}, u32[]{:S(2)}) %collective-permute-start.5) | collective-permute-done | bytes 524320 | tf_op jit(solution)/shard_map/ppermute | solution.py:35
  110.0 0.9 constant_dynamic-update-slice_fusion.refs_4_
  110.9 1.9 collective-permute-start.6
  113.6 1.0 constant_dynamic-slice_fusion
  114.6 1.3 concatenate.11.bias_ref
  116.0 1.7 copy-done
  117.7 1.2 copy-done.2
  119.6 4.0 %shard_map.95.query = bf16[160,512]{1,0:T(8,128)(2,1)S(1)} custom-call(s32[8]{0:T(128)S(1)} %copy-done.5, bf16[8,160,1024]{2,1,0:T(8,128)(2,1)S(1)} %copy-done, bf16[1024,512]{1,0:T(8,128)(2,1)S(1)} %bitcast.22, bf16[1024,512]{1,0:T(8,128)(2,1)} %collective-permute-done.refs_1_, bf16[1024,512]{1,0:T(8,128)(2,1)S(1)} %collective-permute-done.1.refs_2_, ...), custom_call_target="tpu_custom_call" | custom-call | tf_op jit(solution)/shard_map/pallas_call | solution.py:49
  123.7 3.2 %shard_map.97 = (bf16[160,512]{1,0:T(8,128)(2,1)}, bf16[8,128,256]{2,1,0:T(8,128)(2,1)S(1)}) custom-call(bf16[160,512]{1,0:T(8,128)(2,1)S(1)} %shard_map.95.query, bf16[8,128,256]{2,1,0:T(8,128)(2,1)} %all-to-all-done.arrived, f32[160,128]{1,0:T(8,128)S(1)} %concatenate.11.bias_ref, bf16[160,512]{1,0:T(8,128)(2,1)S(1)} %bitcast.23, f32[1,1]{1,0:T(1,128)} %bitcast.18.gate), custom_call_target="tpu_custom_call" | custom-call | tf_op jit(solution)/shard_map/pallas_call | solution.py:49
  126.8 38.6 %all_to_all.10.gradients = bf16[8,128,256]{2,1,0:T(8,128)(2,1)S(1)} all-to-all(bf16[8,128,256]{2,1,0:T(8,128)(2,1)S(1)} %get-tuple-element.9), channel_id=1, replica_groups=mesh['section'=8,'dp'=8,'tensor'=8] {'tensor'}, dimensions={0} | all-to-all | bytes 1048576 | tf_op jit(solution)/shard_map/all_to_all | solution.py:179
  166.0 3.3 %shard_map.98 = (f32[32,1024]{1,0:T(8,128)S(1)}, bf16[32,1024]{1,0:T(8,128)(2,1)S(1)}, bf16[32,1024]{1,0:T(8,128)(2,1)S(1)}, bf16[32,1024]{1,0:T(8,128)(2,1)S(1)}) custom-call(s32[8]{0:T(128)S(1)} %copy-done.6, bf16[8,128,256]{2,1,0:T(8,128)(2,1)S(1)} %all_to_all.10.gradients, bf16[1024,256]{1,0:T(8,128)(2,1)S(1)} %pad_maximum_fusion.refs_0_, ...), custom_call_target="tpu_custom_call" | custom-call | tf_op jit(solution)/shard_map/pallas_call | solution.py:49
  169.3 2.5 %collective-permute-start.21 = (bf16[32,1024]{1,0:T(8,128)(2,1)S(1)}, bf16[32,1024]{1,0:T(8,128)(2,1)S(1)}, u32[]{:S(2)}, u32[]{:S(2)}) collective-permute-start(bf16[32,1024]{1,0:T(8,128)(2,1)S(1)} %get-tuple-element.13), channel_id=1, source_target_pairs={{0,64},{64,128},{128,192},{192,0},{256,320},{320,384},{384,448},{4... | collective-permute-start | bytes 196616 | tf_op jit(solution)/shard_map/ppermute | solution.py:26
  171.8 3.1 %collective-permute-start.20 = (bf16[32,1024]{1,0:T(8,128)(2,1)S(1)}, bf16[32,1024]{1,0:T(8,128)(2,1)S(1)}, u32[]{:S(2)}, u32[]{:S(2)}) collective-permute-start(bf16[32,1024]{1,0:T(8,128)(2,1)S(1)} %get-tuple-element.12), channel_id=1, source_target_pairs={{0,128},{64,192},{128,0},{192,64},{256,384},{320,448},{384,256},{4... | collective-permute-start | bytes 196616 | tf_op jit(solution)/shard_map/ppermute | solution.py:26
  174.9 3.4 %collective-permute-start.19 = (bf16[32,1024]{1,0:T(8,128)(2,1)S(1)}, bf16[32,1024]{1,0:T(8,128)(2,1)S(1)}, u32[]{:S(2)}, u32[]{:S(2)}) collective-permute-start(bf16[32,1024]{1,0:T(8,128)(2,1)S(1)} %get-tuple-element.11), channel_id=1, source_target_pairs={{0,192},{64,0},{128,64},{192,128},{256,448},{320,256},{384,320},{4... | collective-permute-start | bytes 196616 | tf_op jit(solution)/shard_map/ppermute | solution.py:26
  178.4 1.1 collective-permute-done.20
  179.5 1.9 collective-permute-done.19
  181.5 8.1 %collective-permute-start.22 = (f32[16,1024]{1,0:T(8,128)S(1)}, f32[16,1024]{1,0:T(8,128)S(1)}, u32[]{:S(2)}, u32[]{:S(2)}) collective-permute-start(f32[16,1024]{1,0:T(8,128)S(1)} %slice.19), channel_id=1, source_target_pairs={{0,256},{64,320},{128,384},{192,448},{256,0},{320,64},{384,128},{4... | collective-permute-start | bytes 196616 | tf_op jit(solution)/shard_map/ppermute | solution.py:30
  189.6 7.0 %collective-permute-done.22 = f32[16,1024]{1,0:T(8,128)S(1)} collective-permute-done((f32[16,1024]{1,0:T(8,128)S(1)}, f32[16,1024]{1,0:T(8,128)S(1)}, u32[]{:S(2)}, u32[]{:S(2)}) %collective-permute-start.22) | collective-permute-done | bytes 65568 | tf_op jit(solution)/shard_map/ppermute | solution.py:30
  (36 shorter events, 3.7 us)
Async XLA Ops:
  7.2 108.8 %all-gather.2.cloned.1.call-start = ((), (), s32[]{:S(2)}) async-start(), calls=%async_computation.2 | async-start | bytes 2949120 | tf_op jit(solution)/shard_map/all_gather | solution.py:134
  9.0 45.9 %collective-permute-start.12 = (bf16[1024,256]{1,0:T(8,128)(2,1)S(1)}, bf16[1024,256]{1,0:T(8,128)(2,1)S(1)}, u32[]{:S(2)}, u32[]{:S(2)}) collective-permute-start(bf16[1024,256]{1,0:T(8,128)(2,1)S(1)} %pad_maximum_fusion.refs_0_), channel_id=1, source_target_pairs={{0,8},{8,0},{16,24},{24,16},{32,40},{40,32},{48,56},{56,48},{1,9},... | collective-permute-start | bytes 1572872 | tf_op jit(solution)/shard_map/ppermute | solution.py:39
  10.9 18.1 %collective-permute-start.8 = (bf16[16,1024]{1,0:T(8,128)(2,1)}, bf16[16,1024]{1,0:T(8,128)(2,1)S(1)}, u32[]{:S(2)}, u32[]{:S(2)}) collective-permute-start(bf16[16,1024]{1,0:T(8,128)(2,1)} %bitcast.26), channel_id=1, source_target_pairs={{0,256},{64,320},{128,384},{192,448},{256,0},{320,64},{384,128},{4... | collective-permute-start | bytes 98312 | tf_op jit(solution)/shard_map/ppermute | solution.py:30
  29.8 13.5 %collective-permute-start.9 = (bf16[2,16,1024]{2,1,0:T(8,128)(2,1)S(1)}, bf16[2,16,1024]{2,1,0:T(8,128)(2,1)S(1)}, u32[]{:S(2)}, u32[]{:S(2)}) collective-permute-start(bf16[2,16,1024]{2,1,0:T(8,128)(2,1)S(1)} %pad_maximum_fusion.1.i0), channel_id=1, source_target_pairs={{0,64},{64,128},{128,192},{192,0},{256,320},{320,384},{384,448},{4... | collective-permute-start | bytes 196616 | tf_op jit(solution)/shard_map/ppermute | solution.py:26
  33.2 14.7 %collective-permute-start.10 = (bf16[2,16,1024]{2,1,0:T(8,128)(2,1)S(1)}, bf16[2,16,1024]{2,1,0:T(8,128)(2,1)S(1)}, u32[]{:S(2)}, u32[]{:S(2)}) collective-permute-start(bf16[2,16,1024]{2,1,0:T(8,128)(2,1)S(1)} %pad_maximum_fusion.1.i0), channel_id=1, source_target_pairs={{0,128},{64,192},{128,0},{192,64},{256,384},{320,448},{384,256},{4... | collective-permute-start | bytes 196616 | tf_op jit(solution)/shard_map/ppermute | solution.py:26
  37.8 11.9 %collective-permute-start.11 = (bf16[2,16,1024]{2,1,0:T(8,128)(2,1)S(1)}, bf16[2,16,1024]{2,1,0:T(8,128)(2,1)S(1)}, u32[]{:S(2)}, u32[]{:S(2)}) collective-permute-start(bf16[2,16,1024]{2,1,0:T(8,128)(2,1)S(1)} %pad_maximum_fusion.1.i0), channel_id=1, source_target_pairs={{0,192},{64,0},{128,64},{192,128},{256,448},{320,256},{384,320},{4... | collective-permute-start | bytes 196616 | tf_op jit(solution)/shard_map/ppermute | solution.py:26
  41.2 16.9 %collective-permute-start.13 = (bf16[1024,256]{1,0:T(8,128)(2,1)S(1)}, bf16[1024,256]{1,0:T(8,128)(2,1)}, u32[]{:S(2)}, u32[]{:S(2)}) collective-permute-start(bf16[1024,256]{1,0:T(8,128)(2,1)S(1)} %pad_maximum_fusion.refs_0_), channel_id=1, source_target_pairs={{0,16},{8,24},{16,32},{24,40},{32,48},{40,56},{48,0},{56,8},{1,17}... | collective-permute-start | bytes 1572872 | tf_op jit(solution)/shard_map/ppermute | solution.py:35
  43.3 18.4 %collective-permute-start.15 = (bf16[1024,256]{1,0:T(8,128)(2,1)S(1)}, bf16[1024,256]{1,0:T(8,128)(2,1)}, u32[]{:S(2)}, u32[]{:S(2)}) collective-permute-start(bf16[1024,256]{1,0:T(8,128)(2,1)S(1)} %pad_maximum_fusion.refs_0_), channel_id=1, source_target_pairs={{0,32},{8,40},{16,48},{24,56},{32,0},{40,8},{48,16},{56,24},{1,33}... | collective-permute-start | bytes 1572872 | tf_op jit(solution)/shard_map/ppermute | solution.py:35
  47.8 23.6 %collective-permute-start.17 = (bf16[1024,256]{1,0:T(8,128)(2,1)S(1)}, bf16[1024,256]{1,0:T(8,128)(2,1)}, u32[]{:S(2)}, u32[]{:S(2)}) collective-permute-start(bf16[1024,256]{1,0:T(8,128)(2,1)S(1)} %pad_maximum_fusion.refs_0_), channel_id=1, source_target_pairs={{0,48},{8,56},{16,0},{24,8},{32,16},{40,24},{48,32},{56,40},{1,49}... | collective-permute-start | bytes 1572872 | tf_op jit(solution)/shard_map/ppermute | solution.py:35
  49.8 39.8 %collective-permute-start.1 = (bf16[1024,512]{1,0:T(8,128)(2,1)}, bf16[1024,512]{1,0:T(8,128)(2,1)S(1)}, u32[]{:S(2)}, u32[]{:S(2)}) collective-permute-start(bf16[1024,512]{1,0:T(8,128)(2,1)} %bitcast.19), channel_id=1, source_target_pairs={{0,16},{8,24},{16,32},{24,40},{32,48},{40,56},{48,0},{56,8},{1,17}... | collective-permute-start | bytes 3145736 | tf_op jit(solution)/shard_map/ppermute | solution.py:35
  54.9 38.1 %collective-permute-start.4 = (bf16[1024,512]{1,0:T(8,128)(2,1)}, bf16[1024,512]{1,0:T(8,128)(2,1)S(1)}, u32[]{:S(2)}, u32[]{:S(2)}) collective-permute-start(bf16[1024,512]{1,0:T(8,128)(2,1)} %bitcast.20), channel_id=1, source_target_pairs={{0,48},{8,56},{16,0},{24,8},{32,16},{40,24},{48,32},{56,40},{1,49}... | collective-permute-start | bytes 3145736 | tf_op jit(solution)/shard_map/ppermute | solution.py:35
  58.0 15.5 %collective-permute-start.14 = (bf16[1024,256]{1,0:T(8,128)(2,1)}, bf16[1024,256]{1,0:T(8,128)(2,1)}, u32[]{:S(2)}, u32[]{:S(2)}) collective-permute-start(bf16[1024,256]{1,0:T(8,128)(2,1)} %collective-permute-done.13.refs_2_), channel_id=1, source_target_pairs={{0,8},{8,0},{16,24},{24,16},{32,40},{40,32},{48,56},{56,48},{1,9},... | collective-permute-start | bytes 1572872 | tf_op jit(solution)/shard_map/ppermute | solution.py:39
  61.7 11.8 %collective-permute-start.16 = (bf16[1024,256]{1,0:T(8,128)(2,1)}, bf16[1024,256]{1,0:T(8,128)(2,1)}, u32[]{:S(2)}, u32[]{:S(2)}) collective-permute-start(bf16[1024,256]{1,0:T(8,128)(2,1)} %collective-permute-done.15.refs_4_), channel_id=1, source_target_pairs={{0,8},{8,0},{16,24},{24,16},{32,40},{40,32},{48,56},{56,48},{1,9},... | collective-permute-start | bytes 1572872 | tf_op jit(solution)/shard_map/ppermute | solution.py:39
  71.5 4.1 %collective-permute-start.18 = (bf16[1024,256]{1,0:T(8,128)(2,1)}, bf16[1024,256]{1,0:T(8,128)(2,1)}, u32[]{:S(2)}, u32[]{:S(2)}) collective-permute-start(bf16[1024,256]{1,0:T(8,128)(2,1)} %collective-permute-done.17.refs_6_), channel_id=1, source_target_pairs={{0,8},{8,0},{16,24},{24,16},{32,40},{40,32},{48,56},{56,48},{1,9},... | collective-permute-start | bytes 1572872 | tf_op jit(solution)/shard_map/ppermute | solution.py:39
  73.6 5.4 %copy-start.4 = (s32[8]{0:T(128)}, s32[8]{0:T(128)S(1)}, u32[]{:S(2)}) copy-start(s32[8]{0:T(128)S(1)} %stack.41.dp_ref) | copy-start | bytes 100
  78.2 0.8 copy-start.1
  79.0 34.6 %copy-start.7 = (f32[160,128]{1,0:T(8,128)S(1)}, f32[160,128]{1,0:T(8,128)}, u32[]{:S(2)}) copy-start(f32[160,128]{1,0:T(8,128)} %param.13) | copy-start | bytes 245764
  79.0 44.6 %all-to-all-start = ((bf16[8,128,256]{2,1,0:T(8,128)(2,1)}), bf16[8,128,256]{2,1,0:T(8,128)(2,1)}, u32[]{:S(2)}, u32[]{:S(2)}) async-start(bf16[8,128,256]{2,1,0:T(8,128)(2,1)} %copy-done.1), calls=%async_computation | async-start | bytes 1048576 | tf_op jit(solution)/shard_map/all_to_all | solution.py:151
  89.6 15.4 %collective-permute-start.3 = (bf16[512,512]{1,0:T(8,128)(2,1)S(1)}, bf16[512,512]{1,0:T(8,128)(2,1)S(1)}, u32[]{:S(2)}, u32[]{:S(2)}) collective-permute-start(bf16[512,512]{1,0:T(8,128)(2,1)S(1)} %slice.16), channel_id=1, source_target_pairs={{0,16},{8,24},{16,32},{24,40},{32,48},{40,56},{48,0},{56,8},{1,17}... | collective-permute-start | bytes 1572872 | tf_op jit(solution)/shard_map/ppermute | solution.py:35
  93.1 16.9 %collective-permute-start.5 = (bf16[512,512]{1,0:T(8,128)(2,1)S(1)}, bf16[512,512]{1,0:T(8,128)(2,1)S(1)}, u32[]{:S(2)}, u32[]{:S(2)}) collective-permute-start(bf16[512,512]{1,0:T(8,128)(2,1)S(1)} %slice.17), channel_id=1, source_target_pairs={{0,48},{8,56},{16,0},{24,8},{32,16},{40,24},{48,32},{56,40},{1,49}... | collective-permute-start | bytes 1572872 | tf_op jit(solution)/shard_map/ppermute | solution.py:35
  96.0 19.9 %collective-permute-start = (bf16[1024,512]{1,0:T(8,128)(2,1)}, bf16[1024,512]{1,0:T(8,128)(2,1)}, u32[]{:S(2)}, u32[]{:S(2)}) collective-permute-start(bf16[1024,512]{1,0:T(8,128)(2,1)} %bitcast.21), channel_id=1, source_target_pairs={{0,8},{8,0},{16,24},{24,16},{32,40},{40,32},{48,56},{56,48},{1,9},... | collective-permute-start | bytes 3145736 | tf_op jit(solution)/shard_map/ppermute | solution.py:39
  98.0 18.0 %collective-permute-start.2 = (bf16[1024,512]{1,0:T(8,128)(2,1)S(1)}, bf16[1024,512]{1,0:T(8,128)(2,1)}, u32[]{:S(2)}, u32[]{:S(2)}) collective-permute-start(bf16[1024,512]{1,0:T(8,128)(2,1)S(1)} %collective-permute-done.1.refs_2_), channel_id=1, source_target_pairs={{0,8},{8,0},{16,24},{24,16},{32,40},{40,32},{48,56},{56,48},{1,9},... | collective-permute-start | bytes 3145736 | tf_op jit(solution)/shard_map/ppermute | solution.py:39
  100.4 15.6 %collective-permute-start.7 = (bf16[1024,512]{1,0:T(8,128)(2,1)S(1)}, bf16[1024,512]{1,0:T(8,128)(2,1)}, u32[]{:S(2)}, u32[]{:S(2)}) collective-permute-start(bf16[1024,512]{1,0:T(8,128)(2,1)S(1)} %collective-permute-done.4.refs_6_), channel_id=1, source_target_pairs={{0,8},{8,0},{16,24},{24,16},{32,40},{40,32},{48,56},{56,48},{1,9},... | collective-permute-start | bytes 3145736 | tf_op jit(solution)/shard_map/ppermute | solution.py:39
  110.9 5.1 %collective-permute-start.6 = (bf16[1024,512]{1,0:T(8,128)(2,1)}, bf16[1024,512]{1,0:T(8,128)(2,1)}, u32[]{:S(2)}, u32[]{:S(2)}) collective-permute-start(bf16[1024,512]{1,0:T(8,128)(2,1)} %constant_dynamic-update-slice_fusion.refs_4_), channel_id=1, source_target_pairs={{0,8},{8,0},{16,24},{24,16},{32,40},{40,32},{48,56},{56,48},{1,9},... | collective-permute-start | bytes 3145736 | tf_op jit(solution)/shard_map/ppermute | solution.py:39
  114.6 9.1 %copy-start.3 = (bf16[1,160,512]{2,1,0:T(8,128)(2,1)S(1)}, bf16[1,160,512]{2,1,0:T(8,128)(2,1)}, u32[]{:S(2)}) copy-start(bf16[1,160,512]{2,1,0:T(8,128)(2,1)} %param.15) | copy-start | bytes 491524
  116.0 1.7 copy-start
  117.7 1.2 copy-start.2
  119.0 0.7 copy-start.5
  165.4 0.7 copy-start.6
  169.3 9.0 %collective-permute-start.21 = (bf16[32,1024]{1,0:T(8,128)(2,1)S(1)}, bf16[32,1024]{1,0:T(8,128)(2,1)S(1)}, u32[]{:S(2)}, u32[]{:S(2)}) collective-permute-start(bf16[32,1024]{1,0:T(8,128)(2,1)S(1)} %get-tuple-element.13), channel_id=1, source_target_pairs={{0,64},{64,128},{128,192},{192,0},{256,320},{320,384},{384,448},{4... | collective-permute-start | bytes 196616 | tf_op jit(solution)/shard_map/ppermute | solution.py:26
  171.8 7.7 %collective-permute-start.20 = (bf16[32,1024]{1,0:T(8,128)(2,1)S(1)}, bf16[32,1024]{1,0:T(8,128)(2,1)S(1)}, u32[]{:S(2)}, u32[]{:S(2)}) collective-permute-start(bf16[32,1024]{1,0:T(8,128)(2,1)S(1)} %get-tuple-element.12), channel_id=1, source_target_pairs={{0,128},{64,192},{128,0},{192,64},{256,384},{320,448},{384,256},{4... | collective-permute-start | bytes 196616 | tf_op jit(solution)/shard_map/ppermute | solution.py:26
  174.9 6.5 %collective-permute-start.19 = (bf16[32,1024]{1,0:T(8,128)(2,1)S(1)}, bf16[32,1024]{1,0:T(8,128)(2,1)S(1)}, u32[]{:S(2)}, u32[]{:S(2)}) collective-permute-start(bf16[32,1024]{1,0:T(8,128)(2,1)S(1)} %get-tuple-element.11), channel_id=1, source_target_pairs={{0,192},{64,0},{128,64},{192,128},{256,448},{320,256},{384,320},{4... | collective-permute-start | bytes 196616 | tf_op jit(solution)/shard_map/ppermute | solution.py:26
  181.5 15.2 %collective-permute-start.22 = (f32[16,1024]{1,0:T(8,128)S(1)}, f32[16,1024]{1,0:T(8,128)S(1)}, u32[]{:S(2)}, u32[]{:S(2)}) collective-permute-start(f32[16,1024]{1,0:T(8,128)S(1)} %slice.19), channel_id=1, source_target_pairs={{0,256},{64,320},{128,384},{192,448},{256,0},{320,64},{384,128},{4... | collective-permute-start | bytes 196616 | tf_op jit(solution)/shard_map/ppermute | solution.py:30
Sparse Core Ops, SparseCore 0:
  10.1 78.6 all-gather.1

commit v3 on v2

--- a/solution.py
+++ b/solution.py
@@ -1,5 +1,3 @@
-import functools
-
 import jax
 import jax.numpy as jnp
 from jax import lax
@@ -8,7 +6,6 @@
 from jax.sharding import PartitionSpec as P
 
 HEAD_SIZE = 128
-X_SIZE = 4
 Y_SIZE = 4
 N_BLOCKS = 8
 BF16 = jnp.bfloat16
@@ -17,17 +14,6 @@
 SMEM = pl.BlockSpec(memory_space=pltpu.SMEM)
 BY_ROWS = (((0,), (0,)), ((), ()))
 BY_COLUMNS = (((1,), (1,)), ((), ()))
-
-
-def x_shift(a, k):
-    pairs = [
-        (z * X_SIZE + x, z * X_SIZE + (x + k) % X_SIZE) for z in range(2) for x in range(X_SIZE)
-    ]
-    return lax.ppermute(a, "section", pairs)
-
-
-def z_swap(a):
-    return lax.ppermute(a, "section", [(s, (s + X_SIZE) % (2 * X_SIZE)) for s in range(2 * X_SIZE)])
 
 
 def y_shift(a, k):
@@ -55,9 +41,9 @@
     )(*args)
 
 
-def pair_kernel(dp_ref, i0, i1, i2, i3, *refs):
+def pair_kernel(dp_ref, images, *refs):
     weights, out = refs[:-1], refs[-1]
-    rows = jnp.concatenate([r[...].reshape(-1, r.shape[-1]) for r in (i0, i1, i2, i3)], axis=0)
+    rows = images[...].reshape(-1, images.shape[-1])
     for slot, w in enumerate(weights):
         out[dp_ref[slot]] = dot(rows, w[...]).astype(BF16)
 
@@ -100,13 +86,11 @@
 
 
 def image_kernel(dp_ref, gradients, *refs):
-    weights, outs = refs[:N_BLOCKS], refs[N_BLOCKS:]
+    weights, out = refs[:-1], refs[-1]
     total = dot(gradients[dp_ref[0]], weights[0][...], BY_COLUMNS)
     for slot in range(1, N_BLOCKS):
         total = total + dot(gradients[dp_ref[slot]], weights[slot][...], BY_COLUMNS)
-    size = total.shape[0] // X_SIZE
-    for k, out in enumerate(outs):
-        out[...] = total[k * size : (k + 1) * size].astype(out.dtype)
+    out[...] = total.astype(BF16)
 
 
 def local(
@@ -121,21 +105,16 @@
 ):
     tok_rows = hidden.shape[1]
     columns = w_query.shape[2]
-    section = lax.axis_index("section")
     dp = lax.axis_index("dp")
-    z_hi, x = section // X_SIZE, section % X_SIZE
-    y, core = dp // 2, dp % 2
-    dp_of = [((y - k) % Y_SIZE) * 2 + (core ^ m) for k in range(Y_SIZE) for m in range(2)]
-    dp_order = jnp.stack(dp_of).astype(jnp.int32)
-    section_of = [
-        (z_hi ^ m) * X_SIZE + (x - k) % X_SIZE for k in range(X_SIZE) for m in range(2)
-    ]
+    y, core = dp >> 1, dp & 1
+    dp_order = jnp.stack(
+        [(((y - k) & (Y_SIZE - 1)) << 1) | (core ^ m) for k in range(Y_SIZE) for m in range(2)]
+    ).astype(jnp.int32)
 
     features = lax.all_gather(hidden[0], "tensor", axis=0)
 
     own = image_tokens[0]
-    both = jnp.stack([own, z_swap(own)])
-    images = [both, x_shift(both, 1), x_shift(both, 2), x_shift(both, -1)]
+    images = [lax.all_to_all(jnp.broadcast_to(own[None], (8, *own.shape)), "section", 0, 0)]
     image_count = 8 * own.shape[0]
     width = own.shape[1]
 
@@ -145,7 +124,7 @@
     portions = call(
         pair_kernel,
         jax.ShapeDtypeStruct((N_BLOCKS, image_count, 2 * HEAD_SIZE), BF16),
-        [SMEM] + [VMEM] * 12,
+        [SMEM] + [VMEM] * 9,
         (dp_order, *images, *pair_weights),
     )
     arrived = lax.all_to_all(portions, "tensor", 0, 0)
@@ -162,10 +141,6 @@
         (dp_order, features, *query_weights),
     )
 
-    bias = jnp.concatenate(
-        [lax.dynamic_slice_in_dim(score_bias, s * own.shape[0], own.shape[0], 1) for s in section_of],
-        axis=1,
-    )
     gated_out, copies = call(
         attention_kernel,
         (
@@ -173,22 +148,18 @@
             jax.ShapeDtypeStruct((N_BLOCKS, image_count, 2 * HEAD_SIZE), BF16),
         ),
         [VMEM] * 5,
-        (query, arrived, bias, cotangent[0], gate_logit.reshape(1, 1)),
+        (query, arrived, score_bias, cotangent[0], gate_logit.reshape(1, 1)),
     )
 
     every_gradient = lax.all_to_all(copies, "tensor", 0, 0)
-    rows = image_count // X_SIZE
-    mine, *away = call(
+    portion = call(
         image_kernel,
-        [jax.ShapeDtypeStruct((rows, width), F32)]
-        + [jax.ShapeDtypeStruct((rows, width), BF16)] * 3,
+        jax.ShapeDtypeStruct((image_count, width), BF16),
         [SMEM] + [VMEM] * 9,
         (dp_order, every_gradient, *pair_weights),
     )
-    for block, shift in zip(away, (-1, 2, 1)):
-        mine = mine + x_shift(block, shift).astype(F32)
-    size = own.shape[0]
-    image_grad = mine[:size] + z_swap(mine[size:])
+    portion = portion.reshape(8, *own.shape)
+    image_grad = jnp.sum(lax.all_to_all(portion, "section", 0, 0).astype(F32), axis=0)
     return (gated_out[None], image_grad[None])
 
 

time: 207 us -> 210 us (1.014)
  the two profiles are of different devices: /device:TPU:24 before, /device:TPU:32 now
where the time goes in v3:
time: 210 us; the launch traced here: 209 us
  blocking collectives  74.9 us (36%)
  starting transfers between devices  63.5 us (30%)
  waiting for transfers between devices  24.5 us (12%)
  local copies, waits for them, and re-layouts  17.9 us (9%)
  between operations  15 us (7%)
  Pallas kernels  11.1 us (5%)
    all_to_all x1, blocking collectives, local(): every_gradient = lax.all_to_all(copies, 'tensor', 0, 0)  38.9 us
    all_to_all x1, blocking collectives, local(): lax.all_to_all(portion, 'section', 0, 0).astype(F32)  36 us
    ppermute x7, starting transfers between devices, y_shift(): return lax.ppermute(a, 'dp', pairs)  25.7 us
    all_to_all x1, waiting for transfers between devices, local(): lax.all_to_all(jnp.broadcast_to(own[None], (8, *own.shape)), 'section', 0...  19.4 us
    all_to_all x1, starting transfers between devices, local(): lax.all_to_all(jnp.broadcast_to(own[None], (8, *own.shape)), 'section', 0...  16.7 us
    ppermute x8, starting transfers between devices, core_swap(): return lax.ppermute(a, 'dp', [(d, d ^ 1) for d in range(2 * Y_SIZE)])  16.5 us
    unnamed x37, local copies, waits for them, and re-layouts  16.2 us
    pallas_call x4, Pallas kernels, call(): pl.pallas_call(kernel, out_shape=outs, in_specs=in_specs, out_specs=jax.t...  11.1 us
  transfers between devices with their start and end apart: 18, of which 4 were waited for; matrix products, arithmetic and copies ran while one was open for 1% of the time, Pallas kernels for 2%

profile of v3, /device:TPU:32, one launch (start us, length us, event | category | flops | bytes accessed | tf_op | source)
XLA Modules:
  0.0 208.6 jit_solution(16544275367038247226)
XLA Ops:
  7.2 0.0 all-gather.2.cloned.1.call-start
  7.2 0.7 all-gather.2.cloned.1.call-update
  7.9 1.1 pad_maximum_fusion.refs_0_
  9.0 3.5 %collective-permute-start.9 = (bf16[1024,256]{1,0:T(8,128)(2,1)S(1)}, bf16[1024,256]{1,0:T(8,128)(2,1)S(1)}, u32[]{:S(2)}, u32[]{:S(2)}) collective-permute-start(bf16[1024,256]{1,0:T(8,128)(2,1)S(1)} %pad_maximum_fusion.refs_0_), channel_id=1, source_target_pairs={{0,16},{8,24},{16,32},{24,40},{32,48},{40,56},{48,0},{56,8},{1,17}... | collective-permute-start | bytes 1572872 | tf_op jit(solution)/shard_map/ppermute | solution.py:21
  12.5 4.8 %collective-permute-start.11 = (bf16[1024,256]{1,0:T(8,128)(2,1)S(1)}, bf16[1024,256]{1,0:T(8,128)(2,1)}, u32[]{:S(2)}, u32[]{:S(2)}) collective-permute-start(bf16[1024,256]{1,0:T(8,128)(2,1)S(1)} %pad_maximum_fusion.refs_0_), channel_id=1, source_target_pairs={{0,32},{8,40},{16,48},{24,56},{32,0},{40,8},{48,16},{56,24},{1,33}... | collective-permute-start | bytes 1572872 | tf_op jit(solution)/shard_map/ppermute | solution.py:21
  17.3 3.3 %collective-permute-start.13 = (bf16[1024,256]{1,0:T(8,128)(2,1)S(1)}, bf16[1024,256]{1,0:T(8,128)(2,1)}, u32[]{:S(2)}, u32[]{:S(2)}) collective-permute-start(bf16[1024,256]{1,0:T(8,128)(2,1)S(1)} %pad_maximum_fusion.refs_0_), channel_id=1, source_target_pairs={{0,48},{8,56},{16,0},{24,8},{32,16},{40,24},{48,32},{56,40},{1,49}... | collective-permute-start | bytes 1572872 | tf_op jit(solution)/shard_map/ppermute | solution.py:21
  20.6 1.9 collective-permute-start.8
  22.5 2.6 %collective-permute-start.1 = (bf16[1024,512]{1,0:T(8,128)(2,1)}, bf16[1024,512]{1,0:T(8,128)(2,1)S(1)}, u32[]{:S(2)}, u32[]{:S(2)}) collective-permute-start(bf16[1024,512]{1,0:T(8,128)(2,1)} %bitcast.19), channel_id=1, source_target_pairs={{0,16},{8,24},{16,32},{24,40},{32,48},{40,56},{48,0},{56,8},{1,17}... | collective-permute-start | bytes 3145736 | tf_op jit(solution)/shard_map/ppermute | solution.py:21
  25.1 1.5 broadcast_in_dim.14
  26.6 16.7 %all-to-all-start = ((bf16[8,16,1024]{2,1,0:T(8,128)(2,1)}), bf16[8,16,1024]{2,1,0:T(8,128)(2,1)S(1)}, u32[]{:S(2)}, u32[]{:S(2)}) async-start(bf16[8,16,1024]{2,1,0:T(8,128)(2,1)} %broadcast_in_dim.14), calls=%async_computation | async-start | bytes 524288 | tf_op jit(solution)/shard_map/all_to_all | solution.py:117
  43.2 4.5 %collective-permute-start.4 = (bf16[1024,512]{1,0:T(8,128)(2,1)}, bf16[1024,512]{1,0:T(8,128)(2,1)S(1)}, u32[]{:S(2)}, u32[]{:S(2)}) collective-permute-start(bf16[1024,512]{1,0:T(8,128)(2,1)} %bitcast.20), channel_id=1, source_target_pairs={{0,48},{8,56},{16,0},{24,8},{32,16},{40,24},{48,32},{56,40},{1,49}... | collective-permute-start | bytes 3145736 | tf_op jit(solution)/shard_map/ppermute | solution.py:21
  47.7 1.9 collective-permute-start.10
  49.7 2.4 %collective-permute-start.12 = (bf16[1024,256]{1,0:T(8,128)(2,1)}, bf16[1024,256]{1,0:T(8,128)(2,1)}, u32[]{:S(2)}, u32[]{:S(2)}) collective-permute-start(bf16[1024,256]{1,0:T(8,128)(2,1)} %collective-permute-done.11.refs_4_), channel_id=1, source_target_pairs={{0,8},{8,0},{16,24},{24,16},{32,40},{40,32},{48,56},{56,48},{1,9},... | collective-permute-start | bytes 1572872 | tf_op jit(solution)/shard_map/ppermute | solution.py:25
  52.1 1.9 collective-permute-start.14
  54.0 0.1 stack.35.dp_ref
  54.1 19.4 %all-to-all-done.images = bf16[8,16,1024]{2,1,0:T(8,128)(2,1)S(1)} async-done(((bf16[8,16,1024]{2,1,0:T(8,128)(2,1)}), bf16[8,16,1024]{2,1,0:T(8,128)(2,1)S(1)}, u32[]{:S(2)}, u32[]{:S(2)}) %all-to-all-start) | async-done | bytes 262176 | tf_op jit(solution)/shard_map/all_to_all | solution.py:117
  73.6 2.6 %shard_map.96 = bf16[8,128,256]{2,1,0:T(8,128)(2,1)S(1)} custom-call(s32[8]{0:T(128)S(1)} %stack.35.dp_ref, bf16[8,16,1024]{2,1,0:T(8,128)(2,1)S(1)} %all-to-all-done.images, bf16[1024,256]{1,0:T(8,128)(2,1)S(1)} %pad_maximum_fusion.refs_0_, bf16[1024,256]{1,0:T(8,128)(2,1)} %collective-permute-done.8.refs_1_, ...), custom_call_target="tpu_custom_call" | custom-call | tf_op jit(solution)/shard_map/pallas_call | solution.py:35
  76.2 0.8 copy-done.3
  77.0 4.7 %all-to-all-start.1 = ((bf16[8,128,256]{2,1,0:T(8,128)(2,1)}), bf16[8,128,256]{2,1,0:T(8,128)(2,1)}, u32[]{:S(2)}, u32[]{:S(2)}) async-start(bf16[8,128,256]{2,1,0:T(8,128)(2,1)} %copy-done.3), calls=%async_computation.1 | async-start | bytes 1048576 | tf_op jit(solution)/shard_map/all_to_all | solution.py:130
  81.7 1.9 collective-permute-start.3
  83.7 5.1 %collective-permute-start.5 = (bf16[512,512]{1,0:T(8,128)(2,1)S(1)}, bf16[512,512]{1,0:T(8,128)(2,1)S(1)}, u32[]{:S(2)}, u32[]{:S(2)}) collective-permute-start(bf16[512,512]{1,0:T(8,128)(2,1)S(1)} %slice.9), channel_id=1, source_target_pairs={{0,48},{8,56},{16,0},{24,8},{32,16},{40,24},{48,32},{56,40},{1,49}... | collective-permute-start | bytes 1572872 | tf_op jit(solution)/shard_map/ppermute | solution.py:21
  88.8 1.9 collective-permute-start
  90.8 2.4 %collective-permute-start.2 = (bf16[1024,512]{1,0:T(8,128)(2,1)S(1)}, bf16[1024,512]{1,0:T(8,128)(2,1)S(1)}, u32[]{:S(2)}, u32[]{:S(2)}) collective-permute-start(bf16[1024,512]{1,0:T(8,128)(2,1)S(1)} %collective-permute-done.1.refs_2_), channel_id=1, source_target_pairs={{0,8},{8,0},{16,24},{24,16},{32,40},{40,32},{48,56},{56,48},{1,9},... | collective-permute-start | bytes 3145736 | tf_op jit(solution)/shard_map/ppermute | solution.py:25
  93.2 1.9 collective-permute-start.7
  95.1 1.0 collective-permute-done.3
  96.2 1.3 collective-permute-done.5
  97.5 2.1 collective-permute-start.6
  99.6 1.0 copy-done.1
  101.2 1.0 copy-done.5
  102.2 1.0 copy-done.7
  103.2 1.0 copy-done.9
  104.2 1.0 copy-done.11
  105.2 2.0 all-gather.2.cloned.1.call-done.features
  107.2 1.7 copy-done
  108.9 1.2 copy-done.2
  110.2 1.2 copy-done.4
  111.4 1.2 copy-done.6
  112.6 1.2 copy-done.8
  113.8 1.2 copy-done.10
  115.1 1.2 copy-done.12
  116.3 0.7 copy-done.16
  116.9 2.1 shard_map.95.query
  119.0 3.2 %shard_map.97 = (bf16[160,512]{1,0:T(8,128)(2,1)}, bf16[8,128,256]{2,1,0:T(8,128)(2,1)S(1)}) custom-call(bf16[160,512]{1,0:T(8,128)(2,1)S(1)} %shard_map.95.query, bf16[8,128,256]{2,1,0:T(8,128)(2,1)} %all-to-all-done.1.arrived, f32[160,128]{1,0:T(8,128)S(1)} %copy-done.14, bf16[160,512]{1,0:T(8,128)(2,1)S(1)} %bitcast.23, f32[1,1]{1,0:T(1,128)} %bitcast.17.gate), custom_call_target="tpu_custom_call" | custom-call | tf_op jit(solution)/shard_map/pallas_call | solution.py:35
  122.2 38.9 %all_to_all.20.gradients = bf16[8,128,256]{2,1,0:T(8,128)(2,1)S(1)} all-to-all(bf16[8,128,256]{2,1,0:T(8,128)(2,1)S(1)} %get-tuple-element.5), channel_id=1, replica_groups=mesh['section'=8,'dp'=8,'tensor'=8] {'tensor'}, dimensions={0} | all-to-all | bytes 1048576 | tf_op jit(solution)/shard_map/all_to_all | solution.py:154
  161.1 0.7 copy-done.17
  161.8 3.3 %shard_map.98 = bf16[128,1024]{1,0:T(8,128)(2,1)S(1)} custom-call(s32[8]{0:T(128)S(1)} %copy-done.17, bf16[8,128,256]{2,1,0:T(8,128)(2,1)S(1)} %all_to_all.20.gradients, bf16[1024,256]{1,0:T(8,128)(2,1)S(1)} %pad_maximum_fusion.refs_0_, bf16[1024,256]{1,0:T(8,128)(2,1)} %collective-permute-done.8.refs_1_, ...), custom_call_target="tpu_custom_call" | custom-call | tf_op jit(solution)/shard_map/pallas_call | solution.py:35
  165.1 36.0 %all_to_all.21 = bf16[8,16,1024]{2,1,0:T(8,128)(2,1)S(1)} all-to-all(bf16[8,16,1024]{2,1,0:T(8,128)(2,1)S(1)} %bitcast.18), channel_id=1, replica_groups=mesh['section'=8,'dp'=8,'tensor'=8] {'section'}, dimensions={0} | all-to-all | bytes 524288 | tf_op jit(solution)/shard_map/all_to_all | solution.py:162
  201.0 0.7 convert_reduce_fusion
  (39 shorter events, 0.2 us)
Async XLA Ops:
  7.2 100.0 %all-gather.2.cloned.1.call-start = ((), (), s32[]{:S(2)}) async-start(), calls=%async_computation.4 | async-start | bytes 2949120 | tf_op jit(solution)/shard_map/all_gather | solution.py:114
  9.0 34.2 %collective-permute-start.9 = (bf16[1024,256]{1,0:T(8,128)(2,1)S(1)}, bf16[1024,256]{1,0:T(8,128)(2,1)S(1)}, u32[]{:S(2)}, u32[]{:S(2)}) collective-permute-start(bf16[1024,256]{1,0:T(8,128)(2,1)S(1)} %pad_maximum_fusion.refs_0_), channel_id=1, source_target_pairs={{0,16},{8,24},{16,32},{24,40},{32,48},{40,56},{48,0},{56,8},{1,17}... | collective-permute-start | bytes 1572872 | tf_op jit(solution)/shard_map/ppermute | solution.py:21
  12.5 35.2 %collective-permute-start.11 = (bf16[1024,256]{1,0:T(8,128)(2,1)S(1)}, bf16[1024,256]{1,0:T(8,128)(2,1)}, u32[]{:S(2)}, u32[]{:S(2)}) collective-permute-start(bf16[1024,256]{1,0:T(8,128)(2,1)S(1)} %pad_maximum_fusion.refs_0_), channel_id=1, source_target_pairs={{0,32},{8,40},{16,48},{24,56},{32,0},{40,8},{48,16},{56,24},{1,33}... | collective-permute-start | bytes 1572872 | tf_op jit(solution)/shard_map/ppermute | solution.py:21
  17.3 32.4 %collective-permute-start.13 = (bf16[1024,256]{1,0:T(8,128)(2,1)S(1)}, bf16[1024,256]{1,0:T(8,128)(2,1)}, u32[]{:S(2)}, u32[]{:S(2)}) collective-permute-start(bf16[1024,256]{1,0:T(8,128)(2,1)S(1)} %pad_maximum_fusion.refs_0_), channel_id=1, source_target_pairs={{0,48},{8,56},{16,0},{24,8},{32,16},{40,24},{48,32},{56,40},{1,49}... | collective-permute-start | bytes 1572872 | tf_op jit(solution)/shard_map/ppermute | solution.py:21
  20.6 31.5 %collective-permute-start.8 = (bf16[1024,256]{1,0:T(8,128)(2,1)S(1)}, bf16[1024,256]{1,0:T(8,128)(2,1)}, u32[]{:S(2)}, u32[]{:S(2)}) collective-permute-start(bf16[1024,256]{1,0:T(8,128)(2,1)S(1)} %pad_maximum_fusion.refs_0_), channel_id=1, source_target_pairs={{0,8},{8,0},{16,24},{24,16},{32,40},{40,32},{48,56},{56,48},{1,9},... | collective-permute-start | bytes 1572872 | tf_op jit(solution)/shard_map/ppermute | solution.py:25
  22.5 59.2 %collective-permute-start.1 = (bf16[1024,512]{1,0:T(8,128)(2,1)}, bf16[1024,512]{1,0:T(8,128)(2,1)S(1)}, u32[]{:S(2)}, u32[]{:S(2)}) collective-permute-start(bf16[1024,512]{1,0:T(8,128)(2,1)} %bitcast.19), channel_id=1, source_target_pairs={{0,16},{8,24},{16,32},{24,40},{32,48},{40,56},{48,0},{56,8},{1,17}... | collective-permute-start | bytes 3145736 | tf_op jit(solution)/shard_map/ppermute | solution.py:21
  26.6 47.0 %all-to-all-start = ((bf16[8,16,1024]{2,1,0:T(8,128)(2,1)}), bf16[8,16,1024]{2,1,0:T(8,128)(2,1)S(1)}, u32[]{:S(2)}, u32[]{:S(2)}) async-start(bf16[8,16,1024]{2,1,0:T(8,128)(2,1)} %broadcast_in_dim.14), calls=%async_computation | async-start | bytes 524288 | tf_op jit(solution)/shard_map/all_to_all | solution.py:117
  43.2 40.4 %collective-permute-start.4 = (bf16[1024,512]{1,0:T(8,128)(2,1)}, bf16[1024,512]{1,0:T(8,128)(2,1)S(1)}, u32[]{:S(2)}, u32[]{:S(2)}) collective-permute-start(bf16[1024,512]{1,0:T(8,128)(2,1)} %bitcast.20), channel_id=1, source_target_pairs={{0,48},{8,56},{16,0},{24,8},{32,16},{40,24},{48,32},{56,40},{1,49}... | collective-permute-start | bytes 3145736 | tf_op jit(solution)/shard_map/ppermute | solution.py:21
  47.7 25.8 %collective-permute-start.10 = (bf16[1024,256]{1,0:T(8,128)(2,1)S(1)}, bf16[1024,256]{1,0:T(8,128)(2,1)}, u32[]{:S(2)}, u32[]{:S(2)}) collective-permute-start(bf16[1024,256]{1,0:T(8,128)(2,1)S(1)} %collective-permute-done.9.refs_2_), channel_id=1, source_target_pairs={{0,8},{8,0},{16,24},{24,16},{32,40},{40,32},{48,56},{56,48},{1,9},... | collective-permute-start | bytes 1572872 | tf_op jit(solution)/shard_map/ppermute | solution.py:25
  49.7 23.9 %collective-permute-start.12 = (bf16[1024,256]{1,0:T(8,128)(2,1)}, bf16[1024,256]{1,0:T(8,128)(2,1)}, u32[]{:S(2)}, u32[]{:S(2)}) collective-permute-start(bf16[1024,256]{1,0:T(8,128)(2,1)} %collective-permute-done.11.refs_4_), channel_id=1, source_target_pairs={{0,8},{8,0},{16,24},{24,16},{32,40},{40,32},{48,56},{56,48},{1,9},... | collective-permute-start | bytes 1572872 | tf_op jit(solution)/shard_map/ppermute | solution.py:25
  52.1 21.5 %collective-permute-start.14 = (bf16[1024,256]{1,0:T(8,128)(2,1)}, bf16[1024,256]{1,0:T(8,128)(2,1)}, u32[]{:S(2)}, u32[]{:S(2)}) collective-permute-start(bf16[1024,256]{1,0:T(8,128)(2,1)} %collective-permute-done.13.refs_6_), channel_id=1, source_target_pairs={{0,8},{8,0},{16,24},{24,16},{32,40},{40,32},{48,56},{56,48},{1,9},... | collective-permute-start | bytes 1572872 | tf_op jit(solution)/shard_map/ppermute | solution.py:25
  54.1 22.8 %copy-start.15 = (s32[8]{0:T(128)}, s32[8]{0:T(128)S(1)}, u32[]{:S(2)}) copy-start(s32[8]{0:T(128)S(1)} %stack.35.dp_ref) | copy-start | bytes 100
  76.2 0.8 copy-start.3
  77.0 42.1 %all-to-all-start.1 = ((bf16[8,128,256]{2,1,0:T(8,128)(2,1)}), bf16[8,128,256]{2,1,0:T(8,128)(2,1)}, u32[]{:S(2)}, u32[]{:S(2)}) async-start(bf16[8,128,256]{2,1,0:T(8,128)(2,1)} %copy-done.3), calls=%async_computation.1 | async-start | bytes 1048576 | tf_op jit(solution)/shard_map/all_to_all | solution.py:130
  81.7 14.4 %collective-permute-start.3 = (bf16[512,512]{1,0:T(8,128)(2,1)S(1)}, bf16[512,512]{1,0:T(8,128)(2,1)S(1)}, u32[]{:S(2)}, u32[]{:S(2)}) collective-permute-start(bf16[512,512]{1,0:T(8,128)(2,1)S(1)} %slice.8), channel_id=1, source_target_pairs={{0,16},{8,24},{16,32},{24,40},{32,48},{40,56},{48,0},{56,8},{1,17}... | collective-permute-start | bytes 1572872 | tf_op jit(solution)/shard_map/ppermute | solution.py:21
  83.7 13.8 %collective-permute-start.5 = (bf16[512,512]{1,0:T(8,128)(2,1)S(1)}, bf16[512,512]{1,0:T(8,128)(2,1)S(1)}, u32[]{:S(2)}, u32[]{:S(2)}) collective-permute-start(bf16[512,512]{1,0:T(8,128)(2,1)S(1)} %slice.9), channel_id=1, source_target_pairs={{0,48},{8,56},{16,0},{24,8},{32,16},{40,24},{48,32},{56,40},{1,49}... | collective-permute-start | bytes 1572872 | tf_op jit(solution)/shard_map/ppermute | solution.py:21
  88.8 12.4 %collective-permute-start = (bf16[1024,512]{1,0:T(8,128)(2,1)}, bf16[1024,512]{1,0:T(8,128)(2,1)S(1)}, u32[]{:S(2)}, u32[]{:S(2)}) collective-permute-start(bf16[1024,512]{1,0:T(8,128)(2,1)} %bitcast.21), channel_id=1, source_target_pairs={{0,8},{8,0},{16,24},{24,16},{32,40},{40,32},{48,56},{56,48},{1,9},... | collective-permute-start | bytes 3145736 | tf_op jit(solution)/shard_map/ppermute | solution.py:25
  90.8 11.4 %collective-permute-start.2 = (bf16[1024,512]{1,0:T(8,128)(2,1)S(1)}, bf16[1024,512]{1,0:T(8,128)(2,1)S(1)}, u32[]{:S(2)}, u32[]{:S(2)}) collective-permute-start(bf16[1024,512]{1,0:T(8,128)(2,1)S(1)} %collective-permute-done.1.refs_2_), channel_id=1, source_target_pairs={{0,8},{8,0},{16,24},{24,16},{32,40},{40,32},{48,56},{56,48},{1,9},... | collective-permute-start | bytes 3145736 | tf_op jit(solution)/shard_map/ppermute | solution.py:25
  93.2 10.0 %collective-permute-start.7 = (bf16[1024,512]{1,0:T(8,128)(2,1)S(1)}, bf16[1024,512]{1,0:T(8,128)(2,1)S(1)}, u32[]{:S(2)}, u32[]{:S(2)}) collective-permute-start(bf16[1024,512]{1,0:T(8,128)(2,1)S(1)} %collective-permute-done.4.refs_6_), channel_id=1, source_target_pairs={{0,8},{8,0},{16,24},{24,16},{32,40},{40,32},{48,56},{56,48},{1,9},... | collective-permute-start | bytes 3145736 | tf_op jit(solution)/shard_map/ppermute | solution.py:25
  97.5 21.6 %copy-start.13 = (bf16[1,160,512]{2,1,0:T(8,128)(2,1)S(1)}, bf16[1,160,512]{2,1,0:T(8,128)(2,1)}, u32[]{:S(2)}) copy-start(bf16[1,160,512]{2,1,0:T(8,128)(2,1)} %param.15) | copy-start | bytes 491524
  97.5 21.6 %copy-start.14 = (f32[160,128]{1,0:T(8,128)S(1)}, f32[160,128]{1,0:T(8,128)}, u32[]{:S(2)}) copy-start(f32[160,128]{1,0:T(8,128)} %bias_ref.1) | copy-start | bytes 245764
  97.5 6.7 %collective-permute-start.6 = (bf16[1024,512]{1,0:T(8,128)(2,1)S(1)}, bf16[1024,512]{1,0:T(8,128)(2,1)S(1)}, u32[]{:S(2)}, u32[]{:S(2)}) collective-permute-start(bf16[1024,512]{1,0:T(8,128)(2,1)S(1)} %constant_dynamic-update-slice_fusion.refs_4_), channel_id=1, source_target_pairs={{0,8},{8,0},{16,24},{24,16},{32,40},{40,32},{48,56},{56,48},{1,9},... | collective-permute-start | bytes 3145736 | tf_op jit(solution)/shard_map/ppermute | solution.py:25
  99.6 1.0 copy-start.1
  101.2 1.0 copy-start.5
  102.2 1.0 copy-start.7
  103.2 1.0 copy-start.9
  104.2 1.0 copy-start.11
  107.2 1.7 copy-start
  108.9 1.2 copy-start.2
  110.2 1.2 copy-start.4
  111.4 1.2 copy-start.6
  112.6 1.2 copy-start.8
  113.8 1.2 copy-start.10
  115.1 1.2 copy-start.12
  116.3 0.7 copy-start.16
  161.1 0.7 copy-start.17
Sparse Core Ops, SparseCore 0:
  10.1 97.0 all-gather.1

commit v4 on v3

v4 whole, which is shorter than its diff:
```python
import jax
import jax.numpy as jnp
from jax import lax
from jax.experimental import pallas as pl
from jax.experimental.pallas import tpu as pltpu
from jax.sharding import PartitionSpec as P

HEAD_SIZE = 128
X_SIZE = 4
Y_SIZE = 4
N_BLOCKS = 8
BF16 = jnp.bfloat16
F32 = jnp.float32
VMEM = pl.BlockSpec(memory_space=pltpu.VMEM)
SMEM = pl.BlockSpec(memory_space=pltpu.SMEM)
BY_ROWS = (((0,), (0,)), ((), ()))
BY_COLUMNS = (((1,), (1,)), ((), ()))


def z_swap(a):
    return lax.ppermute(a, "section", [(s, (s + X_SIZE) % (2 * X_SIZE)) for s in range(2 * X_SIZE)])


def x_exchange(a):
    groups = [[z * X_SIZE + x for x in range(X_SIZE)] for z in range(2)]
    return lax.all_to_all(a, "section", 0, 0, axis_index_groups=groups)


def t_swap(a, k):
    return lax.ppermute(a, "tensor", [(t, t ^ k) for t in range(8)])


def y_shift(a, k):
    pairs = [(y * 2 + c, ((y + k) % Y_SIZE) * 2 + c) for y in range(Y_SIZE) for c in range(2)]
    return lax.ppermute(a, "dp", pairs)


def core_swap(a):
    return lax.ppermute(a, "dp", [(d, d ^ 1) for d in range(2 * Y_SIZE)])


def dot(a, b, dims=None):
    if dims is None:
        return jnp.dot(a, b, preferred_element_type=F32)
    return lax.dot_general(a, b, dims, preferred_element_type=F32)


def call(kernel, outs, in_specs, args, scratch=(), limit=10 << 20):
    return pl.pallas_call(
        kernel,
        out_shape=outs,
        in_specs=in_specs,
        out_specs=jax.tree.map(lambda _: VMEM, outs),
        scratch_shapes=scratch,
        compiler_params=pltpu.CompilerParams(vmem_limit_bytes=limit),
    )(*args)


def spread_kernel(own, other, out):
    for x in range(X_SIZE):
        out[x, 0] = own[...]
        out[x, 1] = other[...]


def pair_kernel(place_ref, half_ref, images, *refs):
    weights, (keep, send, buffer) = refs[:N_BLOCKS], refs[N_BLOCKS:]
    rows = jnp.concatenate(
        [images[x, half_ref[0] ^ z] for z in range(2) for x in range(X_SIZE)], axis=0
    )
    for slot, w in enumerate(weights):
        buffer[place_ref[slot]] = dot(rows, w[...])
    half = N_BLOCKS // 2
    keep[...] = buffer[:half]
    send[...] = buffer[half:].astype(BF16)


def fold_kernel(kept, arrived, keep, send):
    half = keep.shape[0]
    keep[...] = kept[:half] + arrived[:half].astype(F32)
    send[...] = (kept[half:] + arrived[half:].astype(F32)).astype(BF16)


def fold(keep, arrived):
    half = (keep.shape[0] // 2, *keep.shape[1:])
    outs = (jax.ShapeDtypeStruct(half, F32), jax.ShapeDtypeStruct(half, BF16))
    return call(fold_kernel, outs, [VMEM] * 2, (keep, arrived))


def query_kernel(dp_ref, features, *refs):
    weights, (out, rows, columns, sems) = refs[:N_BLOCKS], refs[N_BLOCKS:]
    copies = []
    for slot in range(N_BLOCKS):
        copies.append(
            (
                pltpu.make_async_copy(features.at[dp_ref[slot]], rows.at[slot], sems.at[0, slot]),
                pltpu.make_async_copy(weights[slot], columns.at[slot], sems.at[1, slot]),
            )
        )
    for pair in copies:
        for copy in pair:
            copy.start()
    total = None
    for slot, pair in enumerate(copies):
        for copy in pair:
            copy.wait()
        part = dot(rows[slot], columns[slot])
        total = part if total is None else total + part
    out[...] = total.astype(BF16)


def attention_kernel(query, kept, arrived, bias_ref, cotangent, gate, gated, packed):
    pairs = (kept[...] + arrived[...].astype(F32)).astype(BF16)
    keys, values = pairs[:, :HEAD_SIZE], pairs[:, HEAD_SIZE:]
    scaling = HEAD_SIZE ** (-0.5)
    scale_factor = jnp.tanh(gate[...])
    bias = bias_ref[...]
    key_gradient = jnp.zeros((keys.shape[0], HEAD_SIZE), F32)
    value_gradient = key_gradient
    for g in range(query.shape[1] // HEAD_SIZE):
        cols = slice(g * HEAD_SIZE, (g + 1) * HEAD_SIZE)
        q = query[:, cols]
        scores = dot(q, keys, BY_COLUMNS) * scaling + bias
        exponent = jnp.exp(scores - jnp.max(scores, axis=-1, keepdims=True))
        attn_weights = exponent / jnp.sum(exponent, axis=-1, keepdims=True)
        weights_low = attn_weights.astype(BF16)
        gated[:, cols] = (scale_factor * dot(weights_low, values)).astype(BF16)
        attended_gradient = (scale_factor * cotangent[:, cols].astype(F32)).astype(BF16)
        value_gradient += dot(weights_low, attended_gradient, BY_ROWS)
        grad_weights = dot(attended_gradient, values, BY_COLUMNS)
        inner = jnp.sum(attn_weights * grad_weights, axis=-1, keepdims=True)
        grad_low = (attn_weights * (grad_weights - inner)).astype(BF16)
        key_gradient += dot(grad_low, q, BY_ROWS)
    packed[0] = jnp.concatenate(
        [(key_gradient * scaling).astype(BF16), value_gradient.astype(BF16)], axis=1
    )


def image_kernel(place_ref, near, far, *refs):
    weights, (out, buffer) = refs[:N_BLOCKS], refs[N_BLOCKS:]
    half = N_BLOCKS // 2
    buffer[:half] = near[...]
    buffer[half:] = far[...]
    total = dot(buffer[place_ref[0]], weights[0][...], BY_COLUMNS)
    for slot in range(1, N_BLOCKS):
        total = total + dot(buffer[place_ref[slot]], weights[slot][...], BY_COLUMNS)
    out[...] = total.astype(BF16)


def local(
    hidden,
    w_query,
    key_weight_stack,
    value_weight_stack,
    image_tokens,
    score_bias,
    gate_logit,
    cotangent,
):
    tok_rows = hidden.shape[1]
    columns = w_query.shape[2]
    dp = lax.axis_index("dp")
    slots = jnp.arange(N_BLOCKS, dtype=jnp.int32)
    dp_order = ((((dp >> 1) - (slots >> 1)) & (Y_SIZE - 1)) << 1) | ((dp ^ slots) & 1)
    apart = lax.axis_index("tensor") ^ dp_order
    place = ((apart & 1) << 2) | (apart & 2) | (apart >> 2)

    features = lax.all_gather(hidden[0], "tensor", axis=0)

    own = image_tokens[0]
    rows, width = own.shape
    pair = jnp.concatenate([key_weight_stack[0], value_weight_stack[0]], axis=1)
    cut = pair.shape[0] // 2
    first = (y_shift(pair, 1), y_shift(pair, -1), z_swap(own), core_swap(pair))
    before, behind, other, pair_swapped = lax.optimization_barrier(first)
    across = (y_shift(before[:cut], 1), y_shift(behind[cut:], -1))
    swapped = (core_swap(before), core_swap(behind))

    copies = call(
        spread_kernel,
        jax.ShapeDtypeStruct((X_SIZE, 2, rows, width), BF16),
        [VMEM] * 2,
        (own, other),
    )
    images = x_exchange(copies)
    across, swapped, images, w = lax.optimization_barrier((across, swapped, images, w_query[0]))
    opposite = jnp.concatenate(across, axis=0)
    pair_weights = [
        pair,
        pair_swapped,
        before,
        swapped[0],
        opposite,
        core_swap(opposite),
        behind,
        swapped[1],
    ]
    image_count = 2 * X_SIZE * rows
    block = (image_count, 2 * HEAD_SIZE)
    half = N_BLOCKS // 2

    keep, send = call(
        pair_kernel,
        (jax.ShapeDtypeStruct((half, *block), F32), jax.ShapeDtypeStruct((half, *block), BF16)),
        [SMEM] * 2 + [VMEM] * 9,
        (place, lax.axis_index("section")[None] >> 2, images, *pair_weights),
        [pltpu.VMEM((N_BLOCKS, *block), F32)],
    )
    before, behind = y_shift(w, 1), y_shift(w, -1)
    keep, send = fold(keep, t_swap(send, 1))
    (keep, send), before, behind = lax.optimization_barrier(((keep, send), before, behind))
    cut = w.shape[0] // 2
    across = (y_shift(before[:cut], 1), y_shift(behind[cut:], -1))
    keep, send = fold(keep, t_swap(send, 2))
    (keep, send), across, w = lax.optimization_barrier(((keep, send), across, w))
    arrived = t_swap(send, 4)
    opposite = jnp.concatenate(across, axis=0)
    query_weights = [v for b in (w, before, opposite, behind) for v in (b, core_swap(b))]
    tokens, columns = hidden.shape[1], w_query.shape[2]
    query = call(
        query_kernel,
        jax.ShapeDtypeStruct((tokens, columns), BF16),
        [SMEM] + [pl.BlockSpec(memory_space=pl.ANY)] * 9,
        (dp_order, features, *query_weights),
        [
            pltpu.VMEM(features.shape, BF16),
            pltpu.VMEM((N_BLOCKS, *w.shape), BF16),
            pltpu.SemaphoreType.DMA((2, N_BLOCKS)),
        ],
        limit=60 << 20,
    )

    gated_out, packed = call(
        attention_kernel,
        (jax.ShapeDtypeStruct((tokens, columns), BF16), jax.ShapeDtypeStruct((1, *block), BF16)),
        [VMEM] * 6,
        (query, keep[0], arrived[0], score_bias, cotangent[0], gate_logit.reshape(1, 1)),
    )

    near = jnp.concatenate([packed, t_swap(packed, 4)])
    near = jnp.concatenate([near, t_swap(near, 2)])
    far = t_swap(near, 1)
    portion = call(
        image_kernel,
        jax.ShapeDtypeStruct((image_count, width), BF16),
        [SMEM] + [VMEM] * 10,
        (place, near, far, *pair_weights),
        [pltpu.VMEM((N_BLOCKS, *block), BF16)],
    )
    portion = portion.reshape(2 * X_SIZE, rows, width)
    image_grad = jnp.sum(lax.all_to_all(portion, "section", 0, 0).astype(F32), axis=0)
    return (gated_out[None], image_grad[None])


def solution(mesh):
    in_specs = (
        P("section", "dp", "tensor"),
        P("section", "dp", "tensor"),
        P("section", "tensor", "dp"),
        P("section", "tensor", "dp"),
        P("dp", "section", "tensor"),
        P("dp", None),
        P("section"),
        P("section", "dp", "tensor"),
    )
    out_specs = (P("section", "dp", "tensor"), P("dp", "section", "tensor"))
    return jax.shard_map(local, mesh=mesh, in_specs=in_specs, out_specs=out_specs, check_vma=False)
```

time: 210 us -> 211 us (level)
  the two profiles are of different devices: /device:TPU:32 before, /device:TPU:56 now
where the time goes in v4:
time: 211 us; the launch traced here: 210 us
  starting transfers between devices  80.2 us (38%)
  waiting for transfers between devices  44.5 us (21%)
  blocking collectives  44.4 us (21%)
  between operations  15.1 us (7%)
  Pallas kernels  14.2 us (7%)
  local copies, waits for them, and re-layouts  9.17 us (4%)
  other arithmetic  2.35 us (1%)
    ppermute x6, waiting for transfers between devices, t_swap(): return lax.ppermute(a, 'tensor', [(t, t ^ k) for t in range(8)])  35.7 us
    all_to_all x1, blocking collectives, local(): lax.all_to_all(portion, 'section', 0, 0).astype(F32)  33.2 us
    ppermute x6, starting transfers between devices, t_swap(): return lax.ppermute(a, 'tensor', [(t, t ^ k) for t in range(8)])  25.2 us
    ppermute x8, starting transfers between devices, y_shift(): return lax.ppermute(a, 'dp', pairs)  23.4 us
    ppermute x8, starting transfers between devices, core_swap(): return lax.ppermute(a, 'dp', [(d, d ^ 1) for d in range(2 * Y_SIZE)])  16.8 us
    ppermute x1, starting transfers between devices, z_swap(): lax.ppermute(a, 'section', [(s, (s + X_SIZE) % (2 * X_SIZE)) for s in ran...  14.8 us
    pallas_call x7, Pallas kernels, call(): pl.pallas_call(kernel, out_shape=outs, in_specs=in_specs, out_specs=jax.t...  14.2 us
    all_to_all x1, blocking collectives, x_exchange(): return lax.all_to_all(a, 'section', 0, 0, axis_index_groups=groups)  11.2 us
  transfers between devices with their start and end apart: 24, of which 9 were waited for; matrix products, arithmetic and copies ran while one was open for 2% of the time, Pallas kernels for 4%

profile of v4, /device:TPU:56, one launch (start us, length us, event | category | flops | bytes accessed | tf_op | source)
XLA Modules:
  0.0 210.0 jit_solution(4507087395793904132)
XLA Ops:
  7.2 0.7 all-gather.2.cloned.1.call-update
  7.9 1.1 pad_maximum_fusion.refs_0_
  9.0 2.1 %collective-permute-start = (bf16[1024,256]{1,0:T(8,128)(2,1)S(1)}, bf16[1024,256]{1,0:T(8,128)(2,1)S(1)}, u32[]{:S(2)}, u32[]{:S(2)}) collective-permute-start(bf16[1024,256]{1,0:T(8,128)(2,1)S(1)} %pad_maximum_fusion.refs_0_), channel_id=1, source_target_pairs={{0,16},{8,24},{16,32},{24,40},{32,48},{40,56},{48,0},{56,8},{1,17}... | collective-permute-start | bytes 1572872 | tf_op jit(solution)/shard_map/ppermute | solution.py:35
  11.1 3.7 %collective-permute-start.1 = (bf16[1024,256]{1,0:T(8,128)(2,1)S(1)}, bf16[1024,256]{1,0:T(8,128)(2,1)S(1)}, u32[]{:S(2)}, u32[]{:S(2)}) collective-permute-start(bf16[1024,256]{1,0:T(8,128)(2,1)S(1)} %pad_maximum_fusion.refs_0_), channel_id=1, source_target_pairs={{0,48},{8,56},{16,0},{24,8},{32,16},{40,24},{48,32},{56,40},{1,49}... | collective-permute-start | bytes 1572872 | tf_op jit(solution)/shard_map/ppermute | solution.py:35
  14.8 1.9 collective-permute-start.3
  16.8 14.8 %collective-permute-start.2 = (bf16[16,1024]{1,0:T(8,128)(2,1)}, bf16[16,1024]{1,0:T(8,128)(2,1)S(1)}, u32[]{:S(2)}, u32[]{:S(2)}) collective-permute-start(bf16[16,1024]{1,0:T(8,128)(2,1)} %bitcast.16), channel_id=1, source_target_pairs={{0,256},{64,320},{128,384},{192,448},{256,0},{320,64},{384,128},{4... | collective-permute-start | bytes 98312 | tf_op jit(solution)/shard_map/ppermute | solution.py:21
  31.6 2.6 %collective-permute-done.2.other = bf16[16,1024]{1,0:T(8,128)(2,1)S(1)} collective-permute-done((bf16[16,1024]{1,0:T(8,128)(2,1)}, bf16[16,1024]{1,0:T(8,128)(2,1)S(1)}, u32[]{:S(2)}, u32[]{:S(2)}) %collective-permute-start.2) | collective-permute-done | bytes 32800 | tf_op jit(solution)/shard_map/ppermute | solution.py:21
  34.3 1.9 collective-permute-start.6
  36.2 2.4 %collective-permute-start.7 = (bf16[1024,256]{1,0:T(8,128)(2,1)S(1)}, bf16[1024,256]{1,0:T(8,128)(2,1)S(1)}, u32[]{:S(2)}, u32[]{:S(2)}) collective-permute-start(bf16[1024,256]{1,0:T(8,128)(2,1)S(1)} %collective-permute-done.1.refs_6_), channel_id=1, source_target_pairs={{0,8},{8,0},{16,24},{24,16},{32,40},{40,32},{48,56},{56,48},{1,9},... | collective-permute-start | bytes 1572872 | tf_op jit(solution)/shard_map/ppermute | solution.py:39
  38.7 3.1 %collective-permute-start.4 = (bf16[512,256]{1,0:T(8,128)(2,1)S(1)}, bf16[512,256]{1,0:T(8,128)(2,1)S(1)}, u32[]{:S(2)}, u32[]{:S(2)}) collective-permute-start(bf16[512,256]{1,0:T(8,128)(2,1)S(1)} %slice.12), channel_id=1, source_target_pairs={{0,16},{8,24},{16,32},{24,40},{32,48},{40,56},{48,0},{56,8},{1,17}... | collective-permute-start | bytes 786440 | tf_op jit(solution)/shard_map/ppermute | solution.py:35
  41.8 2.7 %collective-permute-start.5 = (bf16[512,256]{1,0:T(8,128)(2,1)S(1)}, bf16[512,256]{1,0:T(8,128)(2,1)S(1)}, u32[]{:S(2)}, u32[]{:S(2)}) collective-permute-start(bf16[512,256]{1,0:T(8,128)(2,1)S(1)} %slice.13), channel_id=1, source_target_pairs={{0,48},{8,56},{16,0},{24,8},{32,16},{40,24},{48,32},{56,40},{1,49}... | collective-permute-start | bytes 786440 | tf_op jit(solution)/shard_map/ppermute | solution.py:35
  44.5 0.7 copy-done.6
  45.3 11.2 %all_to_all.10.images = bf16[4,2,16,1024]{3,2,1,0:T(8,128)(2,1)S(1)} all-to-all(bf16[4,2,16,1024]{3,2,1,0:T(8,128)(2,1)S(1)} %shard_map.95), channel_id=1, replica_groups={{0,64,128,192},{256,320,384,448},{1,65,129,193},{257,321,385,449},{2,66..., dimensions={0} | all-to-all | bytes 524288 | tf_op jit(solution)/shard_map/all_to_all | solution.py:26
  56.5 0.8 copy-done
  57.3 3.9 %collective-permute-start.10 = (bf16[1024,512]{1,0:T(8,128)(2,1)}, bf16[1024,512]{1,0:T(8,128)(2,1)}, u32[]{:S(2)}, u32[]{:S(2)}) collective-permute-start(bf16[1024,512]{1,0:T(8,128)(2,1)} %bitcast.4.refs_0_), channel_id=1, source_target_pairs={{0,16},{8,24},{16,32},{24,40},{32,48},{40,56},{48,0},{56,8},{1,17}... | collective-permute-start | bytes 3145736 | tf_op jit(solution)/shard_map/ppermute | solution.py:35
  61.2 1.9 collective-permute-start.11
  63.2 1.9 collective-permute-start.8
  65.8 1.4 collective-permute-done.8.refs_5_
  67.2 1.0 copy-done.1
  68.2 1.9 shard_map.96
  70.1 3.4 %collective-permute-start.9 = (bf16[4,128,256]{2,1,0:T(8,128)(2,1)S(1)}, bf16[4,128,256]{2,1,0:T(8,128)(2,1)S(1)}, u32[]{:S(2)}, u32[]{:S(2)}) collective-permute-start(bf16[4,128,256]{2,1,0:T(8,128)(2,1)S(1)} %get-tuple-element.39), channel_id=1, source_target_pairs={{0,1},{1,0},{2,3},{3,2},{4,5},{5,4},{6,7},{7,6},{8,9},{9,8},{10,11... | collective-permute-start | bytes 786440 | tf_op jit(solution)/shard_map/ppermute | solution.py:30
  73.5 13.8 %collective-permute-done.9.arrived = bf16[4,128,256]{2,1,0:T(8,128)(2,1)S(1)} collective-permute-done((bf16[4,128,256]{2,1,0:T(8,128)(2,1)S(1)}, bf16[4,128,256]{2,1,0:T(8,128)(2,1)S(1)}, u32[]{:S(2)}, u32[]{:S(2)}) %collective-permute-start.9) | collective-permute-done | bytes 262176 | tf_op jit(solution)/shard_map/ppermute | solution.py:30
  87.5 1.1 slice.14
  88.5 4.0 %collective-permute-start.13 = (bf16[512,512]{1,0:T(8,128)(2,1)S(1)}, bf16[512,512]{1,0:T(8,128)(2,1)S(1)}, u32[]{:S(2)}, u32[]{:S(2)}) collective-permute-start(bf16[512,512]{1,0:T(8,128)(2,1)S(1)} %slice.14), channel_id=1, source_target_pairs={{0,16},{8,24},{16,32},{24,40},{32,48},{40,56},{48,0},{56,8},{1,17}... | collective-permute-start | bytes 1572872 | tf_op jit(solution)/shard_map/ppermute | solution.py:35
  92.5 1.1 slice.15
  93.6 1.9 collective-permute-start.14
  95.5 4.6 %collective-permute-start.12 = (bf16[2,128,256]{2,1,0:T(8,128)(2,1)S(1)}, bf16[2,128,256]{2,1,0:T(8,128)(2,1)S(1)}, u32[]{:S(2)}, u32[]{:S(2)}) collective-permute-start(bf16[2,128,256]{2,1,0:T(8,128)(2,1)S(1)} %get-tuple-element.44), channel_id=1, source_target_pairs={{0,2},{1,3},{2,0},{3,1},{4,6},{5,7},{6,4},{7,5},{8,10},{9,11},{10,... | collective-permute-start | bytes 393224 | tf_op jit(solution)/shard_map/ppermute | solution.py:30
  100.1 1.9 collective-permute-start.16
  102.0 2.4 %collective-permute-start.18 = (bf16[1024,512]{1,0:T(8,128)(2,1)}, bf16[1024,512]{1,0:T(8,128)(2,1)S(1)}, u32[]{:S(2)}, u32[]{:S(2)}) collective-permute-start(bf16[1024,512]{1,0:T(8,128)(2,1)} %collective-permute-done.11.refs_6_), channel_id=1, source_target_pairs={{0,8},{8,0},{16,24},{24,16},{32,40},{40,32},{48,56},{56,48},{1,9},... | collective-permute-start | bytes 3145736 | tf_op jit(solution)/shard_map/ppermute | solution.py:39
  104.5 0.9 collective-permute-done.12.arrived
  106.0 4.0 %collective-permute-done.14 = bf16[512,512]{1,0:T(8,128)(2,1)S(1)} collective-permute-done((bf16[512,512]{1,0:T(8,128)(2,1)S(1)}, bf16[512,512]{1,0:T(8,128)(2,1)S(1)}, u32[]{:S(2)}, u32[]{:S(2)}) %collective-permute-start.14) | collective-permute-done | bytes 524320 | tf_op jit(solution)/shard_map/ppermute | solution.py:35
  110.1 1.0 copy-done.7
  111.1 1.9 collective-permute-start.17
  113.0 2.4 %collective-permute-start.15 = (bf16[1024,512]{1,0:T(8,128)(2,1)}, bf16[1024,512]{1,0:T(8,128)(2,1)}, u32[]{:S(2)}, u32[]{:S(2)}) collective-permute-start(bf16[1024,512]{1,0:T(8,128)(2,1)} %bitcast.4.refs_0_), channel_id=1, source_target_pairs={{0,8},{8,0},{16,24},{24,16},{32,40},{40,32},{48,56},{56,48},{1,9},... | collective-permute-start | bytes 3145736 | tf_op jit(solution)/shard_map/ppermute | solution.py:39
  115.4 6.1 %collective-permute-start.19 = (bf16[1,128,256]{2,1,0:T(8,128)(2,1)}, bf16[1,128,256]{2,1,0:T(8,128)(2,1)}, u32[]{:S(2)}, u32[]{:S(2)}) collective-permute-start(bf16[1,128,256]{2,1,0:T(8,128)(2,1)} %get-tuple-element.53), channel_id=1, source_target_pairs={{0,4},{1,5},{2,6},{3,7},{4,0},{5,1},{6,2},{7,3},{8,12},{9,13},{10,... | collective-permute-start | bytes 196616 | tf_op jit(solution)/shard_map/ppermute | solution.py:30
  122.2 1.0 copy-done.8
  123.5 1.0 copy-done.10
  124.5 6.1 %shard_map.99.query = bf16[160,512]{1,0:T(8,128)(2,1)} custom-call(s32[8]{0:T(128)} %get-tuple-element.57.dp_ref, bf16[8,160,1024]{2,1,0:T(8,128)(2,1)} %all-gather.2.cloned.1.call-done.features, bf16[1024,512]{1,0:T(8,128)(2,1)} %bitcast.4.refs_0_, bf16[1024,512]{1,0:T(8,128)(2,1)} %collective-permute-done.15.refs_1_, ...), custom_call_target="tpu_custom_call" | custom-call | tf_op jit(solution)/shard_map/pallas_call | solution.py:49
  130.7 0.9 copy-done.3
  131.6 2.9 %shard_map.100 = (bf16[160,512]{1,0:T(8,128)(2,1)}, bf16[1,128,256]{2,1,0:T(8,128)(2,1)S(1)}) custom-call(bf16[160,512]{1,0:T(8,128)(2,1)S(1)} %copy-done.3, f32[128,256]{1,0:T(8,128)S(1)} %bitcast.15, bf16[128,256]{1,0:T(8,128)(2,1)} %bitcast.6.arrived, f32[160,128]{1,0:T(8,128)S(1)} %copy-done.5, bf16[160,512]{1,0:T(8,128)(2,1)S(1)} %bitcast.14, ...), custom_call_target="tpu_custom_call" | custom-call | tf_op jit(solution)/shard_map/pallas_call | solution.py:49
  134.5 3.7 %collective-permute-start.20 = (bf16[1,128,256]{2,1,0:T(8,128)(2,1)S(1)}, bf16[1,128,256]{2,1,0:T(8,128)(2,1)S(1)}, u32[]{:S(2)}, u32[]{:S(2)}) collective-permute-start(bf16[1,128,256]{2,1,0:T(8,128)(2,1)S(1)} %get-tuple-element.55), channel_id=1, source_target_pairs={{0,4},{1,5},{2,6},{3,7},{4,0},{5,1},{6,2},{7,3},{8,12},{9,13},{10,... | collective-permute-start | bytes 196616 | tf_op jit(solution)/shard_map/ppermute | solution.py:30
  138.2 9.2 %collective-permute-done.20 = bf16[1,128,256]{2,1,0:T(8,128)(2,1)S(1)} collective-permute-done((bf16[1,128,256]{2,1,0:T(8,128)(2,1)S(1)}, bf16[1,128,256]{2,1,0:T(8,128)(2,1)S(1)}, u32[]{:S(2)}, u32[]{:S(2)}) %collective-permute-start.20) | collective-permute-done | bytes 65568 | tf_op jit(solution)/shard_map/ppermute | solution.py:30
  147.4 1.9 collective-permute-start.21
  149.4 5.9 %collective-permute-done.21 = bf16[2,128,256]{2,1,0:T(8,128)(2,1)S(1)} collective-permute-done((bf16[2,128,256]{2,1,0:T(8,128)(2,1)S(1)}, bf16[2,128,256]{2,1,0:T(8,128)(2,1)S(1)}, u32[]{:S(2)}, u32[]{:S(2)}) %collective-permute-start.21) | collective-permute-done | bytes 131104 | tf_op jit(solution)/shard_map/ppermute | solution.py:30
  155.3 5.5 %collective-permute-start.22 = (bf16[4,128,256]{2,1,0:T(8,128)(2,1)S(1)}, bf16[4,128,256]{2,1,0:T(8,128)(2,1)S(1)}, u32[]{:S(2)}, u32[]{:S(2)}) collective-permute-start(bf16[4,128,256]{2,1,0:T(8,128)(2,1)S(1)} %constant_dynamic-update-slice_fusion.4.near), channel_id=1, source_target_pairs={{0,1},{1,0},{2,3},{3,2},{4,5},{5,4},{6,7},{7,6},{8,9},{9,8},{10,11... | collective-permute-start | bytes 786440 | tf_op jit(solution)/shard_map/ppermute | solution.py:30
  160.8 5.9 %collective-permute-done.22.far = bf16[4,128,256]{2,1,0:T(8,128)(2,1)S(1)} collective-permute-done((bf16[4,128,256]{2,1,0:T(8,128)(2,1)S(1)}, bf16[4,128,256]{2,1,0:T(8,128)(2,1)S(1)}, u32[]{:S(2)}, u32[]{:S(2)}) %collective-permute-start.22) | collective-permute-done | bytes 262176 | tf_op jit(solution)/shard_map/ppermute | solution.py:30
  166.7 2.5 %shard_map.101 = bf16[128,1024]{1,0:T(8,128)(2,1)S(1)} custom-call(s32[8]{0:T(128)S(1)} %get-tuple-element.56.place_ref, bf16[4,128,256]{2,1,0:T(8,128)(2,1)S(1)} %constant_dynamic-update-slice_fusion.4.near, bf16[4,128,256]{2,1,0:T(8,128)(2,1)S(1)} %collective-permute-done.22.far, bf16[1024,256]{1,0:T(8,128)(2,1)S(1)} %pad_maximum_fusion.refs_0_, ...), custom_call_target="tpu_custom_call" | custom-call | tf_op jit(solution)/shard_map/pallas_call | solution.py:49
  169.2 33.2 %all_to_all.11 = bf16[8,16,1024]{2,1,0:T(8,128)(2,1)S(1)} all-to-all(bf16[8,16,1024]{2,1,0:T(8,128)(2,1)S(1)} %bitcast.13), channel_id=1, replica_groups=mesh['section'=8,'dp'=8,'tensor'=8] {'section'}, dimensions={0} | all-to-all | bytes 524288 | tf_op jit(solution)/shard_map/all_to_all | solution.py:250
  (47 shorter events, 2.7 us)
Async XLA Ops:
  7.2 117.3 %all-gather.2.cloned.1.call-start = ((), (), s32[]{:S(2)}) async-start(), calls=%async_computation.2 | async-start | bytes 2949120 | tf_op jit(solution)/shard_map/all_gather | solution.py:167
  9.0 25.3 %collective-permute-start = (bf16[1024,256]{1,0:T(8,128)(2,1)S(1)}, bf16[1024,256]{1,0:T(8,128)(2,1)S(1)}, u32[]{:S(2)}, u32[]{:S(2)}) collective-permute-start(bf16[1024,256]{1,0:T(8,128)(2,1)S(1)} %pad_maximum_fusion.refs_0_), channel_id=1, source_target_pairs={{0,16},{8,24},{16,32},{24,40},{32,48},{40,56},{48,0},{56,8},{1,17}... | collective-permute-start | bytes 1572872 | tf_op jit(solution)/shard_map/ppermute | solution.py:35
  11.1 23.1 %collective-permute-start.1 = (bf16[1024,256]{1,0:T(8,128)(2,1)S(1)}, bf16[1024,256]{1,0:T(8,128)(2,1)S(1)}, u32[]{:S(2)}, u32[]{:S(2)}) collective-permute-start(bf16[1024,256]{1,0:T(8,128)(2,1)S(1)} %pad_maximum_fusion.refs_0_), channel_id=1, source_target_pairs={{0,48},{8,56},{16,0},{24,8},{32,16},{40,24},{48,32},{56,40},{1,49}... | collective-permute-start | bytes 1572872 | tf_op jit(solution)/shard_map/ppermute | solution.py:35
  14.8 19.4 %collective-permute-start.3 = (bf16[1024,256]{1,0:T(8,128)(2,1)S(1)}, bf16[1024,256]{1,0:T(8,128)(2,1)S(1)}, u32[]{:S(2)}, u32[]{:S(2)}) collective-permute-start(bf16[1024,256]{1,0:T(8,128)(2,1)S(1)} %pad_maximum_fusion.refs_0_), channel_id=1, source_target_pairs={{0,8},{8,0},{16,24},{24,16},{32,40},{40,32},{48,56},{56,48},{1,9},... | collective-permute-start | bytes 1572872 | tf_op jit(solution)/shard_map/ppermute | solution.py:39
  16.8 17.5 %collective-permute-start.2 = (bf16[16,1024]{1,0:T(8,128)(2,1)}, bf16[16,1024]{1,0:T(8,128)(2,1)S(1)}, u32[]{:S(2)}, u32[]{:S(2)}) collective-permute-start(bf16[16,1024]{1,0:T(8,128)(2,1)} %bitcast.16), channel_id=1, source_target_pairs={{0,256},{64,320},{128,384},{192,448},{256,0},{320,64},{384,128},{4... | collective-permute-start | bytes 98312 | tf_op jit(solution)/shard_map/ppermute | solution.py:21
  34.3 22.2 %collective-permute-start.6 = (bf16[1024,256]{1,0:T(8,128)(2,1)S(1)}, bf16[1024,256]{1,0:T(8,128)(2,1)S(1)}, u32[]{:S(2)}, u32[]{:S(2)}) collective-permute-start(bf16[1024,256]{1,0:T(8,128)(2,1)S(1)} %collective-permute-done.refs_2_), channel_id=1, source_target_pairs={{0,8},{8,0},{16,24},{24,16},{32,40},{40,32},{48,56},{56,48},{1,9},... | collective-permute-start | bytes 1572872 | tf_op jit(solution)/shard_map/ppermute | solution.py:39
  36.2 20.3 %collective-permute-start.7 = (bf16[1024,256]{1,0:T(8,128)(2,1)S(1)}, bf16[1024,256]{1,0:T(8,128)(2,1)S(1)}, u32[]{:S(2)}, u32[]{:S(2)}) collective-permute-start(bf16[1024,256]{1,0:T(8,128)(2,1)S(1)} %collective-permute-done.1.refs_6_), channel_id=1, source_target_pairs={{0,8},{8,0},{16,24},{24,16},{32,40},{40,32},{48,56},{56,48},{1,9},... | collective-permute-start | bytes 1572872 | tf_op jit(solution)/shard_map/ppermute | solution.py:39
  38.7 17.8 %collective-permute-start.4 = (bf16[512,256]{1,0:T(8,128)(2,1)S(1)}, bf16[512,256]{1,0:T(8,128)(2,1)S(1)}, u32[]{:S(2)}, u32[]{:S(2)}) collective-permute-start(bf16[512,256]{1,0:T(8,128)(2,1)S(1)} %slice.12), channel_id=1, source_target_pairs={{0,16},{8,24},{16,32},{24,40},{32,48},{40,56},{48,0},{56,8},{1,17}... | collective-permute-start | bytes 786440 | tf_op jit(solution)/shard_map/ppermute | solution.py:35
  41.8 14.7 %collective-permute-start.5 = (bf16[512,256]{1,0:T(8,128)(2,1)S(1)}, bf16[512,256]{1,0:T(8,128)(2,1)S(1)}, u32[]{:S(2)}, u32[]{:S(2)}) collective-permute-start(bf16[512,256]{1,0:T(8,128)(2,1)S(1)} %slice.13), channel_id=1, source_target_pairs={{0,48},{8,56},{16,0},{24,8},{32,16},{40,24},{48,32},{56,40},{1,49}... | collective-permute-start | bytes 786440 | tf_op jit(solution)/shard_map/ppermute | solution.py:35
  44.5 0.8 copy-start.6
  56.5 0.8 copy-start
  57.3 30.1 %collective-permute-start.10 = (bf16[1024,512]{1,0:T(8,128)(2,1)}, bf16[1024,512]{1,0:T(8,128)(2,1)}, u32[]{:S(2)}, u32[]{:S(2)}) collective-permute-start(bf16[1024,512]{1,0:T(8,128)(2,1)} %bitcast.4.refs_0_), channel_id=1, source_target_pairs={{0,16},{8,24},{16,32},{24,40},{32,48},{40,56},{48,0},{56,8},{1,17}... | collective-permute-start | bytes 3145736 | tf_op jit(solution)/shard_map/ppermute | solution.py:35
  61.2 26.2 %collective-permute-start.11 = (bf16[1024,512]{1,0:T(8,128)(2,1)}, bf16[1024,512]{1,0:T(8,128)(2,1)}, u32[]{:S(2)}, u32[]{:S(2)}) collective-permute-start(bf16[1024,512]{1,0:T(8,128)(2,1)} %bitcast.4.refs_0_), channel_id=1, source_target_pairs={{0,48},{8,56},{16,0},{24,8},{32,16},{40,24},{48,32},{56,40},{1,49}... | collective-permute-start | bytes 3145736 | tf_op jit(solution)/shard_map/ppermute | solution.py:35
  63.2 3.9 %collective-permute-start.8 = (bf16[1024,256]{1,0:T(8,128)(2,1)S(1)}, bf16[1024,256]{1,0:T(8,128)(2,1)}, u32[]{:S(2)}, u32[]{:S(2)}) collective-permute-start(bf16[1024,256]{1,0:T(8,128)(2,1)S(1)} %constant_dynamic-update-slice_fusion.refs_4_), channel_id=1, source_target_pairs={{0,8},{8,0},{16,24},{24,16},{32,40},{40,32},{48,56},{56,48},{1,9},... | collective-permute-start | bytes 1572872 | tf_op jit(solution)/shard_map/ppermute | solution.py:39
  67.2 1.0 copy-start.1
  70.1 17.2 %collective-permute-start.9 = (bf16[4,128,256]{2,1,0:T(8,128)(2,1)S(1)}, bf16[4,128,256]{2,1,0:T(8,128)(2,1)S(1)}, u32[]{:S(2)}, u32[]{:S(2)}) collective-permute-start(bf16[4,128,256]{2,1,0:T(8,128)(2,1)S(1)} %get-tuple-element.39), channel_id=1, source_target_pairs={{0,1},{1,0},{2,3},{3,2},{4,5},{5,4},{6,7},{7,6},{8,9},{9,8},{10,11... | collective-permute-start | bytes 786440 | tf_op jit(solution)/shard_map/ppermute | solution.py:30
  88.5 17.5 %collective-permute-start.13 = (bf16[512,512]{1,0:T(8,128)(2,1)S(1)}, bf16[512,512]{1,0:T(8,128)(2,1)S(1)}, u32[]{:S(2)}, u32[]{:S(2)}) collective-permute-start(bf16[512,512]{1,0:T(8,128)(2,1)S(1)} %slice.14), channel_id=1, source_target_pairs={{0,16},{8,24},{16,32},{24,40},{32,48},{40,56},{48,0},{56,8},{1,17}... | collective-permute-start | bytes 1572872 | tf_op jit(solution)/shard_map/ppermute | solution.py:35
  93.6 16.4 %collective-permute-start.14 = (bf16[512,512]{1,0:T(8,128)(2,1)S(1)}, bf16[512,512]{1,0:T(8,128)(2,1)S(1)}, u32[]{:S(2)}, u32[]{:S(2)}) collective-permute-start(bf16[512,512]{1,0:T(8,128)(2,1)S(1)} %slice.15), channel_id=1, source_target_pairs={{0,48},{8,56},{16,0},{24,8},{32,16},{40,24},{48,32},{56,40},{1,49}... | collective-permute-start | bytes 1572872 | tf_op jit(solution)/shard_map/ppermute | solution.py:35
  95.5 9.9 %collective-permute-start.12 = (bf16[2,128,256]{2,1,0:T(8,128)(2,1)S(1)}, bf16[2,128,256]{2,1,0:T(8,128)(2,1)S(1)}, u32[]{:S(2)}, u32[]{:S(2)}) collective-permute-start(bf16[2,128,256]{2,1,0:T(8,128)(2,1)S(1)} %get-tuple-element.44), channel_id=1, source_target_pairs={{0,2},{1,3},{2,0},{3,1},{4,6},{5,7},{6,4},{7,5},{8,10},{9,11},{10,... | collective-permute-start | bytes 393224 | tf_op jit(solution)/shard_map/ppermute | solution.py:30
  100.1 22.0 %collective-permute-start.16 = (bf16[1024,512]{1,0:T(8,128)(2,1)}, bf16[1024,512]{1,0:T(8,128)(2,1)S(1)}, u32[]{:S(2)}, u32[]{:S(2)}) collective-permute-start(bf16[1024,512]{1,0:T(8,128)(2,1)} %collective-permute-done.10.refs_2_), channel_id=1, source_target_pairs={{0,8},{8,0},{16,24},{24,16},{32,40},{40,32},{48,56},{56,48},{1,9},... | collective-permute-start | bytes 3145736 | tf_op jit(solution)/shard_map/ppermute | solution.py:39
  102.0 20.1 %collective-permute-start.18 = (bf16[1024,512]{1,0:T(8,128)(2,1)}, bf16[1024,512]{1,0:T(8,128)(2,1)S(1)}, u32[]{:S(2)}, u32[]{:S(2)}) collective-permute-start(bf16[1024,512]{1,0:T(8,128)(2,1)} %collective-permute-done.11.refs_6_), channel_id=1, source_target_pairs={{0,8},{8,0},{16,24},{24,16},{32,40},{40,32},{48,56},{56,48},{1,9},... | collective-permute-start | bytes 3145736 | tf_op jit(solution)/shard_map/ppermute | solution.py:39
  110.1 1.0 copy-start.7
  111.1 11.1 %collective-permute-start.17 = (bf16[1024,512]{1,0:T(8,128)(2,1)S(1)}, bf16[1024,512]{1,0:T(8,128)(2,1)S(1)}, u32[]{:S(2)}, u32[]{:S(2)}) collective-permute-start(bf16[1024,512]{1,0:T(8,128)(2,1)S(1)} %constant_dynamic-update-slice_fusion.2.refs_4_), channel_id=1, source_target_pairs={{0,8},{8,0},{16,24},{24,16},{32,40},{40,32},{48,56},{56,48},{1,9},... | collective-permute-start | bytes 3145736 | tf_op jit(solution)/shard_map/ppermute | solution.py:39
  113.0 11.5 %collective-permute-start.15 = (bf16[1024,512]{1,0:T(8,128)(2,1)}, bf16[1024,512]{1,0:T(8,128)(2,1)}, u32[]{:S(2)}, u32[]{:S(2)}) collective-permute-start(bf16[1024,512]{1,0:T(8,128)(2,1)} %bitcast.4.refs_0_), channel_id=1, source_target_pairs={{0,8},{8,0},{16,24},{24,16},{32,40},{40,32},{48,56},{56,48},{1,9},... | collective-permute-start | bytes 3145736 | tf_op jit(solution)/shard_map/ppermute | solution.py:39
  115.4 15.2 %collective-permute-start.19 = (bf16[1,128,256]{2,1,0:T(8,128)(2,1)}, bf16[1,128,256]{2,1,0:T(8,128)(2,1)}, u32[]{:S(2)}, u32[]{:S(2)}) collective-permute-start(bf16[1,128,256]{2,1,0:T(8,128)(2,1)} %get-tuple-element.53), channel_id=1, source_target_pairs={{0,4},{1,5},{2,6},{3,7},{4,0},{5,1},{6,2},{7,3},{8,12},{9,13},{10,... | collective-permute-start | bytes 196616 | tf_op jit(solution)/shard_map/ppermute | solution.py:30
  122.1 1.0 copy-start.8
  122.2 1.3 copy-start.9
  123.5 1.0 copy-start.10
  124.5 6.2 %copy-start.4 = (bf16[1,160,512]{2,1,0:T(8,128)(2,1)S(1)}, bf16[1,160,512]{2,1,0:T(8,128)(2,1)}, u32[]{:S(2)}) copy-start(bf16[1,160,512]{2,1,0:T(8,128)(2,1)} %param.15) | copy-start | bytes 491524
  124.5 6.2 %copy-start.5 = (f32[160,128]{1,0:T(8,128)S(1)}, f32[160,128]{1,0:T(8,128)}, u32[]{:S(2)}) copy-start(f32[160,128]{1,0:T(8,128)} %bias_ref.1) | copy-start | bytes 245764
  124.5 42.2 %copy-start.2 = (bf16[1024,256]{1,0:T(8,128)(2,1)S(1)}, bf16[1024,256]{1,0:T(8,128)(2,1)}, u32[]{:S(2)}) copy-start(bf16[1024,256]{1,0:T(8,128)(2,1)} %copy-done) | copy-start | bytes 1572868
  130.7 0.9 copy-start.3
  134.5 12.9 %collective-permute-start.20 = (bf16[1,128,256]{2,1,0:T(8,128)(2,1)S(1)}, bf16[1,128,256]{2,1,0:T(8,128)(2,1)S(1)}, u32[]{:S(2)}, u32[]{:S(2)}) collective-permute-start(bf16[1,128,256]{2,1,0:T(8,128)(2,1)S(1)} %get-tuple-element.55), channel_id=1, source_target_pairs={{0,4},{1,5},{2,6},{3,7},{4,0},{5,1},{6,2},{7,3},{8,12},{9,13},{10,... | collective-permute-start | bytes 196616 | tf_op jit(solution)/shard_map/ppermute | solution.py:30
  147.4 7.9 %collective-permute-start.21 = (bf16[2,128,256]{2,1,0:T(8,128)(2,1)S(1)}, bf16[2,128,256]{2,1,0:T(8,128)(2,1)S(1)}, u32[]{:S(2)}, u32[]{:S(2)}) collective-permute-start(bf16[2,128,256]{2,1,0:T(8,128)(2,1)S(1)} %pad_maximum_fusion.1), channel_id=1, source_target_pairs={{0,2},{1,3},{2,0},{3,1},{4,6},{5,7},{6,4},{7,5},{8,10},{9,11},{10,... | collective-permute-start | bytes 393224 | tf_op jit(solution)/shard_map/ppermute | solution.py:30
  155.3 11.4 %collective-permute-start.22 = (bf16[4,128,256]{2,1,0:T(8,128)(2,1)S(1)}, bf16[4,128,256]{2,1,0:T(8,128)(2,1)S(1)}, u32[]{:S(2)}, u32[]{:S(2)}) collective-permute-start(bf16[4,128,256]{2,1,0:T(8,128)(2,1)S(1)} %constant_dynamic-update-slice_fusion.4.near), channel_id=1, source_target_pairs={{0,1},{1,0},{2,3},{3,2},{4,5},{5,4},{6,7},{7,6},{8,9},{9,8},{10,11... | collective-permute-start | bytes 786440 | tf_op jit(solution)/shard_map/ppermute | solution.py:30
Sparse Core Ops, SparseCore 0:
  10.1 79.7 all-gather.1

commit v5 on v4

--- a/solution.py
+++ b/solution.py
@@ -9,6 +9,7 @@
 X_SIZE = 4
 Y_SIZE = 4
 N_BLOCKS = 8
+DEPTH = 3
 BF16 = jnp.bfloat16
 F32 = jnp.float32
 VMEM = pl.BlockSpec(memory_space=pltpu.VMEM)
@@ -33,6 +34,12 @@
 def y_shift(a, k):
     pairs = [(y * 2 + c, ((y + k) % Y_SIZE) * 2 + c) for y in range(Y_SIZE) for c in range(2)]
     return lax.ppermute(a, "dp", pairs)
+
+
+def y_gather(a):
+    groups = [[2 * y + c for y in range(Y_SIZE)] for c in range(2)]
+    copies = jnp.broadcast_to(a[None], (Y_SIZE, *a.shape))
+    return lax.all_to_all(copies, "dp", 0, 0, axis_index_groups=groups)
 
 
 def core_swap(a):
@@ -62,13 +69,13 @@
         out[x, 1] = other[...]
 
 
-def pair_kernel(place_ref, half_ref, images, *refs):
-    weights, (keep, send, buffer) = refs[:N_BLOCKS], refs[N_BLOCKS:]
+def pair_kernel(place_ref, half_ref, images, near, far, keep, send, buffer):
     rows = jnp.concatenate(
         [images[x, half_ref[0] ^ z] for z in range(2) for x in range(X_SIZE)], axis=0
     )
-    for slot, w in enumerate(weights):
-        buffer[place_ref[slot]] = dot(rows, w[...])
+    for slot in range(N_BLOCKS):
+        weights = (near, far)[slot % 2][slot // 2]
+        buffer[place_ref[slot]] = dot(rows, weights)
     half = N_BLOCKS // 2
     keep[...] = buffer[:half]
     send[...] = buffer[half:].astype(BF16)
@@ -86,29 +93,40 @@
     return call(fold_kernel, outs, [VMEM] * 2, (keep, arrived))
 
 
-def query_kernel(dp_ref, features, *refs):
-    weights, (out, rows, columns, sems) = refs[:N_BLOCKS], refs[N_BLOCKS:]
+def attention_kernel(dp_ref, features, *refs):
+    blocks, refs = refs[: 2 * N_BLOCKS - 6], refs[2 * N_BLOCKS - 6 :]
+    kept, arrived, bias_ref, cotangent, gate, gated, packed, rows, columns, sems = refs
+    cut = columns.shape[1] // 2
     copies = []
     for slot in range(N_BLOCKS):
-        copies.append(
-            (
-                pltpu.make_async_copy(features.at[dp_ref[slot]], rows.at[slot], sems.at[0, slot]),
-                pltpu.make_async_copy(weights[slot], columns.at[slot], sems.at[1, slot]),
-            )
-        )
-    for pair in copies:
-        for copy in pair:
+        group = [pltpu.make_async_copy(features.at[dp_ref[slot]], rows.at[slot], sems.at[0, slot])]
+        if slot // 2 == 2:
+            for part in range(2):
+                group.append(
+                    pltpu.make_async_copy(
+                        blocks[4 + 2 * part + slot % 2],
+                        columns.at[slot, pl.ds(part * cut, cut)],
+                        sems.at[1 + part, slot],
+                    )
+                )
+        else:
+            at = slot if slot < 4 else slot + 2
+            group.append(pltpu.make_async_copy(blocks[at], columns.at[slot], sems.at[1, slot]))
+        copies.append(group)
+    for group in copies[:DEPTH]:
+        for copy in group:
             copy.start()
-    total = None
-    for slot, pair in enumerate(copies):
-        for copy in pair:
+    query = None
+    for slot, group in enumerate(copies):
+        for copy in group:
             copy.wait()
+        if slot + DEPTH < N_BLOCKS:
+            for copy in copies[slot + DEPTH]:
+                copy.start()
         part = dot(rows[slot], columns[slot])
-        total = part if total is None else total + part
-    out[...] = total.astype(BF16)
-
-
-def attention_kernel(query, kept, arrived, bias_ref, cotangent, gate, gated, packed):
+        query = part if query is None else query + part
+    query = query.astype(BF16)
+
     pairs = (kept[...] + arrived[...].astype(F32)).astype(BF16)
     keys, values = pairs[:, :HEAD_SIZE], pairs[:, HEAD_SIZE:]
     scaling = HEAD_SIZE ** (-0.5)
@@ -135,14 +153,14 @@
     )
 
 
-def image_kernel(place_ref, near, far, *refs):
-    weights, (out, buffer) = refs[:N_BLOCKS], refs[N_BLOCKS:]
-    half = N_BLOCKS // 2
-    buffer[:half] = near[...]
-    buffer[half:] = far[...]
-    total = dot(buffer[place_ref[0]], weights[0][...], BY_COLUMNS)
-    for slot in range(1, N_BLOCKS):
-        total = total + dot(buffer[place_ref[slot]], weights[slot][...], BY_COLUMNS)
+def image_kernel(place_ref, own, by4, by2, by1, near, far, out, buffer):
+    for at, part in ((0, own), (1, by4), (2, by2), (4, by1)):
+        buffer[at : at + part.shape[0]] = part[...]
+    total = None
+    for slot in range(N_BLOCKS):
+        weights = (near, far)[slot % 2][slot // 2]
+        part = dot(buffer[place_ref[slot]], weights, BY_COLUMNS)
+        total = part if total is None else total + part
     out[...] = total.astype(BF16)
 
 
@@ -161,7 +179,7 @@
     dp = lax.axis_index("dp")
     slots = jnp.arange(N_BLOCKS, dtype=jnp.int32)
     dp_order = ((((dp >> 1) - (slots >> 1)) & (Y_SIZE - 1)) << 1) | ((dp ^ slots) & 1)
-    apart = lax.axis_index("tensor") ^ dp_order
+    apart = lax.axis_index("tensor") ^ (slots ^ (dp & 1))
     place = ((apart & 1) << 2) | (apart & 2) | (apart >> 2)
 
     features = lax.all_gather(hidden[0], "tensor", axis=0)
@@ -169,31 +187,14 @@
     own = image_tokens[0]
     rows, width = own.shape
     pair = jnp.concatenate([key_weight_stack[0], value_weight_stack[0]], axis=1)
-    cut = pair.shape[0] // 2
-    first = (y_shift(pair, 1), y_shift(pair, -1), z_swap(own), core_swap(pair))
-    before, behind, other, pair_swapped = lax.optimization_barrier(first)
-    across = (y_shift(before[:cut], 1), y_shift(behind[cut:], -1))
-    swapped = (core_swap(before), core_swap(behind))
-
     copies = call(
         spread_kernel,
         jax.ShapeDtypeStruct((X_SIZE, 2, rows, width), BF16),
         [VMEM] * 2,
-        (own, other),
-    )
-    images = x_exchange(copies)
-    across, swapped, images, w = lax.optimization_barrier((across, swapped, images, w_query[0]))
-    opposite = jnp.concatenate(across, axis=0)
-    pair_weights = [
-        pair,
-        pair_swapped,
-        before,
-        swapped[0],
-        opposite,
-        core_swap(opposite),
-        behind,
-        swapped[1],
-    ]
+        (own, z_swap(own)),
+    )
+    near_pairs, images = lax.optimization_barrier((y_gather(pair), x_exchange(copies)))
+    far_pairs = core_swap(near_pairs)
     image_count = 2 * X_SIZE * rows
     block = (image_count, 2 * HEAD_SIZE)
     half = N_BLOCKS // 2
@@ -201,49 +202,53 @@
     keep, send = call(
         pair_kernel,
         (jax.ShapeDtypeStruct((half, *block), F32), jax.ShapeDtypeStruct((half, *block), BF16)),
-        [SMEM] * 2 + [VMEM] * 9,
-        (place, lax.axis_index("section")[None] >> 2, images, *pair_weights),
+        [SMEM] * 2 + [VMEM] * 3,
+        (place, lax.axis_index("section")[None] >> 2, images, near_pairs, far_pairs),
         [pltpu.VMEM((N_BLOCKS, *block), F32)],
     )
+
+    w, _ = lax.optimization_barrier((w_query[0], near_pairs))
+    cut = w.shape[0] // 2
     before, behind = y_shift(w, 1), y_shift(w, -1)
     keep, send = fold(keep, t_swap(send, 1))
     (keep, send), before, behind = lax.optimization_barrier(((keep, send), before, behind))
-    cut = w.shape[0] // 2
     across = (y_shift(before[:cut], 1), y_shift(behind[cut:], -1))
     keep, send = fold(keep, t_swap(send, 2))
     (keep, send), across, w = lax.optimization_barrier(((keep, send), across, w))
     arrived = t_swap(send, 4)
-    opposite = jnp.concatenate(across, axis=0)
-    query_weights = [v for b in (w, before, opposite, behind) for v in (b, core_swap(b))]
+    query_weights = [v for b in (w, before, *across, behind) for v in (b, core_swap(b))]
+
     tokens, columns = hidden.shape[1], w_query.shape[2]
-    query = call(
-        query_kernel,
-        jax.ShapeDtypeStruct((tokens, columns), BF16),
-        [SMEM] + [pl.BlockSpec(memory_space=pl.ANY)] * 9,
-        (dp_order, features, *query_weights),
+    gated_out, packed = call(
+        attention_kernel,
+        (jax.ShapeDtypeStruct((tokens, columns), BF16), jax.ShapeDtypeStruct((1, *block), BF16)),
+        [SMEM] + [pl.BlockSpec(memory_space=pl.ANY)] * 11 + [VMEM] * 5,
+        (
+            dp_order,
+            features,
+            *query_weights,
+            keep[0],
+            arrived[0],
+            score_bias,
+            cotangent[0],
+            gate_logit.reshape(1, 1),
+        ),
         [
             pltpu.VMEM(features.shape, BF16),
             pltpu.VMEM((N_BLOCKS, *w.shape), BF16),
-            pltpu.SemaphoreType.DMA((2, N_BLOCKS)),
+            pltpu.SemaphoreType.DMA((3, N_BLOCKS)),
         ],
         limit=60 << 20,
     )
 
-    gated_out, packed = call(
-        attention_kernel,
-        (jax.ShapeDtypeStruct((tokens, columns), BF16), jax.ShapeDtypeStruct((1, *block), BF16)),
-        [VMEM] * 6,
-        (query, keep[0], arrived[0], score_bias, cotangent[0], gate_logit.reshape(1, 1)),
-    )
-
-    near = jnp.concatenate([packed, t_swap(packed, 4)])
-    near = jnp.concatenate([near, t_swap(near, 2)])
-    far = t_swap(near, 1)
+    by4 = t_swap(packed, 4)
+    by2 = t_swap(jnp.concatenate([packed, by4]), 2)
+    by1 = t_swap(jnp.concatenate([packed, by4, by2]), 1)
     portion = call(
         image_kernel,
         jax.ShapeDtypeStruct((image_count, width), BF16),
-        [SMEM] + [VMEM] * 10,
-        (place, near, far, *pair_weights),
+        [SMEM] + [VMEM] * 6,
+        (place, packed, by4, by2, by1, near_pairs, far_pairs),
         [pltpu.VMEM((N_BLOCKS, *block), BF16)],
     )
     portion = portion.reshape(2 * X_SIZE, rows, width)

time: 211 us -> 230 us (1.090)
  the two profiles are of different devices: /device:TPU:56 before, /device:TPU:32 now
where the time goes in v5:
time: 230 us; the launch traced here: 229 us
  waiting for transfers between devices  87.6 us (38%)
  starting transfers between devices  68.2 us (30%)
  blocking collectives  34.2 us (15%)
  Pallas kernels  15 us (7%)
  between operations  14.9 us (6%)
  local copies, waits for them, and re-layouts  4.87 us (2%)
  other arithmetic  3.97 us (2%)
    ppermute x6, waiting for transfers between devices, t_swap(): return lax.ppermute(a, 'tensor', [(t, t ^ k) for t in range(8)])  51.6 us
    all_to_all x1, blocking collectives, local(): lax.all_to_all(portion, 'section', 0, 0).astype(F32)  34.2 us
    all_to_all x1, waiting for transfers between devices, y_gather(): return lax.all_to_all(copies, 'dp', 0, 0, axis_index_groups=groups)  22.9 us
    ppermute x6, starting transfers between devices, t_swap(): return lax.ppermute(a, 'tensor', [(t, t ^ k) for t in range(8)])  20.7 us
    pallas_call x6, Pallas kernels, call(): pl.pallas_call(kernel, out_shape=outs, in_specs=in_specs, out_specs=jax.t...  15 us
    ppermute x1, starting transfers between devices, z_swap(): lax.ppermute(a, 'section', [(s, (s + X_SIZE) % (2 * X_SIZE)) for s in ran...  14.8 us
    ppermute x6, starting transfers between devices, core_swap(): return lax.ppermute(a, 'dp', [(d, d ^ 1) for d in range(2 * Y_SIZE)])  12.2 us
    ppermute x4, starting transfers between devices, y_shift(): return lax.ppermute(a, 'dp', pairs)  11.7 us
  transfers between devices with their start and end apart: 20, of which 11 were waited for; matrix products, arithmetic and copies ran while one was open for 1% of the time, Pallas kernels for 1%

profile of v5, /device:TPU:32, one launch (start us, length us, event | category | flops | bytes accessed | tf_op | source)
XLA Modules:
  0.0 228.7 jit_solution(459328230530093168)
XLA Ops:
  7.2 14.8 %collective-permute-start = (bf16[16,1024]{1,0:T(8,128)(2,1)}, bf16[16,1024]{1,0:T(8,128)(2,1)S(1)}, u32[]{:S(2)}, u32[]{:S(2)}) collective-permute-start(bf16[16,1024]{1,0:T(8,128)(2,1)} %bitcast.15), channel_id=1, source_target_pairs={{0,256},{64,320},{128,384},{192,448},{256,0},{320,64},{384,128},{4... | collective-permute-start | bytes 98312 | tf_op jit(solution)/shard_map/ppermute | solution.py:22
  22.0 2.5 %collective-permute-done.other = bf16[16,1024]{1,0:T(8,128)(2,1)S(1)} collective-permute-done((bf16[16,1024]{1,0:T(8,128)(2,1)}, bf16[16,1024]{1,0:T(8,128)(2,1)S(1)}, u32[]{:S(2)}, u32[]{:S(2)}) %collective-permute-start) | collective-permute-done | bytes 32800 | tf_op jit(solution)/shard_map/ppermute | solution.py:22
  24.5 0.8 copy-done.2
  25.3 0.7 shard_map.95
  26.0 4.3 %all-to-all-start.1 = ((bf16[4,2,16,1024]{3,2,1,0:T(8,128)(2,1)}), bf16[4,2,16,1024]{3,2,1,0:T(8,128)(2,1)S(1)}, u32[]{:S(2)}, u32[]{:S(2)}) async-start(bf16[4,2,16,1024]{3,2,1,0:T(8,128)(2,1)} %shard_map.95), calls=%async_computation.1 | async-start | bytes 524288 | tf_op jit(solution)/shard_map/all_to_all | solution.py:27
  30.3 1.1 pad_maximum_fusion
  31.4 5.6 %all-to-all-done.1.images = bf16[4,2,16,1024]{3,2,1,0:T(8,128)(2,1)S(1)} async-done(((bf16[4,2,16,1024]{3,2,1,0:T(8,128)(2,1)}), bf16[4,2,16,1024]{3,2,1,0:T(8,128)(2,1)S(1)}, u32[]{:S(2)}, u32[]{:S(2)}) %all-to-all-start.1) | async-done | bytes 262176 | tf_op jit(solution)/shard_map/all_to_all | solution.py:27
  37.0 1.5 broadcast_in_dim.6
  38.5 4.5 %all-to-all-start = ((bf16[4,1024,256]{2,1,0:T(8,128)(2,1)}), bf16[4,1024,256]{2,1,0:T(8,128)(2,1)S(1)}, u32[]{:S(2)}, u32[]{:S(2)}) async-start(bf16[4,1024,256]{2,1,0:T(8,128)(2,1)} %broadcast_in_dim.6), calls=%async_computation | async-start | bytes 4194304 | tf_op jit(solution)/shard_map/all_to_all | solution.py:42
  43.0 0.7 all-gather.2.cloned.1.call-update
  43.7 22.9 %all-to-all-done.near = bf16[4,1024,256]{2,1,0:T(8,128)(2,1)S(1)} async-done(((bf16[4,1024,256]{2,1,0:T(8,128)(2,1)}), bf16[4,1024,256]{2,1,0:T(8,128)(2,1)S(1)}, u32[]{:S(2)}, u32[]{:S(2)}) %all-to-all-start) | async-done | bytes 2097184 | tf_op jit(solution)/shard_map/all_to_all | solution.py:42
  66.5 1.9 collective-permute-start.1
  68.5 3.1 %collective-permute-start.4 = (bf16[1024,512]{1,0:T(8,128)(2,1)}, bf16[1024,512]{1,0:T(8,128)(2,1)S(1)}, u32[]{:S(2)}, u32[]{:S(2)}) collective-permute-start(bf16[1024,512]{1,0:T(8,128)(2,1)} %bitcast.4.refs_0_), channel_id=1, source_target_pairs={{0,48},{8,56},{16,0},{24,8},{32,16},{40,24},{48,32},{56,40},{1,49}... | collective-permute-start | bytes 3145736 | tf_op jit(solution)/shard_map/ppermute | solution.py:36
  71.5 2.8 %collective-permute-start.3 = (bf16[1024,512]{1,0:T(8,128)(2,1)}, bf16[1024,512]{1,0:T(8,128)(2,1)}, u32[]{:S(2)}, u32[]{:S(2)}) collective-permute-start(bf16[1024,512]{1,0:T(8,128)(2,1)} %bitcast.4.refs_0_), channel_id=1, source_target_pairs={{0,16},{8,24},{16,32},{24,40},{32,48},{40,56},{48,0},{56,8},{1,17}... | collective-permute-start | bytes 3145736 | tf_op jit(solution)/shard_map/ppermute | solution.py:36
  74.3 0.0 collective-permute-done.1.far
  74.4 2.4 %shard_map.96 = (f32[4,128,256]{2,1,0:T(8,128)S(1)}, bf16[4,128,256]{2,1,0:T(8,128)(2,1)S(1)}) custom-call(s32[8]{0:T(128)S(1)} %shift-right-arithmetic_or_fusion.place_ref, s32[1]{0:T(128)} %bitcast.half_ref, bf16[4,2,16,1024]{3,2,1,0:T(8,128)(2,1)S(1)} %all-to-all-done.1.images, bf16[4,1024,256]{2,1,0:T(8,128)(2,1)S(1)} %all-to-all-done.near, ...), custom_call_target="tpu_custom_call" | custom-call | tf_op jit(solution)/shard_map/pallas_call | solution.py:56
  76.8 3.0 %collective-permute-start.2 = (bf16[4,128,256]{2,1,0:T(8,128)(2,1)S(1)}, bf16[4,128,256]{2,1,0:T(8,128)(2,1)S(1)}, u32[]{:S(2)}, u32[]{:S(2)}) collective-permute-start(bf16[4,128,256]{2,1,0:T(8,128)(2,1)S(1)} %get-tuple-element.25), channel_id=1, source_target_pairs={{0,1},{1,0},{2,3},{3,2},{4,5},{5,4},{6,7},{7,6},{8,9},{9,8},{10,11... | collective-permute-start | bytes 786440 | tf_op jit(solution)/shard_map/ppermute | solution.py:31
  79.8 17.2 %collective-permute-done.2.arrived = bf16[4,128,256]{2,1,0:T(8,128)(2,1)S(1)} collective-permute-done((bf16[4,128,256]{2,1,0:T(8,128)(2,1)S(1)}, bf16[4,128,256]{2,1,0:T(8,128)(2,1)S(1)}, u32[]{:S(2)}, u32[]{:S(2)}) %collective-permute-start.2) | collective-permute-done | bytes 262176 | tf_op jit(solution)/shard_map/ppermute | solution.py:31
  97.0 0.0 collective-permute-done.4.refs_8_
  97.0 3.2 %collective-permute-done.3.refs_2_ = bf16[1024,512]{1,0:T(8,128)(2,1)} collective-permute-done((bf16[1024,512]{1,0:T(8,128)(2,1)}, bf16[1024,512]{1,0:T(8,128)(2,1)}, u32[]{:S(2)}, u32[]{:S(2)}) %collective-permute-start.3) | collective-permute-done | bytes 1048608 | tf_op jit(solution)/shard_map/ppermute | solution.py:36
  100.3 1.1 slice.6
  101.4 1.9 collective-permute-start.7
  103.3 3.9 %collective-permute-start.6 = (bf16[512,512]{1,0:T(8,128)(2,1)S(1)}, bf16[512,512]{1,0:T(8,128)(2,1)}, u32[]{:S(2)}, u32[]{:S(2)}) collective-permute-start(bf16[512,512]{1,0:T(8,128)(2,1)S(1)} %slice.6), channel_id=1, source_target_pairs={{0,16},{8,24},{16,32},{24,40},{32,48},{40,56},{48,0},{56,8},{1,17}... | collective-permute-start | bytes 1572872 | tf_op jit(solution)/shard_map/ppermute | solution.py:36
  107.2 3.5 %collective-permute-start.5 = (bf16[2,128,256]{2,1,0:T(8,128)(2,1)S(1)}, bf16[2,128,256]{2,1,0:T(8,128)(2,1)S(1)}, u32[]{:S(2)}, u32[]{:S(2)}) collective-permute-start(bf16[2,128,256]{2,1,0:T(8,128)(2,1)S(1)} %get-tuple-element.30), channel_id=1, source_target_pairs={{0,2},{1,3},{2,0},{3,1},{4,6},{5,7},{6,4},{7,5},{8,10},{9,11},{10,... | collective-permute-start | bytes 393224 | tf_op jit(solution)/shard_map/ppermute | solution.py:31
  110.7 1.9 collective-permute-start.9
  112.7 2.4 %collective-permute-start.12 = (bf16[1024,512]{1,0:T(8,128)(2,1)S(1)}, bf16[1024,512]{1,0:T(8,128)(2,1)}, u32[]{:S(2)}, u32[]{:S(2)}) collective-permute-start(bf16[1024,512]{1,0:T(8,128)(2,1)S(1)} %collective-permute-done.4.refs_8_), channel_id=1, source_target_pairs={{0,8},{8,0},{16,24},{24,16},{32,40},{40,32},{48,56},{56,48},{1,9},... | collective-permute-start | bytes 3145736 | tf_op jit(solution)/shard_map/ppermute | solution.py:46
  115.1 8.8 %collective-permute-done.5.arrived = bf16[2,128,256]{2,1,0:T(8,128)(2,1)S(1)} collective-permute-done((bf16[2,128,256]{2,1,0:T(8,128)(2,1)S(1)}, bf16[2,128,256]{2,1,0:T(8,128)(2,1)S(1)}, u32[]{:S(2)}, u32[]{:S(2)}) %collective-permute-start.5) | collective-permute-done | bytes 131104 | tf_op jit(solution)/shard_map/ppermute | solution.py:31
  123.9 0.6 copy-done.1
  124.6 1.9 collective-permute-start.8
  126.5 2.4 %collective-permute-start.13 = (bf16[1,128,256]{2,1,0:T(8,128)(2,1)S(1)}, bf16[1,128,256]{2,1,0:T(8,128)(2,1)S(1)}, u32[]{:S(2)}, u32[]{:S(2)}) collective-permute-start(bf16[1,128,256]{2,1,0:T(8,128)(2,1)S(1)} %get-tuple-element.39), channel_id=1, source_target_pairs={{0,4},{1,5},{2,6},{3,7},{4,0},{5,1},{6,2},{7,3},{8,12},{9,13},{10,... | collective-permute-start | bytes 196616 | tf_op jit(solution)/shard_map/ppermute | solution.py:31
  128.9 2.1 collective-permute-start.10
  131.0 6.4 %collective-permute-done.13 = bf16[1,128,256]{2,1,0:T(8,128)(2,1)S(1)} collective-permute-done((bf16[1,128,256]{2,1,0:T(8,128)(2,1)S(1)}, bf16[1,128,256]{2,1,0:T(8,128)(2,1)S(1)}, u32[]{:S(2)}, u32[]{:S(2)}) %collective-permute-start.13) | collective-permute-done | bytes 65568 | tf_op jit(solution)/shard_map/ppermute | solution.py:31
  137.4 1.9 collective-permute-start.11
  140.0 0.5 and_or_fusion.dp_ref
  140.5 1.1 collective-permute-done.11.refs_7_
  141.6 8.7 %shard_map.99 = (bf16[160,512]{1,0:T(8,128)(2,1)}, bf16[1,128,256]{2,1,0:T(8,128)(2,1)}) custom-call(s32[8]{0:T(128)} %and_or_fusion.dp_ref, bf16[8,160,1024]{2,1,0:T(8,128)(2,1)} %all-gather.2.cloned.1.call-done.features, bf16[1024,512]{1,0:T(8,128)(2,1)} %bitcast.4.refs_0_, bf16[1024,512]{1,0:T(8,128)(2,1)} %collective-permute-done.8.refs_1_, ...), custom_call_target="tpu_custom_call" | custom-call | tf_op jit(solution)/shard_map/pallas_call | solution.py:56
  150.3 1.9 collective-permute-start.14
  152.3 8.3 %collective-permute-done.14.by4 = bf16[1,128,256]{2,1,0:T(8,128)(2,1)S(1)} collective-permute-done((bf16[1,128,256]{2,1,0:T(8,128)(2,1)}, bf16[1,128,256]{2,1,0:T(8,128)(2,1)S(1)}, u32[]{:S(2)}, u32[]{:S(2)}) %collective-permute-start.14) | collective-permute-done | bytes 65568 | tf_op jit(solution)/shard_map/ppermute | solution.py:31
  160.6 0.9 pad_maximum_fusion.2
  161.5 4.9 %collective-permute-start.15 = (bf16[2,128,256]{2,1,0:T(8,128)(2,1)S(1)}, bf16[2,128,256]{2,1,0:T(8,128)(2,1)S(1)}, u32[]{:S(2)}, u32[]{:S(2)}) collective-permute-start(bf16[2,128,256]{2,1,0:T(8,128)(2,1)S(1)} %pad_maximum_fusion.2), channel_id=1, source_target_pairs={{0,2},{1,3},{2,0},{3,1},{4,6},{5,7},{6,4},{7,5},{8,10},{9,11},{10,... | collective-permute-start | bytes 393224 | tf_op jit(solution)/shard_map/ppermute | solution.py:31
  166.3 5.3 %collective-permute-done.15.by2 = bf16[2,128,256]{2,1,0:T(8,128)(2,1)S(1)} collective-permute-done((bf16[2,128,256]{2,1,0:T(8,128)(2,1)S(1)}, bf16[2,128,256]{2,1,0:T(8,128)(2,1)S(1)}, u32[]{:S(2)}, u32[]{:S(2)}) %collective-permute-start.15) | collective-permute-done | bytes 131104 | tf_op jit(solution)/shard_map/ppermute | solution.py:31
  171.6 0.9 pad_maximum_fusion.1
  172.5 5.0 %collective-permute-start.16 = (bf16[4,128,256]{2,1,0:T(8,128)(2,1)S(1)}, bf16[4,128,256]{2,1,0:T(8,128)(2,1)S(1)}, u32[]{:S(2)}, u32[]{:S(2)}) collective-permute-start(bf16[4,128,256]{2,1,0:T(8,128)(2,1)S(1)} %pad_maximum_fusion.1), channel_id=1, source_target_pairs={{0,1},{1,0},{2,3},{3,2},{4,5},{5,4},{6,7},{7,6},{8,9},{9,8},{10,11... | collective-permute-start | bytes 786440 | tf_op jit(solution)/shard_map/ppermute | solution.py:31
  177.6 5.6 %collective-permute-done.16.by1 = bf16[4,128,256]{2,1,0:T(8,128)(2,1)S(1)} collective-permute-done((bf16[4,128,256]{2,1,0:T(8,128)(2,1)S(1)}, bf16[4,128,256]{2,1,0:T(8,128)(2,1)S(1)}, u32[]{:S(2)}, u32[]{:S(2)}) %collective-permute-start.16) | collective-permute-done | bytes 262176 | tf_op jit(solution)/shard_map/ppermute | solution.py:31
  183.2 0.8 copy-done
  184.0 3.1 %shard_map.100 = bf16[128,1024]{1,0:T(8,128)(2,1)S(1)} custom-call(s32[8]{0:T(128)S(1)} %shift-right-arithmetic_or_fusion.place_ref, bf16[1,128,256]{2,1,0:T(8,128)(2,1)S(1)} %copy-done, bf16[1,128,256]{2,1,0:T(8,128)(2,1)S(1)} %collective-permute-done.14.by4, bf16[2,128,256]{2,1,0:T(8,128)(2,1)S(1)} %collective-permute-done.15.by2, ...), custom_call_target="tpu_custom_call" | custom-call | tf_op jit(solution)/shard_map/pallas_call | solution.py:56
  187.1 34.2 %all_to_all.15 = bf16[8,16,1024]{2,1,0:T(8,128)(2,1)S(1)} all-to-all(bf16[8,16,1024]{2,1,0:T(8,128)(2,1)S(1)} %bitcast.13), channel_id=1, replica_groups=mesh['section'=8,'dp'=8,'tensor'=8] {'section'}, dimensions={0} | all-to-all | bytes 524288 | tf_op jit(solution)/shard_map/all_to_all | solution.py:255
  221.2 0.7 convert_reduce_fusion
  (19 shorter events, 0.2 us)
Async XLA Ops:
  7.2 17.4 %collective-permute-start = (bf16[16,1024]{1,0:T(8,128)(2,1)}, bf16[16,1024]{1,0:T(8,128)(2,1)S(1)}, u32[]{:S(2)}, u32[]{:S(2)}) collective-permute-start(bf16[16,1024]{1,0:T(8,128)(2,1)} %bitcast.15), channel_id=1, source_target_pairs={{0,256},{64,320},{128,384},{192,448},{256,0},{320,64},{384,128},{4... | collective-permute-start | bytes 98312 | tf_op jit(solution)/shard_map/ppermute | solution.py:22
  24.5 0.8 copy-start.2
  26.0 11.0 %all-to-all-start.1 = ((bf16[4,2,16,1024]{3,2,1,0:T(8,128)(2,1)}), bf16[4,2,16,1024]{3,2,1,0:T(8,128)(2,1)S(1)}, u32[]{:S(2)}, u32[]{:S(2)}) async-start(bf16[4,2,16,1024]{3,2,1,0:T(8,128)(2,1)} %shard_map.95), calls=%async_computation.1 | async-start | bytes 524288 | tf_op jit(solution)/shard_map/all_to_all | solution.py:27
  38.5 28.0 %all-to-all-start = ((bf16[4,1024,256]{2,1,0:T(8,128)(2,1)}), bf16[4,1024,256]{2,1,0:T(8,128)(2,1)S(1)}, u32[]{:S(2)}, u32[]{:S(2)}) async-start(bf16[4,1024,256]{2,1,0:T(8,128)(2,1)} %broadcast_in_dim.6), calls=%async_computation | async-start | bytes 4194304 | tf_op jit(solution)/shard_map/all_to_all | solution.py:42
  43.0 97.5 %all-gather.2.cloned.1.call-start = ((), (), s32[]{:S(2)}) async-start(), calls=%async_computation.3 | async-start | bytes 2949120 | tf_op jit(solution)/shard_map/all_gather | solution.py:185
  66.5 7.8 %collective-permute-start.1 = (bf16[4,1024,256]{2,1,0:T(8,128)(2,1)S(1)}, bf16[4,1024,256]{2,1,0:T(8,128)(2,1)}, u32[]{:S(2)}, u32[]{:S(2)}) collective-permute-start(bf16[4,1024,256]{2,1,0:T(8,128)(2,1)S(1)} %all-to-all-done.near), channel_id=1, source_target_pairs={{0,8},{8,0},{16,24},{24,16},{32,40},{40,32},{48,56},{56,48},{1,9},... | collective-permute-start | bytes 6291464 | tf_op jit(solution)/shard_map/ppermute | solution.py:46
  68.5 28.6 %collective-permute-start.4 = (bf16[1024,512]{1,0:T(8,128)(2,1)}, bf16[1024,512]{1,0:T(8,128)(2,1)S(1)}, u32[]{:S(2)}, u32[]{:S(2)}) collective-permute-start(bf16[1024,512]{1,0:T(8,128)(2,1)} %bitcast.4.refs_0_), channel_id=1, source_target_pairs={{0,48},{8,56},{16,0},{24,8},{32,16},{40,24},{48,32},{56,40},{1,49}... | collective-permute-start | bytes 3145736 | tf_op jit(solution)/shard_map/ppermute | solution.py:36
  71.5 28.7 %collective-permute-start.3 = (bf16[1024,512]{1,0:T(8,128)(2,1)}, bf16[1024,512]{1,0:T(8,128)(2,1)}, u32[]{:S(2)}, u32[]{:S(2)}) collective-permute-start(bf16[1024,512]{1,0:T(8,128)(2,1)} %bitcast.4.refs_0_), channel_id=1, source_target_pairs={{0,16},{8,24},{16,32},{24,40},{32,48},{40,56},{48,0},{56,8},{1,17}... | collective-permute-start | bytes 3145736 | tf_op jit(solution)/shard_map/ppermute | solution.py:36
  76.8 20.2 %collective-permute-start.2 = (bf16[4,128,256]{2,1,0:T(8,128)(2,1)S(1)}, bf16[4,128,256]{2,1,0:T(8,128)(2,1)S(1)}, u32[]{:S(2)}, u32[]{:S(2)}) collective-permute-start(bf16[4,128,256]{2,1,0:T(8,128)(2,1)S(1)} %get-tuple-element.25), channel_id=1, source_target_pairs={{0,1},{1,0},{2,3},{3,2},{4,5},{5,4},{6,7},{7,6},{8,9},{9,8},{10,11... | collective-permute-start | bytes 786440 | tf_op jit(solution)/shard_map/ppermute | solution.py:31
  97.0 44.5 %copy-start.3 = (bf16[1024,512]{1,0:T(8,128)(2,1)}, bf16[1024,512]{1,0:T(8,128)(2,1)S(1)}, u32[]{:S(2)}) copy-start(bf16[1024,512]{1,0:T(8,128)(2,1)S(1)} %collective-permute-done.4.refs_8_) | copy-start | bytes 3145732
  101.4 23.2 %collective-permute-start.7 = (bf16[512,512]{1,0:T(8,128)(2,1)S(1)}, bf16[512,512]{1,0:T(8,128)(2,1)}, u32[]{:S(2)}, u32[]{:S(2)}) collective-permute-start(bf16[512,512]{1,0:T(8,128)(2,1)S(1)} %slice.7), channel_id=1, source_target_pairs={{0,48},{8,56},{16,0},{24,8},{32,16},{40,24},{48,32},{56,40},{1,49}... | collective-permute-start | bytes 1572872 | tf_op jit(solution)/shard_map/ppermute | solution.py:36
  103.3 21.3 %collective-permute-start.6 = (bf16[512,512]{1,0:T(8,128)(2,1)S(1)}, bf16[512,512]{1,0:T(8,128)(2,1)}, u32[]{:S(2)}, u32[]{:S(2)}) collective-permute-start(bf16[512,512]{1,0:T(8,128)(2,1)S(1)} %slice.6), channel_id=1, source_target_pairs={{0,16},{8,24},{16,32},{24,40},{32,48},{40,56},{48,0},{56,8},{1,17}... | collective-permute-start | bytes 1572872 | tf_op jit(solution)/shard_map/ppermute | solution.py:36
  107.2 16.7 %collective-permute-start.5 = (bf16[2,128,256]{2,1,0:T(8,128)(2,1)S(1)}, bf16[2,128,256]{2,1,0:T(8,128)(2,1)S(1)}, u32[]{:S(2)}, u32[]{:S(2)}) collective-permute-start(bf16[2,128,256]{2,1,0:T(8,128)(2,1)S(1)} %get-tuple-element.30), channel_id=1, source_target_pairs={{0,2},{1,3},{2,0},{3,1},{4,6},{5,7},{6,4},{7,5},{8,10},{9,11},{10,... | collective-permute-start | bytes 393224 | tf_op jit(solution)/shard_map/ppermute | solution.py:31
  110.7 30.8 %collective-permute-start.9 = (bf16[1024,512]{1,0:T(8,128)(2,1)}, bf16[1024,512]{1,0:T(8,128)(2,1)}, u32[]{:S(2)}, u32[]{:S(2)}) collective-permute-start(bf16[1024,512]{1,0:T(8,128)(2,1)} %collective-permute-done.3.refs_2_), channel_id=1, source_target_pairs={{0,8},{8,0},{16,24},{24,16},{32,40},{40,32},{48,56},{56,48},{1,9},... | collective-permute-start | bytes 3145736 | tf_op jit(solution)/shard_map/ppermute | solution.py:46
  112.7 28.9 %collective-permute-start.12 = (bf16[1024,512]{1,0:T(8,128)(2,1)S(1)}, bf16[1024,512]{1,0:T(8,128)(2,1)}, u32[]{:S(2)}, u32[]{:S(2)}) collective-permute-start(bf16[1024,512]{1,0:T(8,128)(2,1)S(1)} %collective-permute-done.4.refs_8_), channel_id=1, source_target_pairs={{0,8},{8,0},{16,24},{24,16},{32,40},{40,32},{48,56},{56,48},{1,9},... | collective-permute-start | bytes 3145736 | tf_op jit(solution)/shard_map/ppermute | solution.py:46
  123.9 0.7 copy-start.1
  124.6 17.0 %collective-permute-start.8 = (bf16[1024,512]{1,0:T(8,128)(2,1)}, bf16[1024,512]{1,0:T(8,128)(2,1)}, u32[]{:S(2)}, u32[]{:S(2)}) collective-permute-start(bf16[1024,512]{1,0:T(8,128)(2,1)} %bitcast.4.refs_0_), channel_id=1, source_target_pairs={{0,8},{8,0},{16,24},{24,16},{32,40},{40,32},{48,56},{56,48},{1,9},... | collective-permute-start | bytes 3145736 | tf_op jit(solution)/shard_map/ppermute | solution.py:46
  126.5 10.9 %collective-permute-start.13 = (bf16[1,128,256]{2,1,0:T(8,128)(2,1)S(1)}, bf16[1,128,256]{2,1,0:T(8,128)(2,1)S(1)}, u32[]{:S(2)}, u32[]{:S(2)}) collective-permute-start(bf16[1,128,256]{2,1,0:T(8,128)(2,1)S(1)} %get-tuple-element.39), channel_id=1, source_target_pairs={{0,4},{1,5},{2,6},{3,7},{4,0},{5,1},{6,2},{7,3},{8,12},{9,13},{10,... | collective-permute-start | bytes 196616 | tf_op jit(solution)/shard_map/ppermute | solution.py:31
  128.9 11.6 %collective-permute-start.10 = (bf16[512,512]{1,0:T(8,128)(2,1)}, bf16[512,512]{1,0:T(8,128)(2,1)}, u32[]{:S(2)}, u32[]{:S(2)}) collective-permute-start(bf16[512,512]{1,0:T(8,128)(2,1)} %collective-permute-done.6.refs_4_), channel_id=1, source_target_pairs={{0,8},{8,0},{16,24},{24,16},{32,40},{40,32},{48,56},{56,48},{1,9},... | collective-permute-start | bytes 1572872 | tf_op jit(solution)/shard_map/ppermute | solution.py:46
  137.4 4.2 %copy-start.4 = (bf16[1,128,256]{2,1,0:T(8,128)(2,1)}, bf16[1,128,256]{2,1,0:T(8,128)(2,1)S(1)}, u32[]{:S(2)}) copy-start(bf16[1,128,256]{2,1,0:T(8,128)(2,1)S(1)} %collective-permute-done.13) | copy-start | bytes 196612
  137.4 4.1 %collective-permute-start.11 = (bf16[512,512]{1,0:T(8,128)(2,1)}, bf16[512,512]{1,0:T(8,128)(2,1)}, u32[]{:S(2)}, u32[]{:S(2)}) collective-permute-start(bf16[512,512]{1,0:T(8,128)(2,1)} %collective-permute-done.7.refs_6_), channel_id=1, source_target_pairs={{0,8},{8,0},{16,24},{24,16},{32,40},{40,32},{48,56},{56,48},{1,9},... | collective-permute-start | bytes 1572872 | tf_op jit(solution)/shard_map/ppermute | solution.py:46
  150.3 10.3 %collective-permute-start.14 = (bf16[1,128,256]{2,1,0:T(8,128)(2,1)}, bf16[1,128,256]{2,1,0:T(8,128)(2,1)S(1)}, u32[]{:S(2)}, u32[]{:S(2)}) collective-permute-start(bf16[1,128,256]{2,1,0:T(8,128)(2,1)} %get-tuple-element.41.own), channel_id=1, source_target_pairs={{0,4},{1,5},{2,6},{3,7},{4,0},{5,1},{6,2},{7,3},{8,12},{9,13},{10,... | collective-permute-start | bytes 196616 | tf_op jit(solution)/shard_map/ppermute | solution.py:31
  161.5 10.2 %collective-permute-start.15 = (bf16[2,128,256]{2,1,0:T(8,128)(2,1)S(1)}, bf16[2,128,256]{2,1,0:T(8,128)(2,1)S(1)}, u32[]{:S(2)}, u32[]{:S(2)}) collective-permute-start(bf16[2,128,256]{2,1,0:T(8,128)(2,1)S(1)} %pad_maximum_fusion.2), channel_id=1, source_target_pairs={{0,2},{1,3},{2,0},{3,1},{4,6},{5,7},{6,4},{7,5},{8,10},{9,11},{10,... | collective-permute-start | bytes 393224 | tf_op jit(solution)/shard_map/ppermute | solution.py:31
  172.5 10.6 %collective-permute-start.16 = (bf16[4,128,256]{2,1,0:T(8,128)(2,1)S(1)}, bf16[4,128,256]{2,1,0:T(8,128)(2,1)S(1)}, u32[]{:S(2)}, u32[]{:S(2)}) collective-permute-start(bf16[4,128,256]{2,1,0:T(8,128)(2,1)S(1)} %pad_maximum_fusion.1), channel_id=1, source_target_pairs={{0,1},{1,0},{2,3},{3,2},{4,5},{5,4},{6,7},{7,6},{8,9},{9,8},{10,11... | collective-permute-start | bytes 786440 | tf_op jit(solution)/shard_map/ppermute | solution.py:31
  183.1 0.8 copy-start
Sparse Core Ops, SparseCore 0:
  45.9 78.7 all-gather.1

commit v6 on v5

--- a/solution.py
+++ b/solution.py
@@ -69,33 +69,18 @@
         out[x, 1] = other[...]
 
 
-def pair_kernel(place_ref, half_ref, images, near, far, keep, send, buffer):
+def pair_kernel(head_ref, half_ref, images, near, far, out):
     rows = jnp.concatenate(
         [images[x, half_ref[0] ^ z] for z in range(2) for x in range(X_SIZE)], axis=0
     )
     for slot in range(N_BLOCKS):
         weights = (near, far)[slot % 2][slot // 2]
-        buffer[place_ref[slot]] = dot(rows, weights)
-    half = N_BLOCKS // 2
-    keep[...] = buffer[:half]
-    send[...] = buffer[half:].astype(BF16)
-
-
-def fold_kernel(kept, arrived, keep, send):
-    half = keep.shape[0]
-    keep[...] = kept[:half] + arrived[:half].astype(F32)
-    send[...] = (kept[half:] + arrived[half:].astype(F32)).astype(BF16)
-
-
-def fold(keep, arrived):
-    half = (keep.shape[0] // 2, *keep.shape[1:])
-    outs = (jax.ShapeDtypeStruct(half, F32), jax.ShapeDtypeStruct(half, BF16))
-    return call(fold_kernel, outs, [VMEM] * 2, (keep, arrived))
+        out[head_ref[slot]] = dot(rows, weights).astype(BF16)
 
 
 def attention_kernel(dp_ref, features, *refs):
     blocks, refs = refs[: 2 * N_BLOCKS - 6], refs[2 * N_BLOCKS - 6 :]
-    kept, arrived, bias_ref, cotangent, gate, gated, packed, rows, columns, sems = refs
+    arrived, bias_ref, cotangent, gate, gated, packed, rows, columns, sems = refs
     cut = columns.shape[1] // 2
     copies = []
     for slot in range(N_BLOCKS):
@@ -127,7 +112,7 @@
         query = part if query is None else query + part
     query = query.astype(BF16)
 
-    pairs = (kept[...] + arrived[...].astype(F32)).astype(BF16)
+    pairs = jnp.sum(arrived[...].astype(F32), axis=0).astype(BF16)
     keys, values = pairs[:, :HEAD_SIZE], pairs[:, HEAD_SIZE:]
     scaling = HEAD_SIZE ** (-0.5)
     scale_factor = jnp.tanh(gate[...])
@@ -179,7 +164,8 @@
     dp = lax.axis_index("dp")
     slots = jnp.arange(N_BLOCKS, dtype=jnp.int32)
     dp_order = ((((dp >> 1) - (slots >> 1)) & (Y_SIZE - 1)) << 1) | ((dp ^ slots) & 1)
-    apart = lax.axis_index("tensor") ^ (slots ^ (dp & 1))
+    head_order = slots ^ (dp & 1)
+    apart = lax.axis_index("tensor") ^ head_order
     place = ((apart & 1) << 2) | (apart & 2) | (apart >> 2)
 
     features = lax.all_gather(hidden[0], "tensor", axis=0)
@@ -187,48 +173,42 @@
     own = image_tokens[0]
     rows, width = own.shape
     pair = jnp.concatenate([key_weight_stack[0], value_weight_stack[0]], axis=1)
+    near_pairs, other = lax.optimization_barrier((y_gather(pair), z_swap(own)))
+
     copies = call(
         spread_kernel,
         jax.ShapeDtypeStruct((X_SIZE, 2, rows, width), BF16),
         [VMEM] * 2,
-        (own, z_swap(own)),
-    )
-    near_pairs, images = lax.optimization_barrier((y_gather(pair), x_exchange(copies)))
+        (own, other),
+    )
+    images = x_exchange(copies)
     far_pairs = core_swap(near_pairs)
     image_count = 2 * X_SIZE * rows
     block = (image_count, 2 * HEAD_SIZE)
-    half = N_BLOCKS // 2
-
-    keep, send = call(
+    portions = call(
         pair_kernel,
-        (jax.ShapeDtypeStruct((half, *block), F32), jax.ShapeDtypeStruct((half, *block), BF16)),
+        jax.ShapeDtypeStruct((N_BLOCKS, *block), BF16),
         [SMEM] * 2 + [VMEM] * 3,
-        (place, lax.axis_index("section")[None] >> 2, images, near_pairs, far_pairs),
-        [pltpu.VMEM((N_BLOCKS, *block), F32)],
-    )
+        (head_order, lax.axis_index("section")[None] >> 2, images, near_pairs, far_pairs),
+    )
+    arrived = lax.all_to_all(portions, "tensor", 0, 0)
 
     w, _ = lax.optimization_barrier((w_query[0], near_pairs))
     cut = w.shape[0] // 2
     before, behind = y_shift(w, 1), y_shift(w, -1)
-    keep, send = fold(keep, t_swap(send, 1))
-    (keep, send), before, behind = lax.optimization_barrier(((keep, send), before, behind))
     across = (y_shift(before[:cut], 1), y_shift(behind[cut:], -1))
-    keep, send = fold(keep, t_swap(send, 2))
-    (keep, send), across, w = lax.optimization_barrier(((keep, send), across, w))
-    arrived = t_swap(send, 4)
     query_weights = [v for b in (w, before, *across, behind) for v in (b, core_swap(b))]
 
     tokens, columns = hidden.shape[1], w_query.shape[2]
     gated_out, packed = call(
         attention_kernel,
         (jax.ShapeDtypeStruct((tokens, columns), BF16), jax.ShapeDtypeStruct((1, *block), BF16)),
-        [SMEM] + [pl.BlockSpec(memory_space=pl.ANY)] * 11 + [VMEM] * 5,
+        [SMEM] + [pl.BlockSpec(memory_space=pl.ANY)] * 11 + [VMEM] * 4,
         (
             dp_order,
             features,
             *query_weights,
-            keep[0],
-            arrived[0],
+            arrived,
             score_bias,
             cotangent[0],
             gate_logit.reshape(1, 1),

time: 230 us -> 202 us (0.88)
  waiting for transfers between devices: 87.6 us -> 57.1 us
  starting transfers between devices: 68.2 us -> 72.6 us
    ppermute x6 -> x3, waiting for transfers between devices: 51.6 us -> 21.4 us  [t_swap(): return lax.ppermute(a, 'tensor', [(t, t ^ k) for t in range(8)])]
    all_to_all x1, waiting for transfers between devices: 22.9 us -> 8.66 us  [y_gather(): return lax.all_to_all(copies, 'dp', 0, 0, axis_index_groups=groups)]
    all_to_all x0 -> x1, starting transfers between devices: none -> 12.7 us  [local(): arrived = lax.all_to_all(portions, 'tensor', 0, 0)]
    all_to_all x0 -> x1, waiting for transfers between devices: none -> 11.3 us  [local(): arrived = lax.all_to_all(portions, 'tensor', 0, 0)]
    ppermute x6 -> x3, starting transfers between devices: 20.7 us -> 9.92 us  [t_swap(): return lax.ppermute(a, 'tensor', [(t, t ^ k) for t in range(8)])]
    ppermute x4, starting transfers between devices: 11.7 us -> 14.1 us  [y_shift(): return lax.ppermute(a, 'dp', pairs)]
    pallas_call x6 -> x4, Pallas kernels: 15 us -> 15.7 us  [call(): pl.pallas_call(kernel, out_shape=outs, in_specs=in_specs, out_specs=jax.t...]
  transfers between devices with their start and end apart: 20 -> 18, of which waited for: 11 -> 10; matrix products, arithmetic and copies ran while one was open for 1% -> 1% of each run, Pallas kernels for 1% -> 2%
where the time goes in v6:
time: 202 us; the launch traced here: 201 us
  starting transfers between devices  72.6 us (36%)
  waiting for transfers between devices  57.1 us (28%)
  blocking collectives  32.7 us (16%)
  Pallas kernels  15.7 us (8%)
  between operations  14.9 us (7%)
  other arithmetic  4.01 us (2%)
  local copies, waits for them, and re-layouts  3.45 us (2%)
    all_to_all x1, blocking collectives, local(): lax.all_to_all(portion, 'section', 0, 0).astype(F32)  32.7 us
    ppermute x3, waiting for transfers between devices, t_swap(): return lax.ppermute(a, 'tensor', [(t, t ^ k) for t in range(8)])  21.4 us
    pallas_call x4, Pallas kernels, call(): pl.pallas_call(kernel, out_shape=outs, in_specs=in_specs, out_specs=jax.t...  15.7 us
    ppermute x1, starting transfers between devices, z_swap(): lax.ppermute(a, 'section', [(s, (s + X_SIZE) % (2 * X_SIZE)) for s in ran...  14.8 us
    ppermute x4, starting transfers between devices, y_shift(): return lax.ppermute(a, 'dp', pairs)  14.1 us
    all_to_all x1, starting transfers between devices, local(): arrived = lax.all_to_all(portions, 'tensor', 0, 0)  12.7 us
    ppermute x6, starting transfers between devices, core_swap(): return lax.ppermute(a, 'dp', [(d, d ^ 1) for d in range(2 * Y_SIZE)])  12.2 us
    all_to_all x1, waiting for transfers between devices, local(): arrived = lax.all_to_all(portions, 'tensor', 0, 0)  11.3 us
  transfers between devices with their start and end apart: 18, of which 10 were waited for; matrix products, arithmetic and copies ran while one was open for 1% of the time, Pallas kernels for 2%

profile of v6, /device:TPU:32, one launch (start us, length us, event | category | flops | bytes accessed | tf_op | source)
XLA Modules:
  0.0 200.5 jit_solution(5066636675651829070)
XLA Ops:
  7.2 1.1 pad_maximum_fusion
  8.3 1.5 broadcast_in_dim.6
  9.7 4.6 %all-to-all-start = ((bf16[4,1024,256]{2,1,0:T(8,128)(2,1)}), bf16[4,1024,256]{2,1,0:T(8,128)(2,1)S(1)}, u32[]{:S(2)}, u32[]{:S(2)}) async-start(bf16[4,1024,256]{2,1,0:T(8,128)(2,1)} %broadcast_in_dim.6), calls=%async_computation | async-start | bytes 4194304 | tf_op jit(solution)/shard_map/all_to_all | solution.py:42
  14.3 0.7 all-gather.2.cloned.1.call-update
  15.1 14.8 %collective-permute-start = (bf16[16,1024]{1,0:T(8,128)(2,1)S(1)}, bf16[16,1024]{1,0:T(8,128)(2,1)S(1)}, u32[]{:S(2)}, u32[]{:S(2)}) collective-permute-start(bf16[16,1024]{1,0:T(8,128)(2,1)S(1)} %bitcast.12), channel_id=1, source_target_pairs={{0,256},{64,320},{128,384},{192,448},{256,0},{320,64},{384,128},{4... | collective-permute-start | bytes 98312 | tf_op jit(solution)/shard_map/ppermute | solution.py:22
  29.9 2.1 %collective-permute-done.other = bf16[16,1024]{1,0:T(8,128)(2,1)S(1)} collective-permute-done((bf16[16,1024]{1,0:T(8,128)(2,1)S(1)}, bf16[16,1024]{1,0:T(8,128)(2,1)S(1)}, u32[]{:S(2)}, u32[]{:S(2)}) %collective-permute-start) | collective-permute-done | bytes 32800 | tf_op jit(solution)/shard_map/ppermute | solution.py:22
  32.0 8.7 %all-to-all-done.near = bf16[4,1024,256]{2,1,0:T(8,128)(2,1)S(1)} async-done(((bf16[4,1024,256]{2,1,0:T(8,128)(2,1)}), bf16[4,1024,256]{2,1,0:T(8,128)(2,1)S(1)}, u32[]{:S(2)}, u32[]{:S(2)}) %all-to-all-start) | async-done | bytes 2097184 | tf_op jit(solution)/shard_map/all_to_all | solution.py:42
  40.7 1.9 collective-permute-start.10
  42.6 2.5 %collective-permute-start.2 = (bf16[1024,512]{1,0:T(8,128)(2,1)}, bf16[1024,512]{1,0:T(8,128)(2,1)S(1)}, u32[]{:S(2)}, u32[]{:S(2)}) collective-permute-start(bf16[1024,512]{1,0:T(8,128)(2,1)} %bitcast.14), channel_id=1, source_target_pairs={{0,16},{8,24},{16,32},{24,40},{32,48},{40,56},{48,0},{56,8},{1,17}... | collective-permute-start | bytes 3145736 | tf_op jit(solution)/shard_map/ppermute | solution.py:36
  45.1 4.6 %collective-permute-start.6 = (bf16[1024,512]{1,0:T(8,128)(2,1)}, bf16[1024,512]{1,0:T(8,128)(2,1)}, u32[]{:S(2)}, u32[]{:S(2)}) collective-permute-start(bf16[1024,512]{1,0:T(8,128)(2,1)} %bitcast.15), channel_id=1, source_target_pairs={{0,48},{8,56},{16,0},{24,8},{32,16},{40,24},{48,32},{56,40},{1,49}... | collective-permute-start | bytes 3145736 | tf_op jit(solution)/shard_map/ppermute | solution.py:36
  49.7 0.7 shard_map.95
  50.4 4.3 %all-to-all-start.1 = ((bf16[4,2,16,1024]{3,2,1,0:T(8,128)(2,1)}), bf16[4,2,16,1024]{3,2,1,0:T(8,128)(2,1)S(1)}, u32[]{:S(2)}, u32[]{:S(2)}) async-start(bf16[4,2,16,1024]{3,2,1,0:T(8,128)(2,1)} %shard_map.95), calls=%async_computation.1 | async-start | bytes 524288 | tf_op jit(solution)/shard_map/all_to_all | solution.py:27
  54.7 6.8 %all-to-all-done.1.images = bf16[4,2,16,1024]{3,2,1,0:T(8,128)(2,1)S(1)} async-done(((bf16[4,2,16,1024]{3,2,1,0:T(8,128)(2,1)}), bf16[4,2,16,1024]{3,2,1,0:T(8,128)(2,1)S(1)}, u32[]{:S(2)}, u32[]{:S(2)}) %all-to-all-start.1) | async-done | bytes 262176 | tf_op jit(solution)/shard_map/all_to_all | solution.py:27
  61.4 0.0 collective-permute-done.10.far
  61.4 3.2 %shard_map.96 = bf16[8,128,256]{2,1,0:T(8,128)(2,1)} custom-call(s32[8]{0:T(128)S(1)} %iota_xor_fusion.head_ref, s32[1]{0:T(128)} %bitcast.4.half_ref, bf16[4,2,16,1024]{3,2,1,0:T(8,128)(2,1)S(1)} %all-to-all-done.1.images, bf16[4,1024,256]{2,1,0:T(8,128)(2,1)S(1)} %all-to-all-done.near, bf16[4,1024,256]{2,1,0:T(8,128)(2,1)} %collective-permute-done.10.far), custom_call_target="tpu_custom_call" | custom-call | tf_op jit(solution)/shard_map/pallas_call | solution.py:56
  64.6 12.7 %all-to-all-start.2 = ((bf16[8,128,256]{2,1,0:T(8,128)(2,1)}), bf16[8,128,256]{2,1,0:T(8,128)(2,1)}, u32[]{:S(2)}, u32[]{:S(2)}) async-start(bf16[8,128,256]{2,1,0:T(8,128)(2,1)} %shard_map.96), calls=%async_computation.2 | async-start | bytes 1048576 | tf_op jit(solution)/shard_map/all_to_all | solution.py:194
  77.3 1.9 collective-permute-start.1
  79.2 0.0 collective-permute-done.2.refs_2_
  79.3 1.9 collective-permute-start.4
  81.2 0.0 collective-permute-done.6.refs_8_
  81.2 1.1 slice.9
  82.3 5.1 %collective-permute-start.7 = (bf16[512,512]{1,0:T(8,128)(2,1)S(1)}, bf16[512,512]{1,0:T(8,128)(2,1)}, u32[]{:S(2)}, u32[]{:S(2)}) collective-permute-start(bf16[512,512]{1,0:T(8,128)(2,1)S(1)} %slice.9), channel_id=1, source_target_pairs={{0,48},{8,56},{16,0},{24,8},{32,16},{40,24},{48,32},{56,40},{1,49}... | collective-permute-start | bytes 1572872 | tf_op jit(solution)/shard_map/ppermute | solution.py:36
  87.4 1.9 collective-permute-start.3
  89.3 2.4 %collective-permute-start.9 = (bf16[1024,512]{1,0:T(8,128)(2,1)}, bf16[1024,512]{1,0:T(8,128)(2,1)}, u32[]{:S(2)}, u32[]{:S(2)}) collective-permute-start(bf16[1024,512]{1,0:T(8,128)(2,1)} %collective-permute-done.6.refs_8_), channel_id=1, source_target_pairs={{0,8},{8,0},{16,24},{24,16},{32,40},{40,32},{48,56},{56,48},{1,9},... | collective-permute-start | bytes 3145736 | tf_op jit(solution)/shard_map/ppermute | solution.py:46
  91.8 5.0 %collective-permute-done.4.refs_4_ = bf16[512,512]{1,0:T(8,128)(2,1)} collective-permute-done((bf16[512,512]{1,0:T(8,128)(2,1)S(1)}, bf16[512,512]{1,0:T(8,128)(2,1)}, u32[]{:S(2)}, u32[]{:S(2)}) %collective-permute-start.4) | collective-permute-done | bytes 524320 | tf_op jit(solution)/shard_map/ppermute | solution.py:36
  96.8 1.9 collective-permute-start.5
  98.7 0.3 collective-permute-done.7.refs_6_
  99.0 2.2 %collective-permute-start.8 = (bf16[512,512]{1,0:T(8,128)(2,1)}, bf16[512,512]{1,0:T(8,128)(2,1)}, u32[]{:S(2)}, u32[]{:S(2)}) collective-permute-start(bf16[512,512]{1,0:T(8,128)(2,1)} %collective-permute-done.7.refs_6_), channel_id=1, source_target_pairs={{0,8},{8,0},{16,24},{24,16},{32,40},{40,32},{48,56},{56,48},{1,9},... | collective-permute-start | bytes 1572872 | tf_op jit(solution)/shard_map/ppermute | solution.py:46
  101.8 0.5 and_or_fusion.dp_ref
  102.3 0.0 collective-permute-done.5.refs_5_
  102.3 0.8 collective-permute-done.8.refs_7_
  103.1 0.0 collective-permute-done.3.refs_3_
  103.1 0.0 collective-permute-done.9.refs_9_
  103.1 0.0 all-gather.2.cloned.1.call-done.features
  103.1 11.3 %all-to-all-done.2.refs_10_ = bf16[8,128,256]{2,1,0:T(8,128)(2,1)} async-done(((bf16[8,128,256]{2,1,0:T(8,128)(2,1)}), bf16[8,128,256]{2,1,0:T(8,128)(2,1)}, u32[]{:S(2)}, u32[]{:S(2)}) %all-to-all-start.2) | async-done | bytes 524320 | tf_op jit(solution)/shard_map/all_to_all | solution.py:194
  114.5 8.8 %shard_map.97 = (bf16[160,512]{1,0:T(8,128)(2,1)}, bf16[1,128,256]{2,1,0:T(8,128)(2,1)}) custom-call(s32[8]{0:T(128)} %and_or_fusion.dp_ref, bf16[8,160,1024]{2,1,0:T(8,128)(2,1)} %all-gather.2.cloned.1.call-done.features, bf16[1024,512]{1,0:T(8,128)(2,1)} %bitcast.17, bf16[1024,512]{1,0:T(8,128)(2,1)} %collective-permute-done.1.refs_1_, ...), custom_call_target="tpu_custom_call" | custom-call | tf_op jit(solution)/shard_map/pallas_call | solution.py:56
  123.2 1.9 collective-permute-start.11
  125.2 8.9 %collective-permute-done.11.by4 = bf16[1,128,256]{2,1,0:T(8,128)(2,1)S(1)} collective-permute-done((bf16[1,128,256]{2,1,0:T(8,128)(2,1)}, bf16[1,128,256]{2,1,0:T(8,128)(2,1)S(1)}, u32[]{:S(2)}, u32[]{:S(2)}) %collective-permute-start.11) | collective-permute-done | bytes 65568 | tf_op jit(solution)/shard_map/ppermute | solution.py:31
  134.0 0.9 pad_maximum_fusion.2
  134.9 1.9 collective-permute-start.12
  136.8 6.1 %collective-permute-done.12.by2 = bf16[2,128,256]{2,1,0:T(8,128)(2,1)S(1)} collective-permute-done((bf16[2,128,256]{2,1,0:T(8,128)(2,1)S(1)}, bf16[2,128,256]{2,1,0:T(8,128)(2,1)S(1)}, u32[]{:S(2)}, u32[]{:S(2)}) %collective-permute-start.12) | collective-permute-done | bytes 131104 | tf_op jit(solution)/shard_map/ppermute | solution.py:31
  143.0 0.9 pad_maximum_fusion.1
  143.8 6.1 %collective-permute-start.13 = (bf16[4,128,256]{2,1,0:T(8,128)(2,1)S(1)}, bf16[4,128,256]{2,1,0:T(8,128)(2,1)S(1)}, u32[]{:S(2)}, u32[]{:S(2)}) collective-permute-start(bf16[4,128,256]{2,1,0:T(8,128)(2,1)S(1)} %pad_maximum_fusion.1), channel_id=1, source_target_pairs={{0,1},{1,0},{2,3},{3,2},{4,5},{5,4},{6,7},{7,6},{8,9},{9,8},{10,11... | collective-permute-start | bytes 786440 | tf_op jit(solution)/shard_map/ppermute | solution.py:31
  149.9 6.5 %collective-permute-done.13.by1 = bf16[4,128,256]{2,1,0:T(8,128)(2,1)S(1)} collective-permute-done((bf16[4,128,256]{2,1,0:T(8,128)(2,1)S(1)}, bf16[4,128,256]{2,1,0:T(8,128)(2,1)S(1)}, u32[]{:S(2)}, u32[]{:S(2)}) %collective-permute-start.13) | collective-permute-done | bytes 262176 | tf_op jit(solution)/shard_map/ppermute | solution.py:31
  156.4 0.8 copy-done
  157.2 3.1 %shard_map.98 = bf16[128,1024]{1,0:T(8,128)(2,1)S(1)} custom-call(s32[8]{0:T(128)S(1)} %shift-right-arithmetic_or_fusion.place_ref, bf16[1,128,256]{2,1,0:T(8,128)(2,1)S(1)} %copy-done, bf16[1,128,256]{2,1,0:T(8,128)(2,1)S(1)} %collective-permute-done.11.by4, bf16[2,128,256]{2,1,0:T(8,128)(2,1)S(1)} %collective-permute-done.12.by2, ...), custom_call_target="tpu_custom_call" | custom-call | tf_op jit(solution)/shard_map/pallas_call | solution.py:56
  160.3 32.7 %all_to_all.20 = bf16[8,16,1024]{2,1,0:T(8,128)(2,1)S(1)} all-to-all(bf16[8,16,1024]{2,1,0:T(8,128)(2,1)S(1)} %bitcast.11), channel_id=1, replica_groups=mesh['section'=8,'dp'=8,'tensor'=8] {'section'}, dimensions={0} | all-to-all | bytes 524288 | tf_op jit(solution)/shard_map/all_to_all | solution.py:235
  193.0 0.7 convert_reduce_fusion
  (10 shorter events, 0.1 us)
Async XLA Ops:
  9.7 5.3 %copy-start.1 = (bf16[1,16,1024]{2,1,0:T(8,128)(2,1)S(1)}, bf16[1,16,1024]{2,1,0:T(8,128)(2,1)}, u32[]{:S(2)}) copy-start(bf16[1,16,1024]{2,1,0:T(8,128)(2,1)} %param.12) | copy-start | bytes 98308
  9.7 30.9 %all-to-all-start = ((bf16[4,1024,256]{2,1,0:T(8,128)(2,1)}), bf16[4,1024,256]{2,1,0:T(8,128)(2,1)S(1)}, u32[]{:S(2)}, u32[]{:S(2)}) async-start(bf16[4,1024,256]{2,1,0:T(8,128)(2,1)} %broadcast_in_dim.6), calls=%async_computation | async-start | bytes 4194304 | tf_op jit(solution)/shard_map/all_to_all | solution.py:42
  14.3 88.8 %all-gather.2.cloned.1.call-start = ((), (), s32[]{:S(2)}) async-start(), calls=%async_computation.4 | async-start | bytes 2949120 | tf_op jit(solution)/shard_map/all_gather | solution.py:171
  15.1 16.9 %collective-permute-start = (bf16[16,1024]{1,0:T(8,128)(2,1)S(1)}, bf16[16,1024]{1,0:T(8,128)(2,1)S(1)}, u32[]{:S(2)}, u32[]{:S(2)}) collective-permute-start(bf16[16,1024]{1,0:T(8,128)(2,1)S(1)} %bitcast.12), channel_id=1, source_target_pairs={{0,256},{64,320},{128,384},{192,448},{256,0},{320,64},{384,128},{4... | collective-permute-start | bytes 98312 | tf_op jit(solution)/shard_map/ppermute | solution.py:22
  40.7 20.8 %collective-permute-start.10 = (bf16[4,1024,256]{2,1,0:T(8,128)(2,1)S(1)}, bf16[4,1024,256]{2,1,0:T(8,128)(2,1)}, u32[]{:S(2)}, u32[]{:S(2)}) collective-permute-start(bf16[4,1024,256]{2,1,0:T(8,128)(2,1)S(1)} %all-to-all-done.near), channel_id=1, source_target_pairs={{0,8},{8,0},{16,24},{24,16},{32,40},{40,32},{48,56},{56,48},{1,9},... | collective-permute-start | bytes 6291464 | tf_op jit(solution)/shard_map/ppermute | solution.py:46
  42.6 36.6 %collective-permute-start.2 = (bf16[1024,512]{1,0:T(8,128)(2,1)}, bf16[1024,512]{1,0:T(8,128)(2,1)S(1)}, u32[]{:S(2)}, u32[]{:S(2)}) collective-permute-start(bf16[1024,512]{1,0:T(8,128)(2,1)} %bitcast.14), channel_id=1, source_target_pairs={{0,16},{8,24},{16,32},{24,40},{32,48},{40,56},{48,0},{56,8},{1,17}... | collective-permute-start | bytes 3145736 | tf_op jit(solution)/shard_map/ppermute | solution.py:36
  45.1 36.1 %collective-permute-start.6 = (bf16[1024,512]{1,0:T(8,128)(2,1)}, bf16[1024,512]{1,0:T(8,128)(2,1)}, u32[]{:S(2)}, u32[]{:S(2)}) collective-permute-start(bf16[1024,512]{1,0:T(8,128)(2,1)} %bitcast.15), channel_id=1, source_target_pairs={{0,48},{8,56},{16,0},{24,8},{32,16},{40,24},{48,32},{56,40},{1,49}... | collective-permute-start | bytes 3145736 | tf_op jit(solution)/shard_map/ppermute | solution.py:36
  50.4 11.1 %all-to-all-start.1 = ((bf16[4,2,16,1024]{3,2,1,0:T(8,128)(2,1)}), bf16[4,2,16,1024]{3,2,1,0:T(8,128)(2,1)S(1)}, u32[]{:S(2)}, u32[]{:S(2)}) async-start(bf16[4,2,16,1024]{3,2,1,0:T(8,128)(2,1)} %shard_map.95), calls=%async_computation.1 | async-start | bytes 524288 | tf_op jit(solution)/shard_map/all_to_all | solution.py:27
  64.6 49.8 %all-to-all-start.2 = ((bf16[8,128,256]{2,1,0:T(8,128)(2,1)}), bf16[8,128,256]{2,1,0:T(8,128)(2,1)}, u32[]{:S(2)}, u32[]{:S(2)}) async-start(bf16[8,128,256]{2,1,0:T(8,128)(2,1)} %shard_map.96), calls=%async_computation.2 | async-start | bytes 1048576 | tf_op jit(solution)/shard_map/all_to_all | solution.py:194
  77.3 25.0 %collective-permute-start.1 = (bf16[1024,512]{1,0:T(8,128)(2,1)}, bf16[1024,512]{1,0:T(8,128)(2,1)}, u32[]{:S(2)}, u32[]{:S(2)}) collective-permute-start(bf16[1024,512]{1,0:T(8,128)(2,1)} %bitcast.16), channel_id=1, source_target_pairs={{0,8},{8,0},{16,24},{24,16},{32,40},{40,32},{48,56},{56,48},{1,9},... | collective-permute-start | bytes 3145736 | tf_op jit(solution)/shard_map/ppermute | solution.py:46
  79.2 35.3 %copy-start.2 = (bf16[1024,512]{1,0:T(8,128)(2,1)}, bf16[1024,512]{1,0:T(8,128)(2,1)S(1)}, u32[]{:S(2)}) copy-start(bf16[1024,512]{1,0:T(8,128)(2,1)S(1)} %collective-permute-done.2.refs_2_) | copy-start | bytes 3145732
  79.3 17.5 %collective-permute-start.4 = (bf16[512,512]{1,0:T(8,128)(2,1)S(1)}, bf16[512,512]{1,0:T(8,128)(2,1)}, u32[]{:S(2)}, u32[]{:S(2)}) collective-permute-start(bf16[512,512]{1,0:T(8,128)(2,1)S(1)} %slice.8), channel_id=1, source_target_pairs={{0,16},{8,24},{16,32},{24,40},{32,48},{40,56},{48,0},{56,8},{1,17}... | collective-permute-start | bytes 1572872 | tf_op jit(solution)/shard_map/ppermute | solution.py:36
  82.3 16.7 %collective-permute-start.7 = (bf16[512,512]{1,0:T(8,128)(2,1)S(1)}, bf16[512,512]{1,0:T(8,128)(2,1)}, u32[]{:S(2)}, u32[]{:S(2)}) collective-permute-start(bf16[512,512]{1,0:T(8,128)(2,1)S(1)} %slice.9), channel_id=1, source_target_pairs={{0,48},{8,56},{16,0},{24,8},{32,16},{40,24},{48,32},{56,40},{1,49}... | collective-permute-start | bytes 1572872 | tf_op jit(solution)/shard_map/ppermute | solution.py:36
  87.4 15.7 %collective-permute-start.3 = (bf16[1024,512]{1,0:T(8,128)(2,1)S(1)}, bf16[1024,512]{1,0:T(8,128)(2,1)}, u32[]{:S(2)}, u32[]{:S(2)}) collective-permute-start(bf16[1024,512]{1,0:T(8,128)(2,1)S(1)} %collective-permute-done.2.refs_2_), channel_id=1, source_target_pairs={{0,8},{8,0},{16,24},{24,16},{32,40},{40,32},{48,56},{56,48},{1,9},... | collective-permute-start | bytes 3145736 | tf_op jit(solution)/shard_map/ppermute | solution.py:46
  89.3 13.8 %collective-permute-start.9 = (bf16[1024,512]{1,0:T(8,128)(2,1)}, bf16[1024,512]{1,0:T(8,128)(2,1)}, u32[]{:S(2)}, u32[]{:S(2)}) collective-permute-start(bf16[1024,512]{1,0:T(8,128)(2,1)} %collective-permute-done.6.refs_8_), channel_id=1, source_target_pairs={{0,8},{8,0},{16,24},{24,16},{32,40},{40,32},{48,56},{56,48},{1,9},... | collective-permute-start | bytes 3145736 | tf_op jit(solution)/shard_map/ppermute | solution.py:46
  96.8 5.5 %collective-permute-start.5 = (bf16[512,512]{1,0:T(8,128)(2,1)}, bf16[512,512]{1,0:T(8,128)(2,1)}, u32[]{:S(2)}, u32[]{:S(2)}) collective-permute-start(bf16[512,512]{1,0:T(8,128)(2,1)} %collective-permute-done.4.refs_4_), channel_id=1, source_target_pairs={{0,8},{8,0},{16,24},{24,16},{32,40},{40,32},{48,56},{56,48},{1,9},... | collective-permute-start | bytes 1572872 | tf_op jit(solution)/shard_map/ppermute | solution.py:46
  99.0 4.1 %collective-permute-start.8 = (bf16[512,512]{1,0:T(8,128)(2,1)}, bf16[512,512]{1,0:T(8,128)(2,1)}, u32[]{:S(2)}, u32[]{:S(2)}) collective-permute-start(bf16[512,512]{1,0:T(8,128)(2,1)} %collective-permute-done.7.refs_6_), channel_id=1, source_target_pairs={{0,8},{8,0},{16,24},{24,16},{32,40},{40,32},{48,56},{56,48},{1,9},... | collective-permute-start | bytes 1572872 | tf_op jit(solution)/shard_map/ppermute | solution.py:46
  123.2 10.8 %collective-permute-start.11 = (bf16[1,128,256]{2,1,0:T(8,128)(2,1)}, bf16[1,128,256]{2,1,0:T(8,128)(2,1)S(1)}, u32[]{:S(2)}, u32[]{:S(2)}) collective-permute-start(bf16[1,128,256]{2,1,0:T(8,128)(2,1)} %get-tuple-element.11.own), channel_id=1, source_target_pairs={{0,4},{1,5},{2,6},{3,7},{4,0},{5,1},{6,2},{7,3},{8,12},{9,13},{10,... | collective-permute-start | bytes 196616 | tf_op jit(solution)/shard_map/ppermute | solution.py:31
  134.9 8.0 %collective-permute-start.12 = (bf16[2,128,256]{2,1,0:T(8,128)(2,1)S(1)}, bf16[2,128,256]{2,1,0:T(8,128)(2,1)S(1)}, u32[]{:S(2)}, u32[]{:S(2)}) collective-permute-start(bf16[2,128,256]{2,1,0:T(8,128)(2,1)S(1)} %pad_maximum_fusion.2), channel_id=1, source_target_pairs={{0,2},{1,3},{2,0},{3,1},{4,6},{5,7},{6,4},{7,5},{8,10},{9,11},{10,... | collective-permute-start | bytes 393224 | tf_op jit(solution)/shard_map/ppermute | solution.py:31
  143.8 12.6 %collective-permute-start.13 = (bf16[4,128,256]{2,1,0:T(8,128)(2,1)S(1)}, bf16[4,128,256]{2,1,0:T(8,128)(2,1)S(1)}, u32[]{:S(2)}, u32[]{:S(2)}) collective-permute-start(bf16[4,128,256]{2,1,0:T(8,128)(2,1)S(1)} %pad_maximum_fusion.1), channel_id=1, source_target_pairs={{0,1},{1,0},{2,3},{3,2},{4,5},{5,4},{6,7},{7,6},{8,9},{9,8},{10,11... | collective-permute-start | bytes 786440 | tf_op jit(solution)/shard_map/ppermute | solution.py:31
  156.4 0.8 copy-start
Sparse Core Ops, SparseCore 0:
  17.2 85.7 all-gather.1

commit v7 on v6

--- a/solution.py
+++ b/solution.py
@@ -52,13 +52,14 @@
     return lax.dot_general(a, b, dims, preferred_element_type=F32)
 
 
-def call(kernel, outs, in_specs, args, scratch=(), limit=10 << 20):
+def call(kernel, outs, in_specs, args, scratch=(), limit=10 << 20, cost=None):
     return pl.pallas_call(
         kernel,
         out_shape=outs,
         in_specs=in_specs,
         out_specs=jax.tree.map(lambda _: VMEM, outs),
         scratch_shapes=scratch,
+        cost_estimate=cost,
         compiler_params=pltpu.CompilerParams(vmem_limit_bytes=limit),
     )(*args)
 
@@ -78,9 +79,8 @@
         out[head_ref[slot]] = dot(rows, weights).astype(BF16)
 
 
-def attention_kernel(dp_ref, features, *refs):
-    blocks, refs = refs[: 2 * N_BLOCKS - 6], refs[2 * N_BLOCKS - 6 :]
-    arrived, bias_ref, cotangent, gate, gated, packed, rows, columns, sems = refs
+def query_kernel(dp_ref, features, *refs):
+    blocks, (out, rows, columns, sems) = refs[:10], refs[10:]
     cut = columns.shape[1] // 2
     copies = []
     for slot in range(N_BLOCKS):
@@ -101,7 +101,7 @@
     for group in copies[:DEPTH]:
         for copy in group:
             copy.start()
-    query = None
+    total = None
     for slot, group in enumerate(copies):
         for copy in group:
             copy.wait()
@@ -109,9 +109,11 @@
             for copy in copies[slot + DEPTH]:
                 copy.start()
         part = dot(rows[slot], columns[slot])
-        query = part if query is None else query + part
-    query = query.astype(BF16)
-
+        total = part if total is None else total + part
+    out[...] = total.astype(BF16)
+
+
+def attention_kernel(query, arrived, bias_ref, cotangent, gate, gated, packed):
     pairs = jnp.sum(arrived[...].astype(F32), axis=0).astype(BF16)
     keys, values = pairs[:, :HEAD_SIZE], pairs[:, HEAD_SIZE:]
     scaling = HEAD_SIZE ** (-0.5)
@@ -138,8 +140,8 @@
     )
 
 
-def image_kernel(place_ref, own, by4, by2, by1, near, far, out, buffer):
-    for at, part in ((0, own), (1, by4), (2, by2), (4, by1)):
+def image_kernel(place_ref, own, by4, by2, by1, by5, by3, near, far, out, buffer):
+    for at, part in ((0, own), (1, by4), (2, by2), (4, by1), (5, by5), (6, by3)):
         buffer[at : at + part.shape[0]] = part[...]
     total = None
     for slot in range(N_BLOCKS):
@@ -200,35 +202,39 @@
     query_weights = [v for b in (w, before, *across, behind) for v in (b, core_swap(b))]
 
     tokens, columns = hidden.shape[1], w_query.shape[2]
-    gated_out, packed = call(
-        attention_kernel,
-        (jax.ShapeDtypeStruct((tokens, columns), BF16), jax.ShapeDtypeStruct((1, *block), BF16)),
-        [SMEM] + [pl.BlockSpec(memory_space=pl.ANY)] * 11 + [VMEM] * 4,
-        (
-            dp_order,
-            features,
-            *query_weights,
-            arrived,
-            score_bias,
-            cotangent[0],
-            gate_logit.reshape(1, 1),
-        ),
+    query = call(
+        query_kernel,
+        jax.ShapeDtypeStruct((tokens, columns), BF16),
+        [SMEM] + [pl.BlockSpec(memory_space=pl.ANY)] * 11,
+        (dp_order, features, *query_weights),
         [
             pltpu.VMEM(features.shape, BF16),
             pltpu.VMEM((N_BLOCKS, *w.shape), BF16),
             pltpu.SemaphoreType.DMA((3, N_BLOCKS)),
         ],
         limit=60 << 20,
-    )
-
-    by4 = t_swap(packed, 4)
-    by2 = t_swap(jnp.concatenate([packed, by4]), 2)
-    by1 = t_swap(jnp.concatenate([packed, by4, by2]), 1)
+        cost=pl.CostEstimate(
+            flops=2 * tokens * columns * N_BLOCKS * w.shape[0],
+            bytes_accessed=2 * N_BLOCKS * (w.size + hidden.size),
+            transcendentals=0,
+        ),
+    )
+    gated_out, packed = call(
+        attention_kernel,
+        (jax.ShapeDtypeStruct((tokens, columns), BF16), jax.ShapeDtypeStruct((1, *block), BF16)),
+        [VMEM] * 5,
+        (query, arrived, score_bias, cotangent[0], gate_logit.reshape(1, 1)),
+    )
+
+    by4, by1 = lax.optimization_barrier((t_swap(packed, 4), t_swap(packed, 1)))
+    both = jnp.concatenate([packed, by4])
+    by2, by5 = lax.optimization_barrier((t_swap(both, 2), t_swap(by4, 1)))
+    by3 = t_swap(by2, 1)
     portion = call(
         image_kernel,
         jax.ShapeDtypeStruct((image_count, width), BF16),
-        [SMEM] + [VMEM] * 6,
-        (place, packed, by4, by2, by1, near_pairs, far_pairs),
+        [SMEM] + [VMEM] * 8,
+        (place, packed, by4, by2, by1, by5, by3, near_pairs, far_pairs),
         [pltpu.VMEM((N_BLOCKS, *block), BF16)],
     )
     portion = portion.reshape(2 * X_SIZE, rows, width)

time: 202 us -> 195 us (0.965)
  the two profiles are of different devices: /device:TPU:32 before, /device:TPU:48 now
where the time goes in v7:
time: 195 us; the launch traced here: 194 us
  starting transfers between devices  83 us (43%)
  waiting for transfers between devices  40.8 us (21%)
  blocking collectives  32.7 us (17%)
  Pallas kernels  15.7 us (8%)
  between operations  14.9 us (8%)
  local copies, waits for them, and re-layouts  4.6 us (2%)
  other arithmetic  2.3 us (1%)
    all_to_all x1, blocking collectives, local(): lax.all_to_all(portion, 'section', 0, 0).astype(F32)  32.7 us
    ppermute x5, starting transfers between devices, t_swap(): return lax.ppermute(a, 'tensor', [(t, t ^ k) for t in range(8)])  22.5 us
    pallas_call x5, Pallas kernels, call(): pl.pallas_call(kernel, out_shape=outs, in_specs=in_specs, out_specs=jax.t...  15.7 us
    ppermute x1, starting transfers between devices, z_swap(): lax.ppermute(a, 'section', [(s, (s + X_SIZE) % (2 * X_SIZE)) for s in ran...  14.8 us
    all_to_all x1, starting transfers between devices, local(): arrived = lax.all_to_all(portions, 'tensor', 0, 0)  12.6 us
    ppermute x6, starting transfers between devices, core_swap(): return lax.ppermute(a, 'dp', [(d, d ^ 1) for d in range(2 * Y_SIZE)])  12 us
    ppermute x4, starting transfers between devices, y_shift(): return lax.ppermute(a, 'dp', pairs)  11.8 us
    ppermute x5, waiting for transfers between devices, t_swap(): return lax.ppermute(a, 'tensor', [(t, t ^ k) for t in range(8)])  10.8 us
  transfers between devices with their start and end apart: 20, of which 11 were waited for; matrix products, arithmetic and copies ran while one was open for 1% of the time, Pallas kernels for 5%

profile of v7, /device:TPU:48, one launch (start us, length us, event | category | flops | bytes accessed | tf_op | source)
XLA Modules:
  0.0 193.9 jit_solution(15181374201581597498)
XLA Ops:
  7.2 1.1 pad_maximum_fusion
  8.3 1.5 broadcast_in_dim.6
  9.8 4.9 %all-to-all-start = ((bf16[4,1024,256]{2,1,0:T(8,128)(2,1)}), bf16[4,1024,256]{2,1,0:T(8,128)(2,1)S(1)}, u32[]{:S(2)}, u32[]{:S(2)}) async-start(bf16[4,1024,256]{2,1,0:T(8,128)(2,1)} %broadcast_in_dim.6), calls=%async_computation | async-start | bytes 4194304 | tf_op jit(solution)/shard_map/all_to_all | solution.py:42
  14.7 0.7 all-gather.2.cloned.1.call-update
  15.4 14.8 %collective-permute-start = (bf16[16,1024]{1,0:T(8,128)(2,1)S(1)}, bf16[16,1024]{1,0:T(8,128)(2,1)S(1)}, u32[]{:S(2)}, u32[]{:S(2)}) collective-permute-start(bf16[16,1024]{1,0:T(8,128)(2,1)S(1)} %bitcast.13), channel_id=1, source_target_pairs={{0,256},{64,320},{128,384},{192,448},{256,0},{320,64},{384,128},{4... | collective-permute-start | bytes 98312 | tf_op jit(solution)/shard_map/ppermute | solution.py:22
  30.3 2.0 %collective-permute-done.other = bf16[16,1024]{1,0:T(8,128)(2,1)S(1)} collective-permute-done((bf16[16,1024]{1,0:T(8,128)(2,1)S(1)}, bf16[16,1024]{1,0:T(8,128)(2,1)S(1)}, u32[]{:S(2)}, u32[]{:S(2)}) %collective-permute-start) | collective-permute-done | bytes 32800 | tf_op jit(solution)/shard_map/ppermute | solution.py:22
  32.2 5.8 %all-to-all-done.near = bf16[4,1024,256]{2,1,0:T(8,128)(2,1)S(1)} async-done(((bf16[4,1024,256]{2,1,0:T(8,128)(2,1)}), bf16[4,1024,256]{2,1,0:T(8,128)(2,1)S(1)}, u32[]{:S(2)}, u32[]{:S(2)}) %all-to-all-start) | async-done | bytes 2097184 | tf_op jit(solution)/shard_map/all_to_all | solution.py:42
  38.1 1.9 collective-permute-start.10
  40.0 4.0 %collective-permute-start.2 = (bf16[1024,512]{1,0:T(8,128)(2,1)}, bf16[1024,512]{1,0:T(8,128)(2,1)}, u32[]{:S(2)}, u32[]{:S(2)}) collective-permute-start(bf16[1024,512]{1,0:T(8,128)(2,1)} %bitcast.refs_0_), channel_id=1, source_target_pairs={{0,16},{8,24},{16,32},{24,40},{32,48},{40,56},{48,0},{56,8},{1,17}... | collective-permute-start | bytes 3145736 | tf_op jit(solution)/shard_map/ppermute | solution.py:36
  44.0 1.9 collective-permute-start.6
  45.9 0.7 shard_map.96
  46.6 4.3 %all-to-all-start.1 = ((bf16[4,2,16,1024]{3,2,1,0:T(8,128)(2,1)}), bf16[4,2,16,1024]{3,2,1,0:T(8,128)(2,1)S(1)}, u32[]{:S(2)}, u32[]{:S(2)}) async-start(bf16[4,2,16,1024]{3,2,1,0:T(8,128)(2,1)} %shard_map.96), calls=%async_computation.1 | async-start | bytes 524288 | tf_op jit(solution)/shard_map/all_to_all | solution.py:27
  50.9 7.0 %all-to-all-done.1.images = bf16[4,2,16,1024]{3,2,1,0:T(8,128)(2,1)S(1)} async-done(((bf16[4,2,16,1024]{3,2,1,0:T(8,128)(2,1)}), bf16[4,2,16,1024]{3,2,1,0:T(8,128)(2,1)S(1)}, u32[]{:S(2)}, u32[]{:S(2)}) %all-to-all-start.1) | async-done | bytes 262176 | tf_op jit(solution)/shard_map/all_to_all | solution.py:27
  58.0 0.0 collective-permute-done.10.far
  58.0 3.2 %shard_map.97 = bf16[8,128,256]{2,1,0:T(8,128)(2,1)} custom-call(s32[8]{0:T(128)S(1)} %iota_xor_fusion.head_ref, s32[1]{0:T(128)} %bitcast.4.half_ref, bf16[4,2,16,1024]{3,2,1,0:T(8,128)(2,1)S(1)} %all-to-all-done.1.images, bf16[4,1024,256]{2,1,0:T(8,128)(2,1)S(1)} %all-to-all-done.near, bf16[4,1024,256]{2,1,0:T(8,128)(2,1)} %collective-permute-done.10.far), custom_call_target="tpu_custom_call" | custom-call | tf_op jit(solution)/shard_map/pallas_call | solution.py:56
  61.1 12.6 %all-to-all-start.2 = ((bf16[8,128,256]{2,1,0:T(8,128)(2,1)}), bf16[8,128,256]{2,1,0:T(8,128)(2,1)S(1)}, u32[]{:S(2)}, u32[]{:S(2)}) async-start(bf16[8,128,256]{2,1,0:T(8,128)(2,1)} %shard_map.97), calls=%async_computation.2 | async-start | bytes 1048576 | tf_op jit(solution)/shard_map/all_to_all | solution.py:196
  73.8 1.9 collective-permute-start.1
  75.7 1.1 slice.8
  76.8 4.0 %collective-permute-start.4 = (bf16[512,512]{1,0:T(8,128)(2,1)S(1)}, bf16[512,512]{1,0:T(8,128)(2,1)S(1)}, u32[]{:S(2)}, u32[]{:S(2)}) collective-permute-start(bf16[512,512]{1,0:T(8,128)(2,1)S(1)} %slice.8), channel_id=1, source_target_pairs={{0,16},{8,24},{16,32},{24,40},{32,48},{40,56},{48,0},{56,8},{1,17}... | collective-permute-start | bytes 1572872 | tf_op jit(solution)/shard_map/ppermute | solution.py:36
  80.8 1.1 slice.9
  81.9 1.9 collective-permute-start.7
  83.8 2.1 %collective-permute-start.3 = (bf16[1024,512]{1,0:T(8,128)(2,1)}, bf16[1024,512]{1,0:T(8,128)(2,1)}, u32[]{:S(2)}, u32[]{:S(2)}) collective-permute-start(bf16[1024,512]{1,0:T(8,128)(2,1)} %collective-permute-done.2.refs_2_), channel_id=1, source_target_pairs={{0,8},{8,0},{16,24},{24,16},{32,40},{40,32},{48,56},{56,48},{1,9},... | collective-permute-start | bytes 3145736 | tf_op jit(solution)/shard_map/ppermute | solution.py:46
  85.9 2.2 %collective-permute-start.9 = (bf16[1024,512]{1,0:T(8,128)(2,1)}, bf16[1024,512]{1,0:T(8,128)(2,1)}, u32[]{:S(2)}, u32[]{:S(2)}) collective-permute-start(bf16[1024,512]{1,0:T(8,128)(2,1)} %collective-permute-done.6.refs_8_), channel_id=1, source_target_pairs={{0,8},{8,0},{16,24},{24,16},{32,40},{40,32},{48,56},{56,48},{1,9},... | collective-permute-start | bytes 3145736 | tf_op jit(solution)/shard_map/ppermute | solution.py:46
  88.1 4.9 %collective-permute-done.4.refs_4_ = bf16[512,512]{1,0:T(8,128)(2,1)S(1)} collective-permute-done((bf16[512,512]{1,0:T(8,128)(2,1)S(1)}, bf16[512,512]{1,0:T(8,128)(2,1)S(1)}, u32[]{:S(2)}, u32[]{:S(2)}) %collective-permute-start.4) | collective-permute-done | bytes 524320 | tf_op jit(solution)/shard_map/ppermute | solution.py:36
  93.0 1.9 collective-permute-start.5
  94.9 4.2 %collective-permute-done.7.refs_6_ = bf16[512,512]{1,0:T(8,128)(2,1)} collective-permute-done((bf16[512,512]{1,0:T(8,128)(2,1)S(1)}, bf16[512,512]{1,0:T(8,128)(2,1)}, u32[]{:S(2)}, u32[]{:S(2)}) %collective-permute-start.7) | collective-permute-done | bytes 524320 | tf_op jit(solution)/shard_map/ppermute | solution.py:36
  99.1 1.9 collective-permute-start.8
  101.7 0.5 and_or_fusion.dp_ref
  102.2 1.0 collective-permute-done.8.refs_7_
  103.3 0.0 collective-permute-done.3.refs_3_
  103.3 0.0 collective-permute-done.9.refs_9_
  103.3 1.0 all-gather.2.cloned.1.call-done.features
  104.3 6.6 %shard_map.95.query = bf16[160,512]{1,0:T(8,128)(2,1)} custom-call(s32[8]{0:T(128)} %and_or_fusion.dp_ref, bf16[8,160,1024]{2,1,0:T(8,128)(2,1)} %all-gather.2.cloned.1.call-done.features, bf16[1024,512]{1,0:T(8,128)(2,1)} %bitcast.refs_0_, bf16[1024,512]{1,0:T(8,128)(2,1)} %collective-permute-done.1.refs_1_, ...), custom_call_target="tpu_custom_call" | custom-call | flops 1342177280 | bytes 11010048 | tf_op jit(solution)/shard_map/pallas_call | solution.py:56
  110.9 3.3 %all-to-all-done.2.arrived = bf16[8,128,256]{2,1,0:T(8,128)(2,1)S(1)} async-done(((bf16[8,128,256]{2,1,0:T(8,128)(2,1)}), bf16[8,128,256]{2,1,0:T(8,128)(2,1)S(1)}, u32[]{:S(2)}, u32[]{:S(2)}) %all-to-all-start.2) | async-done | bytes 524320 | tf_op jit(solution)/shard_map/all_to_all | solution.py:196
  114.2 0.9 copy-done
  115.1 2.1 %shard_map.98 = (bf16[160,512]{1,0:T(8,128)(2,1)}, bf16[1,128,256]{2,1,0:T(8,128)(2,1)S(1)}) custom-call(bf16[160,512]{1,0:T(8,128)(2,1)S(1)} %copy-done, bf16[8,128,256]{2,1,0:T(8,128)(2,1)S(1)} %all-to-all-done.2.arrived, f32[160,128]{1,0:T(8,128)S(1)} %copy-done.2, bf16[160,512]{1,0:T(8,128)(2,1)S(1)} %bitcast.12, f32[1,1]{1,0:T(1,128)} %bitcast.10.gate), custom_call_target="tpu_custom_call" | custom-call | tf_op jit(solution)/shard_map/pallas_call | solution.py:56
  117.3 7.5 %collective-permute-start.11 = (bf16[1,128,256]{2,1,0:T(8,128)(2,1)S(1)}, bf16[1,128,256]{2,1,0:T(8,128)(2,1)S(1)}, u32[]{:S(2)}, u32[]{:S(2)}) collective-permute-start(bf16[1,128,256]{2,1,0:T(8,128)(2,1)S(1)} %get-tuple-element.15.own), channel_id=1, source_target_pairs={{0,4},{1,5},{2,6},{3,7},{4,0},{5,1},{6,2},{7,3},{8,12},{9,13},{10,... | collective-permute-start | bytes 196616 | tf_op jit(solution)/shard_map/ppermute | solution.py:31
  124.7 5.7 %collective-permute-start.12 = (bf16[1,128,256]{2,1,0:T(8,128)(2,1)S(1)}, bf16[1,128,256]{2,1,0:T(8,128)(2,1)S(1)}, u32[]{:S(2)}, u32[]{:S(2)}) collective-permute-start(bf16[1,128,256]{2,1,0:T(8,128)(2,1)S(1)} %get-tuple-element.15.own), channel_id=1, source_target_pairs={{0,1},{1,0},{2,3},{3,2},{4,5},{5,4},{6,7},{7,6},{8,9},{9,8},{10,11... | collective-permute-start | bytes 196616 | tf_op jit(solution)/shard_map/ppermute | solution.py:31
  130.4 2.2 %collective-permute-done.12.by1 = bf16[1,128,256]{2,1,0:T(8,128)(2,1)S(1)} collective-permute-done((bf16[1,128,256]{2,1,0:T(8,128)(2,1)S(1)}, bf16[1,128,256]{2,1,0:T(8,128)(2,1)S(1)}, u32[]{:S(2)}, u32[]{:S(2)}) %collective-permute-start.12) | collective-permute-done | bytes 65568 | tf_op jit(solution)/shard_map/ppermute | solution.py:31
  132.6 5.0 %collective-permute-start.13 = (bf16[2,128,256]{2,1,0:T(8,128)(2,1)S(1)}, bf16[2,128,256]{2,1,0:T(8,128)(2,1)S(1)}, u32[]{:S(2)}, u32[]{:S(2)}) collective-permute-start(bf16[2,128,256]{2,1,0:T(8,128)(2,1)S(1)} %pad_maximum_fusion.1), channel_id=1, source_target_pairs={{0,2},{1,3},{2,0},{3,1},{4,6},{5,7},{6,4},{7,5},{8,10},{9,11},{10,... | collective-permute-start | bytes 393224 | tf_op jit(solution)/shard_map/ppermute | solution.py:31
  137.6 1.9 collective-permute-start.14
  139.5 4.2 %collective-permute-done.14.by5 = bf16[1,128,256]{2,1,0:T(8,128)(2,1)S(1)} collective-permute-done((bf16[1,128,256]{2,1,0:T(8,128)(2,1)S(1)}, bf16[1,128,256]{2,1,0:T(8,128)(2,1)S(1)}, u32[]{:S(2)}, u32[]{:S(2)}) %collective-permute-start.14) | collective-permute-done | bytes 65568 | tf_op jit(solution)/shard_map/ppermute | solution.py:31
  143.8 0.0 collective-permute-done.13.by2
  143.8 2.5 %collective-permute-start.15 = (bf16[2,128,256]{2,1,0:T(8,128)(2,1)S(1)}, bf16[2,128,256]{2,1,0:T(8,128)(2,1)S(1)}, u32[]{:S(2)}, u32[]{:S(2)}) collective-permute-start(bf16[2,128,256]{2,1,0:T(8,128)(2,1)S(1)} %collective-permute-done.13.by2), channel_id=1, source_target_pairs={{0,1},{1,0},{2,3},{3,2},{4,5},{5,4},{6,7},{7,6},{8,9},{9,8},{10,11... | collective-permute-start | bytes 393224 | tf_op jit(solution)/shard_map/ppermute | solution.py:31
  146.3 4.3 %collective-permute-done.15.by3 = bf16[2,128,256]{2,1,0:T(8,128)(2,1)S(1)} collective-permute-done((bf16[2,128,256]{2,1,0:T(8,128)(2,1)S(1)}, bf16[2,128,256]{2,1,0:T(8,128)(2,1)S(1)}, u32[]{:S(2)}, u32[]{:S(2)}) %collective-permute-start.15) | collective-permute-done | bytes 131104 | tf_op jit(solution)/shard_map/ppermute | solution.py:31
  150.6 3.1 %shard_map.99 = bf16[128,1024]{1,0:T(8,128)(2,1)S(1)} custom-call(s32[8]{0:T(128)S(1)} %shift-right-arithmetic_or_fusion.place_ref, bf16[1,128,256]{2,1,0:T(8,128)(2,1)S(1)} %get-tuple-element.15.own, bf16[1,128,256]{2,1,0:T(8,128)(2,1)S(1)} %collective-permute-done.11.by4, bf16[2,128,256]{2,1,0:T(8,128)(2,1)S(1)} %collective-permute-done.13.by2, ...), custom_call_target="tpu_custom_call" | custom-call | tf_op jit(solution)/shard_map/pallas_call | solution.py:56
  153.7 32.7 %all_to_all.20 = bf16[8,16,1024]{2,1,0:T(8,128)(2,1)S(1)} all-to-all(bf16[8,16,1024]{2,1,0:T(8,128)(2,1)S(1)} %bitcast.11), channel_id=1, replica_groups=mesh['section'=8,'dp'=8,'tensor'=8] {'section'}, dimensions={0} | all-to-all | bytes 524288 | tf_op jit(solution)/shard_map/all_to_all | solution.py:241
  186.4 0.7 convert_reduce_fusion
  (18 shorter events, 0.1 us)
Async XLA Ops:
  9.8 5.7 %copy-start.3 = (bf16[1,16,1024]{2,1,0:T(8,128)(2,1)S(1)}, bf16[1,16,1024]{2,1,0:T(8,128)(2,1)}, u32[]{:S(2)}) copy-start(bf16[1,16,1024]{2,1,0:T(8,128)(2,1)} %param.12) | copy-start | bytes 98308
  9.8 28.3 %all-to-all-start = ((bf16[4,1024,256]{2,1,0:T(8,128)(2,1)}), bf16[4,1024,256]{2,1,0:T(8,128)(2,1)S(1)}, u32[]{:S(2)}, u32[]{:S(2)}) async-start(bf16[4,1024,256]{2,1,0:T(8,128)(2,1)} %broadcast_in_dim.6), calls=%async_computation | async-start | bytes 4194304 | tf_op jit(solution)/shard_map/all_to_all | solution.py:42
  14.7 89.6 %all-gather.2.cloned.1.call-start = ((), (), s32[]{:S(2)}) async-start(), calls=%async_computation.4 | async-start | bytes 2949120 | tf_op jit(solution)/shard_map/all_gather | solution.py:173
  15.4 16.8 %collective-permute-start = (bf16[16,1024]{1,0:T(8,128)(2,1)S(1)}, bf16[16,1024]{1,0:T(8,128)(2,1)S(1)}, u32[]{:S(2)}, u32[]{:S(2)}) collective-permute-start(bf16[16,1024]{1,0:T(8,128)(2,1)S(1)} %bitcast.13), channel_id=1, source_target_pairs={{0,256},{64,320},{128,384},{192,448},{256,0},{320,64},{384,128},{4... | collective-permute-start | bytes 98312 | tf_op jit(solution)/shard_map/ppermute | solution.py:22
  38.1 19.9 %collective-permute-start.10 = (bf16[4,1024,256]{2,1,0:T(8,128)(2,1)S(1)}, bf16[4,1024,256]{2,1,0:T(8,128)(2,1)}, u32[]{:S(2)}, u32[]{:S(2)}) collective-permute-start(bf16[4,1024,256]{2,1,0:T(8,128)(2,1)S(1)} %all-to-all-done.near), channel_id=1, source_target_pairs={{0,8},{8,0},{16,24},{24,16},{32,40},{40,32},{48,56},{56,48},{1,9},... | collective-permute-start | bytes 6291464 | tf_op jit(solution)/shard_map/ppermute | solution.py:46
  40.0 35.7 %collective-permute-start.2 = (bf16[1024,512]{1,0:T(8,128)(2,1)}, bf16[1024,512]{1,0:T(8,128)(2,1)}, u32[]{:S(2)}, u32[]{:S(2)}) collective-permute-start(bf16[1024,512]{1,0:T(8,128)(2,1)} %bitcast.refs_0_), channel_id=1, source_target_pairs={{0,16},{8,24},{16,32},{24,40},{32,48},{40,56},{48,0},{56,8},{1,17}... | collective-permute-start | bytes 3145736 | tf_op jit(solution)/shard_map/ppermute | solution.py:36
  44.0 36.8 %collective-permute-start.6 = (bf16[1024,512]{1,0:T(8,128)(2,1)}, bf16[1024,512]{1,0:T(8,128)(2,1)}, u32[]{:S(2)}, u32[]{:S(2)}) collective-permute-start(bf16[1024,512]{1,0:T(8,128)(2,1)} %bitcast.refs_0_), channel_id=1, source_target_pairs={{0,48},{8,56},{16,0},{24,8},{32,16},{40,24},{48,32},{56,40},{1,49}... | collective-permute-start | bytes 3145736 | tf_op jit(solution)/shard_map/ppermute | solution.py:36
  46.6 11.3 %all-to-all-start.1 = ((bf16[4,2,16,1024]{3,2,1,0:T(8,128)(2,1)}), bf16[4,2,16,1024]{3,2,1,0:T(8,128)(2,1)S(1)}, u32[]{:S(2)}, u32[]{:S(2)}) async-start(bf16[4,2,16,1024]{3,2,1,0:T(8,128)(2,1)} %shard_map.96), calls=%async_computation.1 | async-start | bytes 524288 | tf_op jit(solution)/shard_map/all_to_all | solution.py:27
  61.1 53.1 %all-to-all-start.2 = ((bf16[8,128,256]{2,1,0:T(8,128)(2,1)}), bf16[8,128,256]{2,1,0:T(8,128)(2,1)S(1)}, u32[]{:S(2)}, u32[]{:S(2)}) async-start(bf16[8,128,256]{2,1,0:T(8,128)(2,1)} %shard_map.97), calls=%async_computation.2 | async-start | bytes 1048576 | tf_op jit(solution)/shard_map/all_to_all | solution.py:196
  73.8 28.4 %collective-permute-start.1 = (bf16[1024,512]{1,0:T(8,128)(2,1)}, bf16[1024,512]{1,0:T(8,128)(2,1)}, u32[]{:S(2)}, u32[]{:S(2)}) collective-permute-start(bf16[1024,512]{1,0:T(8,128)(2,1)} %bitcast.refs_0_), channel_id=1, source_target_pairs={{0,8},{8,0},{16,24},{24,16},{32,40},{40,32},{48,56},{56,48},{1,9},... | collective-permute-start | bytes 3145736 | tf_op jit(solution)/shard_map/ppermute | solution.py:46
  76.8 16.2 %collective-permute-start.4 = (bf16[512,512]{1,0:T(8,128)(2,1)S(1)}, bf16[512,512]{1,0:T(8,128)(2,1)S(1)}, u32[]{:S(2)}, u32[]{:S(2)}) collective-permute-start(bf16[512,512]{1,0:T(8,128)(2,1)S(1)} %slice.8), channel_id=1, source_target_pairs={{0,16},{8,24},{16,32},{24,40},{32,48},{40,56},{48,0},{56,8},{1,17}... | collective-permute-start | bytes 1572872 | tf_op jit(solution)/shard_map/ppermute | solution.py:36
  81.9 17.3 %collective-permute-start.7 = (bf16[512,512]{1,0:T(8,128)(2,1)S(1)}, bf16[512,512]{1,0:T(8,128)(2,1)}, u32[]{:S(2)}, u32[]{:S(2)}) collective-permute-start(bf16[512,512]{1,0:T(8,128)(2,1)S(1)} %slice.9), channel_id=1, source_target_pairs={{0,48},{8,56},{16,0},{24,8},{32,16},{40,24},{48,32},{56,40},{1,49}... | collective-permute-start | bytes 1572872 | tf_op jit(solution)/shard_map/ppermute | solution.py:36
  83.8 19.5 %collective-permute-start.3 = (bf16[1024,512]{1,0:T(8,128)(2,1)}, bf16[1024,512]{1,0:T(8,128)(2,1)}, u32[]{:S(2)}, u32[]{:S(2)}) collective-permute-start(bf16[1024,512]{1,0:T(8,128)(2,1)} %collective-permute-done.2.refs_2_), channel_id=1, source_target_pairs={{0,8},{8,0},{16,24},{24,16},{32,40},{40,32},{48,56},{56,48},{1,9},... | collective-permute-start | bytes 3145736 | tf_op jit(solution)/shard_map/ppermute | solution.py:46
  85.9 17.4 %collective-permute-start.9 = (bf16[1024,512]{1,0:T(8,128)(2,1)}, bf16[1024,512]{1,0:T(8,128)(2,1)}, u32[]{:S(2)}, u32[]{:S(2)}) collective-permute-start(bf16[1024,512]{1,0:T(8,128)(2,1)} %collective-permute-done.6.refs_8_), channel_id=1, source_target_pairs={{0,8},{8,0},{16,24},{24,16},{32,40},{40,32},{48,56},{56,48},{1,9},... | collective-permute-start | bytes 3145736 | tf_op jit(solution)/shard_map/ppermute | solution.py:46
  93.0 11.3 %copy-start.4 = (bf16[512,512]{1,0:T(8,128)(2,1)}, bf16[512,512]{1,0:T(8,128)(2,1)S(1)}, u32[]{:S(2)}) copy-start(bf16[512,512]{1,0:T(8,128)(2,1)S(1)} %collective-permute-done.4.refs_4_) | copy-start | bytes 1572868
  93.0 9.2 %collective-permute-start.5 = (bf16[512,512]{1,0:T(8,128)(2,1)S(1)}, bf16[512,512]{1,0:T(8,128)(2,1)}, u32[]{:S(2)}, u32[]{:S(2)}) collective-permute-start(bf16[512,512]{1,0:T(8,128)(2,1)S(1)} %collective-permute-done.4.refs_4_), channel_id=1, source_target_pairs={{0,8},{8,0},{16,24},{24,16},{32,40},{40,32},{48,56},{56,48},{1,9},... | collective-permute-start | bytes 1572872 | tf_op jit(solution)/shard_map/ppermute | solution.py:46
  99.1 4.1 %collective-permute-start.8 = (bf16[512,512]{1,0:T(8,128)(2,1)}, bf16[512,512]{1,0:T(8,128)(2,1)}, u32[]{:S(2)}, u32[]{:S(2)}) collective-permute-start(bf16[512,512]{1,0:T(8,128)(2,1)} %collective-permute-done.7.refs_6_), channel_id=1, source_target_pairs={{0,8},{8,0},{16,24},{24,16},{32,40},{40,32},{48,56},{56,48},{1,9},... | collective-permute-start | bytes 1572872 | tf_op jit(solution)/shard_map/ppermute | solution.py:46
  102.2 12.0 %copy-start.1 = (bf16[1,160,512]{2,1,0:T(8,128)(2,1)S(1)}, bf16[1,160,512]{2,1,0:T(8,128)(2,1)}, u32[]{:S(2)}) copy-start(bf16[1,160,512]{2,1,0:T(8,128)(2,1)} %param.15) | copy-start | bytes 491524
  102.2 12.0 %copy-start.2 = (f32[160,128]{1,0:T(8,128)S(1)}, f32[160,128]{1,0:T(8,128)}, u32[]{:S(2)}) copy-start(f32[160,128]{1,0:T(8,128)} %bias_ref.1) | copy-start | bytes 245764
  114.2 0.9 copy-start
  117.3 13.1 %collective-permute-start.11 = (bf16[1,128,256]{2,1,0:T(8,128)(2,1)S(1)}, bf16[1,128,256]{2,1,0:T(8,128)(2,1)S(1)}, u32[]{:S(2)}, u32[]{:S(2)}) collective-permute-start(bf16[1,128,256]{2,1,0:T(8,128)(2,1)S(1)} %get-tuple-element.15.own), channel_id=1, source_target_pairs={{0,4},{1,5},{2,6},{3,7},{4,0},{5,1},{6,2},{7,3},{8,12},{9,13},{10,... | collective-permute-start | bytes 196616 | tf_op jit(solution)/shard_map/ppermute | solution.py:31
  124.7 7.9 %collective-permute-start.12 = (bf16[1,128,256]{2,1,0:T(8,128)(2,1)S(1)}, bf16[1,128,256]{2,1,0:T(8,128)(2,1)S(1)}, u32[]{:S(2)}, u32[]{:S(2)}) collective-permute-start(bf16[1,128,256]{2,1,0:T(8,128)(2,1)S(1)} %get-tuple-element.15.own), channel_id=1, source_target_pairs={{0,1},{1,0},{2,3},{3,2},{4,5},{5,4},{6,7},{7,6},{8,9},{9,8},{10,11... | collective-permute-start | bytes 196616 | tf_op jit(solution)/shard_map/ppermute | solution.py:31
  132.6 11.1 %collective-permute-start.13 = (bf16[2,128,256]{2,1,0:T(8,128)(2,1)S(1)}, bf16[2,128,256]{2,1,0:T(8,128)(2,1)S(1)}, u32[]{:S(2)}, u32[]{:S(2)}) collective-permute-start(bf16[2,128,256]{2,1,0:T(8,128)(2,1)S(1)} %pad_maximum_fusion.1), channel_id=1, source_target_pairs={{0,2},{1,3},{2,0},{3,1},{4,6},{5,7},{6,4},{7,5},{8,10},{9,11},{10,... | collective-permute-start | bytes 393224 | tf_op jit(solution)/shard_map/ppermute | solution.py:31
  137.6 6.2 %collective-permute-start.14 = (bf16[1,128,256]{2,1,0:T(8,128)(2,1)S(1)}, bf16[1,128,256]{2,1,0:T(8,128)(2,1)S(1)}, u32[]{:S(2)}, u32[]{:S(2)}) collective-permute-start(bf16[1,128,256]{2,1,0:T(8,128)(2,1)S(1)} %collective-permute-done.11.by4), channel_id=1, source_target_pairs={{0,1},{1,0},{2,3},{3,2},{4,5},{5,4},{6,7},{7,6},{8,9},{9,8},{10,11... | collective-permute-start | bytes 196616 | tf_op jit(solution)/shard_map/ppermute | solution.py:31
  143.8 6.9 %collective-permute-start.15 = (bf16[2,128,256]{2,1,0:T(8,128)(2,1)S(1)}, bf16[2,128,256]{2,1,0:T(8,128)(2,1)S(1)}, u32[]{:S(2)}, u32[]{:S(2)}) collective-permute-start(bf16[2,128,256]{2,1,0:T(8,128)(2,1)S(1)} %collective-permute-done.13.by2), channel_id=1, source_target_pairs={{0,1},{1,0},{2,3},{3,2},{4,5},{5,4},{6,7},{7,6},{8,9},{9,8},{10,11... | collective-permute-start | bytes 393224 | tf_op jit(solution)/shard_map/ppermute | solution.py:31
Sparse Core Ops, SparseCore 0:
  17.6 86.6 all-gather.1

commit v8 on v7

--- a/solution.py
+++ b/solution.py
@@ -140,7 +140,7 @@
     )
 
 
-def image_kernel(place_ref, own, by4, by2, by1, by5, by3, near, far, out, buffer):
+def image_kernel(place_ref, half_ref, own, by4, by2, by1, by5, by3, near, far, out, buffer):
     for at, part in ((0, own), (1, by4), (2, by2), (4, by1), (5, by5), (6, by3)):
         buffer[at : at + part.shape[0]] = part[...]
     total = None
@@ -148,7 +148,17 @@
         weights = (near, far)[slot % 2][slot // 2]
         part = dot(buffer[place_ref[slot]], weights, BY_COLUMNS)
         total = part if total is None else total + part
-    out[...] = total.astype(BF16)
+    rows = out.shape[2]
+    for z in range(2):
+        for x in range(X_SIZE):
+            at = (z * X_SIZE + x) * rows
+            out[x, z ^ half_ref[0]] = total[at : at + rows].astype(BF16)
+
+
+def section_kernel(arrived, keep, send):
+    total = jnp.sum(arrived[...].astype(F32), axis=0)
+    keep[...] = total[0]
+    send[...] = total[1].astype(BF16)
 
 
 def local(
@@ -164,6 +174,7 @@
     tok_rows = hidden.shape[1]
     columns = w_query.shape[2]
     dp = lax.axis_index("dp")
+    half = lax.axis_index("section")[None] >> 2
     slots = jnp.arange(N_BLOCKS, dtype=jnp.int32)
     dp_order = ((((dp >> 1) - (slots >> 1)) & (Y_SIZE - 1)) << 1) | ((dp ^ slots) & 1)
     head_order = slots ^ (dp & 1)
@@ -191,7 +202,7 @@
         pair_kernel,
         jax.ShapeDtypeStruct((N_BLOCKS, *block), BF16),
         [SMEM] * 2 + [VMEM] * 3,
-        (head_order, lax.axis_index("section")[None] >> 2, images, near_pairs, far_pairs),
+        (head_order, half, images, near_pairs, far_pairs),
     )
     arrived = lax.all_to_all(portions, "tensor", 0, 0)
 
@@ -232,13 +243,18 @@
     by3 = t_swap(by2, 1)
     portion = call(
         image_kernel,
-        jax.ShapeDtypeStruct((image_count, width), BF16),
-        [SMEM] + [VMEM] * 8,
-        (place, packed, by4, by2, by1, by5, by3, near_pairs, far_pairs),
+        jax.ShapeDtypeStruct((X_SIZE, 2, rows, width), BF16),
+        [SMEM] * 2 + [VMEM] * 8,
+        (place, half, packed, by4, by2, by1, by5, by3, near_pairs, far_pairs),
         [pltpu.VMEM((N_BLOCKS, *block), BF16)],
     )
-    portion = portion.reshape(2 * X_SIZE, rows, width)
-    image_grad = jnp.sum(lax.all_to_all(portion, "section", 0, 0).astype(F32), axis=0)
+    keep, send = call(
+        section_kernel,
+        (jax.ShapeDtypeStruct((rows, width), F32), jax.ShapeDtypeStruct((rows, width), BF16)),
+        [VMEM],
+        (x_exchange(portion),),
+    )
+    image_grad = keep + z_swap(send).astype(F32)
     return (gated_out[None], image_grad[None])
 
 

time: 195 us -> 189 us (0.969)
  the two profiles are of different devices: /device:TPU:48 before, /device:TPU:24 now
where the time goes in v8:
time: 189 us; the launch traced here: 187 us
  starting transfers between devices  93 us (49%)
  waiting for transfers between devices  45.1 us (24%)
  Pallas kernels  15.7 us (8%)
  between operations  14.9 us (8%)
  blocking collectives  11.7 us (6%)
  local copies, waits for them, and re-layouts  4.6 us (2%)
  other arithmetic  2.27 us (1%)
    ppermute x2, starting transfers between devices, z_swap(): lax.ppermute(a, 'section', [(s, (s + X_SIZE) % (2 * X_SIZE)) for s in ran...  21.2 us
    ppermute x5, starting transfers between devices, t_swap(): return lax.ppermute(a, 'tensor', [(t, t ^ k) for t in range(8)])  21 us
    pallas_call x6, Pallas kernels, call(): pl.pallas_call(kernel, out_shape=outs, in_specs=in_specs, out_specs=jax.t...  15.7 us
    ppermute x4, starting transfers between devices, y_shift(): return lax.ppermute(a, 'dp', pairs)  12.7 us
    all_to_all x1, starting transfers between devices, local(): arrived = lax.all_to_all(portions, 'tensor', 0, 0)  12.5 us
    ppermute x6, starting transfers between devices, core_swap(): return lax.ppermute(a, 'dp', [(d, d ^ 1) for d in range(2 * Y_SIZE)])  12 us
    all_to_all x1, blocking collectives, x_exchange(): return lax.all_to_all(a, 'section', 0, 0, axis_index_groups=groups)  11.7 us
    ppermute x5, waiting for transfers between devices, t_swap(): return lax.ppermute(a, 'tensor', [(t, t ^ k) for t in range(8)])  10.5 us
  transfers between devices with their start and end apart: 21, of which 13 were waited for; matrix products, arithmetic and copies ran while one was open for 1% of the time, Pallas kernels for 6%

profile of v8, /device:TPU:24, one launch (start us, length us, event | category | flops | bytes accessed | tf_op | source)
XLA Modules:
  0.0 187.2 jit_solution(7379322197543726328)
XLA Ops:
  7.2 1.1 pad_maximum_fusion
  8.3 1.5 broadcast_in_dim.6
  9.8 9.3 %all-to-all-start = ((bf16[4,1024,256]{2,1,0:T(8,128)(2,1)}), bf16[4,1024,256]{2,1,0:T(8,128)(2,1)S(1)}, u32[]{:S(2)}, u32[]{:S(2)}) async-start(bf16[4,1024,256]{2,1,0:T(8,128)(2,1)} %broadcast_in_dim.6), calls=%async_computation | async-start | bytes 4194304 | tf_op jit(solution)/shard_map/all_to_all | solution.py:42
  19.1 0.7 all-gather.2.cloned.1.call-update
  19.8 11.2 %collective-permute-start = (bf16[16,1024]{1,0:T(8,128)(2,1)S(1)}, bf16[16,1024]{1,0:T(8,128)(2,1)S(1)}, u32[]{:S(2)}, u32[]{:S(2)}) collective-permute-start(bf16[16,1024]{1,0:T(8,128)(2,1)S(1)} %bitcast.12), channel_id=1, source_target_pairs={{0,256},{64,320},{128,384},{192,448},{256,0},{320,64},{384,128},{4... | collective-permute-start | bytes 98312 | tf_op jit(solution)/shard_map/ppermute | solution.py:22
  31.0 3.3 %collective-permute-done.other = bf16[16,1024]{1,0:T(8,128)(2,1)S(1)} collective-permute-done((bf16[16,1024]{1,0:T(8,128)(2,1)S(1)}, bf16[16,1024]{1,0:T(8,128)(2,1)S(1)}, u32[]{:S(2)}, u32[]{:S(2)}) %collective-permute-start) | collective-permute-done | bytes 32800 | tf_op jit(solution)/shard_map/ppermute | solution.py:22
  34.3 4.5 %all-to-all-done.near = bf16[4,1024,256]{2,1,0:T(8,128)(2,1)S(1)} async-done(((bf16[4,1024,256]{2,1,0:T(8,128)(2,1)}), bf16[4,1024,256]{2,1,0:T(8,128)(2,1)S(1)}, u32[]{:S(2)}, u32[]{:S(2)}) %all-to-all-start) | async-done | bytes 2097184 | tf_op jit(solution)/shard_map/all_to_all | solution.py:42
  38.8 1.9 %collective-permute-start.10 = (bf16[4,1024,256]{2,1,0:T(8,128)(2,1)S(1)}, bf16[4,1024,256]{2,1,0:T(8,128)(2,1)}, u32[]{:S(2)}, u32[]{:S(2)}) collective-permute-start(bf16[4,1024,256]{2,1,0:T(8,128)(2,1)S(1)} %all-to-all-done.near), channel_id=1, source_target_pairs={{0,8},{8,0},{16,24},{24,16},{32,40},{40,32},{48,56},{56,48},{1,9},... | collective-permute-start | bytes 6291464 | tf_op jit(solution)/shard_map/ppermute | solution.py:46
  40.8 4.0 %collective-permute-start.2 = (bf16[1024,512]{1,0:T(8,128)(2,1)}, bf16[1024,512]{1,0:T(8,128)(2,1)}, u32[]{:S(2)}, u32[]{:S(2)}) collective-permute-start(bf16[1024,512]{1,0:T(8,128)(2,1)} %bitcast.refs_0_), channel_id=1, source_target_pairs={{0,16},{8,24},{16,32},{24,40},{32,48},{40,56},{48,0},{56,8},{1,17}... | collective-permute-start | bytes 3145736 | tf_op jit(solution)/shard_map/ppermute | solution.py:36
  44.7 1.9 %collective-permute-start.6 = (bf16[1024,512]{1,0:T(8,128)(2,1)}, bf16[1024,512]{1,0:T(8,128)(2,1)}, u32[]{:S(2)}, u32[]{:S(2)}) collective-permute-start(bf16[1024,512]{1,0:T(8,128)(2,1)} %bitcast.refs_0_), channel_id=1, source_target_pairs={{0,48},{8,56},{16,0},{24,8},{32,16},{40,24},{48,32},{56,40},{1,49}... | collective-permute-start | bytes 3145736 | tf_op jit(solution)/shard_map/ppermute | solution.py:36
  46.7 0.7 shard_map.96
  47.4 4.3 %all-to-all-start.1 = ((bf16[4,2,16,1024]{3,2,1,0:T(8,128)(2,1)}), bf16[4,2,16,1024]{3,2,1,0:T(8,128)(2,1)S(1)}, u32[]{:S(2)}, u32[]{:S(2)}) async-start(bf16[4,2,16,1024]{3,2,1,0:T(8,128)(2,1)} %shard_map.96), calls=%async_computation.1 | async-start | bytes 524288 | tf_op jit(solution)/shard_map/all_to_all | solution.py:27
  51.7 7.0 %all-to-all-done.1.images = bf16[4,2,16,1024]{3,2,1,0:T(8,128)(2,1)S(1)} async-done(((bf16[4,2,16,1024]{3,2,1,0:T(8,128)(2,1)}), bf16[4,2,16,1024]{3,2,1,0:T(8,128)(2,1)S(1)}, u32[]{:S(2)}, u32[]{:S(2)}) %all-to-all-start.1) | async-done | bytes 262176 | tf_op jit(solution)/shard_map/all_to_all | solution.py:27
  58.7 0.0 collective-permute-done.10.far
  58.7 3.2 %shard_map.97 = bf16[8,128,256]{2,1,0:T(8,128)(2,1)} custom-call(s32[8]{0:T(128)S(1)} %iota_xor_fusion.head_ref, s32[1]{0:T(128)} %bitcast.4.half_ref, bf16[4,2,16,1024]{3,2,1,0:T(8,128)(2,1)S(1)} %all-to-all-done.1.images, bf16[4,1024,256]{2,1,0:T(8,128)(2,1)S(1)} %all-to-all-done.near, bf16[4,1024,256]{2,1,0:T(8,128)(2,1)} %collective-permute-done.10.far), custom_call_target="tpu_custom_call" | custom-call | tf_op jit(solution)/shard_map/pallas_call | solution.py:56
  61.9 12.5 %all-to-all-start.2 = ((bf16[8,128,256]{2,1,0:T(8,128)(2,1)}), bf16[8,128,256]{2,1,0:T(8,128)(2,1)S(1)}, u32[]{:S(2)}, u32[]{:S(2)}) async-start(bf16[8,128,256]{2,1,0:T(8,128)(2,1)} %shard_map.97), calls=%async_computation.2 | async-start | bytes 1048576 | tf_op jit(solution)/shard_map/all_to_all | solution.py:207
  74.4 1.9 %collective-permute-start.1 = (bf16[1024,512]{1,0:T(8,128)(2,1)}, bf16[1024,512]{1,0:T(8,128)(2,1)}, u32[]{:S(2)}, u32[]{:S(2)}) collective-permute-start(bf16[1024,512]{1,0:T(8,128)(2,1)} %bitcast.refs_0_), channel_id=1, source_target_pairs={{0,8},{8,0},{16,24},{24,16},{32,40},{40,32},{48,56},{56,48},{1,9},... | collective-permute-start | bytes 3145736 | tf_op jit(solution)/shard_map/ppermute | solution.py:46
  76.4 1.1 slice.8
  77.4 4.9 %collective-permute-start.4 = (bf16[512,512]{1,0:T(8,128)(2,1)S(1)}, bf16[512,512]{1,0:T(8,128)(2,1)S(1)}, u32[]{:S(2)}, u32[]{:S(2)}) collective-permute-start(bf16[512,512]{1,0:T(8,128)(2,1)S(1)} %slice.8), channel_id=1, source_target_pairs={{0,16},{8,24},{16,32},{24,40},{32,48},{40,56},{48,0},{56,8},{1,17}... | collective-permute-start | bytes 1572872 | tf_op jit(solution)/shard_map/ppermute | solution.py:36
  82.3 1.1 slice.9
  83.4 1.9 %collective-permute-start.7 = (bf16[512,512]{1,0:T(8,128)(2,1)S(1)}, bf16[512,512]{1,0:T(8,128)(2,1)}, u32[]{:S(2)}, u32[]{:S(2)}) collective-permute-start(bf16[512,512]{1,0:T(8,128)(2,1)S(1)} %slice.9), channel_id=1, source_target_pairs={{0,48},{8,56},{16,0},{24,8},{32,16},{40,24},{48,32},{56,40},{1,49}... | collective-permute-start | bytes 1572872 | tf_op jit(solution)/shard_map/ppermute | solution.py:36
  85.4 2.1 %collective-permute-start.3 = (bf16[1024,512]{1,0:T(8,128)(2,1)}, bf16[1024,512]{1,0:T(8,128)(2,1)}, u32[]{:S(2)}, u32[]{:S(2)}) collective-permute-start(bf16[1024,512]{1,0:T(8,128)(2,1)} %collective-permute-done.2.refs_2_), channel_id=1, source_target_pairs={{0,8},{8,0},{16,24},{24,16},{32,40},{40,32},{48,56},{56,48},{1,9},... | collective-permute-start | bytes 3145736 | tf_op jit(solution)/shard_map/ppermute | solution.py:46
  87.5 2.2 %collective-permute-start.9 = (bf16[1024,512]{1,0:T(8,128)(2,1)}, bf16[1024,512]{1,0:T(8,128)(2,1)}, u32[]{:S(2)}, u32[]{:S(2)}) collective-permute-start(bf16[1024,512]{1,0:T(8,128)(2,1)} %collective-permute-done.6.refs_8_), channel_id=1, source_target_pairs={{0,8},{8,0},{16,24},{24,16},{32,40},{40,32},{48,56},{56,48},{1,9},... | collective-permute-start | bytes 3145736 | tf_op jit(solution)/shard_map/ppermute | solution.py:46
  89.7 4.4 %collective-permute-done.4.refs_4_ = bf16[512,512]{1,0:T(8,128)(2,1)S(1)} collective-permute-done((bf16[512,512]{1,0:T(8,128)(2,1)S(1)}, bf16[512,512]{1,0:T(8,128)(2,1)S(1)}, u32[]{:S(2)}, u32[]{:S(2)}) %collective-permute-start.4) | collective-permute-done | bytes 524320 | tf_op jit(solution)/shard_map/ppermute | solution.py:36
  94.1 1.9 %collective-permute-start.5 = (bf16[512,512]{1,0:T(8,128)(2,1)S(1)}, bf16[512,512]{1,0:T(8,128)(2,1)}, u32[]{:S(2)}, u32[]{:S(2)}) collective-permute-start(bf16[512,512]{1,0:T(8,128)(2,1)S(1)} %collective-permute-done.4.refs_4_), channel_id=1, source_target_pairs={{0,8},{8,0},{16,24},{24,16},{32,40},{40,32},{48,56},{56,48},{1,9},... | collective-permute-start | bytes 1572872 | tf_op jit(solution)/shard_map/ppermute | solution.py:46
  96.1 4.6 %collective-permute-done.7.refs_6_ = bf16[512,512]{1,0:T(8,128)(2,1)} collective-permute-done((bf16[512,512]{1,0:T(8,128)(2,1)S(1)}, bf16[512,512]{1,0:T(8,128)(2,1)}, u32[]{:S(2)}, u32[]{:S(2)}) %collective-permute-start.7) | collective-permute-done | bytes 524320 | tf_op jit(solution)/shard_map/ppermute | solution.py:36
  100.7 1.9 %collective-permute-start.8 = (bf16[512,512]{1,0:T(8,128)(2,1)}, bf16[512,512]{1,0:T(8,128)(2,1)}, u32[]{:S(2)}, u32[]{:S(2)}) collective-permute-start(bf16[512,512]{1,0:T(8,128)(2,1)} %collective-permute-done.7.refs_6_), channel_id=1, source_target_pairs={{0,8},{8,0},{16,24},{24,16},{32,40},{40,32},{48,56},{56,48},{1,9},... | collective-permute-start | bytes 1572872 | tf_op jit(solution)/shard_map/ppermute | solution.py:46
  103.2 0.5 and_or_fusion.dp_ref
  103.8 1.0 collective-permute-done.8.refs_7_
  104.8 1.4 all-gather.2.cloned.1.call-done.features
  106.2 6.6 %shard_map.95.query = bf16[160,512]{1,0:T(8,128)(2,1)} custom-call(s32[8]{0:T(128)} %and_or_fusion.dp_ref, bf16[8,160,1024]{2,1,0:T(8,128)(2,1)} %all-gather.2.cloned.1.call-done.features, bf16[1024,512]{1,0:T(8,128)(2,1)} %bitcast.refs_0_, bf16[1024,512]{1,0:T(8,128)(2,1)} %collective-permute-done.1.refs_1_, ...), custom_call_target="tpu_custom_call" | custom-call | flops 1342177280 | bytes 11010048 | tf_op jit(solution)/shard_map/pallas_call | solution.py:56
  112.8 3.1 %all-to-all-done.2.arrived = bf16[8,128,256]{2,1,0:T(8,128)(2,1)S(1)} async-done(((bf16[8,128,256]{2,1,0:T(8,128)(2,1)}), bf16[8,128,256]{2,1,0:T(8,128)(2,1)S(1)}, u32[]{:S(2)}, u32[]{:S(2)}) %all-to-all-start.2) | async-done | bytes 524320 | tf_op jit(solution)/shard_map/all_to_all | solution.py:207
  115.9 0.9 copy-done
  116.8 2.1 %shard_map.98 = (bf16[160,512]{1,0:T(8,128)(2,1)}, bf16[1,128,256]{2,1,0:T(8,128)(2,1)S(1)}) custom-call(bf16[160,512]{1,0:T(8,128)(2,1)S(1)} %copy-done, bf16[8,128,256]{2,1,0:T(8,128)(2,1)S(1)} %all-to-all-done.2.arrived, f32[160,128]{1,0:T(8,128)S(1)} %copy-done.2, bf16[160,512]{1,0:T(8,128)(2,1)S(1)} %bitcast.11, f32[1,1]{1,0:T(1,128)} %bitcast.10.gate), custom_call_target="tpu_custom_call" | custom-call | tf_op jit(solution)/shard_map/pallas_call | solution.py:56
  118.9 8.9 %collective-permute-start.11 = (bf16[1,128,256]{2,1,0:T(8,128)(2,1)S(1)}, bf16[1,128,256]{2,1,0:T(8,128)(2,1)S(1)}, u32[]{:S(2)}, u32[]{:S(2)}) collective-permute-start(bf16[1,128,256]{2,1,0:T(8,128)(2,1)S(1)} %get-tuple-element.17.own), channel_id=1, source_target_pairs={{0,4},{1,5},{2,6},{3,7},{4,0},{5,1},{6,2},{7,3},{8,12},{9,13},{10,... | collective-permute-start | bytes 196616 | tf_op jit(solution)/shard_map/ppermute | solution.py:31
  127.8 1.9 %collective-permute-start.12 = (bf16[1,128,256]{2,1,0:T(8,128)(2,1)S(1)}, bf16[1,128,256]{2,1,0:T(8,128)(2,1)S(1)}, u32[]{:S(2)}, u32[]{:S(2)}) collective-permute-start(bf16[1,128,256]{2,1,0:T(8,128)(2,1)S(1)} %get-tuple-element.17.own), channel_id=1, source_target_pairs={{0,1},{1,0},{2,3},{3,2},{4,5},{5,4},{6,7},{7,6},{8,9},{9,8},{10,11... | collective-permute-start | bytes 196616 | tf_op jit(solution)/shard_map/ppermute | solution.py:31
  129.7 0.6 collective-permute-done.11.by4
  130.3 3.7 %collective-permute-done.12.by1 = bf16[1,128,256]{2,1,0:T(8,128)(2,1)S(1)} collective-permute-done((bf16[1,128,256]{2,1,0:T(8,128)(2,1)S(1)}, bf16[1,128,256]{2,1,0:T(8,128)(2,1)S(1)}, u32[]{:S(2)}, u32[]{:S(2)}) %collective-permute-start.12) | collective-permute-done | bytes 65568 | tf_op jit(solution)/shard_map/ppermute | solution.py:31
  134.0 1.9 %collective-permute-start.13 = (bf16[2,128,256]{2,1,0:T(8,128)(2,1)S(1)}, bf16[2,128,256]{2,1,0:T(8,128)(2,1)S(1)}, u32[]{:S(2)}, u32[]{:S(2)}) collective-permute-start(bf16[2,128,256]{2,1,0:T(8,128)(2,1)S(1)} %pad_maximum_fusion.1), channel_id=1, source_target_pairs={{0,2},{1,3},{2,0},{3,1},{4,6},{5,7},{6,4},{7,5},{8,10},{9,11},{10,... | collective-permute-start | bytes 393224 | tf_op jit(solution)/shard_map/ppermute | solution.py:31
  135.9 4.9 %collective-permute-start.14 = (bf16[1,128,256]{2,1,0:T(8,128)(2,1)S(1)}, bf16[1,128,256]{2,1,0:T(8,128)(2,1)S(1)}, u32[]{:S(2)}, u32[]{:S(2)}) collective-permute-start(bf16[1,128,256]{2,1,0:T(8,128)(2,1)S(1)} %collective-permute-done.11.by4), channel_id=1, source_target_pairs={{0,1},{1,0},{2,3},{3,2},{4,5},{5,4},{6,7},{7,6},{8,9},{9,8},{10,11... | collective-permute-start | bytes 196616 | tf_op jit(solution)/shard_map/ppermute | solution.py:31
  140.8 2.8 %collective-permute-done.14.by5 = bf16[1,128,256]{2,1,0:T(8,128)(2,1)S(1)} collective-permute-done((bf16[1,128,256]{2,1,0:T(8,128)(2,1)S(1)}, bf16[1,128,256]{2,1,0:T(8,128)(2,1)S(1)}, u32[]{:S(2)}, u32[]{:S(2)}) %collective-permute-start.14) | collective-permute-done | bytes 65568 | tf_op jit(solution)/shard_map/ppermute | solution.py:31
  143.6 3.4 %collective-permute-start.15 = (bf16[2,128,256]{2,1,0:T(8,128)(2,1)S(1)}, bf16[2,128,256]{2,1,0:T(8,128)(2,1)S(1)}, u32[]{:S(2)}, u32[]{:S(2)}) collective-permute-start(bf16[2,128,256]{2,1,0:T(8,128)(2,1)S(1)} %collective-permute-done.13.by2), channel_id=1, source_target_pairs={{0,1},{1,0},{2,3},{3,2},{4,5},{5,4},{6,7},{7,6},{8,9},{9,8},{10,11... | collective-permute-start | bytes 393224 | tf_op jit(solution)/shard_map/ppermute | solution.py:31
  147.0 3.5 %collective-permute-done.15.by3 = bf16[2,128,256]{2,1,0:T(8,128)(2,1)S(1)} collective-permute-done((bf16[2,128,256]{2,1,0:T(8,128)(2,1)S(1)}, bf16[2,128,256]{2,1,0:T(8,128)(2,1)S(1)}, u32[]{:S(2)}, u32[]{:S(2)}) %collective-permute-start.15) | collective-permute-done | bytes 131104 | tf_op jit(solution)/shard_map/ppermute | solution.py:31
  150.5 3.0 %shard_map.99 = bf16[4,2,16,1024]{3,2,1,0:T(8,128)(2,1)S(1)} custom-call(s32[8]{0:T(128)S(1)} %shift-right-arithmetic_or_fusion.place_ref, s32[1]{0:T(128)} %bitcast.4.half_ref, bf16[1,128,256]{2,1,0:T(8,128)(2,1)S(1)} %get-tuple-element.17.own, bf16[1,128,256]{2,1,0:T(8,128)(2,1)S(1)} %collective-permute-done.11.by4, ...), custom_call_target="tpu_custom_call" | custom-call | tf_op jit(solution)/shard_map/pallas_call | solution.py:56
  153.5 11.7 %all_to_all.20.arrived = bf16[4,2,16,1024]{3,2,1,0:T(8,128)(2,1)S(1)} all-to-all(bf16[4,2,16,1024]{3,2,1,0:T(8,128)(2,1)S(1)} %shard_map.99), channel_id=1, replica_groups={{0,64,128,192},{256,320,384,448},{1,65,129,193},{257,321,385,449},{2,66..., dimensions={0} | all-to-all | bytes 524288 | tf_op jit(solution)/shard_map/all_to_all | solution.py:27
  165.2 10.0 %collective-permute-start.16 = (bf16[16,1024]{1,0:T(8,128)(2,1)S(1)}, bf16[16,1024]{1,0:T(8,128)(2,1)S(1)}, u32[]{:S(2)}, u32[]{:S(2)}) collective-permute-start(bf16[16,1024]{1,0:T(8,128)(2,1)S(1)} %get-tuple-element.23), channel_id=1, source_target_pairs={{0,256},{64,320},{128,384},{192,448},{256,0},{320,64},{384,128},{4... | collective-permute-start | bytes 98312 | tf_op jit(solution)/shard_map/ppermute | solution.py:22
  175.2 4.5 %collective-permute-done.16 = bf16[16,1024]{1,0:T(8,128)(2,1)S(1)} collective-permute-done((bf16[16,1024]{1,0:T(8,128)(2,1)S(1)}, bf16[16,1024]{1,0:T(8,128)(2,1)S(1)}, u32[]{:S(2)}, u32[]{:S(2)}) %collective-permute-start.16) | collective-permute-done | bytes 32800 | tf_op jit(solution)/shard_map/ppermute | solution.py:22
  179.8 0.6 add_bitcast_fusion
  (21 shorter events, 0.1 us)
Async XLA Ops:
  9.8 10.0 %copy-start.3 = (bf16[1,16,1024]{2,1,0:T(8,128)(2,1)S(1)}, bf16[1,16,1024]{2,1,0:T(8,128)(2,1)}, u32[]{:S(2)}) copy-start(bf16[1,16,1024]{2,1,0:T(8,128)(2,1)} %param.12) | copy-start | bytes 98308
  9.8 29.1 %all-to-all-start = ((bf16[4,1024,256]{2,1,0:T(8,128)(2,1)}), bf16[4,1024,256]{2,1,0:T(8,128)(2,1)S(1)}, u32[]{:S(2)}, u32[]{:S(2)}) async-start(bf16[4,1024,256]{2,1,0:T(8,128)(2,1)} %broadcast_in_dim.6), calls=%async_computation | async-start | bytes 4194304 | tf_op jit(solution)/shard_map/all_to_all | solution.py:42
  19.1 87.1 %all-gather.2.cloned.1.call-start = ((), (), s32[]{:S(2)}) async-start(), calls=%async_computation.4 | async-start | bytes 2949120 | tf_op jit(solution)/shard_map/all_gather | solution.py:184
  19.8 14.5 %collective-permute-start = (bf16[16,1024]{1,0:T(8,128)(2,1)S(1)}, bf16[16,1024]{1,0:T(8,128)(2,1)S(1)}, u32[]{:S(2)}, u32[]{:S(2)}) collective-permute-start(bf16[16,1024]{1,0:T(8,128)(2,1)S(1)} %bitcast.12), channel_id=1, source_target_pairs={{0,256},{64,320},{128,384},{192,448},{256,0},{320,64},{384,128},{4... | collective-permute-start | bytes 98312 | tf_op jit(solution)/shard_map/ppermute | solution.py:22
  38.8 19.9 %collective-permute-start.10 = (bf16[4,1024,256]{2,1,0:T(8,128)(2,1)S(1)}, bf16[4,1024,256]{2,1,0:T(8,128)(2,1)}, u32[]{:S(2)}, u32[]{:S(2)}) collective-permute-start(bf16[4,1024,256]{2,1,0:T(8,128)(2,1)S(1)} %all-to-all-done.near), channel_id=1, source_target_pairs={{0,8},{8,0},{16,24},{24,16},{32,40},{40,32},{48,56},{56,48},{1,9},... | collective-permute-start | bytes 6291464 | tf_op jit(solution)/shard_map/ppermute | solution.py:46
  40.8 35.6 %collective-permute-start.2 = (bf16[1024,512]{1,0:T(8,128)(2,1)}, bf16[1024,512]{1,0:T(8,128)(2,1)}, u32[]{:S(2)}, u32[]{:S(2)}) collective-permute-start(bf16[1024,512]{1,0:T(8,128)(2,1)} %bitcast.refs_0_), channel_id=1, source_target_pairs={{0,16},{8,24},{16,32},{24,40},{32,48},{40,56},{48,0},{56,8},{1,17}... | collective-permute-start | bytes 3145736 | tf_op jit(solution)/shard_map/ppermute | solution.py:36
  44.7 37.6 %collective-permute-start.6 = (bf16[1024,512]{1,0:T(8,128)(2,1)}, bf16[1024,512]{1,0:T(8,128)(2,1)}, u32[]{:S(2)}, u32[]{:S(2)}) collective-permute-start(bf16[1024,512]{1,0:T(8,128)(2,1)} %bitcast.refs_0_), channel_id=1, source_target_pairs={{0,48},{8,56},{16,0},{24,8},{32,16},{40,24},{48,32},{56,40},{1,49}... | collective-permute-start | bytes 3145736 | tf_op jit(solution)/shard_map/ppermute | solution.py:36
  47.4 11.3 %all-to-all-start.1 = ((bf16[4,2,16,1024]{3,2,1,0:T(8,128)(2,1)}), bf16[4,2,16,1024]{3,2,1,0:T(8,128)(2,1)S(1)}, u32[]{:S(2)}, u32[]{:S(2)}) async-start(bf16[4,2,16,1024]{3,2,1,0:T(8,128)(2,1)} %shard_map.96), calls=%async_computation.1 | async-start | bytes 524288 | tf_op jit(solution)/shard_map/all_to_all | solution.py:27
  61.9 54.0 %all-to-all-start.2 = ((bf16[8,128,256]{2,1,0:T(8,128)(2,1)}), bf16[8,128,256]{2,1,0:T(8,128)(2,1)S(1)}, u32[]{:S(2)}, u32[]{:S(2)}) async-start(bf16[8,128,256]{2,1,0:T(8,128)(2,1)} %shard_map.97), calls=%async_computation.2 | async-start | bytes 1048576 | tf_op jit(solution)/shard_map/all_to_all | solution.py:207
  74.4 29.3 %collective-permute-start.1 = (bf16[1024,512]{1,0:T(8,128)(2,1)}, bf16[1024,512]{1,0:T(8,128)(2,1)}, u32[]{:S(2)}, u32[]{:S(2)}) collective-permute-start(bf16[1024,512]{1,0:T(8,128)(2,1)} %bitcast.refs_0_), channel_id=1, source_target_pairs={{0,8},{8,0},{16,24},{24,16},{32,40},{40,32},{48,56},{56,48},{1,9},... | collective-permute-start | bytes 3145736 | tf_op jit(solution)/shard_map/ppermute | solution.py:46
  77.4 16.7 %collective-permute-start.4 = (bf16[512,512]{1,0:T(8,128)(2,1)S(1)}, bf16[512,512]{1,0:T(8,128)(2,1)S(1)}, u32[]{:S(2)}, u32[]{:S(2)}) collective-permute-start(bf16[512,512]{1,0:T(8,128)(2,1)S(1)} %slice.8), channel_id=1, source_target_pairs={{0,16},{8,24},{16,32},{24,40},{32,48},{40,56},{48,0},{56,8},{1,17}... | collective-permute-start | bytes 1572872 | tf_op jit(solution)/shard_map/ppermute | solution.py:36
  83.4 17.2 %collective-permute-start.7 = (bf16[512,512]{1,0:T(8,128)(2,1)S(1)}, bf16[512,512]{1,0:T(8,128)(2,1)}, u32[]{:S(2)}, u32[]{:S(2)}) collective-permute-start(bf16[512,512]{1,0:T(8,128)(2,1)S(1)} %slice.9), channel_id=1, source_target_pairs={{0,48},{8,56},{16,0},{24,8},{32,16},{40,24},{48,32},{56,40},{1,49}... | collective-permute-start | bytes 1572872 | tf_op jit(solution)/shard_map/ppermute | solution.py:36
  85.4 19.4 %collective-permute-start.3 = (bf16[1024,512]{1,0:T(8,128)(2,1)}, bf16[1024,512]{1,0:T(8,128)(2,1)}, u32[]{:S(2)}, u32[]{:S(2)}) collective-permute-start(bf16[1024,512]{1,0:T(8,128)(2,1)} %collective-permute-done.2.refs_2_), channel_id=1, source_target_pairs={{0,8},{8,0},{16,24},{24,16},{32,40},{40,32},{48,56},{56,48},{1,9},... | collective-permute-start | bytes 3145736 | tf_op jit(solution)/shard_map/ppermute | solution.py:46
  87.5 17.3 %collective-permute-start.9 = (bf16[1024,512]{1,0:T(8,128)(2,1)}, bf16[1024,512]{1,0:T(8,128)(2,1)}, u32[]{:S(2)}, u32[]{:S(2)}) collective-permute-start(bf16[1024,512]{1,0:T(8,128)(2,1)} %collective-permute-done.6.refs_8_), channel_id=1, source_target_pairs={{0,8},{8,0},{16,24},{24,16},{32,40},{40,32},{48,56},{56,48},{1,9},... | collective-permute-start | bytes 3145736 | tf_op jit(solution)/shard_map/ppermute | solution.py:46
  94.1 12.0 %copy-start.4 = (bf16[512,512]{1,0:T(8,128)(2,1)}, bf16[512,512]{1,0:T(8,128)(2,1)S(1)}, u32[]{:S(2)}) copy-start(bf16[512,512]{1,0:T(8,128)(2,1)S(1)} %collective-permute-done.4.refs_4_) | copy-start | bytes 1572868
  94.1 9.6 %collective-permute-start.5 = (bf16[512,512]{1,0:T(8,128)(2,1)S(1)}, bf16[512,512]{1,0:T(8,128)(2,1)}, u32[]{:S(2)}, u32[]{:S(2)}) collective-permute-start(bf16[512,512]{1,0:T(8,128)(2,1)S(1)} %collective-permute-done.4.refs_4_), channel_id=1, source_target_pairs={{0,8},{8,0},{16,24},{24,16},{32,40},{40,32},{48,56},{56,48},{1,9},... | collective-permute-start | bytes 1572872 | tf_op jit(solution)/shard_map/ppermute | solution.py:46
  100.7 4.1 %collective-permute-start.8 = (bf16[512,512]{1,0:T(8,128)(2,1)}, bf16[512,512]{1,0:T(8,128)(2,1)}, u32[]{:S(2)}, u32[]{:S(2)}) collective-permute-start(bf16[512,512]{1,0:T(8,128)(2,1)} %collective-permute-done.7.refs_6_), channel_id=1, source_target_pairs={{0,8},{8,0},{16,24},{24,16},{32,40},{40,32},{48,56},{56,48},{1,9},... | collective-permute-start | bytes 1572872 | tf_op jit(solution)/shard_map/ppermute | solution.py:46
  103.8 12.1 %copy-start.1 = (bf16[1,160,512]{2,1,0:T(8,128)(2,1)S(1)}, bf16[1,160,512]{2,1,0:T(8,128)(2,1)}, u32[]{:S(2)}) copy-start(bf16[1,160,512]{2,1,0:T(8,128)(2,1)} %param.15) | copy-start | bytes 491524
  103.8 12.1 %copy-start.2 = (f32[160,128]{1,0:T(8,128)S(1)}, f32[160,128]{1,0:T(8,128)}, u32[]{:S(2)}) copy-start(f32[160,128]{1,0:T(8,128)} %bias_ref.1) | copy-start | bytes 245764
  115.9 0.9 copy-start
  118.9 11.4 %collective-permute-start.11 = (bf16[1,128,256]{2,1,0:T(8,128)(2,1)S(1)}, bf16[1,128,256]{2,1,0:T(8,128)(2,1)S(1)}, u32[]{:S(2)}, u32[]{:S(2)}) collective-permute-start(bf16[1,128,256]{2,1,0:T(8,128)(2,1)S(1)} %get-tuple-element.17.own), channel_id=1, source_target_pairs={{0,4},{1,5},{2,6},{3,7},{4,0},{5,1},{6,2},{7,3},{8,12},{9,13},{10,... | collective-permute-start | bytes 196616 | tf_op jit(solution)/shard_map/ppermute | solution.py:31
  127.8 6.2 %collective-permute-start.12 = (bf16[1,128,256]{2,1,0:T(8,128)(2,1)S(1)}, bf16[1,128,256]{2,1,0:T(8,128)(2,1)S(1)}, u32[]{:S(2)}, u32[]{:S(2)}) collective-permute-start(bf16[1,128,256]{2,1,0:T(8,128)(2,1)S(1)} %get-tuple-element.17.own), channel_id=1, source_target_pairs={{0,1},{1,0},{2,3},{3,2},{4,5},{5,4},{6,7},{7,6},{8,9},{9,8},{10,11... | collective-permute-start | bytes 196616 | tf_op jit(solution)/shard_map/ppermute | solution.py:31
  134.0 9.7 %collective-permute-start.13 = (bf16[2,128,256]{2,1,0:T(8,128)(2,1)S(1)}, bf16[2,128,256]{2,1,0:T(8,128)(2,1)S(1)}, u32[]{:S(2)}, u32[]{:S(2)}) collective-permute-start(bf16[2,128,256]{2,1,0:T(8,128)(2,1)S(1)} %pad_maximum_fusion.1), channel_id=1, source_target_pairs={{0,2},{1,3},{2,0},{3,1},{4,6},{5,7},{6,4},{7,5},{8,10},{9,11},{10,... | collective-permute-start | bytes 393224 | tf_op jit(solution)/shard_map/ppermute | solution.py:31
  135.9 7.7 %collective-permute-start.14 = (bf16[1,128,256]{2,1,0:T(8,128)(2,1)S(1)}, bf16[1,128,256]{2,1,0:T(8,128)(2,1)S(1)}, u32[]{:S(2)}, u32[]{:S(2)}) collective-permute-start(bf16[1,128,256]{2,1,0:T(8,128)(2,1)S(1)} %collective-permute-done.11.by4), channel_id=1, source_target_pairs={{0,1},{1,0},{2,3},{3,2},{4,5},{5,4},{6,7},{7,6},{8,9},{9,8},{10,11... | collective-permute-start | bytes 196616 | tf_op jit(solution)/shard_map/ppermute | solution.py:31
  143.6 6.9 %collective-permute-start.15 = (bf16[2,128,256]{2,1,0:T(8,128)(2,1)S(1)}, bf16[2,128,256]{2,1,0:T(8,128)(2,1)S(1)}, u32[]{:S(2)}, u32[]{:S(2)}) collective-permute-start(bf16[2,128,256]{2,1,0:T(8,128)(2,1)S(1)} %collective-permute-done.13.by2), channel_id=1, source_target_pairs={{0,1},{1,0},{2,3},{3,2},{4,5},{5,4},{6,7},{7,6},{8,9},{9,8},{10,11... | collective-permute-start | bytes 393224 | tf_op jit(solution)/shard_map/ppermute | solution.py:31
  165.2 14.5 %collective-permute-start.16 = (bf16[16,1024]{1,0:T(8,128)(2,1)S(1)}, bf16[16,1024]{1,0:T(8,128)(2,1)S(1)}, u32[]{:S(2)}, u32[]{:S(2)}) collective-permute-start(bf16[16,1024]{1,0:T(8,128)(2,1)S(1)} %get-tuple-element.23), channel_id=1, source_target_pairs={{0,256},{64,320},{128,384},{192,448},{256,0},{320,64},{384,128},{4... | collective-permute-start | bytes 98312 | tf_op jit(solution)/shard_map/ppermute | solution.py:22
Sparse Core Ops, SparseCore 0:
  22.0 84.1 all-gather.1

commit v9 on v8

--- a/solution.py
+++ b/solution.py
@@ -9,7 +9,7 @@
 X_SIZE = 4
 Y_SIZE = 4
 N_BLOCKS = 8
-DEPTH = 3
+LATE = (3, 5)
 BF16 = jnp.bfloat16
 F32 = jnp.float32
 VMEM = pl.BlockSpec(memory_space=pltpu.VMEM)
@@ -80,40 +80,41 @@
 
 
 def query_kernel(dp_ref, features, *refs):
-    blocks, (out, rows, columns, sems) = refs[:10], refs[10:]
+    blocks, (out, rows, columns, sems) = refs[:7], refs[7:]
     cut = columns.shape[1] // 2
+    blocks = iter(blocks)
     copies = []
     for slot in range(N_BLOCKS):
+        if slot in LATE:
+            continue
         group = [pltpu.make_async_copy(features.at[dp_ref[slot]], rows.at[slot], sems.at[0, slot])]
-        if slot // 2 == 2:
-            for part in range(2):
-                group.append(
-                    pltpu.make_async_copy(
-                        blocks[4 + 2 * part + slot % 2],
-                        columns.at[slot, pl.ds(part * cut, cut)],
-                        sems.at[1 + part, slot],
-                    )
-                )
-        else:
-            at = slot if slot < 4 else slot + 2
-            group.append(pltpu.make_async_copy(blocks[at], columns.at[slot], sems.at[1, slot]))
-        copies.append(group)
-    for group in copies[:DEPTH]:
+        copies.append((slot, group))
+        if slot // 2 != 2:
+            group.append(pltpu.make_async_copy(next(blocks), columns.at[slot], sems.at[1, slot]))
+            continue
+        for part in range(2):
+            at = pl.ds(part * cut, cut)
+            sem = sems.at[1 + part, slot]
+            group.append(pltpu.make_async_copy(next(blocks), columns.at[slot, at], sem))
+    for _, group in copies:
         for copy in group:
             copy.start()
     total = None
-    for slot, group in enumerate(copies):
+    for slot, group in copies:
         for copy in group:
             copy.wait()
-        if slot + DEPTH < N_BLOCKS:
-            for copy in copies[slot + DEPTH]:
-                copy.start()
         part = dot(rows[slot], columns[slot])
         total = part if total is None else total + part
-    out[...] = total.astype(BF16)
-
-
-def attention_kernel(query, arrived, bias_ref, cotangent, gate, gated, packed):
+    out[...] = total
+
+
+def attention_kernel(
+    partial, rows, late, upper, lower, arrived, bias_ref, cotangent, gate, gated, packed
+):
+    cut = upper.shape[0]
+    query = partial[...] + dot(rows[0], late[...])
+    query = query + dot(rows[1, :, :cut], upper[...]) + dot(rows[1, :, cut:], lower[...])
+    query = query.astype(BF16)
     pairs = jnp.sum(arrived[...].astype(F32), axis=0).astype(BF16)
     keys, values = pairs[:, :HEAD_SIZE], pairs[:, HEAD_SIZE:]
     scaling = HEAD_SIZE ** (-0.5)
@@ -210,14 +211,15 @@
     cut = w.shape[0] // 2
     before, behind = y_shift(w, 1), y_shift(w, -1)
     across = (y_shift(before[:cut], 1), y_shift(behind[cut:], -1))
-    query_weights = [v for b in (w, before, *across, behind) for v in (b, core_swap(b))]
-
+    edges = (w, core_swap(w), behind, core_swap(behind))
+    features, across, before = lax.optimization_barrier((features, across, before))
+    late = [core_swap(v) for v in (before, *across)]
     tokens, columns = hidden.shape[1], w_query.shape[2]
-    query = call(
+    partial = call(
         query_kernel,
-        jax.ShapeDtypeStruct((tokens, columns), BF16),
-        [SMEM] + [pl.BlockSpec(memory_space=pl.ANY)] * 11,
-        (dp_order, features, *query_weights),
+        jax.ShapeDtypeStruct((tokens, columns), F32),
+        [SMEM] + [pl.BlockSpec(memory_space=pl.ANY)] * 8,
+        (dp_order, features, *edges[:2], before, *across, *edges[2:]),
         [
             pltpu.VMEM(features.shape, BF16),
             pltpu.VMEM((N_BLOCKS, *w.shape), BF16),
@@ -225,16 +227,27 @@
         ],
         limit=60 << 20,
         cost=pl.CostEstimate(
-            flops=2 * tokens * columns * N_BLOCKS * w.shape[0],
+            flops=2 * tokens * columns * (N_BLOCKS - 2) * w.shape[0],
             bytes_accessed=2 * N_BLOCKS * (w.size + hidden.size),
             transcendentals=0,
         ),
     )
+    late_rows = jnp.stack(
+        [lax.dynamic_index_in_dim(features, dp_order[slot], 0, keepdims=False) for slot in LATE]
+    )
     gated_out, packed = call(
         attention_kernel,
         (jax.ShapeDtypeStruct((tokens, columns), BF16), jax.ShapeDtypeStruct((1, *block), BF16)),
-        [VMEM] * 5,
-        (query, arrived, score_bias, cotangent[0], gate_logit.reshape(1, 1)),
+        [VMEM] * 9,
+        (
+            partial,
+            late_rows,
+            *late,
+            arrived,
+            score_bias,
+            cotangent[0],
+            gate_logit.reshape(1, 1),
+        ),
     )
 
     by4, by1 = lax.optimization_barrier((t_swap(packed, 4), t_swap(packed, 1)))

time: 189 us -> 195 us (1.032)
  waiting for transfers between devices: 45.1 us -> 40.7 us
  between operations: 14.9 us -> 18.8 us
  local copies, waits for them, and re-layouts: 4.6 us -> 7.31 us
    all_to_all x1, waiting for transfers between devices: 3.07 us -> 0.01 us  [local(): arrived = lax.all_to_all(portions, 'tensor', 0, 0)]
  transfers between devices with their start and end apart: 21 -> 21, of which waited for: 13 -> 9; matrix products, arithmetic and copies ran while one was open for 1% -> 3% of each run, Pallas kernels for 6% -> 5%
where the time goes in v9:
time: 195 us; the launch traced here: 193 us
  starting transfers between devices  94.1 us (48%)
  waiting for transfers between devices  40.7 us (21%)
  between operations  18.8 us (10%)
  Pallas kernels  16.6 us (9%)
  blocking collectives  13.5 us (7%)
  local copies, waits for them, and re-layouts  7.31 us (4%)
    ppermute x5, starting transfers between devices, t_swap(): return lax.ppermute(a, 'tensor', [(t, t ^ k) for t in range(8)])  22 us
    ppermute x2, starting transfers between devices, z_swap(): lax.ppermute(a, 'section', [(s, (s + X_SIZE) % (2 * X_SIZE)) for s in ran...  20.8 us
    pallas_call x6, Pallas kernels, call(): pl.pallas_call(kernel, out_shape=outs, in_specs=in_specs, out_specs=jax.t...  16.6 us
    all_to_all x1, blocking collectives, x_exchange(): return lax.all_to_all(a, 'section', 0, 0, axis_index_groups=groups)  13.5 us
    ppermute x4, starting transfers between devices, y_shift(): return lax.ppermute(a, 'dp', pairs)  12.7 us
    all_to_all x1, starting transfers between devices, local(): arrived = lax.all_to_all(portions, 'tensor', 0, 0)  12.5 us
    ppermute x6, starting transfers between devices, core_swap(): return lax.ppermute(a, 'dp', [(d, d ^ 1) for d in range(2 * Y_SIZE)])  12.5 us
    ppermute x5, waiting for transfers between devices, t_swap(): return lax.ppermute(a, 'tensor', [(t, t ^ k) for t in range(8)])  10.4 us
  transfers between devices with their start and end apart: 21, of which 9 were waited for; matrix products, arithmetic and copies ran while one was open for 3% of the time, Pallas kernels for 5%

profile of v9, /device:TPU:24, one launch (start us, length us, event | category | flops | bytes accessed | tf_op | source)
XLA Modules:
  0.0 192.9 jit_solution(8945956007145598684)
XLA Ops:
  7.2 0.0 all-gather.2.cloned.1.call-start
  7.2 0.7 all-gather.2.cloned.1.call-update
  7.9 1.1 pad_maximum_fusion.1
  9.0 1.5 broadcast_in_dim.6
  10.5 9.3 %all-to-all-start = ((bf16[4,1024,256]{2,1,0:T(8,128)(2,1)}), bf16[4,1024,256]{2,1,0:T(8,128)(2,1)S(1)}, u32[]{:S(2)}, u32[]{:S(2)}) async-start(bf16[4,1024,256]{2,1,0:T(8,128)(2,1)} %broadcast_in_dim.6), calls=%async_computation | async-start | bytes 4194304 | tf_op jit(solution)/shard_map/all_to_all | solution.py:42
  19.8 11.2 %collective-permute-start = (bf16[16,1024]{1,0:T(8,128)(2,1)S(1)}, bf16[16,1024]{1,0:T(8,128)(2,1)S(1)}, u32[]{:S(2)}, u32[]{:S(2)}) collective-permute-start(bf16[16,1024]{1,0:T(8,128)(2,1)S(1)} %bitcast.14), channel_id=1, source_target_pairs={{0,256},{64,320},{128,384},{192,448},{256,0},{320,64},{384,128},{4... | collective-permute-start | bytes 98312 | tf_op jit(solution)/shard_map/ppermute | solution.py:22
  31.0 3.3 %collective-permute-done.other = bf16[16,1024]{1,0:T(8,128)(2,1)S(1)} collective-permute-done((bf16[16,1024]{1,0:T(8,128)(2,1)S(1)}, bf16[16,1024]{1,0:T(8,128)(2,1)S(1)}, u32[]{:S(2)}, u32[]{:S(2)}) %collective-permute-start) | collective-permute-done | bytes 32800 | tf_op jit(solution)/shard_map/ppermute | solution.py:22
  34.3 5.3 %all-to-all-done.near = bf16[4,1024,256]{2,1,0:T(8,128)(2,1)S(1)} async-done(((bf16[4,1024,256]{2,1,0:T(8,128)(2,1)}), bf16[4,1024,256]{2,1,0:T(8,128)(2,1)S(1)}, u32[]{:S(2)}, u32[]{:S(2)}) %all-to-all-start) | async-done | bytes 2097184 | tf_op jit(solution)/shard_map/all_to_all | solution.py:42
  39.6 1.9 collective-permute-start.10
  41.5 4.0 %collective-permute-start.1 = (bf16[1024,512]{1,0:T(8,128)(2,1)}, bf16[1024,512]{1,0:T(8,128)(2,1)}, u32[]{:S(2)}, u32[]{:S(2)}) collective-permute-start(bf16[1024,512]{1,0:T(8,128)(2,1)} %bitcast.refs_0_), channel_id=1, source_target_pairs={{0,16},{8,24},{16,32},{24,40},{32,48},{40,56},{48,0},{56,8},{1,17}... | collective-permute-start | bytes 3145736 | tf_op jit(solution)/shard_map/ppermute | solution.py:36
  45.5 1.9 collective-permute-start.3
  47.4 0.7 shard_map.96
  48.1 4.3 %all-to-all-start.1 = ((bf16[4,2,16,1024]{3,2,1,0:T(8,128)(2,1)}), bf16[4,2,16,1024]{3,2,1,0:T(8,128)(2,1)S(1)}, u32[]{:S(2)}, u32[]{:S(2)}) async-start(bf16[4,2,16,1024]{3,2,1,0:T(8,128)(2,1)} %shard_map.96), calls=%async_computation.1 | async-start | bytes 524288 | tf_op jit(solution)/shard_map/all_to_all | solution.py:27
  52.4 7.0 %all-to-all-done.1.images = bf16[4,2,16,1024]{3,2,1,0:T(8,128)(2,1)S(1)} async-done(((bf16[4,2,16,1024]{3,2,1,0:T(8,128)(2,1)}), bf16[4,2,16,1024]{3,2,1,0:T(8,128)(2,1)S(1)}, u32[]{:S(2)}, u32[]{:S(2)}) %all-to-all-start.1) | async-done | bytes 262176 | tf_op jit(solution)/shard_map/all_to_all | solution.py:27
  59.5 3.1 %shard_map.97 = bf16[8,128,256]{2,1,0:T(8,128)(2,1)} custom-call(s32[8]{0:T(128)S(1)} %iota_xor_fusion.head_ref, s32[1]{0:T(128)} %bitcast.6.half_ref, bf16[4,2,16,1024]{3,2,1,0:T(8,128)(2,1)S(1)} %all-to-all-done.1.images, bf16[4,1024,256]{2,1,0:T(8,128)(2,1)S(1)} %all-to-all-done.near, bf16[4,1024,256]{2,1,0:T(8,128)(2,1)} %collective-permute-done.10.far), custom_call_target="tpu_custom_call" | custom-call | tf_op jit(solution)/shard_map/pallas_call | solution.py:56
  62.6 12.5 %all-to-all-start.2 = ((bf16[8,128,256]{2,1,0:T(8,128)(2,1)}), bf16[8,128,256]{2,1,0:T(8,128)(2,1)S(1)}, u32[]{:S(2)}, u32[]{:S(2)}) async-start(bf16[8,128,256]{2,1,0:T(8,128)(2,1)} %shard_map.97), calls=%async_computation.2 | async-start | bytes 1048576 | tf_op jit(solution)/shard_map/all_to_all | solution.py:208
  75.2 1.1 slice.16
  76.2 4.8 %collective-permute-start.2 = (bf16[512,512]{1,0:T(8,128)(2,1)S(1)}, bf16[512,512]{1,0:T(8,128)(2,1)}, u32[]{:S(2)}, u32[]{:S(2)}) collective-permute-start(bf16[512,512]{1,0:T(8,128)(2,1)S(1)} %slice.16), channel_id=1, source_target_pairs={{0,16},{8,24},{16,32},{24,40},{32,48},{40,56},{48,0},{56,8},{1,17}... | collective-permute-start | bytes 1572872 | tf_op jit(solution)/shard_map/ppermute | solution.py:36
  81.1 1.1 slice.17
  82.2 1.9 collective-permute-start.4
  84.1 1.9 collective-permute-start.5
  86.0 2.4 %collective-permute-start.6 = (bf16[1024,512]{1,0:T(8,128)(2,1)}, bf16[1024,512]{1,0:T(8,128)(2,1)}, u32[]{:S(2)}, u32[]{:S(2)}) collective-permute-start(bf16[1024,512]{1,0:T(8,128)(2,1)} %collective-permute-done.3.refs_5_), channel_id=1, source_target_pairs={{0,8},{8,0},{16,24},{24,16},{32,40},{40,32},{48,56},{56,48},{1,9},... | collective-permute-start | bytes 3145736 | tf_op jit(solution)/shard_map/ppermute | solution.py:46
  88.4 2.5 %collective-permute-done.2.refs_3_ = bf16[512,512]{1,0:T(8,128)(2,1)} collective-permute-done((bf16[512,512]{1,0:T(8,128)(2,1)S(1)}, bf16[512,512]{1,0:T(8,128)(2,1)}, u32[]{:S(2)}, u32[]{:S(2)}) %collective-permute-start.2) | collective-permute-done | bytes 524320 | tf_op jit(solution)/shard_map/ppermute | solution.py:36
  91.0 6.5 %collective-permute-done.4.refs_4_ = bf16[512,512]{1,0:T(8,128)(2,1)} collective-permute-done((bf16[512,512]{1,0:T(8,128)(2,1)S(1)}, bf16[512,512]{1,0:T(8,128)(2,1)}, u32[]{:S(2)}, u32[]{:S(2)}) %collective-permute-start.4) | collective-permute-done | bytes 524320 | tf_op jit(solution)/shard_map/ppermute | solution.py:36
  97.5 1.9 collective-permute-start.7
  99.5 2.4 %collective-permute-start.8 = (bf16[512,512]{1,0:T(8,128)(2,1)}, bf16[512,512]{1,0:T(8,128)(2,1)}, u32[]{:S(2)}, u32[]{:S(2)}) collective-permute-start(bf16[512,512]{1,0:T(8,128)(2,1)} %collective-permute-done.2.refs_3_), channel_id=1, source_target_pairs={{0,8},{8,0},{16,24},{24,16},{32,40},{40,32},{48,56},{56,48},{1,9},... | collective-permute-start | bytes 1572872 | tf_op jit(solution)/shard_map/ppermute | solution.py:46
  101.9 1.9 collective-permute-start.9
  103.8 0.0 copy-start.4
  103.8 0.6 fusion
  109.0 5.4 %shard_map.95.partial = f32[160,512]{1,0:T(8,128)} custom-call(s32[8]{0:T(128)} %copy-done.4, bf16[8,160,1024]{2,1,0:T(8,128)(2,1)} %all-gather.2.cloned.1.call-done.features, bf16[1024,512]{1,0:T(8,128)(2,1)} %bitcast.refs_0_, bf16[1024,512]{1,0:T(8,128)(2,1)} %collective-permute-done.5.refs_1_, bf16[1024,512]{1,0:T(8,128)(2,1)} %collective-permute-done.1.refs_2_, ...), custom_call_target="tpu_custom_call" | custom-call | flops 1006632960 | bytes 11010048 | tf_op jit(solution)/shard_map/pallas_call | solution.py:56
  114.3 1.2 constant_dynamic-slice_fusion.1
  115.5 0.1 pad_maximum_fusion.rows
  115.6 1.0 copy-done
  116.6 0.9 copy-done.2
  117.5 4.3 %shard_map.98 = (bf16[160,512]{1,0:T(8,128)(2,1)}, bf16[1,128,256]{2,1,0:T(8,128)(2,1)S(1)}) custom-call(f32[160,512]{1,0:T(8,128)S(1)} %copy-done, bf16[2,160,1024]{2,1,0:T(8,128)(2,1)S(1)} %pad_maximum_fusion.rows, bf16[1024,512]{1,0:T(8,128)(2,1)} %collective-permute-done.7.late, bf16[512,512]{1,0:T(8,128)(2,1)} %collective-permute-done.8.upper, ...), custom_call_target="tpu_custom_call" | custom-call | tf_op jit(solution)/shard_map/pallas_call | solution.py:56
  121.8 7.5 %collective-permute-start.11 = (bf16[1,128,256]{2,1,0:T(8,128)(2,1)S(1)}, bf16[1,128,256]{2,1,0:T(8,128)(2,1)S(1)}, u32[]{:S(2)}, u32[]{:S(2)}) collective-permute-start(bf16[1,128,256]{2,1,0:T(8,128)(2,1)S(1)} %get-tuple-element.25.own), channel_id=1, source_target_pairs={{0,4},{1,5},{2,6},{3,7},{4,0},{5,1},{6,2},{7,3},{8,12},{9,13},{10,... | collective-permute-start | bytes 196616 | tf_op jit(solution)/shard_map/ppermute | solution.py:31
  129.3 3.4 %collective-permute-start.12 = (bf16[1,128,256]{2,1,0:T(8,128)(2,1)S(1)}, bf16[1,128,256]{2,1,0:T(8,128)(2,1)S(1)}, u32[]{:S(2)}, u32[]{:S(2)}) collective-permute-start(bf16[1,128,256]{2,1,0:T(8,128)(2,1)S(1)} %get-tuple-element.25.own), channel_id=1, source_target_pairs={{0,1},{1,0},{2,3},{3,2},{4,5},{5,4},{6,7},{7,6},{8,9},{9,8},{10,11... | collective-permute-start | bytes 196616 | tf_op jit(solution)/shard_map/ppermute | solution.py:31
  132.7 3.4 %collective-permute-done.11.by4 = bf16[1,128,256]{2,1,0:T(8,128)(2,1)S(1)} collective-permute-done((bf16[1,128,256]{2,1,0:T(8,128)(2,1)S(1)}, bf16[1,128,256]{2,1,0:T(8,128)(2,1)S(1)}, u32[]{:S(2)}, u32[]{:S(2)}) %collective-permute-start.11) | collective-permute-done | bytes 65568 | tf_op jit(solution)/shard_map/ppermute | solution.py:31
  136.1 4.0 %collective-permute-start.13 = (bf16[2,128,256]{2,1,0:T(8,128)(2,1)S(1)}, bf16[2,128,256]{2,1,0:T(8,128)(2,1)S(1)}, u32[]{:S(2)}, u32[]{:S(2)}) collective-permute-start(bf16[2,128,256]{2,1,0:T(8,128)(2,1)S(1)} %pad_maximum_fusion.2), channel_id=1, source_target_pairs={{0,2},{1,3},{2,0},{3,1},{4,6},{5,7},{6,4},{7,5},{8,10},{9,11},{10,... | collective-permute-start | bytes 393224 | tf_op jit(solution)/shard_map/ppermute | solution.py:31
  140.2 4.1 %collective-permute-start.14 = (bf16[1,128,256]{2,1,0:T(8,128)(2,1)S(1)}, bf16[1,128,256]{2,1,0:T(8,128)(2,1)S(1)}, u32[]{:S(2)}, u32[]{:S(2)}) collective-permute-start(bf16[1,128,256]{2,1,0:T(8,128)(2,1)S(1)} %collective-permute-done.11.by4), channel_id=1, source_target_pairs={{0,1},{1,0},{2,3},{3,2},{4,5},{5,4},{6,7},{7,6},{8,9},{9,8},{10,11... | collective-permute-start | bytes 196616 | tf_op jit(solution)/shard_map/ppermute | solution.py:31
  144.2 3.1 %collective-permute-done.14.by5 = bf16[1,128,256]{2,1,0:T(8,128)(2,1)S(1)} collective-permute-done((bf16[1,128,256]{2,1,0:T(8,128)(2,1)S(1)}, bf16[1,128,256]{2,1,0:T(8,128)(2,1)S(1)}, u32[]{:S(2)}, u32[]{:S(2)}) %collective-permute-start.14) | collective-permute-done | bytes 65568 | tf_op jit(solution)/shard_map/ppermute | solution.py:31
  147.4 3.0 %collective-permute-start.15 = (bf16[2,128,256]{2,1,0:T(8,128)(2,1)S(1)}, bf16[2,128,256]{2,1,0:T(8,128)(2,1)S(1)}, u32[]{:S(2)}, u32[]{:S(2)}) collective-permute-start(bf16[2,128,256]{2,1,0:T(8,128)(2,1)S(1)} %collective-permute-done.13.by2), channel_id=1, source_target_pairs={{0,1},{1,0},{2,3},{3,2},{4,5},{5,4},{6,7},{7,6},{8,9},{9,8},{10,11... | collective-permute-start | bytes 393224 | tf_op jit(solution)/shard_map/ppermute | solution.py:31
  150.4 3.8 %collective-permute-done.15.by3 = bf16[2,128,256]{2,1,0:T(8,128)(2,1)S(1)} collective-permute-done((bf16[2,128,256]{2,1,0:T(8,128)(2,1)S(1)}, bf16[2,128,256]{2,1,0:T(8,128)(2,1)S(1)}, u32[]{:S(2)}, u32[]{:S(2)}) %collective-permute-start.15) | collective-permute-done | bytes 131104 | tf_op jit(solution)/shard_map/ppermute | solution.py:31
  154.2 3.1 %shard_map.99 = bf16[4,2,16,1024]{3,2,1,0:T(8,128)(2,1)S(1)} custom-call(s32[8]{0:T(128)S(1)} %shift-right-arithmetic_or_fusion.place_ref, s32[1]{0:T(128)} %bitcast.6.half_ref, bf16[1,128,256]{2,1,0:T(8,128)(2,1)S(1)} %get-tuple-element.25.own, bf16[1,128,256]{2,1,0:T(8,128)(2,1)S(1)} %collective-permute-done.11.by4, ...), custom_call_target="tpu_custom_call" | custom-call | tf_op jit(solution)/shard_map/pallas_call | solution.py:56
  157.3 13.5 %all_to_all.20.arrived = bf16[4,2,16,1024]{3,2,1,0:T(8,128)(2,1)S(1)} all-to-all(bf16[4,2,16,1024]{3,2,1,0:T(8,128)(2,1)S(1)} %shard_map.99), channel_id=1, replica_groups={{0,64,128,192},{256,320,384,448},{1,65,129,193},{257,321,385,449},{2,66..., dimensions={0} | all-to-all | bytes 524288 | tf_op jit(solution)/shard_map/all_to_all | solution.py:27
  170.9 9.5 %collective-permute-start.16 = (bf16[16,1024]{1,0:T(8,128)(2,1)S(1)}, bf16[16,1024]{1,0:T(8,128)(2,1)S(1)}, u32[]{:S(2)}, u32[]{:S(2)}) collective-permute-start(bf16[16,1024]{1,0:T(8,128)(2,1)S(1)} %get-tuple-element.31), channel_id=1, source_target_pairs={{0,256},{64,320},{128,384},{192,448},{256,0},{320,64},{384,128},{4... | collective-permute-start | bytes 98312 | tf_op jit(solution)/shard_map/ppermute | solution.py:22
  180.4 5.0 %collective-permute-done.16 = bf16[16,1024]{1,0:T(8,128)(2,1)S(1)} collective-permute-done((bf16[16,1024]{1,0:T(8,128)(2,1)S(1)}, bf16[16,1024]{1,0:T(8,128)(2,1)S(1)}, u32[]{:S(2)}, u32[]{:S(2)}) %collective-permute-start.16) | collective-permute-done | bytes 32800 | tf_op jit(solution)/shard_map/ppermute | solution.py:22
  185.4 0.6 add_bitcast_fusion
  (24 shorter events, 0.1 us)
Async XLA Ops:
  7.2 90.4 %all-gather.2.cloned.1.call-start = ((), (), s32[]{:S(2)}) async-start(), calls=%async_computation.4 | async-start | bytes 2949120 | tf_op jit(solution)/shard_map/all_gather | solution.py:185
  10.5 9.3 %copy-start.3 = (bf16[1,16,1024]{2,1,0:T(8,128)(2,1)S(1)}, bf16[1,16,1024]{2,1,0:T(8,128)(2,1)}, u32[]{:S(2)}) copy-start(bf16[1,16,1024]{2,1,0:T(8,128)(2,1)} %param.12) | copy-start | bytes 98308
  10.5 29.1 %all-to-all-start = ((bf16[4,1024,256]{2,1,0:T(8,128)(2,1)}), bf16[4,1024,256]{2,1,0:T(8,128)(2,1)S(1)}, u32[]{:S(2)}, u32[]{:S(2)}) async-start(bf16[4,1024,256]{2,1,0:T(8,128)(2,1)} %broadcast_in_dim.6), calls=%async_computation | async-start | bytes 4194304 | tf_op jit(solution)/shard_map/all_to_all | solution.py:42
  19.8 14.5 %collective-permute-start = (bf16[16,1024]{1,0:T(8,128)(2,1)S(1)}, bf16[16,1024]{1,0:T(8,128)(2,1)S(1)}, u32[]{:S(2)}, u32[]{:S(2)}) collective-permute-start(bf16[16,1024]{1,0:T(8,128)(2,1)S(1)} %bitcast.14), channel_id=1, source_target_pairs={{0,256},{64,320},{128,384},{192,448},{256,0},{320,64},{384,128},{4... | collective-permute-start | bytes 98312 | tf_op jit(solution)/shard_map/ppermute | solution.py:22
  39.6 19.9 %collective-permute-start.10 = (bf16[4,1024,256]{2,1,0:T(8,128)(2,1)S(1)}, bf16[4,1024,256]{2,1,0:T(8,128)(2,1)}, u32[]{:S(2)}, u32[]{:S(2)}) collective-permute-start(bf16[4,1024,256]{2,1,0:T(8,128)(2,1)S(1)} %all-to-all-done.near), channel_id=1, source_target_pairs={{0,8},{8,0},{16,24},{24,16},{32,40},{40,32},{48,56},{56,48},{1,9},... | collective-permute-start | bytes 6291464 | tf_op jit(solution)/shard_map/ppermute | solution.py:46
  41.5 33.7 %collective-permute-start.1 = (bf16[1024,512]{1,0:T(8,128)(2,1)}, bf16[1024,512]{1,0:T(8,128)(2,1)}, u32[]{:S(2)}, u32[]{:S(2)}) collective-permute-start(bf16[1024,512]{1,0:T(8,128)(2,1)} %bitcast.refs_0_), channel_id=1, source_target_pairs={{0,16},{8,24},{16,32},{24,40},{32,48},{40,56},{48,0},{56,8},{1,17}... | collective-permute-start | bytes 3145736 | tf_op jit(solution)/shard_map/ppermute | solution.py:36
  45.5 35.6 %collective-permute-start.3 = (bf16[1024,512]{1,0:T(8,128)(2,1)}, bf16[1024,512]{1,0:T(8,128)(2,1)}, u32[]{:S(2)}, u32[]{:S(2)}) collective-permute-start(bf16[1024,512]{1,0:T(8,128)(2,1)} %bitcast.refs_0_), channel_id=1, source_target_pairs={{0,48},{8,56},{16,0},{24,8},{32,16},{40,24},{48,32},{56,40},{1,49}... | collective-permute-start | bytes 3145736 | tf_op jit(solution)/shard_map/ppermute | solution.py:36
  48.1 11.3 %all-to-all-start.1 = ((bf16[4,2,16,1024]{3,2,1,0:T(8,128)(2,1)}), bf16[4,2,16,1024]{3,2,1,0:T(8,128)(2,1)S(1)}, u32[]{:S(2)}, u32[]{:S(2)}) async-start(bf16[4,2,16,1024]{3,2,1,0:T(8,128)(2,1)} %shard_map.96), calls=%async_computation.1 | async-start | bytes 524288 | tf_op jit(solution)/shard_map/all_to_all | solution.py:27
  62.6 53.0 %all-to-all-start.2 = ((bf16[8,128,256]{2,1,0:T(8,128)(2,1)}), bf16[8,128,256]{2,1,0:T(8,128)(2,1)S(1)}, u32[]{:S(2)}, u32[]{:S(2)}) async-start(bf16[8,128,256]{2,1,0:T(8,128)(2,1)} %shard_map.97), calls=%async_computation.2 | async-start | bytes 1048576 | tf_op jit(solution)/shard_map/all_to_all | solution.py:208
  76.2 14.8 %collective-permute-start.2 = (bf16[512,512]{1,0:T(8,128)(2,1)S(1)}, bf16[512,512]{1,0:T(8,128)(2,1)}, u32[]{:S(2)}, u32[]{:S(2)}) collective-permute-start(bf16[512,512]{1,0:T(8,128)(2,1)S(1)} %slice.16), channel_id=1, source_target_pairs={{0,16},{8,24},{16,32},{24,40},{32,48},{40,56},{48,0},{56,8},{1,17}... | collective-permute-start | bytes 1572872 | tf_op jit(solution)/shard_map/ppermute | solution.py:36
  82.2 15.4 %collective-permute-start.4 = (bf16[512,512]{1,0:T(8,128)(2,1)S(1)}, bf16[512,512]{1,0:T(8,128)(2,1)}, u32[]{:S(2)}, u32[]{:S(2)}) collective-permute-start(bf16[512,512]{1,0:T(8,128)(2,1)S(1)} %slice.17), channel_id=1, source_target_pairs={{0,48},{8,56},{16,0},{24,8},{32,16},{40,24},{48,32},{56,40},{1,49}... | collective-permute-start | bytes 1572872 | tf_op jit(solution)/shard_map/ppermute | solution.py:36
  84.1 24.8 %collective-permute-start.5 = (bf16[1024,512]{1,0:T(8,128)(2,1)}, bf16[1024,512]{1,0:T(8,128)(2,1)}, u32[]{:S(2)}, u32[]{:S(2)}) collective-permute-start(bf16[1024,512]{1,0:T(8,128)(2,1)} %bitcast.refs_0_), channel_id=1, source_target_pairs={{0,8},{8,0},{16,24},{24,16},{32,40},{40,32},{48,56},{56,48},{1,9},... | collective-permute-start | bytes 3145736 | tf_op jit(solution)/shard_map/ppermute | solution.py:46
  86.0 22.9 %collective-permute-start.6 = (bf16[1024,512]{1,0:T(8,128)(2,1)}, bf16[1024,512]{1,0:T(8,128)(2,1)}, u32[]{:S(2)}, u32[]{:S(2)}) collective-permute-start(bf16[1024,512]{1,0:T(8,128)(2,1)} %collective-permute-done.3.refs_5_), channel_id=1, source_target_pairs={{0,8},{8,0},{16,24},{24,16},{32,40},{40,32},{48,56},{56,48},{1,9},... | collective-permute-start | bytes 3145736 | tf_op jit(solution)/shard_map/ppermute | solution.py:46
  97.5 18.1 %collective-permute-start.7 = (bf16[1024,512]{1,0:T(8,128)(2,1)}, bf16[1024,512]{1,0:T(8,128)(2,1)}, u32[]{:S(2)}, u32[]{:S(2)}) collective-permute-start(bf16[1024,512]{1,0:T(8,128)(2,1)} %collective-permute-done.1.refs_2_), channel_id=1, source_target_pairs={{0,8},{8,0},{16,24},{24,16},{32,40},{40,32},{48,56},{56,48},{1,9},... | collective-permute-start | bytes 3145736 | tf_op jit(solution)/shard_map/ppermute | solution.py:46
  99.5 16.1 %collective-permute-start.8 = (bf16[512,512]{1,0:T(8,128)(2,1)}, bf16[512,512]{1,0:T(8,128)(2,1)}, u32[]{:S(2)}, u32[]{:S(2)}) collective-permute-start(bf16[512,512]{1,0:T(8,128)(2,1)} %collective-permute-done.2.refs_3_), channel_id=1, source_target_pairs={{0,8},{8,0},{16,24},{24,16},{32,40},{40,32},{48,56},{56,48},{1,9},... | collective-permute-start | bytes 1572872 | tf_op jit(solution)/shard_map/ppermute | solution.py:46
  101.9 13.7 %collective-permute-start.9 = (bf16[512,512]{1,0:T(8,128)(2,1)}, bf16[512,512]{1,0:T(8,128)(2,1)}, u32[]{:S(2)}, u32[]{:S(2)}) collective-permute-start(bf16[512,512]{1,0:T(8,128)(2,1)} %collective-permute-done.4.refs_4_), channel_id=1, source_target_pairs={{0,8},{8,0},{16,24},{24,16},{32,40},{40,32},{48,56},{56,48},{1,9},... | collective-permute-start | bytes 1572872 | tf_op jit(solution)/shard_map/ppermute | solution.py:46
  103.8 5.1 %copy-start.4 = (s32[8]{0:T(128)}, s32[8]{0:T(128)S(1)}, u32[]{:S(2)}) copy-start(s32[8]{0:T(128)S(1)} %and_or_fusion.dp_ref) | copy-start | bytes 100
  114.3 1.3 copy-start.1
  115.6 1.0 copy-start
  116.6 0.9 copy-start.2
  121.8 14.3 %collective-permute-start.11 = (bf16[1,128,256]{2,1,0:T(8,128)(2,1)S(1)}, bf16[1,128,256]{2,1,0:T(8,128)(2,1)S(1)}, u32[]{:S(2)}, u32[]{:S(2)}) collective-permute-start(bf16[1,128,256]{2,1,0:T(8,128)(2,1)S(1)} %get-tuple-element.25.own), channel_id=1, source_target_pairs={{0,4},{1,5},{2,6},{3,7},{4,0},{5,1},{6,2},{7,3},{8,12},{9,13},{10,... | collective-permute-start | bytes 196616 | tf_op jit(solution)/shard_map/ppermute | solution.py:31
  129.3 6.8 %collective-permute-start.12 = (bf16[1,128,256]{2,1,0:T(8,128)(2,1)S(1)}, bf16[1,128,256]{2,1,0:T(8,128)(2,1)S(1)}, u32[]{:S(2)}, u32[]{:S(2)}) collective-permute-start(bf16[1,128,256]{2,1,0:T(8,128)(2,1)S(1)} %get-tuple-element.25.own), channel_id=1, source_target_pairs={{0,1},{1,0},{2,3},{3,2},{4,5},{5,4},{6,7},{7,6},{8,9},{9,8},{10,11... | collective-permute-start | bytes 196616 | tf_op jit(solution)/shard_map/ppermute | solution.py:31
  136.1 11.3 %collective-permute-start.13 = (bf16[2,128,256]{2,1,0:T(8,128)(2,1)S(1)}, bf16[2,128,256]{2,1,0:T(8,128)(2,1)S(1)}, u32[]{:S(2)}, u32[]{:S(2)}) collective-permute-start(bf16[2,128,256]{2,1,0:T(8,128)(2,1)S(1)} %pad_maximum_fusion.2), channel_id=1, source_target_pairs={{0,2},{1,3},{2,0},{3,1},{4,6},{5,7},{6,4},{7,5},{8,10},{9,11},{10,... | collective-permute-start | bytes 393224 | tf_op jit(solution)/shard_map/ppermute | solution.py:31
  140.2 7.2 %collective-permute-start.14 = (bf16[1,128,256]{2,1,0:T(8,128)(2,1)S(1)}, bf16[1,128,256]{2,1,0:T(8,128)(2,1)S(1)}, u32[]{:S(2)}, u32[]{:S(2)}) collective-permute-start(bf16[1,128,256]{2,1,0:T(8,128)(2,1)S(1)} %collective-permute-done.11.by4), channel_id=1, source_target_pairs={{0,1},{1,0},{2,3},{3,2},{4,5},{5,4},{6,7},{7,6},{8,9},{9,8},{10,11... | collective-permute-start | bytes 196616 | tf_op jit(solution)/shard_map/ppermute | solution.py:31
  147.4 6.9 %collective-permute-start.15 = (bf16[2,128,256]{2,1,0:T(8,128)(2,1)S(1)}, bf16[2,128,256]{2,1,0:T(8,128)(2,1)S(1)}, u32[]{:S(2)}, u32[]{:S(2)}) collective-permute-start(bf16[2,128,256]{2,1,0:T(8,128)(2,1)S(1)} %collective-permute-done.13.by2), channel_id=1, source_target_pairs={{0,1},{1,0},{2,3},{3,2},{4,5},{5,4},{6,7},{7,6},{8,9},{9,8},{10,11... | collective-permute-start | bytes 393224 | tf_op jit(solution)/shard_map/ppermute | solution.py:31
  170.9 14.5 %collective-permute-start.16 = (bf16[16,1024]{1,0:T(8,128)(2,1)S(1)}, bf16[16,1024]{1,0:T(8,128)(2,1)S(1)}, u32[]{:S(2)}, u32[]{:S(2)}) collective-permute-start(bf16[16,1024]{1,0:T(8,128)(2,1)S(1)} %get-tuple-element.31), channel_id=1, source_target_pairs={{0,256},{64,320},{128,384},{192,448},{256,0},{320,64},{384,128},{4... | collective-permute-start | bytes 98312 | tf_op jit(solution)/shard_map/ppermute | solution.py:22
Sparse Core Ops, SparseCore 0:
  10.1 82.7 all-gather.1

commit v10 on v8

--- a/solution.py
+++ b/solution.py
@@ -140,14 +140,38 @@
     )
 
 
-def image_kernel(place_ref, half_ref, own, by4, by2, by1, by5, by3, near, far, out, buffer):
-    for at, part in ((0, own), (1, by4), (2, by2), (4, by1), (5, by5), (6, by3)):
-        buffer[at : at + part.shape[0]] = part[...]
+def head_products(y_ref, parts, even, odd):
     total = None
-    for slot in range(N_BLOCKS):
-        weights = (near, far)[slot % 2][slot // 2]
-        part = dot(buffer[place_ref[slot]], weights, BY_COLUMNS)
-        total = part if total is None else total + part
+    for part, distance in parts:
+        weights = (even, odd)[distance & 1][y_ref[distance]]
+        product = dot(part, weights, BY_COLUMNS)
+        total = product if total is None else total + product
+    return total
+
+
+def early_image_kernel(y_ref, flip_ref, own, by4, by2, by1, by5, near, far, out):
+    parts = [(own[0], 0), (by4[0], 4), (by2[0], 2), (by2[1], 6), (by1[0], 1), (by5[0], 5)]
+
+    @pl.when(flip_ref[0] == 0)
+    def _():
+        out[...] = head_products(y_ref, parts, near, far)
+
+    @pl.when(flip_ref[0] != 0)
+    def _():
+        out[...] = head_products(y_ref, parts, far, near)
+
+
+def late_image_kernel(y_ref, flip_ref, half_ref, early, by3, near, far, out, total):
+    parts = [(by3[0], 3), (by3[1], 7)]
+
+    @pl.when(flip_ref[0] == 0)
+    def _():
+        total[...] = early[...] + head_products(y_ref, parts, near, far)
+
+    @pl.when(flip_ref[0] != 0)
+    def _():
+        total[...] = early[...] + head_products(y_ref, parts, far, near)
+
     rows = out.shape[2]
     for z in range(2):
         for x in range(X_SIZE):
@@ -178,8 +202,9 @@
     slots = jnp.arange(N_BLOCKS, dtype=jnp.int32)
     dp_order = ((((dp >> 1) - (slots >> 1)) & (Y_SIZE - 1)) << 1) | ((dp ^ slots) & 1)
     head_order = slots ^ (dp & 1)
-    apart = lax.axis_index("tensor") ^ head_order
-    place = ((apart & 1) << 2) | (apart & 2) | (apart >> 2)
+    tensor = lax.axis_index("tensor")
+    head_y = (tensor ^ slots) >> 1
+    flip = ((tensor ^ dp) & 1)[None]
 
     features = lax.all_gather(hidden[0], "tensor", axis=0)
 
@@ -241,12 +266,23 @@
     both = jnp.concatenate([packed, by4])
     by2, by5 = lax.optimization_barrier((t_swap(both, 2), t_swap(by4, 1)))
     by3 = t_swap(by2, 1)
+    early = call(
+        early_image_kernel,
+        jax.ShapeDtypeStruct((image_count, width), F32),
+        [SMEM] * 2 + [VMEM] * 7,
+        (head_y, flip, packed, by4, by2, by1, by5, near_pairs, far_pairs),
+        cost=pl.CostEstimate(
+            flops=12 * packed.size * width,
+            bytes_accessed=12 * packed.size + 4 * near_pairs.size + 4 * image_count * width,
+            transcendentals=0,
+        ),
+    )
     portion = call(
-        image_kernel,
+        late_image_kernel,
         jax.ShapeDtypeStruct((X_SIZE, 2, rows, width), BF16),
-        [SMEM] * 2 + [VMEM] * 8,
-        (place, half, packed, by4, by2, by1, by5, by3, near_pairs, far_pairs),
-        [pltpu.VMEM((N_BLOCKS, *block), BF16)],
+        [SMEM] * 3 + [VMEM] * 4,
+        (head_y, flip, half, early, by3, near_pairs, far_pairs),
+        [pltpu.VMEM((image_count, width), F32)],
     )
     keep, send = call(
         section_kernel,

time: 189 us -> 188 us (level)
  waiting for transfers between devices: 45.1 us -> 42.3 us
    ppermute x5, waiting for transfers between devices: 10.5 us -> 7.72 us  [t_swap(): return lax.ppermute(a, 'tensor', [(t, t ^ k) for t in range(8)])]
    pallas_call x6 -> x7, Pallas kernels: 15.7 us -> 17.5 us  [call(): pl.pallas_call(kernel, out_shape=outs, in_specs=in_specs, out_specs=jax.t...]
  transfers between devices with their start and end apart: 21 -> 21, of which waited for: 13 -> 13; matrix products, arithmetic and copies ran while one was open for 1% -> 1% of each run, Pallas kernels for 6% -> 7%
where the time goes in v10:
time: 188 us; the launch traced here: 186 us
  starting transfers between devices  93 us (49%)
  waiting for transfers between devices  42.3 us (22%)
  Pallas kernels  17.5 us (9%)
  between operations  14.9 us (8%)
  blocking collectives  11.7 us (6%)
  local copies, waits for them, and re-layouts  4.6 us (2%)
  other arithmetic  2.27 us (1%)
    ppermute x2, starting transfers between devices, z_swap(): lax.ppermute(a, 'section', [(s, (s + X_SIZE) % (2 * X_SIZE)) for s in ran...  21.2 us
    ppermute x5, starting transfers between devices, t_swap(): return lax.ppermute(a, 'tensor', [(t, t ^ k) for t in range(8)])  21 us
    pallas_call x7, Pallas kernels, call(): pl.pallas_call(kernel, out_shape=outs, in_specs=in_specs, out_specs=jax.t...  17.5 us
    ppermute x4, starting transfers between devices, y_shift(): return lax.ppermute(a, 'dp', pairs)  12.7 us
    all_to_all x1, starting transfers between devices, local(): arrived = lax.all_to_all(portions, 'tensor', 0, 0)  12.5 us
    ppermute x6, starting transfers between devices, core_swap(): return lax.ppermute(a, 'dp', [(d, d ^ 1) for d in range(2 * Y_SIZE)])  12 us
    all_to_all x1, blocking collectives, x_exchange(): return lax.all_to_all(a, 'section', 0, 0, axis_index_groups=groups)  11.7 us
    all_to_all x1, starting transfers between devices, y_gather(): return lax.all_to_all(copies, 'dp', 0, 0, axis_index_groups=groups)  9.31 us
  transfers between devices with their start and end apart: 21, of which 13 were waited for; matrix products, arithmetic and copies ran while one was open for 1% of the time, Pallas kernels for 7%

profile of v10, /device:TPU:24, one launch (start us, length us, event | category | flops | bytes accessed | tf_op | source)
XLA Modules:
  0.0 186.3 jit_solution(7146316781910190703)
XLA Ops:
  7.2 1.1 pad_maximum_fusion
  8.3 1.5 broadcast_in_dim.16
  9.8 9.3 %all-to-all-start = ((bf16[4,1024,256]{2,1,0:T(8,128)(2,1)}), bf16[4,1024,256]{2,1,0:T(8,128)(2,1)S(1)}, u32[]{:S(2)}, u32[]{:S(2)}) async-start(bf16[4,1024,256]{2,1,0:T(8,128)(2,1)} %broadcast_in_dim.16), calls=%async_computation | async-start | bytes 4194304 | tf_op jit(solution)/shard_map/all_to_all | solution.py:42
  19.1 0.7 all-gather.2.cloned.1.call-update
  19.8 11.2 %collective-permute-start = (bf16[16,1024]{1,0:T(8,128)(2,1)S(1)}, bf16[16,1024]{1,0:T(8,128)(2,1)S(1)}, u32[]{:S(2)}, u32[]{:S(2)}) collective-permute-start(bf16[16,1024]{1,0:T(8,128)(2,1)S(1)} %bitcast.13), channel_id=1, source_target_pairs={{0,256},{64,320},{128,384},{192,448},{256,0},{320,64},{384,128},{4... | collective-permute-start | bytes 98312 | tf_op jit(solution)/shard_map/ppermute | solution.py:22
  31.0 3.3 %collective-permute-done.other = bf16[16,1024]{1,0:T(8,128)(2,1)S(1)} collective-permute-done((bf16[16,1024]{1,0:T(8,128)(2,1)S(1)}, bf16[16,1024]{1,0:T(8,128)(2,1)S(1)}, u32[]{:S(2)}, u32[]{:S(2)}) %collective-permute-start) | collective-permute-done | bytes 32800 | tf_op jit(solution)/shard_map/ppermute | solution.py:22
  34.3 4.5 %all-to-all-done.near = bf16[4,1024,256]{2,1,0:T(8,128)(2,1)S(1)} async-done(((bf16[4,1024,256]{2,1,0:T(8,128)(2,1)}), bf16[4,1024,256]{2,1,0:T(8,128)(2,1)S(1)}, u32[]{:S(2)}, u32[]{:S(2)}) %all-to-all-start) | async-done | bytes 2097184 | tf_op jit(solution)/shard_map/all_to_all | solution.py:42
  38.8 1.9 %collective-permute-start.10 = (bf16[4,1024,256]{2,1,0:T(8,128)(2,1)S(1)}, bf16[4,1024,256]{2,1,0:T(8,128)(2,1)}, u32[]{:S(2)}, u32[]{:S(2)}) collective-permute-start(bf16[4,1024,256]{2,1,0:T(8,128)(2,1)S(1)} %all-to-all-done.near), channel_id=1, source_target_pairs={{0,8},{8,0},{16,24},{24,16},{32,40},{40,32},{48,56},{56,48},{1,9},... | collective-permute-start | bytes 6291464 | tf_op jit(solution)/shard_map/ppermute | solution.py:46
  40.8 4.0 %collective-permute-start.2 = (bf16[1024,512]{1,0:T(8,128)(2,1)}, bf16[1024,512]{1,0:T(8,128)(2,1)}, u32[]{:S(2)}, u32[]{:S(2)}) collective-permute-start(bf16[1024,512]{1,0:T(8,128)(2,1)} %bitcast.refs_0_), channel_id=1, source_target_pairs={{0,16},{8,24},{16,32},{24,40},{32,48},{40,56},{48,0},{56,8},{1,17}... | collective-permute-start | bytes 3145736 | tf_op jit(solution)/shard_map/ppermute | solution.py:36
  44.7 1.9 %collective-permute-start.6 = (bf16[1024,512]{1,0:T(8,128)(2,1)}, bf16[1024,512]{1,0:T(8,128)(2,1)}, u32[]{:S(2)}, u32[]{:S(2)}) collective-permute-start(bf16[1024,512]{1,0:T(8,128)(2,1)} %bitcast.refs_0_), channel_id=1, source_target_pairs={{0,48},{8,56},{16,0},{24,8},{32,16},{40,24},{48,32},{56,40},{1,49}... | collective-permute-start | bytes 3145736 | tf_op jit(solution)/shard_map/ppermute | solution.py:36
  46.7 0.7 shard_map.96
  47.4 4.3 %all-to-all-start.1 = ((bf16[4,2,16,1024]{3,2,1,0:T(8,128)(2,1)}), bf16[4,2,16,1024]{3,2,1,0:T(8,128)(2,1)S(1)}, u32[]{:S(2)}, u32[]{:S(2)}) async-start(bf16[4,2,16,1024]{3,2,1,0:T(8,128)(2,1)} %shard_map.96), calls=%async_computation.1 | async-start | bytes 524288 | tf_op jit(solution)/shard_map/all_to_all | solution.py:27
  51.7 7.0 %all-to-all-done.1.images = bf16[4,2,16,1024]{3,2,1,0:T(8,128)(2,1)S(1)} async-done(((bf16[4,2,16,1024]{3,2,1,0:T(8,128)(2,1)}), bf16[4,2,16,1024]{3,2,1,0:T(8,128)(2,1)S(1)}, u32[]{:S(2)}, u32[]{:S(2)}) %all-to-all-start.1) | async-done | bytes 262176 | tf_op jit(solution)/shard_map/all_to_all | solution.py:27
  58.7 3.2 %shard_map.97 = bf16[8,128,256]{2,1,0:T(8,128)(2,1)} custom-call(s32[8]{0:T(128)S(1)} %iota_xor_fusion.head_ref, s32[1]{0:T(128)} %bitcast.4.half_ref, bf16[4,2,16,1024]{3,2,1,0:T(8,128)(2,1)S(1)} %all-to-all-done.1.images, bf16[4,1024,256]{2,1,0:T(8,128)(2,1)S(1)} %all-to-all-done.near, bf16[4,1024,256]{2,1,0:T(8,128)(2,1)} %collective-permute-done.10.far), custom_call_target="tpu_custom_call" | custom-call | tf_op jit(solution)/shard_map/pallas_call | solution.py:56
  61.9 12.5 %all-to-all-start.2 = ((bf16[8,128,256]{2,1,0:T(8,128)(2,1)}), bf16[8,128,256]{2,1,0:T(8,128)(2,1)S(1)}, u32[]{:S(2)}, u32[]{:S(2)}) async-start(bf16[8,128,256]{2,1,0:T(8,128)(2,1)} %shard_map.97), calls=%async_computation.2 | async-start | bytes 1048576 | tf_op jit(solution)/shard_map/all_to_all | solution.py:232
  74.4 1.9 %collective-permute-start.1 = (bf16[1024,512]{1,0:T(8,128)(2,1)}, bf16[1024,512]{1,0:T(8,128)(2,1)}, u32[]{:S(2)}, u32[]{:S(2)}) collective-permute-start(bf16[1024,512]{1,0:T(8,128)(2,1)} %bitcast.refs_0_), channel_id=1, source_target_pairs={{0,8},{8,0},{16,24},{24,16},{32,40},{40,32},{48,56},{56,48},{1,9},... | collective-permute-start | bytes 3145736 | tf_op jit(solution)/shard_map/ppermute | solution.py:46
  76.4 1.1 slice.8
  77.4 4.9 %collective-permute-start.4 = (bf16[512,512]{1,0:T(8,128)(2,1)S(1)}, bf16[512,512]{1,0:T(8,128)(2,1)S(1)}, u32[]{:S(2)}, u32[]{:S(2)}) collective-permute-start(bf16[512,512]{1,0:T(8,128)(2,1)S(1)} %slice.8), channel_id=1, source_target_pairs={{0,16},{8,24},{16,32},{24,40},{32,48},{40,56},{48,0},{56,8},{1,17}... | collective-permute-start | bytes 1572872 | tf_op jit(solution)/shard_map/ppermute | solution.py:36
  82.3 1.1 slice.9
  83.4 1.9 %collective-permute-start.7 = (bf16[512,512]{1,0:T(8,128)(2,1)S(1)}, bf16[512,512]{1,0:T(8,128)(2,1)}, u32[]{:S(2)}, u32[]{:S(2)}) collective-permute-start(bf16[512,512]{1,0:T(8,128)(2,1)S(1)} %slice.9), channel_id=1, source_target_pairs={{0,48},{8,56},{16,0},{24,8},{32,16},{40,24},{48,32},{56,40},{1,49}... | collective-permute-start | bytes 1572872 | tf_op jit(solution)/shard_map/ppermute | solution.py:36
  85.4 2.1 %collective-permute-start.3 = (bf16[1024,512]{1,0:T(8,128)(2,1)}, bf16[1024,512]{1,0:T(8,128)(2,1)}, u32[]{:S(2)}, u32[]{:S(2)}) collective-permute-start(bf16[1024,512]{1,0:T(8,128)(2,1)} %collective-permute-done.2.refs_2_), channel_id=1, source_target_pairs={{0,8},{8,0},{16,24},{24,16},{32,40},{40,32},{48,56},{56,48},{1,9},... | collective-permute-start | bytes 3145736 | tf_op jit(solution)/shard_map/ppermute | solution.py:46
  87.5 2.2 %collective-permute-start.9 = (bf16[1024,512]{1,0:T(8,128)(2,1)}, bf16[1024,512]{1,0:T(8,128)(2,1)}, u32[]{:S(2)}, u32[]{:S(2)}) collective-permute-start(bf16[1024,512]{1,0:T(8,128)(2,1)} %collective-permute-done.6.refs_8_), channel_id=1, source_target_pairs={{0,8},{8,0},{16,24},{24,16},{32,40},{40,32},{48,56},{56,48},{1,9},... | collective-permute-start | bytes 3145736 | tf_op jit(solution)/shard_map/ppermute | solution.py:46
  89.7 4.4 %collective-permute-done.4.refs_4_ = bf16[512,512]{1,0:T(8,128)(2,1)S(1)} collective-permute-done((bf16[512,512]{1,0:T(8,128)(2,1)S(1)}, bf16[512,512]{1,0:T(8,128)(2,1)S(1)}, u32[]{:S(2)}, u32[]{:S(2)}) %collective-permute-start.4) | collective-permute-done | bytes 524320 | tf_op jit(solution)/shard_map/ppermute | solution.py:36
  94.1 1.9 %collective-permute-start.5 = (bf16[512,512]{1,0:T(8,128)(2,1)S(1)}, bf16[512,512]{1,0:T(8,128)(2,1)}, u32[]{:S(2)}, u32[]{:S(2)}) collective-permute-start(bf16[512,512]{1,0:T(8,128)(2,1)S(1)} %collective-permute-done.4.refs_4_), channel_id=1, source_target_pairs={{0,8},{8,0},{16,24},{24,16},{32,40},{40,32},{48,56},{56,48},{1,9},... | collective-permute-start | bytes 1572872 | tf_op jit(solution)/shard_map/ppermute | solution.py:46
  96.1 4.6 %collective-permute-done.7.refs_6_ = bf16[512,512]{1,0:T(8,128)(2,1)} collective-permute-done((bf16[512,512]{1,0:T(8,128)(2,1)S(1)}, bf16[512,512]{1,0:T(8,128)(2,1)}, u32[]{:S(2)}, u32[]{:S(2)}) %collective-permute-start.7) | collective-permute-done | bytes 524320 | tf_op jit(solution)/shard_map/ppermute | solution.py:36
  100.7 1.9 %collective-permute-start.8 = (bf16[512,512]{1,0:T(8,128)(2,1)}, bf16[512,512]{1,0:T(8,128)(2,1)}, u32[]{:S(2)}, u32[]{:S(2)}) collective-permute-start(bf16[512,512]{1,0:T(8,128)(2,1)} %collective-permute-done.7.refs_6_), channel_id=1, source_target_pairs={{0,8},{8,0},{16,24},{24,16},{32,40},{40,32},{48,56},{56,48},{1,9},... | collective-permute-start | bytes 1572872 | tf_op jit(solution)/shard_map/ppermute | solution.py:46
  103.2 0.5 and_or_fusion.dp_ref
  103.8 1.0 collective-permute-done.8.refs_7_
  104.8 1.4 all-gather.2.cloned.1.call-done.features
  106.2 6.6 %shard_map.95.query = bf16[160,512]{1,0:T(8,128)(2,1)} custom-call(s32[8]{0:T(128)} %and_or_fusion.dp_ref, bf16[8,160,1024]{2,1,0:T(8,128)(2,1)} %all-gather.2.cloned.1.call-done.features, bf16[1024,512]{1,0:T(8,128)(2,1)} %bitcast.refs_0_, bf16[1024,512]{1,0:T(8,128)(2,1)} %collective-permute-done.1.refs_1_, ...), custom_call_target="tpu_custom_call" | custom-call | flops 1342177280 | bytes 11010048 | tf_op jit(solution)/shard_map/pallas_call | solution.py:56
  112.8 3.1 %all-to-all-done.2.arrived = bf16[8,128,256]{2,1,0:T(8,128)(2,1)S(1)} async-done(((bf16[8,128,256]{2,1,0:T(8,128)(2,1)}), bf16[8,128,256]{2,1,0:T(8,128)(2,1)S(1)}, u32[]{:S(2)}, u32[]{:S(2)}) %all-to-all-start.2) | async-done | bytes 524320 | tf_op jit(solution)/shard_map/all_to_all | solution.py:232
  115.9 0.9 copy-done
  116.8 2.1 %shard_map.98 = (bf16[160,512]{1,0:T(8,128)(2,1)}, bf16[1,128,256]{2,1,0:T(8,128)(2,1)S(1)}) custom-call(bf16[160,512]{1,0:T(8,128)(2,1)S(1)} %copy-done, bf16[8,128,256]{2,1,0:T(8,128)(2,1)S(1)} %all-to-all-done.2.arrived, f32[160,128]{1,0:T(8,128)S(1)} %copy-done.2, bf16[160,512]{1,0:T(8,128)(2,1)S(1)} %bitcast.12, f32[1,1]{1,0:T(1,128)} %bitcast.11.gate), custom_call_target="tpu_custom_call" | custom-call | tf_op jit(solution)/shard_map/pallas_call | solution.py:56
  118.9 8.9 %collective-permute-start.11 = (bf16[1,128,256]{2,1,0:T(8,128)(2,1)S(1)}, bf16[1,128,256]{2,1,0:T(8,128)(2,1)S(1)}, u32[]{:S(2)}, u32[]{:S(2)}) collective-permute-start(bf16[1,128,256]{2,1,0:T(8,128)(2,1)S(1)} %get-tuple-element.17.own), channel_id=1, source_target_pairs={{0,4},{1,5},{2,6},{3,7},{4,0},{5,1},{6,2},{7,3},{8,12},{9,13},{10,... | collective-permute-start | bytes 196616 | tf_op jit(solution)/shard_map/ppermute | solution.py:31
  127.8 1.9 %collective-permute-start.12 = (bf16[1,128,256]{2,1,0:T(8,128)(2,1)S(1)}, bf16[1,128,256]{2,1,0:T(8,128)(2,1)S(1)}, u32[]{:S(2)}, u32[]{:S(2)}) collective-permute-start(bf16[1,128,256]{2,1,0:T(8,128)(2,1)S(1)} %get-tuple-element.17.own), channel_id=1, source_target_pairs={{0,1},{1,0},{2,3},{3,2},{4,5},{5,4},{6,7},{7,6},{8,9},{9,8},{10,11... | collective-permute-start | bytes 196616 | tf_op jit(solution)/shard_map/ppermute | solution.py:31
  129.7 0.6 collective-permute-done.11.by4
  130.3 3.7 %collective-permute-done.12.by1 = bf16[1,128,256]{2,1,0:T(8,128)(2,1)S(1)} collective-permute-done((bf16[1,128,256]{2,1,0:T(8,128)(2,1)S(1)}, bf16[1,128,256]{2,1,0:T(8,128)(2,1)S(1)}, u32[]{:S(2)}, u32[]{:S(2)}) %collective-permute-start.12) | collective-permute-done | bytes 65568 | tf_op jit(solution)/shard_map/ppermute | solution.py:31
  134.0 1.9 %collective-permute-start.13 = (bf16[2,128,256]{2,1,0:T(8,128)(2,1)S(1)}, bf16[2,128,256]{2,1,0:T(8,128)(2,1)S(1)}, u32[]{:S(2)}, u32[]{:S(2)}) collective-permute-start(bf16[2,128,256]{2,1,0:T(8,128)(2,1)S(1)} %pad_maximum_fusion.1), channel_id=1, source_target_pairs={{0,2},{1,3},{2,0},{3,1},{4,6},{5,7},{6,4},{7,5},{8,10},{9,11},{10,... | collective-permute-start | bytes 393224 | tf_op jit(solution)/shard_map/ppermute | solution.py:31
  135.9 4.9 %collective-permute-start.14 = (bf16[1,128,256]{2,1,0:T(8,128)(2,1)S(1)}, bf16[1,128,256]{2,1,0:T(8,128)(2,1)S(1)}, u32[]{:S(2)}, u32[]{:S(2)}) collective-permute-start(bf16[1,128,256]{2,1,0:T(8,128)(2,1)S(1)} %collective-permute-done.11.by4), channel_id=1, source_target_pairs={{0,1},{1,0},{2,3},{3,2},{4,5},{5,4},{6,7},{7,6},{8,9},{9,8},{10,11... | collective-permute-start | bytes 196616 | tf_op jit(solution)/shard_map/ppermute | solution.py:31
  140.9 2.8 %collective-permute-done.14.by5 = bf16[1,128,256]{2,1,0:T(8,128)(2,1)S(1)} collective-permute-done((bf16[1,128,256]{2,1,0:T(8,128)(2,1)S(1)}, bf16[1,128,256]{2,1,0:T(8,128)(2,1)S(1)}, u32[]{:S(2)}, u32[]{:S(2)}) %collective-permute-start.14) | collective-permute-done | bytes 65568 | tf_op jit(solution)/shard_map/ppermute | solution.py:31
  143.6 3.4 %collective-permute-start.15 = (bf16[2,128,256]{2,1,0:T(8,128)(2,1)S(1)}, bf16[2,128,256]{2,1,0:T(8,128)(2,1)S(1)}, u32[]{:S(2)}, u32[]{:S(2)}) collective-permute-start(bf16[2,128,256]{2,1,0:T(8,128)(2,1)S(1)} %collective-permute-done.13.by2), channel_id=1, source_target_pairs={{0,1},{1,0},{2,3},{3,2},{4,5},{5,4},{6,7},{7,6},{8,9},{9,8},{10,11... | collective-permute-start | bytes 393224 | tf_op jit(solution)/shard_map/ppermute | solution.py:31
  147.0 2.7 %shard_map.99.early = f32[128,1024]{1,0:T(8,128)S(1)} custom-call(s32[8]{0:T(128)S(1)} %xor_shift-right-arithmetic_fusion.y_ref, s32[1]{0:T(128)} %bitcast.8.flip_ref, bf16[1,128,256]{2,1,0:T(8,128)(2,1)S(1)} %get-tuple-element.17.own, bf16[1,128,256]{2,1,0:T(8,128)(2,1)S(1)} %collective-permute-done.11.by4, ...), custom_call_target="tpu_custom_call" | custom-call | flops 402653184 | bytes 5111808 | tf_op jit(solution)/shard_map/pallas_call | solution.py:56
  149.8 0.7 collective-permute-done.15.by3
  150.5 2.1 %shard_map.100 = bf16[4,2,16,1024]{3,2,1,0:T(8,128)(2,1)S(1)} custom-call(s32[8]{0:T(128)S(1)} %xor_shift-right-arithmetic_fusion.y_ref, s32[1]{0:T(128)} %bitcast.8.flip_ref, s32[1]{0:T(128)} %bitcast.4.half_ref, f32[128,1024]{1,0:T(8,128)S(1)} %shard_map.99.early, bf16[2,128,256]{2,1,0:T(8,128)(2,1)S(1)} %collective-permute-done.15.by3, ...), custom_call_target="tpu_custom_call" | custom-call | tf_op jit(solution)/shard_map/pallas_call | solution.py:56
  152.6 11.7 %all_to_all.20.arrived = bf16[4,2,16,1024]{3,2,1,0:T(8,128)(2,1)S(1)} all-to-all(bf16[4,2,16,1024]{3,2,1,0:T(8,128)(2,1)S(1)} %shard_map.100), channel_id=1, replica_groups={{0,64,128,192},{256,320,384,448},{1,65,129,193},{257,321,385,449},{2,66..., dimensions={0} | all-to-all | bytes 524288 | tf_op jit(solution)/shard_map/all_to_all | solution.py:27
  164.3 10.0 %collective-permute-start.16 = (bf16[16,1024]{1,0:T(8,128)(2,1)S(1)}, bf16[16,1024]{1,0:T(8,128)(2,1)S(1)}, u32[]{:S(2)}, u32[]{:S(2)}) collective-permute-start(bf16[16,1024]{1,0:T(8,128)(2,1)S(1)} %get-tuple-element.23), channel_id=1, source_target_pairs={{0,256},{64,320},{128,384},{192,448},{256,0},{320,64},{384,128},{4... | collective-permute-start | bytes 98312 | tf_op jit(solution)/shard_map/ppermute | solution.py:22
  174.3 4.5 %collective-permute-done.16 = bf16[16,1024]{1,0:T(8,128)(2,1)S(1)} collective-permute-done((bf16[16,1024]{1,0:T(8,128)(2,1)S(1)}, bf16[16,1024]{1,0:T(8,128)(2,1)S(1)}, u32[]{:S(2)}, u32[]{:S(2)}) %collective-permute-start.16) | collective-permute-done | bytes 32800 | tf_op jit(solution)/shard_map/ppermute | solution.py:22
  178.8 0.6 add_bitcast_fusion
  (22 shorter events, 0.1 us)
Async XLA Ops:
  9.8 10.0 %copy-start.3 = (bf16[1,16,1024]{2,1,0:T(8,128)(2,1)S(1)}, bf16[1,16,1024]{2,1,0:T(8,128)(2,1)}, u32[]{:S(2)}) copy-start(bf16[1,16,1024]{2,1,0:T(8,128)(2,1)} %param.12) | copy-start | bytes 98308
  9.8 29.1 %all-to-all-start = ((bf16[4,1024,256]{2,1,0:T(8,128)(2,1)}), bf16[4,1024,256]{2,1,0:T(8,128)(2,1)S(1)}, u32[]{:S(2)}, u32[]{:S(2)}) async-start(bf16[4,1024,256]{2,1,0:T(8,128)(2,1)} %broadcast_in_dim.16), calls=%async_computation | async-start | bytes 4194304 | tf_op jit(solution)/shard_map/all_to_all | solution.py:42
  19.1 87.1 %all-gather.2.cloned.1.call-start = ((), (), s32[]{:S(2)}) async-start(), calls=%async_computation.4 | async-start | bytes 2949120 | tf_op jit(solution)/shard_map/all_gather | solution.py:209
  19.8 14.5 %collective-permute-start = (bf16[16,1024]{1,0:T(8,128)(2,1)S(1)}, bf16[16,1024]{1,0:T(8,128)(2,1)S(1)}, u32[]{:S(2)}, u32[]{:S(2)}) collective-permute-start(bf16[16,1024]{1,0:T(8,128)(2,1)S(1)} %bitcast.13), channel_id=1, source_target_pairs={{0,256},{64,320},{128,384},{192,448},{256,0},{320,64},{384,128},{4... | collective-permute-start | bytes 98312 | tf_op jit(solution)/shard_map/ppermute | solution.py:22
  38.8 19.9 %collective-permute-start.10 = (bf16[4,1024,256]{2,1,0:T(8,128)(2,1)S(1)}, bf16[4,1024,256]{2,1,0:T(8,128)(2,1)}, u32[]{:S(2)}, u32[]{:S(2)}) collective-permute-start(bf16[4,1024,256]{2,1,0:T(8,128)(2,1)S(1)} %all-to-all-done.near), channel_id=1, source_target_pairs={{0,8},{8,0},{16,24},{24,16},{32,40},{40,32},{48,56},{56,48},{1,9},... | collective-permute-start | bytes 6291464 | tf_op jit(solution)/shard_map/ppermute | solution.py:46
  40.8 35.6 %collective-permute-start.2 = (bf16[1024,512]{1,0:T(8,128)(2,1)}, bf16[1024,512]{1,0:T(8,128)(2,1)}, u32[]{:S(2)}, u32[]{:S(2)}) collective-permute-start(bf16[1024,512]{1,0:T(8,128)(2,1)} %bitcast.refs_0_), channel_id=1, source_target_pairs={{0,16},{8,24},{16,32},{24,40},{32,48},{40,56},{48,0},{56,8},{1,17}... | collective-permute-start | bytes 3145736 | tf_op jit(solution)/shard_map/ppermute | solution.py:36
  44.7 37.6 %collective-permute-start.6 = (bf16[1024,512]{1,0:T(8,128)(2,1)}, bf16[1024,512]{1,0:T(8,128)(2,1)}, u32[]{:S(2)}, u32[]{:S(2)}) collective-permute-start(bf16[1024,512]{1,0:T(8,128)(2,1)} %bitcast.refs_0_), channel_id=1, source_target_pairs={{0,48},{8,56},{16,0},{24,8},{32,16},{40,24},{48,32},{56,40},{1,49}... | collective-permute-start | bytes 3145736 | tf_op jit(solution)/shard_map/ppermute | solution.py:36
  47.4 11.3 %all-to-all-start.1 = ((bf16[4,2,16,1024]{3,2,1,0:T(8,128)(2,1)}), bf16[4,2,16,1024]{3,2,1,0:T(8,128)(2,1)S(1)}, u32[]{:S(2)}, u32[]{:S(2)}) async-start(bf16[4,2,16,1024]{3,2,1,0:T(8,128)(2,1)} %shard_map.96), calls=%async_computation.1 | async-start | bytes 524288 | tf_op jit(solution)/shard_map/all_to_all | solution.py:27
  61.9 54.0 %all-to-all-start.2 = ((bf16[8,128,256]{2,1,0:T(8,128)(2,1)}), bf16[8,128,256]{2,1,0:T(8,128)(2,1)S(1)}, u32[]{:S(2)}, u32[]{:S(2)}) async-start(bf16[8,128,256]{2,1,0:T(8,128)(2,1)} %shard_map.97), calls=%async_computation.2 | async-start | bytes 1048576 | tf_op jit(solution)/shard_map/all_to_all | solution.py:232
  74.4 29.3 %collective-permute-start.1 = (bf16[1024,512]{1,0:T(8,128)(2,1)}, bf16[1024,512]{1,0:T(8,128)(2,1)}, u32[]{:S(2)}, u32[]{:S(2)}) collective-permute-start(bf16[1024,512]{1,0:T(8,128)(2,1)} %bitcast.refs_0_), channel_id=1, source_target_pairs={{0,8},{8,0},{16,24},{24,16},{32,40},{40,32},{48,56},{56,48},{1,9},... | collective-permute-start | bytes 3145736 | tf_op jit(solution)/shard_map/ppermute | solution.py:46
  77.4 16.7 %collective-permute-start.4 = (bf16[512,512]{1,0:T(8,128)(2,1)S(1)}, bf16[512,512]{1,0:T(8,128)(2,1)S(1)}, u32[]{:S(2)}, u32[]{:S(2)}) collective-permute-start(bf16[512,512]{1,0:T(8,128)(2,1)S(1)} %slice.8), channel_id=1, source_target_pairs={{0,16},{8,24},{16,32},{24,40},{32,48},{40,56},{48,0},{56,8},{1,17}... | collective-permute-start | bytes 1572872 | tf_op jit(solution)/shard_map/ppermute | solution.py:36
  83.4 17.2 %collective-permute-start.7 = (bf16[512,512]{1,0:T(8,128)(2,1)S(1)}, bf16[512,512]{1,0:T(8,128)(2,1)}, u32[]{:S(2)}, u32[]{:S(2)}) collective-permute-start(bf16[512,512]{1,0:T(8,128)(2,1)S(1)} %slice.9), channel_id=1, source_target_pairs={{0,48},{8,56},{16,0},{24,8},{32,16},{40,24},{48,32},{56,40},{1,49}... | collective-permute-start | bytes 1572872 | tf_op jit(solution)/shard_map/ppermute | solution.py:36
  85.4 19.4 %collective-permute-start.3 = (bf16[1024,512]{1,0:T(8,128)(2,1)}, bf16[1024,512]{1,0:T(8,128)(2,1)}, u32[]{:S(2)}, u32[]{:S(2)}) collective-permute-start(bf16[1024,512]{1,0:T(8,128)(2,1)} %collective-permute-done.2.refs_2_), channel_id=1, source_target_pairs={{0,8},{8,0},{16,24},{24,16},{32,40},{40,32},{48,56},{56,48},{1,9},... | collective-permute-start | bytes 3145736 | tf_op jit(solution)/shard_map/ppermute | solution.py:46
  87.5 17.3 %collective-permute-start.9 = (bf16[1024,512]{1,0:T(8,128)(2,1)}, bf16[1024,512]{1,0:T(8,128)(2,1)}, u32[]{:S(2)}, u32[]{:S(2)}) collective-permute-start(bf16[1024,512]{1,0:T(8,128)(2,1)} %collective-permute-done.6.refs_8_), channel_id=1, source_target_pairs={{0,8},{8,0},{16,24},{24,16},{32,40},{40,32},{48,56},{56,48},{1,9},... | collective-permute-start | bytes 3145736 | tf_op jit(solution)/shard_map/ppermute | solution.py:46
  94.1 12.0 %copy-start.4 = (bf16[512,512]{1,0:T(8,128)(2,1)}, bf16[512,512]{1,0:T(8,128)(2,1)S(1)}, u32[]{:S(2)}) copy-start(bf16[512,512]{1,0:T(8,128)(2,1)S(1)} %collective-permute-done.4.refs_4_) | copy-start | bytes 1572868
  94.1 9.6 %collective-permute-start.5 = (bf16[512,512]{1,0:T(8,128)(2,1)S(1)}, bf16[512,512]{1,0:T(8,128)(2,1)}, u32[]{:S(2)}, u32[]{:S(2)}) collective-permute-start(bf16[512,512]{1,0:T(8,128)(2,1)S(1)} %collective-permute-done.4.refs_4_), channel_id=1, source_target_pairs={{0,8},{8,0},{16,24},{24,16},{32,40},{40,32},{48,56},{56,48},{1,9},... | collective-permute-start | bytes 1572872 | tf_op jit(solution)/shard_map/ppermute | solution.py:46
  100.7 4.1 %collective-permute-start.8 = (bf16[512,512]{1,0:T(8,128)(2,1)}, bf16[512,512]{1,0:T(8,128)(2,1)}, u32[]{:S(2)}, u32[]{:S(2)}) collective-permute-start(bf16[512,512]{1,0:T(8,128)(2,1)} %collective-permute-done.7.refs_6_), channel_id=1, source_target_pairs={{0,8},{8,0},{16,24},{24,16},{32,40},{40,32},{48,56},{56,48},{1,9},... | collective-permute-start | bytes 1572872 | tf_op jit(solution)/shard_map/ppermute | solution.py:46
  103.8 12.1 %copy-start.1 = (bf16[1,160,512]{2,1,0:T(8,128)(2,1)S(1)}, bf16[1,160,512]{2,1,0:T(8,128)(2,1)}, u32[]{:S(2)}) copy-start(bf16[1,160,512]{2,1,0:T(8,128)(2,1)} %param.15) | copy-start | bytes 491524
  103.8 12.1 %copy-start.2 = (f32[160,128]{1,0:T(8,128)S(1)}, f32[160,128]{1,0:T(8,128)}, u32[]{:S(2)}) copy-start(f32[160,128]{1,0:T(8,128)} %bias_ref.1) | copy-start | bytes 245764
  115.9 0.9 copy-start
  118.9 11.4 %collective-permute-start.11 = (bf16[1,128,256]{2,1,0:T(8,128)(2,1)S(1)}, bf16[1,128,256]{2,1,0:T(8,128)(2,1)S(1)}, u32[]{:S(2)}, u32[]{:S(2)}) collective-permute-start(bf16[1,128,256]{2,1,0:T(8,128)(2,1)S(1)} %get-tuple-element.17.own), channel_id=1, source_target_pairs={{0,4},{1,5},{2,6},{3,7},{4,0},{5,1},{6,2},{7,3},{8,12},{9,13},{10,... | collective-permute-start | bytes 196616 | tf_op jit(solution)/shard_map/ppermute | solution.py:31
  127.8 6.2 %collective-permute-start.12 = (bf16[1,128,256]{2,1,0:T(8,128)(2,1)S(1)}, bf16[1,128,256]{2,1,0:T(8,128)(2,1)S(1)}, u32[]{:S(2)}, u32[]{:S(2)}) collective-permute-start(bf16[1,128,256]{2,1,0:T(8,128)(2,1)S(1)} %get-tuple-element.17.own), channel_id=1, source_target_pairs={{0,1},{1,0},{2,3},{3,2},{4,5},{5,4},{6,7},{7,6},{8,9},{9,8},{10,11... | collective-permute-start | bytes 196616 | tf_op jit(solution)/shard_map/ppermute | solution.py:31
  134.0 9.7 %collective-permute-start.13 = (bf16[2,128,256]{2,1,0:T(8,128)(2,1)S(1)}, bf16[2,128,256]{2,1,0:T(8,128)(2,1)S(1)}, u32[]{:S(2)}, u32[]{:S(2)}) collective-permute-start(bf16[2,128,256]{2,1,0:T(8,128)(2,1)S(1)} %pad_maximum_fusion.1), channel_id=1, source_target_pairs={{0,2},{1,3},{2,0},{3,1},{4,6},{5,7},{6,4},{7,5},{8,10},{9,11},{10,... | collective-permute-start | bytes 393224 | tf_op jit(solution)/shard_map/ppermute | solution.py:31
  135.9 7.7 %collective-permute-start.14 = (bf16[1,128,256]{2,1,0:T(8,128)(2,1)S(1)}, bf16[1,128,256]{2,1,0:T(8,128)(2,1)S(1)}, u32[]{:S(2)}, u32[]{:S(2)}) collective-permute-start(bf16[1,128,256]{2,1,0:T(8,128)(2,1)S(1)} %collective-permute-done.11.by4), channel_id=1, source_target_pairs={{0,1},{1,0},{2,3},{3,2},{4,5},{5,4},{6,7},{7,6},{8,9},{9,8},{10,11... | collective-permute-start | bytes 196616 | tf_op jit(solution)/shard_map/ppermute | solution.py:31
  143.6 6.9 %collective-permute-start.15 = (bf16[2,128,256]{2,1,0:T(8,128)(2,1)S(1)}, bf16[2,128,256]{2,1,0:T(8,128)(2,1)S(1)}, u32[]{:S(2)}, u32[]{:S(2)}) collective-permute-start(bf16[2,128,256]{2,1,0:T(8,128)(2,1)S(1)} %collective-permute-done.13.by2), channel_id=1, source_target_pairs={{0,1},{1,0},{2,3},{3,2},{4,5},{5,4},{6,7},{7,6},{8,9},{9,8},{10,11... | collective-permute-start | bytes 393224 | tf_op jit(solution)/shard_map/ppermute | solution.py:31
  164.3 14.5 %collective-permute-start.16 = (bf16[16,1024]{1,0:T(8,128)(2,1)S(1)}, bf16[16,1024]{1,0:T(8,128)(2,1)S(1)}, u32[]{:S(2)}, u32[]{:S(2)}) collective-permute-start(bf16[16,1024]{1,0:T(8,128)(2,1)S(1)} %get-tuple-element.23), channel_id=1, source_target_pairs={{0,256},{64,320},{128,384},{192,448},{256,0},{320,64},{384,128},{4... | collective-permute-start | bytes 98312 | tf_op jit(solution)/shard_map/ppermute | solution.py:22
Sparse Core Ops, SparseCore 0:
  22.0 84.1 all-gather.1

commit v11 on v10

--- a/solution.py
+++ b/solution.py
@@ -235,6 +235,7 @@
     cut = w.shape[0] // 2
     before, behind = y_shift(w, 1), y_shift(w, -1)
     across = (y_shift(before[:cut], 1), y_shift(behind[cut:], -1))
+    features, across, before = lax.optimization_barrier((features, across, before))
     query_weights = [v for b in (w, before, *across, behind) for v in (b, core_swap(b))]
 
     tokens, columns = hidden.shape[1], w_query.shape[2]

time: 188 us -> 187 us (level)
  waiting for transfers between devices: 42.3 us -> 36.3 us
  blocking collectives: 11.7 us -> 16.1 us
    all_to_all x1, blocking collectives: 11.7 us -> 16.1 us  [x_exchange(): return lax.all_to_all(a, 'section', 0, 0, axis_index_groups=groups)]
    ppermute x4, waiting for transfers between devices: 9.05 us -> 5.28 us  [y_shift(): return lax.ppermute(a, 'dp', pairs)]
    ppermute x2, starting transfers between devices: 21.2 us -> 18 us  [z_swap(): lax.ppermute(a, 'section', [(s, (s + X_SIZE) % (2 * X_SIZE)) for s in ran...]
    ppermute x2, waiting for transfers between devices: 7.82 us -> 11 us  [z_swap(): lax.ppermute(a, 'section', [(s, (s + X_SIZE) % (2 * X_SIZE)) for s in ran...]
    all_to_all x1, waiting for transfers between devices: 3.07 us -> 0.01 us  [local(): arrived = lax.all_to_all(portions, 'tensor', 0, 0)]
  transfers between devices with their start and end apart: 21 -> 21, of which waited for: 13 -> 11; matrix products, arithmetic and copies ran while one was open for 1% -> 3% of each run, Pallas kernels for 7% -> 7%
where the time goes in v11:
time: 187 us; the launch traced here: 185 us
  starting transfers between devices  93.3 us (50%)
  waiting for transfers between devices  36.3 us (19%)
  Pallas kernels  17.5 us (9%)
  blocking collectives  16.1 us (9%)
  between operations  14.9 us (8%)
  local copies, waits for them, and re-layouts  4.58 us (2%)
  other arithmetic  2.27 us (1%)
    ppermute x5, starting transfers between devices, t_swap(): return lax.ppermute(a, 'tensor', [(t, t ^ k) for t in range(8)])  22.6 us
    ppermute x2, starting transfers between devices, z_swap(): lax.ppermute(a, 'section', [(s, (s + X_SIZE) % (2 * X_SIZE)) for s in ran...  18 us
    pallas_call x7, Pallas kernels, call(): pl.pallas_call(kernel, out_shape=outs, in_specs=in_specs, out_specs=jax.t...  17.5 us
    all_to_all x1, blocking collectives, x_exchange(): return lax.all_to_all(a, 'section', 0, 0, axis_index_groups=groups)  16.1 us
    ppermute x4, starting transfers between devices, y_shift(): return lax.ppermute(a, 'dp', pairs)  14.1 us
    all_to_all x1, starting transfers between devices, local(): arrived = lax.all_to_all(portions, 'tensor', 0, 0)  12.5 us
    ppermute x6, starting transfers between devices, core_swap(): return lax.ppermute(a, 'dp', [(d, d ^ 1) for d in range(2 * Y_SIZE)])  12.5 us
    ppermute x2, waiting for transfers between devices, z_swap(): lax.ppermute(a, 'section', [(s, (s + X_SIZE) % (2 * X_SIZE)) for s in ran...  11 us
  transfers between devices with their start and end apart: 21, of which 11 were waited for; matrix products, arithmetic and copies ran while one was open for 3% of the time, Pallas kernels for 7%

profile of v11, /device:TPU:24, one launch (start us, length us, event | category | flops | bytes accessed | tf_op | source)
XLA Modules:
  0.0 185.0 jit_solution(8575532187239264569)
XLA Ops:
  7.2 0.0 all-gather.2.cloned.1.call-start
  7.2 0.7 all-gather.2.cloned.1.call-update
  7.9 1.1 pad_maximum_fusion
  9.0 1.5 broadcast_in_dim.16
  10.5 9.3 %all-to-all-start = ((bf16[4,1024,256]{2,1,0:T(8,128)(2,1)}), bf16[4,1024,256]{2,1,0:T(8,128)(2,1)S(1)}, u32[]{:S(2)}, u32[]{:S(2)}) async-start(bf16[4,1024,256]{2,1,0:T(8,128)(2,1)} %broadcast_in_dim.16), calls=%async_computation | async-start | bytes 4194304 | tf_op jit(solution)/shard_map/all_to_all | solution.py:42
  19.8 11.2 %collective-permute-start = (bf16[16,1024]{1,0:T(8,128)(2,1)S(1)}, bf16[16,1024]{1,0:T(8,128)(2,1)S(1)}, u32[]{:S(2)}, u32[]{:S(2)}) collective-permute-start(bf16[16,1024]{1,0:T(8,128)(2,1)S(1)} %bitcast.13), channel_id=1, source_target_pairs={{0,256},{64,320},{128,384},{192,448},{256,0},{320,64},{384,128},{4... | collective-permute-start | bytes 98312 | tf_op jit(solution)/shard_map/ppermute | solution.py:22
  31.0 3.3 %collective-permute-done.other = bf16[16,1024]{1,0:T(8,128)(2,1)S(1)} collective-permute-done((bf16[16,1024]{1,0:T(8,128)(2,1)S(1)}, bf16[16,1024]{1,0:T(8,128)(2,1)S(1)}, u32[]{:S(2)}, u32[]{:S(2)}) %collective-permute-start) | collective-permute-done | bytes 32800 | tf_op jit(solution)/shard_map/ppermute | solution.py:22
  34.3 5.3 %all-to-all-done.near = bf16[4,1024,256]{2,1,0:T(8,128)(2,1)S(1)} async-done(((bf16[4,1024,256]{2,1,0:T(8,128)(2,1)}), bf16[4,1024,256]{2,1,0:T(8,128)(2,1)S(1)}, u32[]{:S(2)}, u32[]{:S(2)}) %all-to-all-start) | async-done | bytes 2097184 | tf_op jit(solution)/shard_map/all_to_all | solution.py:42
  39.6 1.9 %collective-permute-start.10 = (bf16[4,1024,256]{2,1,0:T(8,128)(2,1)S(1)}, bf16[4,1024,256]{2,1,0:T(8,128)(2,1)}, u32[]{:S(2)}, u32[]{:S(2)}) collective-permute-start(bf16[4,1024,256]{2,1,0:T(8,128)(2,1)S(1)} %all-to-all-done.near), channel_id=1, source_target_pairs={{0,8},{8,0},{16,24},{24,16},{32,40},{40,32},{48,56},{56,48},{1,9},... | collective-permute-start | bytes 6291464 | tf_op jit(solution)/shard_map/ppermute | solution.py:46
  41.5 1.9 %collective-permute-start.3 = (bf16[1024,512]{1,0:T(8,128)(2,1)}, bf16[1024,512]{1,0:T(8,128)(2,1)}, u32[]{:S(2)}, u32[]{:S(2)}) collective-permute-start(bf16[1024,512]{1,0:T(8,128)(2,1)} %bitcast.refs_0_), channel_id=1, source_target_pairs={{0,48},{8,56},{16,0},{24,8},{32,16},{40,24},{48,32},{56,40},{1,49}... | collective-permute-start | bytes 3145736 | tf_op jit(solution)/shard_map/ppermute | solution.py:36
  43.4 5.1 %collective-permute-start.1 = (bf16[1024,512]{1,0:T(8,128)(2,1)}, bf16[1024,512]{1,0:T(8,128)(2,1)}, u32[]{:S(2)}, u32[]{:S(2)}) collective-permute-start(bf16[1024,512]{1,0:T(8,128)(2,1)} %bitcast.refs_0_), channel_id=1, source_target_pairs={{0,16},{8,24},{16,32},{24,40},{32,48},{40,56},{48,0},{56,8},{1,17}... | collective-permute-start | bytes 3145736 | tf_op jit(solution)/shard_map/ppermute | solution.py:36
  48.6 0.7 shard_map.96
  49.3 4.3 %all-to-all-start.1 = ((bf16[4,2,16,1024]{3,2,1,0:T(8,128)(2,1)}), bf16[4,2,16,1024]{3,2,1,0:T(8,128)(2,1)S(1)}, u32[]{:S(2)}, u32[]{:S(2)}) async-start(bf16[4,2,16,1024]{3,2,1,0:T(8,128)(2,1)} %shard_map.96), calls=%async_computation.1 | async-start | bytes 524288 | tf_op jit(solution)/shard_map/all_to_all | solution.py:27
  53.6 6.8 %all-to-all-done.1.images = bf16[4,2,16,1024]{3,2,1,0:T(8,128)(2,1)S(1)} async-done(((bf16[4,2,16,1024]{3,2,1,0:T(8,128)(2,1)}), bf16[4,2,16,1024]{3,2,1,0:T(8,128)(2,1)S(1)}, u32[]{:S(2)}, u32[]{:S(2)}) %all-to-all-start.1) | async-done | bytes 262176 | tf_op jit(solution)/shard_map/all_to_all | solution.py:27
  60.4 3.2 %shard_map.97 = bf16[8,128,256]{2,1,0:T(8,128)(2,1)} custom-call(s32[8]{0:T(128)S(1)} %iota_xor_fusion.head_ref, s32[1]{0:T(128)} %bitcast.4.half_ref, bf16[4,2,16,1024]{3,2,1,0:T(8,128)(2,1)S(1)} %all-to-all-done.1.images, bf16[4,1024,256]{2,1,0:T(8,128)(2,1)S(1)} %all-to-all-done.near, bf16[4,1024,256]{2,1,0:T(8,128)(2,1)} %collective-permute-done.10.far), custom_call_target="tpu_custom_call" | custom-call | tf_op jit(solution)/shard_map/pallas_call | solution.py:56
  63.5 12.5 %all-to-all-start.2 = ((bf16[8,128,256]{2,1,0:T(8,128)(2,1)}), bf16[8,128,256]{2,1,0:T(8,128)(2,1)S(1)}, u32[]{:S(2)}, u32[]{:S(2)}) async-start(bf16[8,128,256]{2,1,0:T(8,128)(2,1)} %shard_map.97), calls=%async_computation.2 | async-start | bytes 1048576 | tf_op jit(solution)/shard_map/all_to_all | solution.py:232
  76.0 1.1 slice.9
  77.1 1.9 %collective-permute-start.4 = (bf16[512,512]{1,0:T(8,128)(2,1)S(1)}, bf16[512,512]{1,0:T(8,128)(2,1)S(1)}, u32[]{:S(2)}, u32[]{:S(2)}) collective-permute-start(bf16[512,512]{1,0:T(8,128)(2,1)S(1)} %slice.9), channel_id=1, source_target_pairs={{0,48},{8,56},{16,0},{24,8},{32,16},{40,24},{48,32},{56,40},{1,49}... | collective-permute-start | bytes 1572872 | tf_op jit(solution)/shard_map/ppermute | solution.py:36
  79.1 1.1 slice.8
  80.1 5.1 %collective-permute-start.2 = (bf16[512,512]{1,0:T(8,128)(2,1)S(1)}, bf16[512,512]{1,0:T(8,128)(2,1)}, u32[]{:S(2)}, u32[]{:S(2)}) collective-permute-start(bf16[512,512]{1,0:T(8,128)(2,1)S(1)} %slice.8), channel_id=1, source_target_pairs={{0,16},{8,24},{16,32},{24,40},{32,48},{40,56},{48,0},{56,8},{1,17}... | collective-permute-start | bytes 1572872 | tf_op jit(solution)/shard_map/ppermute | solution.py:36
  85.3 1.9 %collective-permute-start.5 = (bf16[1024,512]{1,0:T(8,128)(2,1)}, bf16[1024,512]{1,0:T(8,128)(2,1)}, u32[]{:S(2)}, u32[]{:S(2)}) collective-permute-start(bf16[1024,512]{1,0:T(8,128)(2,1)} %bitcast.refs_0_), channel_id=1, source_target_pairs={{0,8},{8,0},{16,24},{24,16},{32,40},{40,32},{48,56},{56,48},{1,9},... | collective-permute-start | bytes 3145736 | tf_op jit(solution)/shard_map/ppermute | solution.py:46
  87.2 2.4 %collective-permute-start.9 = (bf16[1024,512]{1,0:T(8,128)(2,1)}, bf16[1024,512]{1,0:T(8,128)(2,1)}, u32[]{:S(2)}, u32[]{:S(2)}) collective-permute-start(bf16[1024,512]{1,0:T(8,128)(2,1)} %collective-permute-done.3.refs_8_), channel_id=1, source_target_pairs={{0,8},{8,0},{16,24},{24,16},{32,40},{40,32},{48,56},{56,48},{1,9},... | collective-permute-start | bytes 3145736 | tf_op jit(solution)/shard_map/ppermute | solution.py:46
  89.6 3.0 %collective-permute-done.4.refs_6_ = bf16[512,512]{1,0:T(8,128)(2,1)S(1)} collective-permute-done((bf16[512,512]{1,0:T(8,128)(2,1)S(1)}, bf16[512,512]{1,0:T(8,128)(2,1)S(1)}, u32[]{:S(2)}, u32[]{:S(2)}) %collective-permute-start.4) | collective-permute-done | bytes 524320 | tf_op jit(solution)/shard_map/ppermute | solution.py:36
  92.6 2.3 %collective-permute-done.2.refs_4_ = bf16[512,512]{1,0:T(8,128)(2,1)} collective-permute-done((bf16[512,512]{1,0:T(8,128)(2,1)S(1)}, bf16[512,512]{1,0:T(8,128)(2,1)}, u32[]{:S(2)}, u32[]{:S(2)}) %collective-permute-start.2) | collective-permute-done | bytes 524320 | tf_op jit(solution)/shard_map/ppermute | solution.py:36
  94.9 1.9 %collective-permute-start.6 = (bf16[1024,512]{1,0:T(8,128)(2,1)}, bf16[1024,512]{1,0:T(8,128)(2,1)}, u32[]{:S(2)}, u32[]{:S(2)}) collective-permute-start(bf16[1024,512]{1,0:T(8,128)(2,1)} %collective-permute-done.1.refs_2_), channel_id=1, source_target_pairs={{0,8},{8,0},{16,24},{24,16},{32,40},{40,32},{48,56},{56,48},{1,9},... | collective-permute-start | bytes 3145736 | tf_op jit(solution)/shard_map/ppermute | solution.py:46
  96.8 2.4 %collective-permute-start.7 = (bf16[512,512]{1,0:T(8,128)(2,1)}, bf16[512,512]{1,0:T(8,128)(2,1)}, u32[]{:S(2)}, u32[]{:S(2)}) collective-permute-start(bf16[512,512]{1,0:T(8,128)(2,1)} %collective-permute-done.2.refs_4_), channel_id=1, source_target_pairs={{0,8},{8,0},{16,24},{24,16},{32,40},{40,32},{48,56},{56,48},{1,9},... | collective-permute-start | bytes 1572872 | tf_op jit(solution)/shard_map/ppermute | solution.py:46
  99.3 1.9 %collective-permute-start.8 = (bf16[512,512]{1,0:T(8,128)(2,1)S(1)}, bf16[512,512]{1,0:T(8,128)(2,1)}, u32[]{:S(2)}, u32[]{:S(2)}) collective-permute-start(bf16[512,512]{1,0:T(8,128)(2,1)S(1)} %collective-permute-done.4.refs_6_), channel_id=1, source_target_pairs={{0,8},{8,0},{16,24},{24,16},{32,40},{40,32},{48,56},{56,48},{1,9},... | collective-permute-start | bytes 1572872 | tf_op jit(solution)/shard_map/ppermute | solution.py:46
  101.8 0.5 and_or_fusion.dp_ref
  102.4 0.8 collective-permute-done.8.refs_7_
  103.2 6.6 %shard_map.95.query = bf16[160,512]{1,0:T(8,128)(2,1)} custom-call(s32[8]{0:T(128)} %and_or_fusion.dp_ref, bf16[8,160,1024]{2,1,0:T(8,128)(2,1)} %all-gather.2.cloned.1.call-done.features, bf16[1024,512]{1,0:T(8,128)(2,1)} %bitcast.refs_0_, bf16[1024,512]{1,0:T(8,128)(2,1)} %collective-permute-done.5.refs_1_, ...), custom_call_target="tpu_custom_call" | custom-call | flops 1342177280 | bytes 11010048 | tf_op jit(solution)/shard_map/pallas_call | solution.py:56
  109.9 0.0 copy-start
  109.9 0.9 copy-done
  110.8 2.1 %shard_map.98 = (bf16[160,512]{1,0:T(8,128)(2,1)}, bf16[1,128,256]{2,1,0:T(8,128)(2,1)S(1)}) custom-call(bf16[160,512]{1,0:T(8,128)(2,1)S(1)} %copy-done, bf16[8,128,256]{2,1,0:T(8,128)(2,1)S(1)} %all-to-all-done.2.arrived, f32[160,128]{1,0:T(8,128)S(1)} %copy-done.2, bf16[160,512]{1,0:T(8,128)(2,1)S(1)} %bitcast.12, f32[1,1]{1,0:T(1,128)} %bitcast.11.gate), custom_call_target="tpu_custom_call" | custom-call | tf_op jit(solution)/shard_map/pallas_call | solution.py:56
  112.9 7.5 %collective-permute-start.11 = (bf16[1,128,256]{2,1,0:T(8,128)(2,1)S(1)}, bf16[1,128,256]{2,1,0:T(8,128)(2,1)S(1)}, u32[]{:S(2)}, u32[]{:S(2)}) collective-permute-start(bf16[1,128,256]{2,1,0:T(8,128)(2,1)S(1)} %get-tuple-element.25.own), channel_id=1, source_target_pairs={{0,4},{1,5},{2,6},{3,7},{4,0},{5,1},{6,2},{7,3},{8,12},{9,13},{10,... | collective-permute-start | bytes 196616 | tf_op jit(solution)/shard_map/ppermute | solution.py:31
  120.4 3.4 %collective-permute-start.12 = (bf16[1,128,256]{2,1,0:T(8,128)(2,1)S(1)}, bf16[1,128,256]{2,1,0:T(8,128)(2,1)S(1)}, u32[]{:S(2)}, u32[]{:S(2)}) collective-permute-start(bf16[1,128,256]{2,1,0:T(8,128)(2,1)S(1)} %get-tuple-element.25.own), channel_id=1, source_target_pairs={{0,1},{1,0},{2,3},{3,2},{4,5},{5,4},{6,7},{7,6},{8,9},{9,8},{10,11... | collective-permute-start | bytes 196616 | tf_op jit(solution)/shard_map/ppermute | solution.py:31
  123.8 1.6 collective-permute-done.11.by4
  125.5 1.1 collective-permute-done.12.by1
  126.6 4.3 %collective-permute-start.13 = (bf16[2,128,256]{2,1,0:T(8,128)(2,1)S(1)}, bf16[2,128,256]{2,1,0:T(8,128)(2,1)S(1)}, u32[]{:S(2)}, u32[]{:S(2)}) collective-permute-start(bf16[2,128,256]{2,1,0:T(8,128)(2,1)S(1)} %pad_maximum_fusion.1), channel_id=1, source_target_pairs={{0,2},{1,3},{2,0},{3,1},{4,6},{5,7},{6,4},{7,5},{8,10},{9,11},{10,... | collective-permute-start | bytes 393224 | tf_op jit(solution)/shard_map/ppermute | solution.py:31
  130.9 4.1 %collective-permute-start.14 = (bf16[1,128,256]{2,1,0:T(8,128)(2,1)S(1)}, bf16[1,128,256]{2,1,0:T(8,128)(2,1)S(1)}, u32[]{:S(2)}, u32[]{:S(2)}) collective-permute-start(bf16[1,128,256]{2,1,0:T(8,128)(2,1)S(1)} %collective-permute-done.11.by4), channel_id=1, source_target_pairs={{0,1},{1,0},{2,3},{3,2},{4,5},{5,4},{6,7},{7,6},{8,9},{9,8},{10,11... | collective-permute-start | bytes 196616 | tf_op jit(solution)/shard_map/ppermute | solution.py:31
  135.0 2.9 %collective-permute-done.14.by5 = bf16[1,128,256]{2,1,0:T(8,128)(2,1)S(1)} collective-permute-done((bf16[1,128,256]{2,1,0:T(8,128)(2,1)S(1)}, bf16[1,128,256]{2,1,0:T(8,128)(2,1)S(1)}, u32[]{:S(2)}, u32[]{:S(2)}) %collective-permute-start.14) | collective-permute-done | bytes 65568 | tf_op jit(solution)/shard_map/ppermute | solution.py:31
  137.9 3.3 %collective-permute-start.15 = (bf16[2,128,256]{2,1,0:T(8,128)(2,1)S(1)}, bf16[2,128,256]{2,1,0:T(8,128)(2,1)S(1)}, u32[]{:S(2)}, u32[]{:S(2)}) collective-permute-start(bf16[2,128,256]{2,1,0:T(8,128)(2,1)S(1)} %collective-permute-done.13.by2), channel_id=1, source_target_pairs={{0,1},{1,0},{2,3},{3,2},{4,5},{5,4},{6,7},{7,6},{8,9},{9,8},{10,11... | collective-permute-start | bytes 393224 | tf_op jit(solution)/shard_map/ppermute | solution.py:31
  141.2 2.7 %shard_map.99.early = f32[128,1024]{1,0:T(8,128)S(1)} custom-call(s32[8]{0:T(128)S(1)} %xor_shift-right-arithmetic_fusion.y_ref, s32[1]{0:T(128)} %bitcast.8.flip_ref, bf16[1,128,256]{2,1,0:T(8,128)(2,1)S(1)} %get-tuple-element.25.own, bf16[1,128,256]{2,1,0:T(8,128)(2,1)S(1)} %collective-permute-done.11.by4, ...), custom_call_target="tpu_custom_call" | custom-call | flops 402653184 | bytes 5111808 | tf_op jit(solution)/shard_map/pallas_call | solution.py:56
  143.9 0.8 collective-permute-done.15.by3
  144.8 2.1 %shard_map.100 = bf16[4,2,16,1024]{3,2,1,0:T(8,128)(2,1)S(1)} custom-call(s32[8]{0:T(128)S(1)} %xor_shift-right-arithmetic_fusion.y_ref, s32[1]{0:T(128)} %bitcast.8.flip_ref, s32[1]{0:T(128)} %bitcast.4.half_ref, f32[128,1024]{1,0:T(8,128)S(1)} %shard_map.99.early, bf16[2,128,256]{2,1,0:T(8,128)(2,1)S(1)} %collective-permute-done.15.by3, ...), custom_call_target="tpu_custom_call" | custom-call | tf_op jit(solution)/shard_map/pallas_call | solution.py:56
  146.9 16.1 %all_to_all.20.arrived = bf16[4,2,16,1024]{3,2,1,0:T(8,128)(2,1)S(1)} all-to-all(bf16[4,2,16,1024]{3,2,1,0:T(8,128)(2,1)S(1)} %shard_map.100), channel_id=1, replica_groups={{0,64,128,192},{256,320,384,448},{1,65,129,193},{257,321,385,449},{2,66..., dimensions={0} | all-to-all | bytes 524288 | tf_op jit(solution)/shard_map/all_to_all | solution.py:27
  163.0 6.8 %collective-permute-start.16 = (bf16[16,1024]{1,0:T(8,128)(2,1)S(1)}, bf16[16,1024]{1,0:T(8,128)(2,1)S(1)}, u32[]{:S(2)}, u32[]{:S(2)}) collective-permute-start(bf16[16,1024]{1,0:T(8,128)(2,1)S(1)} %get-tuple-element.31), channel_id=1, source_target_pairs={{0,256},{64,320},{128,384},{192,448},{256,0},{320,64},{384,128},{4... | collective-permute-start | bytes 98312 | tf_op jit(solution)/shard_map/ppermute | solution.py:22
  169.8 7.8 %collective-permute-done.16 = bf16[16,1024]{1,0:T(8,128)(2,1)S(1)} collective-permute-done((bf16[16,1024]{1,0:T(8,128)(2,1)S(1)}, bf16[16,1024]{1,0:T(8,128)(2,1)S(1)}, u32[]{:S(2)}, u32[]{:S(2)}) %collective-permute-start.16) | collective-permute-done | bytes 32800 | tf_op jit(solution)/shard_map/ppermute | solution.py:22
  177.6 0.6 add_bitcast_fusion
  (22 shorter events, 0.1 us)
Async XLA Ops:
  7.2 87.8 %all-gather.2.cloned.1.call-start = ((), (), s32[]{:S(2)}) async-start(), calls=%async_computation.4 | async-start | bytes 2949120 | tf_op jit(solution)/shard_map/all_gather | solution.py:209
  10.5 9.3 %copy-start.3 = (bf16[1,16,1024]{2,1,0:T(8,128)(2,1)S(1)}, bf16[1,16,1024]{2,1,0:T(8,128)(2,1)}, u32[]{:S(2)}) copy-start(bf16[1,16,1024]{2,1,0:T(8,128)(2,1)} %param.12) | copy-start | bytes 98308
  10.5 29.1 %all-to-all-start = ((bf16[4,1024,256]{2,1,0:T(8,128)(2,1)}), bf16[4,1024,256]{2,1,0:T(8,128)(2,1)S(1)}, u32[]{:S(2)}, u32[]{:S(2)}) async-start(bf16[4,1024,256]{2,1,0:T(8,128)(2,1)} %broadcast_in_dim.16), calls=%async_computation | async-start | bytes 4194304 | tf_op jit(solution)/shard_map/all_to_all | solution.py:42
  19.8 14.5 %collective-permute-start = (bf16[16,1024]{1,0:T(8,128)(2,1)S(1)}, bf16[16,1024]{1,0:T(8,128)(2,1)S(1)}, u32[]{:S(2)}, u32[]{:S(2)}) collective-permute-start(bf16[16,1024]{1,0:T(8,128)(2,1)S(1)} %bitcast.13), channel_id=1, source_target_pairs={{0,256},{64,320},{128,384},{192,448},{256,0},{320,64},{384,128},{4... | collective-permute-start | bytes 98312 | tf_op jit(solution)/shard_map/ppermute | solution.py:22
  39.6 20.8 %collective-permute-start.10 = (bf16[4,1024,256]{2,1,0:T(8,128)(2,1)S(1)}, bf16[4,1024,256]{2,1,0:T(8,128)(2,1)}, u32[]{:S(2)}, u32[]{:S(2)}) collective-permute-start(bf16[4,1024,256]{2,1,0:T(8,128)(2,1)S(1)} %all-to-all-done.near), channel_id=1, source_target_pairs={{0,8},{8,0},{16,24},{24,16},{32,40},{40,32},{48,56},{56,48},{1,9},... | collective-permute-start | bytes 6291464 | tf_op jit(solution)/shard_map/ppermute | solution.py:46
  41.5 34.5 %collective-permute-start.3 = (bf16[1024,512]{1,0:T(8,128)(2,1)}, bf16[1024,512]{1,0:T(8,128)(2,1)}, u32[]{:S(2)}, u32[]{:S(2)}) collective-permute-start(bf16[1024,512]{1,0:T(8,128)(2,1)} %bitcast.refs_0_), channel_id=1, source_target_pairs={{0,48},{8,56},{16,0},{24,8},{32,16},{40,24},{48,32},{56,40},{1,49}... | collective-permute-start | bytes 3145736 | tf_op jit(solution)/shard_map/ppermute | solution.py:36
  43.4 35.6 %collective-permute-start.1 = (bf16[1024,512]{1,0:T(8,128)(2,1)}, bf16[1024,512]{1,0:T(8,128)(2,1)}, u32[]{:S(2)}, u32[]{:S(2)}) collective-permute-start(bf16[1024,512]{1,0:T(8,128)(2,1)} %bitcast.refs_0_), channel_id=1, source_target_pairs={{0,16},{8,24},{16,32},{24,40},{32,48},{40,56},{48,0},{56,8},{1,17}... | collective-permute-start | bytes 3145736 | tf_op jit(solution)/shard_map/ppermute | solution.py:36
  49.3 11.1 %all-to-all-start.1 = ((bf16[4,2,16,1024]{3,2,1,0:T(8,128)(2,1)}), bf16[4,2,16,1024]{3,2,1,0:T(8,128)(2,1)S(1)}, u32[]{:S(2)}, u32[]{:S(2)}) async-start(bf16[4,2,16,1024]{3,2,1,0:T(8,128)(2,1)} %shard_map.96), calls=%async_computation.1 | async-start | bytes 524288 | tf_op jit(solution)/shard_map/all_to_all | solution.py:27
  63.5 46.3 %all-to-all-start.2 = ((bf16[8,128,256]{2,1,0:T(8,128)(2,1)}), bf16[8,128,256]{2,1,0:T(8,128)(2,1)S(1)}, u32[]{:S(2)}, u32[]{:S(2)}) async-start(bf16[8,128,256]{2,1,0:T(8,128)(2,1)} %shard_map.97), calls=%async_computation.2 | async-start | bytes 1048576 | tf_op jit(solution)/shard_map/all_to_all | solution.py:232
  77.1 15.5 %collective-permute-start.4 = (bf16[512,512]{1,0:T(8,128)(2,1)S(1)}, bf16[512,512]{1,0:T(8,128)(2,1)S(1)}, u32[]{:S(2)}, u32[]{:S(2)}) collective-permute-start(bf16[512,512]{1,0:T(8,128)(2,1)S(1)} %slice.9), channel_id=1, source_target_pairs={{0,48},{8,56},{16,0},{24,8},{32,16},{40,24},{48,32},{56,40},{1,49}... | collective-permute-start | bytes 1572872 | tf_op jit(solution)/shard_map/ppermute | solution.py:36
  80.1 14.8 %collective-permute-start.2 = (bf16[512,512]{1,0:T(8,128)(2,1)S(1)}, bf16[512,512]{1,0:T(8,128)(2,1)}, u32[]{:S(2)}, u32[]{:S(2)}) collective-permute-start(bf16[512,512]{1,0:T(8,128)(2,1)S(1)} %slice.8), channel_id=1, source_target_pairs={{0,16},{8,24},{16,32},{24,40},{32,48},{40,56},{48,0},{56,8},{1,17}... | collective-permute-start | bytes 1572872 | tf_op jit(solution)/shard_map/ppermute | solution.py:36
  85.3 17.1 %collective-permute-start.5 = (bf16[1024,512]{1,0:T(8,128)(2,1)}, bf16[1024,512]{1,0:T(8,128)(2,1)}, u32[]{:S(2)}, u32[]{:S(2)}) collective-permute-start(bf16[1024,512]{1,0:T(8,128)(2,1)} %bitcast.refs_0_), channel_id=1, source_target_pairs={{0,8},{8,0},{16,24},{24,16},{32,40},{40,32},{48,56},{56,48},{1,9},... | collective-permute-start | bytes 3145736 | tf_op jit(solution)/shard_map/ppermute | solution.py:46
  87.2 15.1 %collective-permute-start.9 = (bf16[1024,512]{1,0:T(8,128)(2,1)}, bf16[1024,512]{1,0:T(8,128)(2,1)}, u32[]{:S(2)}, u32[]{:S(2)}) collective-permute-start(bf16[1024,512]{1,0:T(8,128)(2,1)} %collective-permute-done.3.refs_8_), channel_id=1, source_target_pairs={{0,8},{8,0},{16,24},{24,16},{32,40},{40,32},{48,56},{56,48},{1,9},... | collective-permute-start | bytes 3145736 | tf_op jit(solution)/shard_map/ppermute | solution.py:46
  92.6 10.6 %copy-start.4 = (bf16[512,512]{1,0:T(8,128)(2,1)}, bf16[512,512]{1,0:T(8,128)(2,1)S(1)}, u32[]{:S(2)}) copy-start(bf16[512,512]{1,0:T(8,128)(2,1)S(1)} %collective-permute-done.4.refs_6_) | copy-start | bytes 1572868
  94.9 8.3 %collective-permute-start.6 = (bf16[1024,512]{1,0:T(8,128)(2,1)}, bf16[1024,512]{1,0:T(8,128)(2,1)}, u32[]{:S(2)}, u32[]{:S(2)}) collective-permute-start(bf16[1024,512]{1,0:T(8,128)(2,1)} %collective-permute-done.1.refs_2_), channel_id=1, source_target_pairs={{0,8},{8,0},{16,24},{24,16},{32,40},{40,32},{48,56},{56,48},{1,9},... | collective-permute-start | bytes 3145736 | tf_op jit(solution)/shard_map/ppermute | solution.py:46
  96.8 5.5 %collective-permute-start.7 = (bf16[512,512]{1,0:T(8,128)(2,1)}, bf16[512,512]{1,0:T(8,128)(2,1)}, u32[]{:S(2)}, u32[]{:S(2)}) collective-permute-start(bf16[512,512]{1,0:T(8,128)(2,1)} %collective-permute-done.2.refs_4_), channel_id=1, source_target_pairs={{0,8},{8,0},{16,24},{24,16},{32,40},{40,32},{48,56},{56,48},{1,9},... | collective-permute-start | bytes 1572872 | tf_op jit(solution)/shard_map/ppermute | solution.py:46
  99.3 3.9 %collective-permute-start.8 = (bf16[512,512]{1,0:T(8,128)(2,1)S(1)}, bf16[512,512]{1,0:T(8,128)(2,1)}, u32[]{:S(2)}, u32[]{:S(2)}) collective-permute-start(bf16[512,512]{1,0:T(8,128)(2,1)S(1)} %collective-permute-done.4.refs_6_), channel_id=1, source_target_pairs={{0,8},{8,0},{16,24},{24,16},{32,40},{40,32},{48,56},{56,48},{1,9},... | collective-permute-start | bytes 1572872 | tf_op jit(solution)/shard_map/ppermute | solution.py:46
  102.4 7.5 %copy-start.1 = (bf16[1,160,512]{2,1,0:T(8,128)(2,1)S(1)}, bf16[1,160,512]{2,1,0:T(8,128)(2,1)}, u32[]{:S(2)}) copy-start(bf16[1,160,512]{2,1,0:T(8,128)(2,1)} %param.15) | copy-start | bytes 491524
  102.4 7.5 %copy-start.2 = (f32[160,128]{1,0:T(8,128)S(1)}, f32[160,128]{1,0:T(8,128)}, u32[]{:S(2)}) copy-start(f32[160,128]{1,0:T(8,128)} %bias_ref.1) | copy-start | bytes 245764
  109.9 0.9 copy-start
  112.9 12.6 %collective-permute-start.11 = (bf16[1,128,256]{2,1,0:T(8,128)(2,1)S(1)}, bf16[1,128,256]{2,1,0:T(8,128)(2,1)S(1)}, u32[]{:S(2)}, u32[]{:S(2)}) collective-permute-start(bf16[1,128,256]{2,1,0:T(8,128)(2,1)S(1)} %get-tuple-element.25.own), channel_id=1, source_target_pairs={{0,4},{1,5},{2,6},{3,7},{4,0},{5,1},{6,2},{7,3},{8,12},{9,13},{10,... | collective-permute-start | bytes 196616 | tf_op jit(solution)/shard_map/ppermute | solution.py:31
  120.4 6.2 %collective-permute-start.12 = (bf16[1,128,256]{2,1,0:T(8,128)(2,1)S(1)}, bf16[1,128,256]{2,1,0:T(8,128)(2,1)S(1)}, u32[]{:S(2)}, u32[]{:S(2)}) collective-permute-start(bf16[1,128,256]{2,1,0:T(8,128)(2,1)S(1)} %get-tuple-element.25.own), channel_id=1, source_target_pairs={{0,1},{1,0},{2,3},{3,2},{4,5},{5,4},{6,7},{7,6},{8,9},{9,8},{10,11... | collective-permute-start | bytes 196616 | tf_op jit(solution)/shard_map/ppermute | solution.py:31
  126.6 11.3 %collective-permute-start.13 = (bf16[2,128,256]{2,1,0:T(8,128)(2,1)S(1)}, bf16[2,128,256]{2,1,0:T(8,128)(2,1)S(1)}, u32[]{:S(2)}, u32[]{:S(2)}) collective-permute-start(bf16[2,128,256]{2,1,0:T(8,128)(2,1)S(1)} %pad_maximum_fusion.1), channel_id=1, source_target_pairs={{0,2},{1,3},{2,0},{3,1},{4,6},{5,7},{6,4},{7,5},{8,10},{9,11},{10,... | collective-permute-start | bytes 393224 | tf_op jit(solution)/shard_map/ppermute | solution.py:31
  130.9 7.0 %collective-permute-start.14 = (bf16[1,128,256]{2,1,0:T(8,128)(2,1)S(1)}, bf16[1,128,256]{2,1,0:T(8,128)(2,1)S(1)}, u32[]{:S(2)}, u32[]{:S(2)}) collective-permute-start(bf16[1,128,256]{2,1,0:T(8,128)(2,1)S(1)} %collective-permute-done.11.by4), channel_id=1, source_target_pairs={{0,1},{1,0},{2,3},{3,2},{4,5},{5,4},{6,7},{7,6},{8,9},{9,8},{10,11... | collective-permute-start | bytes 196616 | tf_op jit(solution)/shard_map/ppermute | solution.py:31
  137.9 6.9 %collective-permute-start.15 = (bf16[2,128,256]{2,1,0:T(8,128)(2,1)S(1)}, bf16[2,128,256]{2,1,0:T(8,128)(2,1)S(1)}, u32[]{:S(2)}, u32[]{:S(2)}) collective-permute-start(bf16[2,128,256]{2,1,0:T(8,128)(2,1)S(1)} %collective-permute-done.13.by2), channel_id=1, source_target_pairs={{0,1},{1,0},{2,3},{3,2},{4,5},{5,4},{6,7},{7,6},{8,9},{9,8},{10,11... | collective-permute-start | bytes 393224 | tf_op jit(solution)/shard_map/ppermute | solution.py:31
  163.0 14.5 %collective-permute-start.16 = (bf16[16,1024]{1,0:T(8,128)(2,1)S(1)}, bf16[16,1024]{1,0:T(8,128)(2,1)S(1)}, u32[]{:S(2)}, u32[]{:S(2)}) collective-permute-start(bf16[16,1024]{1,0:T(8,128)(2,1)S(1)} %get-tuple-element.31), channel_id=1, source_target_pairs={{0,256},{64,320},{128,384},{192,448},{256,0},{320,64},{384,128},{4... | collective-permute-start | bytes 98312 | tf_op jit(solution)/shard_map/ppermute | solution.py:22
Sparse Core Ops, SparseCore 0:
  10.1 82.0 all-gather.1

commit v12 on v10

--- a/solution.py
+++ b/solution.py
@@ -80,24 +80,15 @@
 
 
 def query_kernel(dp_ref, features, *refs):
-    blocks, (out, rows, columns, sems) = refs[:10], refs[10:]
-    cut = columns.shape[1] // 2
+    blocks, (out, rows, columns, sems) = refs[:N_BLOCKS], refs[N_BLOCKS:]
     copies = []
     for slot in range(N_BLOCKS):
-        group = [pltpu.make_async_copy(features.at[dp_ref[slot]], rows.at[slot], sems.at[0, slot])]
-        if slot // 2 == 2:
-            for part in range(2):
-                group.append(
-                    pltpu.make_async_copy(
-                        blocks[4 + 2 * part + slot % 2],
-                        columns.at[slot, pl.ds(part * cut, cut)],
-                        sems.at[1 + part, slot],
-                    )
-                )
-        else:
-            at = slot if slot < 4 else slot + 2
-            group.append(pltpu.make_async_copy(blocks[at], columns.at[slot], sems.at[1, slot]))
-        copies.append(group)
+        copies.append(
+            (
+                pltpu.make_async_copy(features.at[dp_ref[slot]], rows.at[slot], sems.at[0, slot]),
+                pltpu.make_async_copy(blocks[slot], columns.at[slot], sems.at[1, slot]),
+            )
+        )
     for group in copies[:DEPTH]:
         for copy in group:
             copy.start()
@@ -232,21 +223,20 @@
     arrived = lax.all_to_all(portions, "tensor", 0, 0)
 
     w, _ = lax.optimization_barrier((w_query[0], near_pairs))
-    cut = w.shape[0] // 2
-    before, behind = y_shift(w, 1), y_shift(w, -1)
-    across = (y_shift(before[:cut], 1), y_shift(behind[cut:], -1))
-    query_weights = [v for b in (w, before, *across, behind) for v in (b, core_swap(b))]
+    before, opposite, behind = y_shift(w, 1), y_shift(w, 2), y_shift(w, -1)
+    features, opposite, before = lax.optimization_barrier((features, opposite, before))
+    query_weights = [v for b in (w, before, opposite, behind) for v in (b, core_swap(b))]
 
     tokens, columns = hidden.shape[1], w_query.shape[2]
     query = call(
         query_kernel,
         jax.ShapeDtypeStruct((tokens, columns), BF16),
-        [SMEM] + [pl.BlockSpec(memory_space=pl.ANY)] * 11,
+        [SMEM] + [pl.BlockSpec(memory_space=pl.ANY)] * 9,
         (dp_order, features, *query_weights),
         [
             pltpu.VMEM(features.shape, BF16),
             pltpu.VMEM((N_BLOCKS, *w.shape), BF16),
-            pltpu.SemaphoreType.DMA((3, N_BLOCKS)),
+            pltpu.SemaphoreType.DMA((2, N_BLOCKS)),
         ],
         limit=60 << 20,
         cost=pl.CostEstimate(
@@ -262,7 +252,7 @@
         (query, arrived, score_bias, cotangent[0], gate_logit.reshape(1, 1)),
     )
 
-    by4, by1 = lax.optimization_barrier((t_swap(packed, 4), t_swap(packed, 1)))
+    by1, by4 = lax.optimization_barrier((t_swap(packed, 1), t_swap(packed, 4)))
     both = jnp.concatenate([packed, by4])
     by2, by5 = lax.optimization_barrier((t_swap(both, 2), t_swap(by4, 1)))
     by3 = t_swap(by2, 1)

time: 188 us -> 184 us (0.979)
  waiting for transfers between devices: 42.3 us -> 36.1 us
  starting transfers between devices: 93 us -> 97.8 us
  local copies, waits for them, and re-layouts: 4.6 us -> 2.42 us
    ppermute x5, starting transfers between devices: 21 us -> 25.6 us  [t_swap(): return lax.ppermute(a, 'tensor', [(t, t ^ k) for t in range(8)])]
    ppermute x2, starting transfers between devices: 21.2 us -> 25 us  [z_swap(): lax.ppermute(a, 'section', [(s, (s + X_SIZE) % (2 * X_SIZE)) for s in ran...]
    all_to_all x1, waiting for transfers between devices: 3.07 us -> 0.01 us  [local(): arrived = lax.all_to_all(portions, 'tensor', 0, 0)]
    ppermute x4 -> x3, waiting for transfers between devices: 9.05 us -> 11.8 us  [y_shift(): return lax.ppermute(a, 'dp', pairs)]
    ppermute x2, waiting for transfers between devices: 7.82 us -> 5.16 us  [z_swap(): lax.ppermute(a, 'section', [(s, (s + X_SIZE) % (2 * X_SIZE)) for s in ran...]
    ppermute x5, waiting for transfers between devices: 7.72 us -> 5.13 us  [t_swap(): return lax.ppermute(a, 'tensor', [(t, t ^ k) for t in range(8)])]
    ppermute x4 -> x3, starting transfers between devices: 12.7 us -> 10.4 us  [y_shift(): return lax.ppermute(a, 'dp', pairs)]
    slice x2 -> x0, local copies, waits for them, and re-layouts: 2.16 us -> none  [local(): across = (y_shift(before[:cut], 1), y_shift(behind[cut:], -1))]
  transfers between devices with their start and end apart: 21 -> 19, of which waited for: 13 -> 10; matrix products, arithmetic and copies ran while one was open for 1% -> 2% of each run, Pallas kernels for 7% -> 7%
where the time goes in v12:
time: 184 us; the launch traced here: 182 us
  starting transfers between devices  97.8 us (53%)
  waiting for transfers between devices  36.1 us (20%)
  Pallas kernels  17.5 us (10%)
  between operations  14.9 us (8%)
  blocking collectives  10.8 us (6%)
  local copies, waits for them, and re-layouts  2.42 us (1%)
  other arithmetic  2.27 us (1%)
    ppermute x5, starting transfers between devices, t_swap(): return lax.ppermute(a, 'tensor', [(t, t ^ k) for t in range(8)])  25.6 us
    ppermute x2, starting transfers between devices, z_swap(): lax.ppermute(a, 'section', [(s, (s + X_SIZE) % (2 * X_SIZE)) for s in ran...  25 us
    pallas_call x7, Pallas kernels, call(): pl.pallas_call(kernel, out_shape=outs, in_specs=in_specs, out_specs=jax.t...  17.5 us
    all_to_all x1, starting transfers between devices, local(): arrived = lax.all_to_all(portions, 'tensor', 0, 0)  12.5 us
    ppermute x3, waiting for transfers between devices, y_shift(): return lax.ppermute(a, 'dp', pairs)  11.8 us
    all_to_all x1, blocking collectives, x_exchange(): return lax.all_to_all(a, 'section', 0, 0, axis_index_groups=groups)  10.8 us
    ppermute x5, starting transfers between devices, core_swap(): return lax.ppermute(a, 'dp', [(d, d ^ 1) for d in range(2 * Y_SIZE)])  10.5 us
    ppermute x3, starting transfers between devices, y_shift(): return lax.ppermute(a, 'dp', pairs)  10.4 us
  transfers between devices with their start and end apart: 19, of which 10 were waited for; matrix products, arithmetic and copies ran while one was open for 2% of the time, Pallas kernels for 7%

profile of v12, /device:TPU:24, one launch (start us, length us, event | category | flops | bytes accessed | tf_op | source)
XLA Modules:
  0.0 181.7 jit_solution(17296640472124875108)
XLA Ops:
  7.2 0.0 all-gather.2.cloned.1.call-start
  7.2 0.7 all-gather.2.cloned.1.call-update
  7.9 1.1 pad_maximum_fusion
  9.0 1.5 broadcast_in_dim.16
  10.5 9.3 %all-to-all-start = ((bf16[4,1024,256]{2,1,0:T(8,128)(2,1)}), bf16[4,1024,256]{2,1,0:T(8,128)(2,1)S(1)}, u32[]{:S(2)}, u32[]{:S(2)}) async-start(bf16[4,1024,256]{2,1,0:T(8,128)(2,1)} %broadcast_in_dim.16), calls=%async_computation | async-start | bytes 4194304 | tf_op jit(solution)/shard_map/all_to_all | solution.py:42
  19.8 11.2 %collective-permute-start = (bf16[16,1024]{1,0:T(8,128)(2,1)S(1)}, bf16[16,1024]{1,0:T(8,128)(2,1)S(1)}, u32[]{:S(2)}, u32[]{:S(2)}) collective-permute-start(bf16[16,1024]{1,0:T(8,128)(2,1)S(1)} %bitcast.13), channel_id=1, source_target_pairs={{0,256},{64,320},{128,384},{192,448},{256,0},{320,64},{384,128},{4... | collective-permute-start | bytes 98312 | tf_op jit(solution)/shard_map/ppermute | solution.py:22
  31.0 3.3 %collective-permute-done.other = bf16[16,1024]{1,0:T(8,128)(2,1)S(1)} collective-permute-done((bf16[16,1024]{1,0:T(8,128)(2,1)S(1)}, bf16[16,1024]{1,0:T(8,128)(2,1)S(1)}, u32[]{:S(2)}, u32[]{:S(2)}) %collective-permute-start) | collective-permute-done | bytes 32800 | tf_op jit(solution)/shard_map/ppermute | solution.py:22
  34.3 5.3 %all-to-all-done.near = bf16[4,1024,256]{2,1,0:T(8,128)(2,1)S(1)} async-done(((bf16[4,1024,256]{2,1,0:T(8,128)(2,1)}), bf16[4,1024,256]{2,1,0:T(8,128)(2,1)S(1)}, u32[]{:S(2)}, u32[]{:S(2)}) %all-to-all-start) | async-done | bytes 2097184 | tf_op jit(solution)/shard_map/all_to_all | solution.py:42
  39.6 1.9 %collective-permute-start.8 = (bf16[4,1024,256]{2,1,0:T(8,128)(2,1)S(1)}, bf16[4,1024,256]{2,1,0:T(8,128)(2,1)}, u32[]{:S(2)}, u32[]{:S(2)}) collective-permute-start(bf16[4,1024,256]{2,1,0:T(8,128)(2,1)S(1)} %all-to-all-done.near), channel_id=1, source_target_pairs={{0,8},{8,0},{16,24},{24,16},{32,40},{40,32},{48,56},{56,48},{1,9},... | collective-permute-start | bytes 6291464 | tf_op jit(solution)/shard_map/ppermute | solution.py:46
  41.5 1.9 %collective-permute-start.6 = (bf16[1024,512]{1,0:T(8,128)(2,1)}, bf16[1024,512]{1,0:T(8,128)(2,1)}, u32[]{:S(2)}, u32[]{:S(2)}) collective-permute-start(bf16[1024,512]{1,0:T(8,128)(2,1)} %bitcast.refs_0_), channel_id=1, source_target_pairs={{0,48},{8,56},{16,0},{24,8},{32,16},{40,24},{48,32},{56,40},{1,49}... | collective-permute-start | bytes 3145736 | tf_op jit(solution)/shard_map/ppermute | solution.py:36
  43.4 5.4 %collective-permute-start.1 = (bf16[1024,512]{1,0:T(8,128)(2,1)}, bf16[1024,512]{1,0:T(8,128)(2,1)}, u32[]{:S(2)}, u32[]{:S(2)}) collective-permute-start(bf16[1024,512]{1,0:T(8,128)(2,1)} %bitcast.refs_0_), channel_id=1, source_target_pairs={{0,32},{8,40},{16,48},{24,56},{32,0},{40,8},{48,16},{56,24},{1,33}... | collective-permute-start | bytes 3145736 | tf_op jit(solution)/shard_map/ppermute | solution.py:36
  48.9 3.1 %collective-permute-start.2 = (bf16[1024,512]{1,0:T(8,128)(2,1)}, bf16[1024,512]{1,0:T(8,128)(2,1)}, u32[]{:S(2)}, u32[]{:S(2)}) collective-permute-start(bf16[1024,512]{1,0:T(8,128)(2,1)} %bitcast.refs_0_), channel_id=1, source_target_pairs={{0,16},{8,24},{16,32},{24,40},{32,48},{40,56},{48,0},{56,8},{1,17}... | collective-permute-start | bytes 3145736 | tf_op jit(solution)/shard_map/ppermute | solution.py:36
  51.9 0.7 shard_map.96
  52.7 4.3 %all-to-all-start.1 = ((bf16[4,2,16,1024]{3,2,1,0:T(8,128)(2,1)}), bf16[4,2,16,1024]{3,2,1,0:T(8,128)(2,1)S(1)}, u32[]{:S(2)}, u32[]{:S(2)}) async-start(bf16[4,2,16,1024]{3,2,1,0:T(8,128)(2,1)} %shard_map.96), calls=%async_computation.1 | async-start | bytes 524288 | tf_op jit(solution)/shard_map/all_to_all | solution.py:27
  57.0 6.7 %all-to-all-done.1.images = bf16[4,2,16,1024]{3,2,1,0:T(8,128)(2,1)S(1)} async-done(((bf16[4,2,16,1024]{3,2,1,0:T(8,128)(2,1)}), bf16[4,2,16,1024]{3,2,1,0:T(8,128)(2,1)S(1)}, u32[]{:S(2)}, u32[]{:S(2)}) %all-to-all-start.1) | async-done | bytes 262176 | tf_op jit(solution)/shard_map/all_to_all | solution.py:27
  63.7 0.0 collective-permute-done.8.far
  63.7 3.2 %shard_map.97 = bf16[8,128,256]{2,1,0:T(8,128)(2,1)} custom-call(s32[8]{0:T(128)S(1)} %iota_xor_fusion.head_ref, s32[1]{0:T(128)} %bitcast.4.half_ref, bf16[4,2,16,1024]{3,2,1,0:T(8,128)(2,1)S(1)} %all-to-all-done.1.images, bf16[4,1024,256]{2,1,0:T(8,128)(2,1)S(1)} %all-to-all-done.near, bf16[4,1024,256]{2,1,0:T(8,128)(2,1)} %collective-permute-done.8.far), custom_call_target="tpu_custom_call" | custom-call | tf_op jit(solution)/shard_map/pallas_call | solution.py:56
  66.8 12.5 %all-to-all-start.2 = ((bf16[8,128,256]{2,1,0:T(8,128)(2,1)}), bf16[8,128,256]{2,1,0:T(8,128)(2,1)S(1)}, u32[]{:S(2)}, u32[]{:S(2)}) async-start(bf16[8,128,256]{2,1,0:T(8,128)(2,1)} %shard_map.97), calls=%async_computation.2 | async-start | bytes 1048576 | tf_op jit(solution)/shard_map/all_to_all | solution.py:223
  79.3 1.9 %collective-permute-start.3 = (bf16[1024,512]{1,0:T(8,128)(2,1)}, bf16[1024,512]{1,0:T(8,128)(2,1)}, u32[]{:S(2)}, u32[]{:S(2)}) collective-permute-start(bf16[1024,512]{1,0:T(8,128)(2,1)} %bitcast.refs_0_), channel_id=1, source_target_pairs={{0,8},{8,0},{16,24},{24,16},{32,40},{40,32},{48,56},{56,48},{1,9},... | collective-permute-start | bytes 3145736 | tf_op jit(solution)/shard_map/ppermute | solution.py:46
  81.3 2.4 %collective-permute-start.7 = (bf16[1024,512]{1,0:T(8,128)(2,1)}, bf16[1024,512]{1,0:T(8,128)(2,1)}, u32[]{:S(2)}, u32[]{:S(2)}) collective-permute-start(bf16[1024,512]{1,0:T(8,128)(2,1)} %collective-permute-done.6.refs_6_), channel_id=1, source_target_pairs={{0,8},{8,0},{16,24},{24,16},{32,40},{40,32},{48,56},{56,48},{1,9},... | collective-permute-start | bytes 3145736 | tf_op jit(solution)/shard_map/ppermute | solution.py:46
  83.7 9.6 %collective-permute-done.1.refs_4_ = bf16[1024,512]{1,0:T(8,128)(2,1)} collective-permute-done((bf16[1024,512]{1,0:T(8,128)(2,1)}, bf16[1024,512]{1,0:T(8,128)(2,1)}, u32[]{:S(2)}, u32[]{:S(2)}) %collective-permute-start.1) | collective-permute-done | bytes 1048608 | tf_op jit(solution)/shard_map/ppermute | solution.py:36
  93.2 2.2 %collective-permute-done.2.refs_2_ = bf16[1024,512]{1,0:T(8,128)(2,1)} collective-permute-done((bf16[1024,512]{1,0:T(8,128)(2,1)}, bf16[1024,512]{1,0:T(8,128)(2,1)}, u32[]{:S(2)}, u32[]{:S(2)}) %collective-permute-start.2) | collective-permute-done | bytes 1048608 | tf_op jit(solution)/shard_map/ppermute | solution.py:36
  95.5 1.9 %collective-permute-start.4 = (bf16[1024,512]{1,0:T(8,128)(2,1)}, bf16[1024,512]{1,0:T(8,128)(2,1)}, u32[]{:S(2)}, u32[]{:S(2)}) collective-permute-start(bf16[1024,512]{1,0:T(8,128)(2,1)} %collective-permute-done.2.refs_2_), channel_id=1, source_target_pairs={{0,8},{8,0},{16,24},{24,16},{32,40},{40,32},{48,56},{56,48},{1,9},... | collective-permute-start | bytes 3145736 | tf_op jit(solution)/shard_map/ppermute | solution.py:46
  97.4 2.4 %collective-permute-start.5 = (bf16[1024,512]{1,0:T(8,128)(2,1)}, bf16[1024,512]{1,0:T(8,128)(2,1)}, u32[]{:S(2)}, u32[]{:S(2)}) collective-permute-start(bf16[1024,512]{1,0:T(8,128)(2,1)} %collective-permute-done.1.refs_4_), channel_id=1, source_target_pairs={{0,8},{8,0},{16,24},{24,16},{32,40},{40,32},{48,56},{56,48},{1,9},... | collective-permute-start | bytes 3145736 | tf_op jit(solution)/shard_map/ppermute | solution.py:46
  100.5 0.5 and_or_fusion.dp_ref
  101.0 0.0 collective-permute-done.3.refs_1_
  101.0 0.0 collective-permute-done.7.refs_7_
  101.0 1.4 collective-permute-done.5.refs_5_
  102.4 6.5 %shard_map.95.query = bf16[160,512]{1,0:T(8,128)(2,1)} custom-call(s32[8]{0:T(128)} %and_or_fusion.dp_ref, bf16[8,160,1024]{2,1,0:T(8,128)(2,1)} %all-gather.2.cloned.1.call-done.features, bf16[1024,512]{1,0:T(8,128)(2,1)} %bitcast.refs_0_, bf16[1024,512]{1,0:T(8,128)(2,1)} %collective-permute-done.3.refs_1_, ...), custom_call_target="tpu_custom_call" | custom-call | flops 1342177280 | bytes 11010048 | tf_op jit(solution)/shard_map/pallas_call | solution.py:56
  109.0 0.0 all-to-all-done.2.arrived
  109.0 0.0 copy-start
  109.0 0.9 copy-done
  109.9 2.1 %shard_map.98 = (bf16[160,512]{1,0:T(8,128)(2,1)}, bf16[1,128,256]{2,1,0:T(8,128)(2,1)S(1)}) custom-call(bf16[160,512]{1,0:T(8,128)(2,1)S(1)} %copy-done, bf16[8,128,256]{2,1,0:T(8,128)(2,1)S(1)} %all-to-all-done.2.arrived, f32[160,128]{1,0:T(8,128)S(1)} %copy-done.2, bf16[160,512]{1,0:T(8,128)(2,1)S(1)} %bitcast.12, f32[1,1]{1,0:T(1,128)} %bitcast.11.gate), custom_call_target="tpu_custom_call" | custom-call | tf_op jit(solution)/shard_map/pallas_call | solution.py:56
  112.1 9.1 %collective-permute-start.10 = (bf16[1,128,256]{2,1,0:T(8,128)(2,1)S(1)}, bf16[1,128,256]{2,1,0:T(8,128)(2,1)S(1)}, u32[]{:S(2)}, u32[]{:S(2)}) collective-permute-start(bf16[1,128,256]{2,1,0:T(8,128)(2,1)S(1)} %get-tuple-element.23.own), channel_id=1, source_target_pairs={{0,4},{1,5},{2,6},{3,7},{4,0},{5,1},{6,2},{7,3},{8,12},{9,13},{10,... | collective-permute-start | bytes 196616 | tf_op jit(solution)/shard_map/ppermute | solution.py:31
  121.2 3.8 %collective-permute-start.9 = (bf16[1,128,256]{2,1,0:T(8,128)(2,1)S(1)}, bf16[1,128,256]{2,1,0:T(8,128)(2,1)S(1)}, u32[]{:S(2)}, u32[]{:S(2)}) collective-permute-start(bf16[1,128,256]{2,1,0:T(8,128)(2,1)S(1)} %get-tuple-element.23.own), channel_id=1, source_target_pairs={{0,1},{1,0},{2,3},{3,2},{4,5},{5,4},{6,7},{7,6},{8,9},{9,8},{10,11... | collective-permute-start | bytes 196616 | tf_op jit(solution)/shard_map/ppermute | solution.py:31
  125.0 0.0 collective-permute-done.10.by4
  125.0 2.3 %collective-permute-done.9.by1 = bf16[1,128,256]{2,1,0:T(8,128)(2,1)S(1)} collective-permute-done((bf16[1,128,256]{2,1,0:T(8,128)(2,1)S(1)}, bf16[1,128,256]{2,1,0:T(8,128)(2,1)S(1)}, u32[]{:S(2)}, u32[]{:S(2)}) %collective-permute-start.9) | collective-permute-done | bytes 65568 | tf_op jit(solution)/shard_map/ppermute | solution.py:31
  127.3 5.2 %collective-permute-start.11 = (bf16[2,128,256]{2,1,0:T(8,128)(2,1)S(1)}, bf16[2,128,256]{2,1,0:T(8,128)(2,1)S(1)}, u32[]{:S(2)}, u32[]{:S(2)}) collective-permute-start(bf16[2,128,256]{2,1,0:T(8,128)(2,1)S(1)} %pad_maximum_fusion.1), channel_id=1, source_target_pairs={{0,2},{1,3},{2,0},{3,1},{4,6},{5,7},{6,4},{7,5},{8,10},{9,11},{10,... | collective-permute-start | bytes 393224 | tf_op jit(solution)/shard_map/ppermute | solution.py:31
  132.5 3.8 %collective-permute-start.12 = (bf16[1,128,256]{2,1,0:T(8,128)(2,1)S(1)}, bf16[1,128,256]{2,1,0:T(8,128)(2,1)S(1)}, u32[]{:S(2)}, u32[]{:S(2)}) collective-permute-start(bf16[1,128,256]{2,1,0:T(8,128)(2,1)S(1)} %collective-permute-done.10.by4), channel_id=1, source_target_pairs={{0,1},{1,0},{2,3},{3,2},{4,5},{5,4},{6,7},{7,6},{8,9},{9,8},{10,11... | collective-permute-start | bytes 196616 | tf_op jit(solution)/shard_map/ppermute | solution.py:31
  136.4 2.4 %collective-permute-done.12.by5 = bf16[1,128,256]{2,1,0:T(8,128)(2,1)S(1)} collective-permute-done((bf16[1,128,256]{2,1,0:T(8,128)(2,1)S(1)}, bf16[1,128,256]{2,1,0:T(8,128)(2,1)S(1)}, u32[]{:S(2)}, u32[]{:S(2)}) %collective-permute-start.12) | collective-permute-done | bytes 65568 | tf_op jit(solution)/shard_map/ppermute | solution.py:31
  138.8 3.7 %collective-permute-start.13 = (bf16[2,128,256]{2,1,0:T(8,128)(2,1)S(1)}, bf16[2,128,256]{2,1,0:T(8,128)(2,1)S(1)}, u32[]{:S(2)}, u32[]{:S(2)}) collective-permute-start(bf16[2,128,256]{2,1,0:T(8,128)(2,1)S(1)} %collective-permute-done.11.by2), channel_id=1, source_target_pairs={{0,1},{1,0},{2,3},{3,2},{4,5},{5,4},{6,7},{7,6},{8,9},{9,8},{10,11... | collective-permute-start | bytes 393224 | tf_op jit(solution)/shard_map/ppermute | solution.py:31
  142.5 2.7 %shard_map.99.early = f32[128,1024]{1,0:T(8,128)S(1)} custom-call(s32[8]{0:T(128)S(1)} %xor_shift-right-arithmetic_fusion.y_ref, s32[1]{0:T(128)} %bitcast.8.flip_ref, bf16[1,128,256]{2,1,0:T(8,128)(2,1)S(1)} %get-tuple-element.23.own, bf16[1,128,256]{2,1,0:T(8,128)(2,1)S(1)} %collective-permute-done.10.by4, ...), custom_call_target="tpu_custom_call" | custom-call | flops 402653184 | bytes 5111808 | tf_op jit(solution)/shard_map/pallas_call | solution.py:56
  145.3 0.4 collective-permute-done.13.by3
  145.7 2.1 %shard_map.100 = bf16[4,2,16,1024]{3,2,1,0:T(8,128)(2,1)S(1)} custom-call(s32[8]{0:T(128)S(1)} %xor_shift-right-arithmetic_fusion.y_ref, s32[1]{0:T(128)} %bitcast.8.flip_ref, s32[1]{0:T(128)} %bitcast.4.half_ref, f32[128,1024]{1,0:T(8,128)S(1)} %shard_map.99.early, bf16[2,128,256]{2,1,0:T(8,128)(2,1)S(1)} %collective-permute-done.13.by3, ...), custom_call_target="tpu_custom_call" | custom-call | tf_op jit(solution)/shard_map/pallas_call | solution.py:56
  147.8 10.8 %all_to_all.20.arrived = bf16[4,2,16,1024]{3,2,1,0:T(8,128)(2,1)S(1)} all-to-all(bf16[4,2,16,1024]{3,2,1,0:T(8,128)(2,1)S(1)} %shard_map.100), channel_id=1, replica_groups={{0,64,128,192},{256,320,384,448},{1,65,129,193},{257,321,385,449},{2,66..., dimensions={0} | all-to-all | bytes 524288 | tf_op jit(solution)/shard_map/all_to_all | solution.py:27
  158.6 13.8 %collective-permute-start.14 = (bf16[16,1024]{1,0:T(8,128)(2,1)S(1)}, bf16[16,1024]{1,0:T(8,128)(2,1)S(1)}, u32[]{:S(2)}, u32[]{:S(2)}) collective-permute-start(bf16[16,1024]{1,0:T(8,128)(2,1)S(1)} %get-tuple-element.29), channel_id=1, source_target_pairs={{0,256},{64,320},{128,384},{192,448},{256,0},{320,64},{384,128},{4... | collective-permute-start | bytes 98312 | tf_op jit(solution)/shard_map/ppermute | solution.py:22
  172.4 1.9 %collective-permute-done.14 = bf16[16,1024]{1,0:T(8,128)(2,1)S(1)} collective-permute-done((bf16[16,1024]{1,0:T(8,128)(2,1)S(1)}, bf16[16,1024]{1,0:T(8,128)(2,1)S(1)}, u32[]{:S(2)}, u32[]{:S(2)}) %collective-permute-start.14) | collective-permute-done | bytes 32800 | tf_op jit(solution)/shard_map/ppermute | solution.py:22
  174.3 0.6 add_bitcast_fusion
  (14 shorter events, 0.1 us)
Async XLA Ops:
  7.2 88.3 %all-gather.2.cloned.1.call-start = ((), (), s32[]{:S(2)}) async-start(), calls=%async_computation.4 | async-start | bytes 2949120 | tf_op jit(solution)/shard_map/all_gather | solution.py:200
  10.5 9.3 %copy-start.3 = (bf16[1,16,1024]{2,1,0:T(8,128)(2,1)S(1)}, bf16[1,16,1024]{2,1,0:T(8,128)(2,1)}, u32[]{:S(2)}) copy-start(bf16[1,16,1024]{2,1,0:T(8,128)(2,1)} %param.12) | copy-start | bytes 98308
  10.5 29.1 %all-to-all-start = ((bf16[4,1024,256]{2,1,0:T(8,128)(2,1)}), bf16[4,1024,256]{2,1,0:T(8,128)(2,1)S(1)}, u32[]{:S(2)}, u32[]{:S(2)}) async-start(bf16[4,1024,256]{2,1,0:T(8,128)(2,1)} %broadcast_in_dim.16), calls=%async_computation | async-start | bytes 4194304 | tf_op jit(solution)/shard_map/all_to_all | solution.py:42
  19.8 14.5 %collective-permute-start = (bf16[16,1024]{1,0:T(8,128)(2,1)S(1)}, bf16[16,1024]{1,0:T(8,128)(2,1)S(1)}, u32[]{:S(2)}, u32[]{:S(2)}) collective-permute-start(bf16[16,1024]{1,0:T(8,128)(2,1)S(1)} %bitcast.13), channel_id=1, source_target_pairs={{0,256},{64,320},{128,384},{192,448},{256,0},{320,64},{384,128},{4... | collective-permute-start | bytes 98312 | tf_op jit(solution)/shard_map/ppermute | solution.py:22
  39.6 24.1 %collective-permute-start.8 = (bf16[4,1024,256]{2,1,0:T(8,128)(2,1)S(1)}, bf16[4,1024,256]{2,1,0:T(8,128)(2,1)}, u32[]{:S(2)}, u32[]{:S(2)}) collective-permute-start(bf16[4,1024,256]{2,1,0:T(8,128)(2,1)S(1)} %all-to-all-done.near), channel_id=1, source_target_pairs={{0,8},{8,0},{16,24},{24,16},{32,40},{40,32},{48,56},{56,48},{1,9},... | collective-permute-start | bytes 6291464 | tf_op jit(solution)/shard_map/ppermute | solution.py:46
  41.5 39.8 %collective-permute-start.6 = (bf16[1024,512]{1,0:T(8,128)(2,1)}, bf16[1024,512]{1,0:T(8,128)(2,1)}, u32[]{:S(2)}, u32[]{:S(2)}) collective-permute-start(bf16[1024,512]{1,0:T(8,128)(2,1)} %bitcast.refs_0_), channel_id=1, source_target_pairs={{0,48},{8,56},{16,0},{24,8},{32,16},{40,24},{48,32},{56,40},{1,49}... | collective-permute-start | bytes 3145736 | tf_op jit(solution)/shard_map/ppermute | solution.py:36
  43.4 49.8 %collective-permute-start.1 = (bf16[1024,512]{1,0:T(8,128)(2,1)}, bf16[1024,512]{1,0:T(8,128)(2,1)}, u32[]{:S(2)}, u32[]{:S(2)}) collective-permute-start(bf16[1024,512]{1,0:T(8,128)(2,1)} %bitcast.refs_0_), channel_id=1, source_target_pairs={{0,32},{8,40},{16,48},{24,56},{32,0},{40,8},{48,16},{56,24},{1,33}... | collective-permute-start | bytes 3145736 | tf_op jit(solution)/shard_map/ppermute | solution.py:36
  48.9 46.6 %collective-permute-start.2 = (bf16[1024,512]{1,0:T(8,128)(2,1)}, bf16[1024,512]{1,0:T(8,128)(2,1)}, u32[]{:S(2)}, u32[]{:S(2)}) collective-permute-start(bf16[1024,512]{1,0:T(8,128)(2,1)} %bitcast.refs_0_), channel_id=1, source_target_pairs={{0,16},{8,24},{16,32},{24,40},{32,48},{40,56},{48,0},{56,8},{1,17}... | collective-permute-start | bytes 3145736 | tf_op jit(solution)/shard_map/ppermute | solution.py:36
  52.7 11.0 %all-to-all-start.1 = ((bf16[4,2,16,1024]{3,2,1,0:T(8,128)(2,1)}), bf16[4,2,16,1024]{3,2,1,0:T(8,128)(2,1)S(1)}, u32[]{:S(2)}, u32[]{:S(2)}) async-start(bf16[4,2,16,1024]{3,2,1,0:T(8,128)(2,1)} %shard_map.96), calls=%async_computation.1 | async-start | bytes 524288 | tf_op jit(solution)/shard_map/all_to_all | solution.py:27
  66.8 42.2 %all-to-all-start.2 = ((bf16[8,128,256]{2,1,0:T(8,128)(2,1)}), bf16[8,128,256]{2,1,0:T(8,128)(2,1)S(1)}, u32[]{:S(2)}, u32[]{:S(2)}) async-start(bf16[8,128,256]{2,1,0:T(8,128)(2,1)} %shard_map.97), calls=%async_computation.2 | async-start | bytes 1048576 | tf_op jit(solution)/shard_map/all_to_all | solution.py:223
  79.3 21.7 %collective-permute-start.3 = (bf16[1024,512]{1,0:T(8,128)(2,1)}, bf16[1024,512]{1,0:T(8,128)(2,1)}, u32[]{:S(2)}, u32[]{:S(2)}) collective-permute-start(bf16[1024,512]{1,0:T(8,128)(2,1)} %bitcast.refs_0_), channel_id=1, source_target_pairs={{0,8},{8,0},{16,24},{24,16},{32,40},{40,32},{48,56},{56,48},{1,9},... | collective-permute-start | bytes 3145736 | tf_op jit(solution)/shard_map/ppermute | solution.py:46
  81.3 19.7 %collective-permute-start.7 = (bf16[1024,512]{1,0:T(8,128)(2,1)}, bf16[1024,512]{1,0:T(8,128)(2,1)}, u32[]{:S(2)}, u32[]{:S(2)}) collective-permute-start(bf16[1024,512]{1,0:T(8,128)(2,1)} %collective-permute-done.6.refs_6_), channel_id=1, source_target_pairs={{0,8},{8,0},{16,24},{24,16},{32,40},{40,32},{48,56},{56,48},{1,9},... | collective-permute-start | bytes 3145736 | tf_op jit(solution)/shard_map/ppermute | solution.py:46
  95.5 5.5 %collective-permute-start.4 = (bf16[1024,512]{1,0:T(8,128)(2,1)}, bf16[1024,512]{1,0:T(8,128)(2,1)}, u32[]{:S(2)}, u32[]{:S(2)}) collective-permute-start(bf16[1024,512]{1,0:T(8,128)(2,1)} %collective-permute-done.2.refs_2_), channel_id=1, source_target_pairs={{0,8},{8,0},{16,24},{24,16},{32,40},{40,32},{48,56},{56,48},{1,9},... | collective-permute-start | bytes 3145736 | tf_op jit(solution)/shard_map/ppermute | solution.py:46
  97.4 5.0 %collective-permute-start.5 = (bf16[1024,512]{1,0:T(8,128)(2,1)}, bf16[1024,512]{1,0:T(8,128)(2,1)}, u32[]{:S(2)}, u32[]{:S(2)}) collective-permute-start(bf16[1024,512]{1,0:T(8,128)(2,1)} %collective-permute-done.1.refs_4_), channel_id=1, source_target_pairs={{0,8},{8,0},{16,24},{24,16},{32,40},{40,32},{48,56},{56,48},{1,9},... | collective-permute-start | bytes 3145736 | tf_op jit(solution)/shard_map/ppermute | solution.py:46
  101.0 8.0 %copy-start.1 = (bf16[1,160,512]{2,1,0:T(8,128)(2,1)S(1)}, bf16[1,160,512]{2,1,0:T(8,128)(2,1)}, u32[]{:S(2)}) copy-start(bf16[1,160,512]{2,1,0:T(8,128)(2,1)} %param.15) | copy-start | bytes 491524
  101.0 8.0 %copy-start.2 = (f32[160,128]{1,0:T(8,128)S(1)}, f32[160,128]{1,0:T(8,128)}, u32[]{:S(2)}) copy-start(f32[160,128]{1,0:T(8,128)} %bias_ref.1) | copy-start | bytes 245764
  109.0 0.9 copy-start
  112.1 12.9 %collective-permute-start.10 = (bf16[1,128,256]{2,1,0:T(8,128)(2,1)S(1)}, bf16[1,128,256]{2,1,0:T(8,128)(2,1)S(1)}, u32[]{:S(2)}, u32[]{:S(2)}) collective-permute-start(bf16[1,128,256]{2,1,0:T(8,128)(2,1)S(1)} %get-tuple-element.23.own), channel_id=1, source_target_pairs={{0,4},{1,5},{2,6},{3,7},{4,0},{5,1},{6,2},{7,3},{8,12},{9,13},{10,... | collective-permute-start | bytes 196616 | tf_op jit(solution)/shard_map/ppermute | solution.py:31
  121.2 6.2 %collective-permute-start.9 = (bf16[1,128,256]{2,1,0:T(8,128)(2,1)S(1)}, bf16[1,128,256]{2,1,0:T(8,128)(2,1)S(1)}, u32[]{:S(2)}, u32[]{:S(2)}) collective-permute-start(bf16[1,128,256]{2,1,0:T(8,128)(2,1)S(1)} %get-tuple-element.23.own), channel_id=1, source_target_pairs={{0,1},{1,0},{2,3},{3,2},{4,5},{5,4},{6,7},{7,6},{8,9},{9,8},{10,11... | collective-permute-start | bytes 196616 | tf_op jit(solution)/shard_map/ppermute | solution.py:31
  127.3 11.5 %collective-permute-start.11 = (bf16[2,128,256]{2,1,0:T(8,128)(2,1)S(1)}, bf16[2,128,256]{2,1,0:T(8,128)(2,1)S(1)}, u32[]{:S(2)}, u32[]{:S(2)}) collective-permute-start(bf16[2,128,256]{2,1,0:T(8,128)(2,1)S(1)} %pad_maximum_fusion.1), channel_id=1, source_target_pairs={{0,2},{1,3},{2,0},{3,1},{4,6},{5,7},{6,4},{7,5},{8,10},{9,11},{10,... | collective-permute-start | bytes 393224 | tf_op jit(solution)/shard_map/ppermute | solution.py:31
  132.5 6.3 %collective-permute-start.12 = (bf16[1,128,256]{2,1,0:T(8,128)(2,1)S(1)}, bf16[1,128,256]{2,1,0:T(8,128)(2,1)S(1)}, u32[]{:S(2)}, u32[]{:S(2)}) collective-permute-start(bf16[1,128,256]{2,1,0:T(8,128)(2,1)S(1)} %collective-permute-done.10.by4), channel_id=1, source_target_pairs={{0,1},{1,0},{2,3},{3,2},{4,5},{5,4},{6,7},{7,6},{8,9},{9,8},{10,11... | collective-permute-start | bytes 196616 | tf_op jit(solution)/shard_map/ppermute | solution.py:31
  138.8 6.9 %collective-permute-start.13 = (bf16[2,128,256]{2,1,0:T(8,128)(2,1)S(1)}, bf16[2,128,256]{2,1,0:T(8,128)(2,1)S(1)}, u32[]{:S(2)}, u32[]{:S(2)}) collective-permute-start(bf16[2,128,256]{2,1,0:T(8,128)(2,1)S(1)} %collective-permute-done.11.by2), channel_id=1, source_target_pairs={{0,1},{1,0},{2,3},{3,2},{4,5},{5,4},{6,7},{7,6},{8,9},{9,8},{10,11... | collective-permute-start | bytes 393224 | tf_op jit(solution)/shard_map/ppermute | solution.py:31
  158.6 15.7 %collective-permute-start.14 = (bf16[16,1024]{1,0:T(8,128)(2,1)S(1)}, bf16[16,1024]{1,0:T(8,128)(2,1)S(1)}, u32[]{:S(2)}, u32[]{:S(2)}) collective-permute-start(bf16[16,1024]{1,0:T(8,128)(2,1)S(1)} %get-tuple-element.29), channel_id=1, source_target_pairs={{0,256},{64,320},{128,384},{192,448},{256,0},{320,64},{384,128},{4... | collective-permute-start | bytes 98312 | tf_op jit(solution)/shard_map/ppermute | solution.py:22
Sparse Core Ops, SparseCore 0:
  10.1 79.3 all-gather.1

commit v13 on v12

--- a/solution.py
+++ b/solution.py
@@ -79,8 +79,9 @@
         out[head_ref[slot]] = dot(rows, weights).astype(BF16)
 
 
-def query_kernel(dp_ref, features, *refs):
-    blocks, (out, rows, columns, sems) = refs[:N_BLOCKS], refs[N_BLOCKS:]
+def attention_kernel(dp_ref, features, *refs):
+    blocks, refs = refs[:N_BLOCKS], refs[N_BLOCKS:]
+    arrived, bias_ref, cotangent, gate, gated, packed, rows, columns, sems = refs
     copies = []
     for slot in range(N_BLOCKS):
         copies.append(
@@ -101,10 +102,8 @@
                 copy.start()
         part = dot(rows[slot], columns[slot])
         total = part if total is None else total + part
-    out[...] = total.astype(BF16)
-
-
-def attention_kernel(query, arrived, bias_ref, cotangent, gate, gated, packed):
+    query = total.astype(BF16)
+
     pairs = jnp.sum(arrived[...].astype(F32), axis=0).astype(BF16)
     keys, values = pairs[:, :HEAD_SIZE], pairs[:, HEAD_SIZE:]
     scaling = HEAD_SIZE ** (-0.5)
@@ -228,11 +227,19 @@
     query_weights = [v for b in (w, before, opposite, behind) for v in (b, core_swap(b))]
 
     tokens, columns = hidden.shape[1], w_query.shape[2]
-    query = call(
-        query_kernel,
-        jax.ShapeDtypeStruct((tokens, columns), BF16),
-        [SMEM] + [pl.BlockSpec(memory_space=pl.ANY)] * 9,
-        (dp_order, features, *query_weights),
+    gated_out, packed = call(
+        attention_kernel,
+        (jax.ShapeDtypeStruct((tokens, columns), BF16), jax.ShapeDtypeStruct((1, *block), BF16)),
+        [SMEM] + [pl.BlockSpec(memory_space=pl.ANY)] * 9 + [VMEM] * 4,
+        (
+            dp_order,
+            features,
+            *query_weights,
+            arrived,
+            score_bias,
+            cotangent[0],
+            gate_logit.reshape(1, 1),
+        ),
         [
             pltpu.VMEM(features.shape, BF16),
             pltpu.VMEM((N_BLOCKS, *w.shape), BF16),
@@ -244,12 +251,6 @@
             bytes_accessed=2 * N_BLOCKS * (w.size + hidden.size),
             transcendentals=0,
         ),
-    )
-    gated_out, packed = call(
-        attention_kernel,
-        (jax.ShapeDtypeStruct((tokens, columns), BF16), jax.ShapeDtypeStruct((1, *block), BF16)),
-        [VMEM] * 5,
-        (query, arrived, score_bias, cotangent[0], gate_logit.reshape(1, 1)),
     )
 
     by1, by4 = lax.optimization_barrier((t_swap(packed, 1), t_swap(packed, 4)))

time: 184 us -> 186 us (1.011)
  waiting for transfers between devices: 36.1 us -> 52.3 us
  starting transfers between devices: 97.8 us -> 82.3 us
    ppermute x5, starting transfers between devices: 25.6 us -> 13.9 us  [t_swap(): return lax.ppermute(a, 'tensor', [(t, t ^ k) for t in range(8)])]
    all_to_all x1, waiting for transfers between devices: 0.01 us -> 7.77 us  [local(): arrived = lax.all_to_all(portions, 'tensor', 0, 0)]
    ppermute x5, waiting for transfers between devices: 5.13 us -> 11.7 us  [t_swap(): return lax.ppermute(a, 'tensor', [(t, t ^ k) for t in range(8)])]
    ppermute x2, starting transfers between devices: 25 us -> 21.2 us  [z_swap(): lax.ppermute(a, 'section', [(s, (s + X_SIZE) % (2 * X_SIZE)) for s in ran...]
    ppermute x2, waiting for transfers between devices: 5.16 us -> 8.43 us  [z_swap(): lax.ppermute(a, 'section', [(s, (s + X_SIZE) % (2 * X_SIZE)) for s in ran...]
    pallas_call x7 -> x6, Pallas kernels: 17.5 us -> 17.5 us  [call(): pl.pallas_call(kernel, out_shape=outs, in_specs=in_specs, out_specs=jax.t...]
  transfers between devices with their start and end apart: 19 -> 19, of which waited for: 10 -> 10; matrix products, arithmetic and copies ran while one was open for 2% -> 2% of each run, Pallas kernels for 7% -> 4%
where the time goes in v13:
time: 186 us; the launch traced here: 185 us
  starting transfers between devices  82.3 us (44%)
  waiting for transfers between devices  52.3 us (28%)
  Pallas kernels  17.5 us (9%)
  between operations  14.9 us (8%)
  blocking collectives  11.9 us (6%)
  local copies, waits for them, and re-layouts  3.15 us (2%)
  other arithmetic  3.09 us (2%)
    ppermute x2, starting transfers between devices, z_swap(): lax.ppermute(a, 'section', [(s, (s + X_SIZE) % (2 * X_SIZE)) for s in ran...  21.2 us
    pallas_call x6, Pallas kernels, call(): pl.pallas_call(kernel, out_shape=outs, in_specs=in_specs, out_specs=jax.t...  17.5 us
    ppermute x5, starting transfers between devices, t_swap(): return lax.ppermute(a, 'tensor', [(t, t ^ k) for t in range(8)])  13.9 us
    all_to_all x1, starting transfers between devices, local(): arrived = lax.all_to_all(portions, 'tensor', 0, 0)  12.5 us
    all_to_all x1, blocking collectives, x_exchange(): return lax.all_to_all(a, 'section', 0, 0, axis_index_groups=groups)  11.9 us
    ppermute x3, waiting for transfers between devices, y_shift(): return lax.ppermute(a, 'dp', pairs)  11.8 us
    ppermute x5, waiting for transfers between devices, t_swap(): return lax.ppermute(a, 'tensor', [(t, t ^ k) for t in range(8)])  11.7 us
    ppermute x5, starting transfers between devices, core_swap(): return lax.ppermute(a, 'dp', [(d, d ^ 1) for d in range(2 * Y_SIZE)])  10.5 us
  transfers between devices with their start and end apart: 19, of which 10 were waited for; matrix products, arithmetic and copies ran while one was open for 2% of the time, Pallas kernels for 4%

profile of v13, /device:TPU:24, one launch (start us, length us, event | category | flops | bytes accessed | tf_op | source)
XLA Modules:
  0.0 185.2 jit_solution(13069323441121466735)
XLA Ops:
  7.2 0.0 all-gather.2.cloned.1.call-start
  7.2 0.7 all-gather.2.cloned.1.call-update
  7.9 1.1 pad_maximum_fusion
  9.0 1.5 broadcast_in_dim.16
  10.5 9.3 %all-to-all-start = ((bf16[4,1024,256]{2,1,0:T(8,128)(2,1)}), bf16[4,1024,256]{2,1,0:T(8,128)(2,1)S(1)}, u32[]{:S(2)}, u32[]{:S(2)}) async-start(bf16[4,1024,256]{2,1,0:T(8,128)(2,1)} %broadcast_in_dim.16), calls=%async_computation | async-start | bytes 4194304 | tf_op jit(solution)/shard_map/all_to_all | solution.py:42
  19.8 11.2 %collective-permute-start = (bf16[16,1024]{1,0:T(8,128)(2,1)S(1)}, bf16[16,1024]{1,0:T(8,128)(2,1)S(1)}, u32[]{:S(2)}, u32[]{:S(2)}) collective-permute-start(bf16[16,1024]{1,0:T(8,128)(2,1)S(1)} %bitcast.12), channel_id=1, source_target_pairs={{0,256},{64,320},{128,384},{192,448},{256,0},{320,64},{384,128},{4... | collective-permute-start | bytes 98312 | tf_op jit(solution)/shard_map/ppermute | solution.py:22
  31.0 3.3 %collective-permute-done.other = bf16[16,1024]{1,0:T(8,128)(2,1)S(1)} collective-permute-done((bf16[16,1024]{1,0:T(8,128)(2,1)S(1)}, bf16[16,1024]{1,0:T(8,128)(2,1)S(1)}, u32[]{:S(2)}, u32[]{:S(2)}) %collective-permute-start) | collective-permute-done | bytes 32800 | tf_op jit(solution)/shard_map/ppermute | solution.py:22
  34.3 5.3 %all-to-all-done.near = bf16[4,1024,256]{2,1,0:T(8,128)(2,1)S(1)} async-done(((bf16[4,1024,256]{2,1,0:T(8,128)(2,1)}), bf16[4,1024,256]{2,1,0:T(8,128)(2,1)S(1)}, u32[]{:S(2)}, u32[]{:S(2)}) %all-to-all-start) | async-done | bytes 2097184 | tf_op jit(solution)/shard_map/all_to_all | solution.py:42
  39.6 1.9 %collective-permute-start.8 = (bf16[4,1024,256]{2,1,0:T(8,128)(2,1)S(1)}, bf16[4,1024,256]{2,1,0:T(8,128)(2,1)}, u32[]{:S(2)}, u32[]{:S(2)}) collective-permute-start(bf16[4,1024,256]{2,1,0:T(8,128)(2,1)S(1)} %all-to-all-done.near), channel_id=1, source_target_pairs={{0,8},{8,0},{16,24},{24,16},{32,40},{40,32},{48,56},{56,48},{1,9},... | collective-permute-start | bytes 6291464 | tf_op jit(solution)/shard_map/ppermute | solution.py:46
  41.5 1.9 %collective-permute-start.6 = (bf16[1024,512]{1,0:T(8,128)(2,1)}, bf16[1024,512]{1,0:T(8,128)(2,1)}, u32[]{:S(2)}, u32[]{:S(2)}) collective-permute-start(bf16[1024,512]{1,0:T(8,128)(2,1)} %bitcast.refs_0_), channel_id=1, source_target_pairs={{0,48},{8,56},{16,0},{24,8},{32,16},{40,24},{48,32},{56,40},{1,49}... | collective-permute-start | bytes 3145736 | tf_op jit(solution)/shard_map/ppermute | solution.py:36
  43.4 5.4 %collective-permute-start.1 = (bf16[1024,512]{1,0:T(8,128)(2,1)}, bf16[1024,512]{1,0:T(8,128)(2,1)}, u32[]{:S(2)}, u32[]{:S(2)}) collective-permute-start(bf16[1024,512]{1,0:T(8,128)(2,1)} %bitcast.refs_0_), channel_id=1, source_target_pairs={{0,32},{8,40},{16,48},{24,56},{32,0},{40,8},{48,16},{56,24},{1,33}... | collective-permute-start | bytes 3145736 | tf_op jit(solution)/shard_map/ppermute | solution.py:36
  48.9 3.1 %collective-permute-start.2 = (bf16[1024,512]{1,0:T(8,128)(2,1)}, bf16[1024,512]{1,0:T(8,128)(2,1)}, u32[]{:S(2)}, u32[]{:S(2)}) collective-permute-start(bf16[1024,512]{1,0:T(8,128)(2,1)} %bitcast.refs_0_), channel_id=1, source_target_pairs={{0,16},{8,24},{16,32},{24,40},{32,48},{40,56},{48,0},{56,8},{1,17}... | collective-permute-start | bytes 3145736 | tf_op jit(solution)/shard_map/ppermute | solution.py:36
  52.0 0.7 shard_map.95
  52.7 4.3 %all-to-all-start.1 = ((bf16[4,2,16,1024]{3,2,1,0:T(8,128)(2,1)}), bf16[4,2,16,1024]{3,2,1,0:T(8,128)(2,1)S(1)}, u32[]{:S(2)}, u32[]{:S(2)}) async-start(bf16[4,2,16,1024]{3,2,1,0:T(8,128)(2,1)} %shard_map.95), calls=%async_computation.1 | async-start | bytes 524288 | tf_op jit(solution)/shard_map/all_to_all | solution.py:27
  57.0 6.7 %all-to-all-done.1.images = bf16[4,2,16,1024]{3,2,1,0:T(8,128)(2,1)S(1)} async-done(((bf16[4,2,16,1024]{3,2,1,0:T(8,128)(2,1)}), bf16[4,2,16,1024]{3,2,1,0:T(8,128)(2,1)S(1)}, u32[]{:S(2)}, u32[]{:S(2)}) %all-to-all-start.1) | async-done | bytes 262176 | tf_op jit(solution)/shard_map/all_to_all | solution.py:27
  63.7 0.0 collective-permute-done.8.far
  63.7 3.2 %shard_map.96 = bf16[8,128,256]{2,1,0:T(8,128)(2,1)} custom-call(s32[8]{0:T(128)S(1)} %iota_xor_fusion.head_ref, s32[1]{0:T(128)} %bitcast.4.half_ref, bf16[4,2,16,1024]{3,2,1,0:T(8,128)(2,1)S(1)} %all-to-all-done.1.images, bf16[4,1024,256]{2,1,0:T(8,128)(2,1)S(1)} %all-to-all-done.near, bf16[4,1024,256]{2,1,0:T(8,128)(2,1)} %collective-permute-done.8.far), custom_call_target="tpu_custom_call" | custom-call | tf_op jit(solution)/shard_map/pallas_call | solution.py:56
  66.8 12.5 %all-to-all-start.2 = ((bf16[8,128,256]{2,1,0:T(8,128)(2,1)}), bf16[8,128,256]{2,1,0:T(8,128)(2,1)S(1)}, u32[]{:S(2)}, u32[]{:S(2)}) async-start(bf16[8,128,256]{2,1,0:T(8,128)(2,1)} %shard_map.96), calls=%async_computation.2 | async-start | bytes 1048576 | tf_op jit(solution)/shard_map/all_to_all | solution.py:222
  79.3 1.9 %collective-permute-start.3 = (bf16[1024,512]{1,0:T(8,128)(2,1)}, bf16[1024,512]{1,0:T(8,128)(2,1)}, u32[]{:S(2)}, u32[]{:S(2)}) collective-permute-start(bf16[1024,512]{1,0:T(8,128)(2,1)} %bitcast.refs_0_), channel_id=1, source_target_pairs={{0,8},{8,0},{16,24},{24,16},{32,40},{40,32},{48,56},{56,48},{1,9},... | collective-permute-start | bytes 3145736 | tf_op jit(solution)/shard_map/ppermute | solution.py:46
  81.3 0.0 collective-permute-done.6.refs_6_
  81.3 2.4 %collective-permute-start.7 = (bf16[1024,512]{1,0:T(8,128)(2,1)}, bf16[1024,512]{1,0:T(8,128)(2,1)}, u32[]{:S(2)}, u32[]{:S(2)}) collective-permute-start(bf16[1024,512]{1,0:T(8,128)(2,1)} %collective-permute-done.6.refs_6_), channel_id=1, source_target_pairs={{0,8},{8,0},{16,24},{24,16},{32,40},{40,32},{48,56},{56,48},{1,9},... | collective-permute-start | bytes 3145736 | tf_op jit(solution)/shard_map/ppermute | solution.py:46
  83.7 9.6 %collective-permute-done.1.refs_4_ = bf16[1024,512]{1,0:T(8,128)(2,1)} collective-permute-done((bf16[1024,512]{1,0:T(8,128)(2,1)}, bf16[1024,512]{1,0:T(8,128)(2,1)}, u32[]{:S(2)}, u32[]{:S(2)}) %collective-permute-start.1) | collective-permute-done | bytes 1048608 | tf_op jit(solution)/shard_map/ppermute | solution.py:36
  93.2 2.2 %collective-permute-done.2.refs_2_ = bf16[1024,512]{1,0:T(8,128)(2,1)} collective-permute-done((bf16[1024,512]{1,0:T(8,128)(2,1)}, bf16[1024,512]{1,0:T(8,128)(2,1)}, u32[]{:S(2)}, u32[]{:S(2)}) %collective-permute-start.2) | collective-permute-done | bytes 1048608 | tf_op jit(solution)/shard_map/ppermute | solution.py:36
  95.5 1.9 %collective-permute-start.4 = (bf16[1024,512]{1,0:T(8,128)(2,1)}, bf16[1024,512]{1,0:T(8,128)(2,1)}, u32[]{:S(2)}, u32[]{:S(2)}) collective-permute-start(bf16[1024,512]{1,0:T(8,128)(2,1)} %collective-permute-done.2.refs_2_), channel_id=1, source_target_pairs={{0,8},{8,0},{16,24},{24,16},{32,40},{40,32},{48,56},{56,48},{1,9},... | collective-permute-start | bytes 3145736 | tf_op jit(solution)/shard_map/ppermute | solution.py:46
  97.4 2.4 %collective-permute-start.5 = (bf16[1024,512]{1,0:T(8,128)(2,1)}, bf16[1024,512]{1,0:T(8,128)(2,1)}, u32[]{:S(2)}, u32[]{:S(2)}) collective-permute-start(bf16[1024,512]{1,0:T(8,128)(2,1)} %collective-permute-done.1.refs_4_), channel_id=1, source_target_pairs={{0,8},{8,0},{16,24},{24,16},{32,40},{40,32},{48,56},{56,48},{1,9},... | collective-permute-start | bytes 3145736 | tf_op jit(solution)/shard_map/ppermute | solution.py:46
  100.5 0.5 and_or_fusion.dp_ref
  101.0 0.0 collective-permute-done.3.refs_1_
  101.0 7.8 %all-to-all-done.2.refs_8_ = bf16[8,128,256]{2,1,0:T(8,128)(2,1)S(1)} async-done(((bf16[8,128,256]{2,1,0:T(8,128)(2,1)}), bf16[8,128,256]{2,1,0:T(8,128)(2,1)S(1)}, u32[]{:S(2)}, u32[]{:S(2)}) %all-to-all-start.2) | async-done | bytes 524320 | tf_op jit(solution)/shard_map/all_to_all | solution.py:222
  108.8 0.0 collective-permute-done.5.refs_5_
  108.8 0.8 copy-done.2
  109.6 8.7 %shard_map.97 = (bf16[160,512]{1,0:T(8,128)(2,1)}, bf16[1,128,256]{2,1,0:T(8,128)(2,1)}) custom-call(s32[8]{0:T(128)} %and_or_fusion.dp_ref, bf16[8,160,1024]{2,1,0:T(8,128)(2,1)} %all-gather.2.cloned.1.call-done.features, bf16[1024,512]{1,0:T(8,128)(2,1)} %bitcast.refs_0_, bf16[1024,512]{1,0:T(8,128)(2,1)} %collective-permute-done.3.refs_1_, ...), custom_call_target="tpu_custom_call" | custom-call | flops 1342177280 | bytes 11010048 | tf_op jit(solution)/shard_map/pallas_call | solution.py:56
  118.3 2.2 %collective-permute-start.10 = (bf16[1,128,256]{2,1,0:T(8,128)(2,1)}, bf16[1,128,256]{2,1,0:T(8,128)(2,1)S(1)}, u32[]{:S(2)}, u32[]{:S(2)}) collective-permute-start(bf16[1,128,256]{2,1,0:T(8,128)(2,1)} %get-tuple-element.23.own), channel_id=1, source_target_pairs={{0,4},{1,5},{2,6},{3,7},{4,0},{5,1},{6,2},{7,3},{8,12},{9,13},{10,... | collective-permute-start | bytes 196616 | tf_op jit(solution)/shard_map/ppermute | solution.py:31
  120.5 3.6 %collective-permute-start.9 = (bf16[1,128,256]{2,1,0:T(8,128)(2,1)}, bf16[1,128,256]{2,1,0:T(8,128)(2,1)S(1)}, u32[]{:S(2)}, u32[]{:S(2)}) collective-permute-start(bf16[1,128,256]{2,1,0:T(8,128)(2,1)} %get-tuple-element.23.own), channel_id=1, source_target_pairs={{0,1},{1,0},{2,3},{3,2},{4,5},{5,4},{6,7},{7,6},{8,9},{9,8},{10,11... | collective-permute-start | bytes 196616 | tf_op jit(solution)/shard_map/ppermute | solution.py:31
  124.1 5.4 %collective-permute-done.10.by4 = bf16[1,128,256]{2,1,0:T(8,128)(2,1)S(1)} collective-permute-done((bf16[1,128,256]{2,1,0:T(8,128)(2,1)}, bf16[1,128,256]{2,1,0:T(8,128)(2,1)S(1)}, u32[]{:S(2)}, u32[]{:S(2)}) %collective-permute-start.10) | collective-permute-done | bytes 65568 | tf_op jit(solution)/shard_map/ppermute | solution.py:31
  129.5 0.9 pad_maximum_fusion.1
  130.3 3.8 %collective-permute-start.11 = (bf16[2,128,256]{2,1,0:T(8,128)(2,1)S(1)}, bf16[2,128,256]{2,1,0:T(8,128)(2,1)S(1)}, u32[]{:S(2)}, u32[]{:S(2)}) collective-permute-start(bf16[2,128,256]{2,1,0:T(8,128)(2,1)S(1)} %pad_maximum_fusion.1), channel_id=1, source_target_pairs={{0,2},{1,3},{2,0},{3,1},{4,6},{5,7},{6,4},{7,5},{8,10},{9,11},{10,... | collective-permute-start | bytes 393224 | tf_op jit(solution)/shard_map/ppermute | solution.py:31
  134.1 2.5 %collective-permute-start.12 = (bf16[1,128,256]{2,1,0:T(8,128)(2,1)S(1)}, bf16[1,128,256]{2,1,0:T(8,128)(2,1)S(1)}, u32[]{:S(2)}, u32[]{:S(2)}) collective-permute-start(bf16[1,128,256]{2,1,0:T(8,128)(2,1)S(1)} %collective-permute-done.10.by4), channel_id=1, source_target_pairs={{0,1},{1,0},{2,3},{3,2},{4,5},{5,4},{6,7},{7,6},{8,9},{9,8},{10,11... | collective-permute-start | bytes 196616 | tf_op jit(solution)/shard_map/ppermute | solution.py:31
  136.6 4.5 %collective-permute-done.12.by5 = bf16[1,128,256]{2,1,0:T(8,128)(2,1)S(1)} collective-permute-done((bf16[1,128,256]{2,1,0:T(8,128)(2,1)S(1)}, bf16[1,128,256]{2,1,0:T(8,128)(2,1)S(1)}, u32[]{:S(2)}, u32[]{:S(2)}) %collective-permute-start.12) | collective-permute-done | bytes 65568 | tf_op jit(solution)/shard_map/ppermute | solution.py:31
  141.1 1.9 %collective-permute-start.13 = (bf16[2,128,256]{2,1,0:T(8,128)(2,1)S(1)}, bf16[2,128,256]{2,1,0:T(8,128)(2,1)S(1)}, u32[]{:S(2)}, u32[]{:S(2)}) collective-permute-start(bf16[2,128,256]{2,1,0:T(8,128)(2,1)S(1)} %collective-permute-done.11.by2), channel_id=1, source_target_pairs={{0,1},{1,0},{2,3},{3,2},{4,5},{5,4},{6,7},{7,6},{8,9},{9,8},{10,11... | collective-permute-start | bytes 393224 | tf_op jit(solution)/shard_map/ppermute | solution.py:31
  143.0 0.0 copy-start
  143.0 0.8 copy-done
  143.9 2.7 %shard_map.98.early = f32[128,1024]{1,0:T(8,128)S(1)} custom-call(s32[8]{0:T(128)S(1)} %xor_shift-right-arithmetic_fusion.y_ref, s32[1]{0:T(128)} %bitcast.8.flip_ref, bf16[1,128,256]{2,1,0:T(8,128)(2,1)S(1)} %copy-done, bf16[1,128,256]{2,1,0:T(8,128)(2,1)S(1)} %collective-permute-done.10.by4, bf16[2,128,256]{2,1,0:T(8,128)(2,1)S(1)} %collective-permute-done.11.by2, ...), custom_call_target="tpu_custom_call" | custom-call | flops 402653184 | bytes 5111808 | tf_op jit(solution)/shard_map/pallas_call | solution.py:56
  146.6 1.8 collective-permute-done.13.by3
  148.4 2.1 %shard_map.99 = bf16[4,2,16,1024]{3,2,1,0:T(8,128)(2,1)S(1)} custom-call(s32[8]{0:T(128)S(1)} %xor_shift-right-arithmetic_fusion.y_ref, s32[1]{0:T(128)} %bitcast.8.flip_ref, s32[1]{0:T(128)} %bitcast.4.half_ref, f32[128,1024]{1,0:T(8,128)S(1)} %shard_map.98.early, bf16[2,128,256]{2,1,0:T(8,128)(2,1)S(1)} %collective-permute-done.13.by3, ...), custom_call_target="tpu_custom_call" | custom-call | tf_op jit(solution)/shard_map/pallas_call | solution.py:56
  150.5 11.9 %all_to_all.20.arrived = bf16[4,2,16,1024]{3,2,1,0:T(8,128)(2,1)S(1)} all-to-all(bf16[4,2,16,1024]{3,2,1,0:T(8,128)(2,1)S(1)} %shard_map.99), channel_id=1, replica_groups={{0,64,128,192},{256,320,384,448},{1,65,129,193},{257,321,385,449},{2,66..., dimensions={0} | all-to-all | bytes 524288 | tf_op jit(solution)/shard_map/all_to_all | solution.py:27
  162.5 10.0 %collective-permute-start.14 = (bf16[16,1024]{1,0:T(8,128)(2,1)S(1)}, bf16[16,1024]{1,0:T(8,128)(2,1)S(1)}, u32[]{:S(2)}, u32[]{:S(2)}) collective-permute-start(bf16[16,1024]{1,0:T(8,128)(2,1)S(1)} %get-tuple-element.29), channel_id=1, source_target_pairs={{0,256},{64,320},{128,384},{192,448},{256,0},{320,64},{384,128},{4... | collective-permute-start | bytes 98312 | tf_op jit(solution)/shard_map/ppermute | solution.py:22
  172.5 5.2 %collective-permute-done.14 = bf16[16,1024]{1,0:T(8,128)(2,1)S(1)} collective-permute-done((bf16[16,1024]{1,0:T(8,128)(2,1)S(1)}, bf16[16,1024]{1,0:T(8,128)(2,1)S(1)}, u32[]{:S(2)}, u32[]{:S(2)}) %collective-permute-start.14) | collective-permute-done | bytes 32800 | tf_op jit(solution)/shard_map/ppermute | solution.py:22
  177.7 0.6 add_bitcast_fusion
  (11 shorter events, 0.1 us)
Async XLA Ops:
  7.2 88.3 %all-gather.2.cloned.1.call-start = ((), (), s32[]{:S(2)}) async-start(), calls=%async_computation.4 | async-start | bytes 2949120 | tf_op jit(solution)/shard_map/all_gather | solution.py:199
  10.5 9.3 %copy-start.1 = (bf16[1,16,1024]{2,1,0:T(8,128)(2,1)S(1)}, bf16[1,16,1024]{2,1,0:T(8,128)(2,1)}, u32[]{:S(2)}) copy-start(bf16[1,16,1024]{2,1,0:T(8,128)(2,1)} %param.12) | copy-start | bytes 98308
  10.5 29.1 %all-to-all-start = ((bf16[4,1024,256]{2,1,0:T(8,128)(2,1)}), bf16[4,1024,256]{2,1,0:T(8,128)(2,1)S(1)}, u32[]{:S(2)}, u32[]{:S(2)}) async-start(bf16[4,1024,256]{2,1,0:T(8,128)(2,1)} %broadcast_in_dim.16), calls=%async_computation | async-start | bytes 4194304 | tf_op jit(solution)/shard_map/all_to_all | solution.py:42
  19.8 14.5 %collective-permute-start = (bf16[16,1024]{1,0:T(8,128)(2,1)S(1)}, bf16[16,1024]{1,0:T(8,128)(2,1)S(1)}, u32[]{:S(2)}, u32[]{:S(2)}) collective-permute-start(bf16[16,1024]{1,0:T(8,128)(2,1)S(1)} %bitcast.12), channel_id=1, source_target_pairs={{0,256},{64,320},{128,384},{192,448},{256,0},{320,64},{384,128},{4... | collective-permute-start | bytes 98312 | tf_op jit(solution)/shard_map/ppermute | solution.py:22
  39.6 24.1 %collective-permute-start.8 = (bf16[4,1024,256]{2,1,0:T(8,128)(2,1)S(1)}, bf16[4,1024,256]{2,1,0:T(8,128)(2,1)}, u32[]{:S(2)}, u32[]{:S(2)}) collective-permute-start(bf16[4,1024,256]{2,1,0:T(8,128)(2,1)S(1)} %all-to-all-done.near), channel_id=1, source_target_pairs={{0,8},{8,0},{16,24},{24,16},{32,40},{40,32},{48,56},{56,48},{1,9},... | collective-permute-start | bytes 6291464 | tf_op jit(solution)/shard_map/ppermute | solution.py:46
  41.5 39.8 %collective-permute-start.6 = (bf16[1024,512]{1,0:T(8,128)(2,1)}, bf16[1024,512]{1,0:T(8,128)(2,1)}, u32[]{:S(2)}, u32[]{:S(2)}) collective-permute-start(bf16[1024,512]{1,0:T(8,128)(2,1)} %bitcast.refs_0_), channel_id=1, source_target_pairs={{0,48},{8,56},{16,0},{24,8},{32,16},{40,24},{48,32},{56,40},{1,49}... | collective-permute-start | bytes 3145736 | tf_op jit(solution)/shard_map/ppermute | solution.py:36
  43.4 49.8 %collective-permute-start.1 = (bf16[1024,512]{1,0:T(8,128)(2,1)}, bf16[1024,512]{1,0:T(8,128)(2,1)}, u32[]{:S(2)}, u32[]{:S(2)}) collective-permute-start(bf16[1024,512]{1,0:T(8,128)(2,1)} %bitcast.refs_0_), channel_id=1, source_target_pairs={{0,32},{8,40},{16,48},{24,56},{32,0},{40,8},{48,16},{56,24},{1,33}... | collective-permute-start | bytes 3145736 | tf_op jit(solution)/shard_map/ppermute | solution.py:36
  48.9 46.6 %collective-permute-start.2 = (bf16[1024,512]{1,0:T(8,128)(2,1)}, bf16[1024,512]{1,0:T(8,128)(2,1)}, u32[]{:S(2)}, u32[]{:S(2)}) collective-permute-start(bf16[1024,512]{1,0:T(8,128)(2,1)} %bitcast.refs_0_), channel_id=1, source_target_pairs={{0,16},{8,24},{16,32},{24,40},{32,48},{40,56},{48,0},{56,8},{1,17}... | collective-permute-start | bytes 3145736 | tf_op jit(solution)/shard_map/ppermute | solution.py:36
  52.7 11.0 %all-to-all-start.1 = ((bf16[4,2,16,1024]{3,2,1,0:T(8,128)(2,1)}), bf16[4,2,16,1024]{3,2,1,0:T(8,128)(2,1)S(1)}, u32[]{:S(2)}, u32[]{:S(2)}) async-start(bf16[4,2,16,1024]{3,2,1,0:T(8,128)(2,1)} %shard_map.95), calls=%async_computation.1 | async-start | bytes 524288 | tf_op jit(solution)/shard_map/all_to_all | solution.py:27
  66.8 41.9 %all-to-all-start.2 = ((bf16[8,128,256]{2,1,0:T(8,128)(2,1)}), bf16[8,128,256]{2,1,0:T(8,128)(2,1)S(1)}, u32[]{:S(2)}, u32[]{:S(2)}) async-start(bf16[8,128,256]{2,1,0:T(8,128)(2,1)} %shard_map.96), calls=%async_computation.2 | async-start | bytes 1048576 | tf_op jit(solution)/shard_map/all_to_all | solution.py:222
  79.3 21.7 %collective-permute-start.3 = (bf16[1024,512]{1,0:T(8,128)(2,1)}, bf16[1024,512]{1,0:T(8,128)(2,1)}, u32[]{:S(2)}, u32[]{:S(2)}) collective-permute-start(bf16[1024,512]{1,0:T(8,128)(2,1)} %bitcast.refs_0_), channel_id=1, source_target_pairs={{0,8},{8,0},{16,24},{24,16},{32,40},{40,32},{48,56},{56,48},{1,9},... | collective-permute-start | bytes 3145736 | tf_op jit(solution)/shard_map/ppermute | solution.py:46
  81.3 19.7 %collective-permute-start.7 = (bf16[1024,512]{1,0:T(8,128)(2,1)}, bf16[1024,512]{1,0:T(8,128)(2,1)}, u32[]{:S(2)}, u32[]{:S(2)}) collective-permute-start(bf16[1024,512]{1,0:T(8,128)(2,1)} %collective-permute-done.6.refs_6_), channel_id=1, source_target_pairs={{0,8},{8,0},{16,24},{24,16},{32,40},{40,32},{48,56},{56,48},{1,9},... | collective-permute-start | bytes 3145736 | tf_op jit(solution)/shard_map/ppermute | solution.py:46
  95.5 13.3 %collective-permute-start.4 = (bf16[1024,512]{1,0:T(8,128)(2,1)}, bf16[1024,512]{1,0:T(8,128)(2,1)}, u32[]{:S(2)}, u32[]{:S(2)}) collective-permute-start(bf16[1024,512]{1,0:T(8,128)(2,1)} %collective-permute-done.2.refs_2_), channel_id=1, source_target_pairs={{0,8},{8,0},{16,24},{24,16},{32,40},{40,32},{48,56},{56,48},{1,9},... | collective-permute-start | bytes 3145736 | tf_op jit(solution)/shard_map/ppermute | solution.py:46
  97.4 11.4 %collective-permute-start.5 = (bf16[1024,512]{1,0:T(8,128)(2,1)}, bf16[1024,512]{1,0:T(8,128)(2,1)}, u32[]{:S(2)}, u32[]{:S(2)}) collective-permute-start(bf16[1024,512]{1,0:T(8,128)(2,1)} %collective-permute-done.1.refs_4_), channel_id=1, source_target_pairs={{0,8},{8,0},{16,24},{24,16},{32,40},{40,32},{48,56},{56,48},{1,9},... | collective-permute-start | bytes 3145736 | tf_op jit(solution)/shard_map/ppermute | solution.py:46
  108.8 0.8 copy-start.2
  118.3 11.2 %collective-permute-start.10 = (bf16[1,128,256]{2,1,0:T(8,128)(2,1)}, bf16[1,128,256]{2,1,0:T(8,128)(2,1)S(1)}, u32[]{:S(2)}, u32[]{:S(2)}) collective-permute-start(bf16[1,128,256]{2,1,0:T(8,128)(2,1)} %get-tuple-element.23.own), channel_id=1, source_target_pairs={{0,4},{1,5},{2,6},{3,7},{4,0},{5,1},{6,2},{7,3},{8,12},{9,13},{10,... | collective-permute-start | bytes 196616 | tf_op jit(solution)/shard_map/ppermute | solution.py:31
  120.5 8.9 %collective-permute-start.9 = (bf16[1,128,256]{2,1,0:T(8,128)(2,1)}, bf16[1,128,256]{2,1,0:T(8,128)(2,1)S(1)}, u32[]{:S(2)}, u32[]{:S(2)}) collective-permute-start(bf16[1,128,256]{2,1,0:T(8,128)(2,1)} %get-tuple-element.23.own), channel_id=1, source_target_pairs={{0,1},{1,0},{2,3},{3,2},{4,5},{5,4},{6,7},{7,6},{8,9},{9,8},{10,11... | collective-permute-start | bytes 196616 | tf_op jit(solution)/shard_map/ppermute | solution.py:31
  130.3 10.8 %collective-permute-start.11 = (bf16[2,128,256]{2,1,0:T(8,128)(2,1)S(1)}, bf16[2,128,256]{2,1,0:T(8,128)(2,1)S(1)}, u32[]{:S(2)}, u32[]{:S(2)}) collective-permute-start(bf16[2,128,256]{2,1,0:T(8,128)(2,1)S(1)} %pad_maximum_fusion.1), channel_id=1, source_target_pairs={{0,2},{1,3},{2,0},{3,1},{4,6},{5,7},{6,4},{7,5},{8,10},{9,11},{10,... | collective-permute-start | bytes 393224 | tf_op jit(solution)/shard_map/ppermute | solution.py:31
  134.1 7.0 %collective-permute-start.12 = (bf16[1,128,256]{2,1,0:T(8,128)(2,1)S(1)}, bf16[1,128,256]{2,1,0:T(8,128)(2,1)S(1)}, u32[]{:S(2)}, u32[]{:S(2)}) collective-permute-start(bf16[1,128,256]{2,1,0:T(8,128)(2,1)S(1)} %collective-permute-done.10.by4), channel_id=1, source_target_pairs={{0,1},{1,0},{2,3},{3,2},{4,5},{5,4},{6,7},{7,6},{8,9},{9,8},{10,11... | collective-permute-start | bytes 196616 | tf_op jit(solution)/shard_map/ppermute | solution.py:31
  141.1 7.3 %collective-permute-start.13 = (bf16[2,128,256]{2,1,0:T(8,128)(2,1)S(1)}, bf16[2,128,256]{2,1,0:T(8,128)(2,1)S(1)}, u32[]{:S(2)}, u32[]{:S(2)}) collective-permute-start(bf16[2,128,256]{2,1,0:T(8,128)(2,1)S(1)} %collective-permute-done.11.by2), channel_id=1, source_target_pairs={{0,1},{1,0},{2,3},{3,2},{4,5},{5,4},{6,7},{7,6},{8,9},{9,8},{10,11... | collective-permute-start | bytes 393224 | tf_op jit(solution)/shard_map/ppermute | solution.py:31
  143.0 0.8 copy-start
  162.5 15.2 %collective-permute-start.14 = (bf16[16,1024]{1,0:T(8,128)(2,1)S(1)}, bf16[16,1024]{1,0:T(8,128)(2,1)S(1)}, u32[]{:S(2)}, u32[]{:S(2)}) collective-permute-start(bf16[16,1024]{1,0:T(8,128)(2,1)S(1)} %get-tuple-element.29), channel_id=1, source_target_pairs={{0,256},{64,320},{128,384},{192,448},{256,0},{320,64},{384,128},{4... | collective-permute-start | bytes 98312 | tf_op jit(solution)/shard_map/ppermute | solution.py:22
Sparse Core Ops, SparseCore 0:
  10.1 79.3 all-gather.1
